TPU v7x, 512 devices: a whole 4x4x16 slice. The times are simulated.
512 devices in a mesh: dp: 64 (over y, z), tensor: 8 (over x, core).
Axes of the slice: x: 4, y: 4, z: 16, core: 2. Of those that a mesh axis runs over, the one named last changes fastest.
Arguments:
- features: bfloat16 [8192, 8192], P('dp', 'tensor'), may hold values from -300 to 300
- gate_pre: bfloat16 [8192, 14336], P('dp', 'tensor'), may hold values from -6 to 6
- up_pre: bfloat16 [8192, 14336], P('dp', 'tensor'), may hold values from -6 to 6
- hidden_grad: bfloat16 [8192, 14336], P('dp', 'tensor'), may hold values from -6 to 6
- tile_rows: int32 [8, 112], P('tensor'), may hold values from 0 to 63, as said below
- tile_cols: int32 [8, 112], P('tensor'), may hold values from 0 to 13, as said below
- owner_counts: int32 [8, 64], P('tensor'), may hold values from 1 to 2, 112 in all within a row
- delta_value: float32 [8, 128, 128, 128], P('tensor', 'dp'), may hold values from -1 to 1
- moment_one: float32 [8, 128, 128, 128], P('tensor', 'dp'), may hold values from -6 to 6
- moment_two: float32 [8, 128, 128, 128], P('tensor', 'dp'), may hold values from 0.05 to 5
Outputs:
- input_grad: bfloat16 [8192, 8192], P('dp')
- new_delta: float32 [8, 128, 128, 128], P('tensor', 'dp')
- new_moment_one: float32 [8, 128, 128, 128], P('tensor', 'dp')
- new_moment_two: float32 [8, 128, 128, 128], P('tensor', 'dp')
Inputs may be any that keep to these rules, and one draw needn't show every extreme that they name: `tile_rows`: in each tensor shard the 112 tiles are distinct cells and are listed in increasing order of row tile, then column tile. `tile_cols`: pairs with tile_rows. `owner_counts`: each row sums to 112; the largest entry of each row is 2.
All inputs are finite; a program needn't handle non-finite values.
Results may differ from a plain program's by a relative error of at most 0.013.
Values may be sent and summed in bfloat16 or wider, within the bound.
No kernel may reach another device: no remote copies, remote signals or barrier semaphores. Data moves between devices by JAX's collectives and lax.ppermute only.
A program may use at most 128 MiB of HBM per device.

v0:
```python
import jax
import jax.numpy as jnp
from jax import lax
from jax.sharding import PartitionSpec as P


def slot_maps(counts, tile_total, slot_cap):
    owner_total = counts.shape[0]
    ends = jnp.cumsum(counts)
    starts = ends - counts
    slot_rank = jnp.arange(owner_total * slot_cap, dtype=jnp.int32) % slot_cap
    slot_valid = slot_rank < jnp.repeat(counts, slot_cap)
    slot_list = jnp.minimum(jnp.repeat(starts, slot_cap) + slot_rank, tile_total - 1)
    positions = jnp.arange(tile_total, dtype=jnp.int32)
    owner_of = jnp.sum((ends[None, :] <= positions[:, None]).astype(jnp.int32), axis=1)
    owner_ids = jnp.arange(owner_total, dtype=jnp.int32)
    start_of = jnp.sum(
        jnp.where(owner_of[:, None] == owner_ids[None, :], starts[None, :], 0), axis=1
    )
    list_slot = owner_of * slot_cap + positions - start_of
    return (slot_valid, slot_list, list_slot)


def adam_update(grads, valid, delta_value, moment_one, moment_two, factor):
    clipped = factor * grads
    first = 0.9 * moment_one + 0.1 * clipped
    second = 0.95 * moment_two + 0.05 * clipped * clipped
    step_size = first / (1.0 - 0.9**10) / (jnp.sqrt(second / (1.0 - 0.95**10)) + 1e-08)
    updated = delta_value - 0.02 * (step_size + 0.1 * delta_value)
    return (
        jnp.where(valid, updated, delta_value),
        jnp.where(valid, first, moment_one),
        jnp.where(valid, second, moment_two),
    )


def body(
    features,
    gate_pre,
    up_pre,
    hidden_grad,
    tile_rows,
    tile_cols,
    owner_counts,
    delta_value,
    moment_one,
    moment_two,
):
    tile_size = delta_value.shape[-1]
    slot_cap = delta_value.shape[1]
    dp_count = lax.axis_size("dp")
    tensor_count = lax.axis_size("tensor")
    my_owner = lax.axis_index("dp")
    whole = lax.all_gather(features, "tensor", axis=1, tiled=True)
    tok_rows = whole.shape[0]
    width = whole.shape[1]
    row_tiles = width // tile_size
    pre_gate = gate_pre.astype(jnp.float32)
    sig = jax.nn.sigmoid(pre_gate)
    gate_grad = (
        hidden_grad.astype(jnp.float32)
        * up_pre.astype(jnp.float32)
        * sig
        * (1.0 + pre_gate * (1.0 - sig))
    ).astype(jnp.bfloat16)
    tile_row = tile_rows[0]
    tile_col = tile_cols[0]
    counts = owner_counts[0]
    tile_total = tile_row.shape[0]
    x_tiles = jnp.take(whole.reshape(tok_rows, row_tiles, tile_size), tile_row, axis=1)
    g_tiles = jnp.take(gate_grad.reshape(tok_rows, -1, tile_size), tile_col, axis=1)
    slot_valid, slot_list, list_slot = slot_maps(counts, tile_total, slot_cap)
    partial_grads = jnp.einsum("tkr,tkc->krc", x_tiles, g_tiles, preferred_element_type=jnp.float32)
    slot_terms = jnp.where(
        slot_valid[:, None, None], jnp.take(partial_grads, slot_list, axis=0), 0.0
    )
    arrived = lax.all_to_all(
        slot_terms.reshape(dp_count, slot_cap, tile_size, tile_size).astype(jnp.bfloat16),
        "dp",
        split_axis=0,
        concat_axis=0,
        tiled=True,
    ).astype(jnp.float32)
    own_grad = jnp.sum(arrived, axis=0)
    own_count = lax.dynamic_index_in_dim(counts, my_owner, axis=0, keepdims=False)
    own_valid = (jnp.arange(slot_cap, dtype=jnp.int32) < own_count)[None, :, None, None]
    own_grad = jnp.where(own_valid, own_grad[None], 0.0)
    squares = lax.psum(jnp.sum(own_grad * own_grad), ("dp", "tensor"))
    root_mean = jnp.sqrt(squares / (tensor_count * tile_total * tile_size * tile_size) + 1e-06)
    factor = jnp.minimum(1.0, 1.0 / root_mean)
    new_delta, new_first, new_second = adam_update(
        own_grad, own_valid, delta_value, moment_one, moment_two, factor
    )
    delta_all = lax.all_gather(delta_value.astype(jnp.bfloat16), "dp", axis=1, tiled=True)
    delta_list = jnp.take(delta_all[0], list_slot, axis=0)
    contribs = jnp.einsum("tkc,krc->ktr", g_tiles, delta_list, preferred_element_type=jnp.float32)
    onehot = (tile_row[None, :] == jnp.arange(row_tiles, dtype=jnp.int32)[:, None]).astype(
        jnp.float32
    )
    blocks = jnp.dot(
        onehot,
        contribs.reshape(tile_total, tok_rows * tile_size),
        precision=lax.Precision.HIGHEST,
        preferred_element_type=jnp.float32,
    )
    partial_value = (
        blocks.reshape(row_tiles, tok_rows, tile_size)
        .transpose(1, 0, 2)
        .reshape(tok_rows, width)
        .astype(jnp.bfloat16)
    )
    input_grad = lax.psum(partial_value, "tensor").astype(jnp.float32).astype(jnp.bfloat16)
    return (input_grad, new_delta, new_first, new_second)


def solution(mesh):
    placed = (
        P("dp", "tensor"),
        P("dp", "tensor"),
        P("dp", "tensor"),
        P("dp", "tensor"),
        P("tensor", None),
        P("tensor", None),
        P("tensor", None),
        P("tensor", "dp", None, None),
        P("tensor", "dp", None, None),
        P("tensor", "dp", None, None),
    )
    return jax.shard_map(
        body,
        mesh=mesh,
        in_specs=placed,
        out_specs=(
            P("dp", None),
            P("tensor", "dp", None, None),
            P("tensor", "dp", None, None),
            P("tensor", "dp", None, None),
        ),
        check_vma=False,
    )
```

profile of v0, /device:TPU:1, one launch (start us, length us, event | category | flops | bytes accessed | tf_op | source)
XLA Modules:
  0.0 626.4 jit_solution(330092692168806555)
XLA Ops:
  7.2 0.0 copy-start.5
  7.2 0.0 all-gather.5.cloned.1.call-start
  7.2 1.8 copy.61
  9.0 0.0 all-gather.5.cloned.1.call-update
  9.0 0.7 broadcast_compare_fusion
  9.7 0.1 copy.59
  9.8 0.7 copy.56
  10.6 0.1 reduce-window.4
  10.7 0.1 reduce.1
  10.8 0.7 bitcast_subtract_fusion.2
  11.5 0.1 copy.60
  11.6 0.1 broadcast_in_dim.118.clone
  11.7 0.1 reshape.256
  11.8 1.3 copy.54
  13.1 1.3 copy.53
  14.4 1.3 copy.52
  15.6 0.4 fusion.22
  16.1 0.3 copy.55
  16.3 0.0 copy-done.5
  16.4 0.0 copy-start.3
  16.4 2.9 gather_fusion
  19.3 0.0 copy-done.3
  19.4 29.9 %all-gather.5.cloned.1.call-done = bf16[128,8192]{0,1:T(8,128)(2,1)} async-done(((bf16[128,1024]{0,1:T(8,128)(2,1)}), bf16[128,8192]{0,1:T(8,128)(2,1)}) %all-gather.5.cloned.1.call-update) | async-done | bytes 2097168 | tf_op jit(solution)/shard_map/all_gather | solution.py:54
  49.3 3.2 copy.62
  52.5 2.9 gather_fusion.2
  55.4 6.6 %fusion.3 = bf16[112,128,128]{2,1,0:T(8,128)(2,1)} fusion(bf16[112,128,128]{2,1,0:T(8,128)(2,1)} %gather_fusion.2, pred[112]{0:T(512)(128)(4,1)S(1)} %get-tuple-element.8, bf16[112,128,128]{2,1,0:T(8,128)(2,1)} %gather_fusion, pred[112]{0:T(512)(128)(4,1)S(1)} %get-tuple-element.9), kind=kOutput, calls=%fused_computation.10 | convolution fusion | flops 473432064 | bytes 11010272 | tf_op jit(solution)/shard_map/tkr,tkc->krc/dot_general | solution.py:73
  62.0 5.0 gather_fusion.3
  67.0 4.3 select_convert_fusion
  71.3 0.0 copy-start.4
  71.3 15.8 %all-to-all-start = ((bf16[64,2,128,128]{3,2,1,0:T(8,128)(2,1)}), bf16[64,2,128,128]{3,2,1,0:T(8,128)(2,1)}, u32[]{:S(2)}, u32[]{:S(2)}) async-start(bf16[64,2,128,128]{3,2,1,0:T(8,128)(2,1)} %select_convert_fusion), calls=%async_computation | async-start | bytes 8388608 | tf_op jit(solution)/shard_map/all_to_all | solution.py:77
  87.1 0.0 copy-start
  87.1 0.0 copy-start.1
  87.1 0.0 copy-start.2
  87.1 0.0 all-gather.3.cloned.1.call-start
  87.2 0.0 copy-done.4
  87.2 0.6 constant_dynamic-slice_fusion
  87.8 0.6 iota_compare_fusion.3
  88.4 182.3 %all-to-all-done = bf16[64,2,128,128]{3,2,1,0:T(8,128)(2,1)} async-done(((bf16[64,2,128,128]{3,2,1,0:T(8,128)(2,1)}), bf16[64,2,128,128]{3,2,1,0:T(8,128)(2,1)}, u32[]{:S(2)}, u32[]{:S(2)}) %all-to-all-start) | async-done | bytes 4194336 | tf_op jit(solution)/shard_map/all_to_all | solution.py:77
  270.7 2.9 convert_reduce_fusion
  273.6 0.7 multiply_reduce_fusion
  274.3 105.1 %psum.15 = f32[]{:T(128)} all-reduce(f32[]{:T(128)} %multiply_reduce_fusion), channel_id=1, replica_groups=mesh['dp'=64,'tensor'=8] {'dp','tensor'}, use_global_device_ids=true, to_apply=%region_6.7 | all-reduce | flops 1 | bytes 8 | tf_op jit(solution)/shard_map/psum | solution.py:88
  380.1 0.0 copy-done
  380.1 0.0 copy-done.1
  380.1 0.0 copy-done.2
  380.1 1.0 fusion.26
  381.1 0.0 all-gather.3.cloned.1.call-update
  381.1 0.2 all-reduce.2.cloned.1.call-start
  381.4 0.1 convert_reduce_fusion.1
  381.5 0.1 select_reduce_fusion
  381.6 129.3 %all-gather.3.cloned.1.call-done = bf16[1,128,128,128]{3,2,0,1:T(8,128)(2,1)} async-done(((bf16[1,2,128,128]{3,2,0,1:T(8,128)(2,1)}), bf16[1,128,128,128]{3,2,0,1:T(8,128)(2,1)}) %all-gather.3.cloned.1.call-update) | async-done | bytes 4194320 | tf_op jit(solution)/shard_map/all_gather | solution.py:94
  511.0 5.1 gather_fusion.1
  516.0 5.9 fusion.6
  521.9 9.5 %fusion.12 = bf16[64,128,128]{2,0,1:T(8,128)(2,1)S(1)} fusion(s32[112]{0:T(128)S(1)} %bitcast.94, f32[14,8,128,128]{3,2,1,0:T(8,128)S(1)} %bitcast.87), kind=kOutput, calls=%fused_computation.21 | convolution fusion | flops 1410341888 | bytes 9437632 | tf_op jit(solution)/shard_map/dot_general | solution.py:100
  531.4 3.1 copy.79
  534.6 0.0 all-reduce.2.cloned.1.call-update
  534.6 82.2 %all-reduce.2.cloned.1.call-done = bf16[128,8192]{1,0:T(8,128)(2,1)} async-done(((bf16[128,8192]{1,0:T(8,128)(2,1)}), bf16[128,8192]{1,0:T(8,128)(2,1)}) %all-reduce.2.cloned.1.call-update) | async-done | bytes 2097168 | tf_op jit(solution)/shard_map/psum | solution.py:112
  616.8 3.1 copy.81
  (12 shorter events, 0.1 us)
Async XLA Ops:
  7.2 9.2 %copy-start.5 = (s32[1,112]{1,0:T(1,128)S(1)}, s32[1,112]{1,0:T(1,128)}, u32[]{:S(2)}) copy-start(s32[1,112]{1,0:T(1,128)} %param.15) | copy-start | bytes 1348
  7.2 42.1 %all-gather.5.cloned.1.call-start = ((), (), s32[]{:S(2)}) async-start(), calls=%async_computation.3 | async-start | bytes 2359296 | tf_op jit(solution)/shard_map/all_gather | solution.py:54
  16.4 3.0 copy-start.3
  71.3 15.9 %copy-start.4 = (s32[1,64]{1,0:T(1,128)S(1)}, s32[1,64]{1,0:T(1,128)}, u32[]{:S(2)}) copy-start(s32[1,64]{1,0:T(1,128)} %param.16) | copy-start | bytes 772
  71.3 199.4 %all-to-all-start = ((bf16[64,2,128,128]{3,2,1,0:T(8,128)(2,1)}), bf16[64,2,128,128]{3,2,1,0:T(8,128)(2,1)}, u32[]{:S(2)}, u32[]{:S(2)}) async-start(bf16[64,2,128,128]{3,2,1,0:T(8,128)(2,1)} %select_convert_fusion), calls=%async_computation | async-start | bytes 8388608 | tf_op jit(solution)/shard_map/all_to_all | solution.py:77
  87.1 293.0 %copy-start = (f32[1,2,128,128]{3,2,1,0:T(8,128)S(1)}, f32[1,2,128,128]{3,2,1,0:T(8,128)}, u32[]{:S(2)}) copy-start(f32[1,2,128,128]{3,2,1,0:T(8,128)} %param.19) | copy-start | bytes 393220
  87.1 293.0 %copy-start.1 = (f32[1,2,128,128]{3,2,1,0:T(8,128)S(1)}, f32[1,2,128,128]{3,2,1,0:T(8,128)}, u32[]{:S(2)}) copy-start(f32[1,2,128,128]{3,2,1,0:T(8,128)} %param.17) | copy-start | bytes 393220
  87.1 293.0 %copy-start.2 = (f32[1,2,128,128]{3,2,1,0:T(8,128)S(1)}, f32[1,2,128,128]{3,2,1,0:T(8,128)}, u32[]{:S(2)}) copy-start(f32[1,2,128,128]{3,2,1,0:T(8,128)} %param.18) | copy-start | bytes 393220
  87.1 423.8 %all-gather.3.cloned.1.call-start = ((), (), s32[]{:S(2)}) async-start(), calls=%async_computation.1 | async-start | bytes 4259840 | tf_op jit(solution)/shard_map/all_gather | solution.py:94
  381.1 235.7 %all-reduce.2.cloned.1.call-start = ((), (), s32[]{:S(2)}) async-start(), calls=%async_computation.2 | async-start | bytes 4194304 | tf_op jit(solution)/shard_map/psum | solution.py:112
Sparse Core Ops, SparseCore 0:
  10.7 38.5 all-gather.4
  381.3 129.6 all-gather.2
  534.7 82.0 all-reduce.1
where the time goes:
time: 628 us; the launch traced here: 626 us
  waiting for transfers between devices  424 us (68%)
  blocking collectives  105 us (17%)
  local copies, waits for them, and re-layouts  33.1 us (5%)
  matrix products  22 us (4%)
  starting transfers between devices  16.1 us (3%)
  between operations  14.6 us (2%)
  other arithmetic  11.7 us (2%)
    all_to_all x1, waiting for transfers between devices, body(): lax.all_to_all(slot_terms.reshape(dp_count, slot_cap, tile_size, tile_siz...  182 us
    all_gather x1, waiting for transfers between devices, body(): lax.all_gather(delta_value.astype(jnp.bfloat16), 'dp', axis=1, tiled=True)  129 us
    psum x1, blocking collectives, body(): squares = lax.psum(jnp.sum(own_grad * own_grad), ('dp', 'tensor'))  105 us
    psum x1, waiting for transfers between devices, body(): lax.psum(partial_value, 'tensor').astype(jnp.float32).astype(jnp.bfloat16)  82.2 us
    all_gather x1, waiting for transfers between devices, body(): whole = lax.all_gather(features, 'tensor', axis=1, tiled=True)  29.9 us
    all_to_all x1, starting transfers between devices, body(): lax.all_to_all(slot_terms.reshape(dp_count, slot_cap, tile_size, tile_siz...  15.8 us
  transfers between devices with their start and end apart: 4, of which 4 were waited for; matrix products, arithmetic and copies ran while one was open for 2% of the time, Pallas kernels for 0%

commit v1 on v0

v1 whole, which is shorter than its diff:
```python
import functools

import jax
import jax.numpy as jnp
import numpy as np
from jax import lax
from jax.experimental import pallas as pl
from jax.experimental.pallas import tpu as pltpu
from jax.sharding import Mesh, PartitionSpec as P

TILE = 128
VMEM_LIMIT = 48 * 1024 * 1024
SMEM = pl.BlockSpec(memory_space=pltpu.SMEM)
VMEM = pl.BlockSpec(memory_space=pltpu.VMEM)
ANY = pl.BlockSpec(memory_space=pl.ANY)


def shift(value, axis, step):
    size = lax.axis_size(axis)
    return lax.ppermute(value, axis, [(i, (i + step) % size) for i in range(size)])


def exchange(value, axis):
    return lax.all_to_all(value, axis, split_axis=0, concat_axis=0, tiled=True)


def spread(value, axis):
    copies = jnp.broadcast_to(value[None], (lax.axis_size(axis),) + value.shape)
    return exchange(copies, axis)


def gate_kernel(gate_ref, up_ref, hidden_ref, grad_ref, turned_ref):
    for col in range(grad_ref.shape[0]):
        cut = slice(col * TILE, (col + 1) * TILE)
        gate = gate_ref[:, cut].astype(jnp.float32)
        sig = 1.0 / (1.0 + jnp.exp(-gate))
        value = (
            hidden_ref[:, cut].astype(jnp.float32)
            * up_ref[:, cut].astype(jnp.float32)
            * sig
            * (1.0 + gate * (1.0 - sig))
        )
        grad_ref[col] = value.astype(jnp.bfloat16)
        turned_ref[col] = value.T.astype(jnp.bfloat16)


def find_slots(counts_ref, slot_ref, empty=None):
    def owner_step(owner, start):
        count = counts_ref[0, owner]
        slot_ref[start] = 2 * owner
        slot_ref[start + 1] = 2 * owner + 1
        if empty is not None:

            @pl.when(count < 2)
            def _():
                empty(2 * owner + 1)

        return start + count

    lax.fori_loop(0, counts_ref.shape[1], owner_step, 0)


def tile_kernel(
    core_ref, rows_ref, cols_ref, counts_ref, own_ref, other_ref, turned_ref,
    out_ref, features, slots, sems,
):
    first = pltpu.make_async_copy(own_ref, features.at[0], sems.at[0])
    second = pltpu.make_async_copy(other_ref, features.at[1], sems.at[1])
    first.start()
    second.start()

    def empty(slot):
        out_ref[slot] = jnp.zeros((TILE, TILE), jnp.bfloat16)

    find_slots(counts_ref, slots, empty)
    first.wait()
    second.wait()
    core = core_ref[0]
    per_step = 4

    def step(index, carry):
        for part in range(per_step):
            k = index * per_step + part
            row = rows_ref[0, k]
            side = ((row >> 3) & 1) ^ core
            lane = pl.multiple_of((row & 7) * TILE, TILE)
            x = features[side, row >> 4, :, pl.ds(lane, TILE)]
            product = jnp.dot(
                turned_ref[cols_ref[0, k]], x, preferred_element_type=jnp.float32
            )
            out_ref[slots[k]] = product.astype(jnp.bfloat16)
        return carry

    lax.fori_loop(0, rows_ref.shape[1] // per_step, step, 0)


def contrib_kernel(rows_ref, cols_ref, counts_ref, grad_ref, delta_ref, out_ref, slots):
    out_ref[...] = jnp.zeros_like(out_ref)
    find_slots(counts_ref, slots)
    per_step = 4

    def step(index, carry):
        last, total = carry
        for part in range(per_step):
            k = index * per_step + part
            row = rows_ref[0, k]
            slot = slots[k]
            owner = slot >> 1
            place = (((owner & 15) * 4 + (owner >> 4)) << 1) + (slot & 1)
            product = lax.dot_general(
                grad_ref[cols_ref[0, k]], delta_ref[place],
                (((1,), (1,)), ((), ())), preferred_element_type=jnp.float32,
            )
            total = jnp.where(row == last, total, 0.0) + product
            lane = pl.multiple_of(row * TILE, TILE)
            out_ref[:, pl.ds(lane, TILE)] = total.astype(jnp.bfloat16)
            last = row
        return last, total

    lax.fori_loop(
        0, rows_ref.shape[1] // per_step, step,
        (jnp.int32(-1), jnp.zeros((TILE, TILE), jnp.float32)),
    )


def adam_update(grads, valid, delta_value, moment_one, moment_two, factor):
    clipped = factor * grads
    first = 0.9 * moment_one + 0.1 * clipped
    second = 0.95 * moment_two + 0.05 * clipped * clipped
    step_size = first / (1.0 - 0.9**10) / (jnp.sqrt(second / (1.0 - 0.95**10)) + 1e-08)
    updated = delta_value - 0.02 * (step_size + 0.1 * delta_value)
    return (
        jnp.where(valid, updated, delta_value),
        jnp.where(valid, first, moment_one),
        jnp.where(valid, second, moment_two),
    )


def body(
    features, gate_pre, up_pre, hidden_grad, tile_rows, tile_cols, owner_counts,
    delta_value, moment_one, moment_two,
):
    ny, nz, nx = (lax.axis_size(name) for name in ("y", "z", "x"))
    core = lax.axis_index("core")
    owner = lax.axis_index("y") * nz + lax.axis_index("z")
    tokens, hidden = gate_pre.shape
    col_tiles = hidden // TILE
    width = features.shape[1] * nx * 2
    slot_cap = delta_value.shape[1]
    slot_total = ny * nz * slot_cap
    tile_total = tile_rows.shape[1]
    params = pltpu.CompilerParams(vmem_limit_bytes=VMEM_LIMIT)
    bf16 = jnp.bfloat16

    delta_y = lax.all_gather(delta_value[0].astype(bf16), "y", axis=0, tiled=True)
    delta_all = lax.all_gather(delta_y, "z", axis=0, tiled=True)

    own = spread(features, "x")
    other = shift(own, "core", 1)

    grads, turned = pl.pallas_call(
        gate_kernel,
        out_shape=[jax.ShapeDtypeStruct((col_tiles, tokens, TILE), bf16)] * 2,
        in_specs=[VMEM] * 3,
        out_specs=[VMEM] * 2,
        compiler_params=params,
        cost_estimate=pl.CostEstimate(
            flops=tokens * hidden * 12, bytes_accessed=tokens * hidden * 10, transcendentals=0
        ),
        name="gate",
    )(gate_pre, up_pre, hidden_grad)

    terms = pl.pallas_call(
        tile_kernel,
        out_shape=jax.ShapeDtypeStruct((slot_total, TILE, TILE), bf16),
        in_specs=[SMEM] * 4 + [ANY, ANY, VMEM],
        out_specs=VMEM,
        scratch_shapes=[
            pltpu.VMEM((2, nx, tokens, features.shape[1]), bf16),
            pltpu.SMEM((tile_total + 8,), jnp.int32),
            pltpu.SemaphoreType.DMA((2,)),
        ],
        compiler_params=params,
        cost_estimate=pl.CostEstimate(
            flops=2 * tile_total * TILE**3, bytes_accessed=8 << 20, transcendentals=0
        ),
        name="tiles",
    )(core[None], tile_rows, tile_cols, owner_counts, own, other, turned)

    arrived = exchange(terms, "y").reshape(ny, nz * slot_cap, TILE, TILE)
    summed = jnp.sum(arrived.astype(jnp.float32), axis=0).astype(bf16)
    arrived = exchange(summed, "z").reshape(nz, slot_cap, TILE, TILE)
    own_grad = jnp.sum(arrived.astype(jnp.float32), axis=0)
    own_count = lax.dynamic_index_in_dim(owner_counts[0], owner, axis=0, keepdims=False)
    own_valid = (jnp.arange(slot_cap, dtype=jnp.int32) < own_count)[:, None, None]
    own_grad = jnp.where(own_valid, own_grad, 0.0)

    squares = jnp.sum(own_grad * own_grad)
    for axes in (("x", "core"), "y", "z"):
        piece = jnp.broadcast_to(squares[None, None], (8, TILE))
        squares = jnp.sum(spread(piece, axes)[:, 0, 0])
    root_mean = jnp.sqrt(
        squares / (nx * 2 * tile_total * TILE * TILE) + 1e-06
    )
    factor = jnp.minimum(1.0, 1.0 / root_mean)
    new_delta, new_first, new_second = adam_update(
        own_grad.transpose(0, 2, 1)[None], own_valid[None], delta_value, moment_one,
        moment_two, factor,
    )

    partial = pl.pallas_call(
        contrib_kernel,
        out_shape=jax.ShapeDtypeStruct((tokens, width), bf16),
        in_specs=[SMEM] * 3 + [VMEM] * 2,
        out_specs=VMEM,
        scratch_shapes=[pltpu.SMEM((tile_total + 8,), jnp.int32)],
        compiler_params=params,
        cost_estimate=pl.CostEstimate(
            flops=2 * tile_total * TILE**3, bytes_accessed=8 << 20, transcendentals=0
        ),
        name="contribs",
    )(tile_rows, tile_cols, owner_counts, grads, delta_all)

    half = tokens // 2
    keep = lax.dynamic_slice_in_dim(partial, core * half, half, axis=0)
    give = lax.dynamic_slice_in_dim(partial, (1 - core) * half, half, axis=0)
    taken = shift(give, "core", 1)
    pair = (keep.astype(jnp.float32) + taken.astype(jnp.float32)).astype(bf16)
    quarters = exchange(pair, "x").reshape(nx, half // nx, width)
    mine = jnp.sum(quarters.astype(jnp.float32), axis=0).astype(bf16)
    near = spread(mine, "x").reshape(half, width)
    far = shift(near, "core", 1)
    input_grad = jnp.concatenate(
        [jnp.where(core == 0, near, far), jnp.where(core == 0, far, near)], axis=0
    )
    return (input_grad, new_delta, new_first, new_second)


def solution(mesh):
    grid = Mesh(mesh.devices.reshape(4, 16, 4, 2), ("y", "z", "x", "core"))
    dp, tensor = ("y", "z"), ("x", "core")
    tokens = P(dp, tensor)
    lists = P(tensor, None)
    slots = P(tensor, dp, None, None)
    return jax.shard_map(
        body,
        mesh=grid,
        in_specs=(tokens,) * 4 + (lists,) * 3 + (slots,) * 3,
        out_specs=(P(dp, None),) + (slots,) * 3,
        check_vma=False,
    )
```

time: 628 us -> 343 us (0.55)
  waiting for transfers between devices: 424 us -> 199 us
  blocking collectives: 105 us -> 30.5 us
  starting transfers between devices: 16.1 us -> 51.2 us
  matrix products: 22 us -> 0 us
  local copies, waits for them, and re-layouts: 33.1 us -> 13.7 us
  Pallas kernels: 0 us -> 18.5 us
    psum x1 -> x0, blocking collectives: 105 us -> none  [body(): squares = lax.psum(jnp.sum(own_grad * own_grad), ('dp', 'tensor'))]
    all_gather x2 -> x1, waiting for transfers between devices: 159 us -> 72.5 us  [body(): delta_all = lax.all_gather(delta_y, 'z', axis=0, tiled=True)]
    psum x1 -> x0, waiting for transfers between devices: 82.2 us -> none  [body(): lax.psum(partial_value, 'tensor').astype(jnp.float32).astype(jnp.bfloat16)]
    all_to_all x1 -> x6, waiting for transfers between devices: 182 us -> 127 us  [exchange(): return lax.all_to_all(value, axis, split_axis=0, concat_axis=0, tiled=True)]
    dot_general x3 -> x0, matrix products: 22 us -> none  [the longest x1 9.49 us: body(): jnp.dot(onehot, contribs.reshape(tile_total, tok_rows * tile_size), preci...]
    ppermute x0 -> x3, starting transfers between devices: none -> 19.3 us  [shift(): lax.ppermute(value, axis, [(i, (i + step) % size) for i in range(size)])]
    all_to_all x0 -> x2, blocking collectives: none -> 19.1 us  [exchange(): return lax.all_to_all(value, axis, split_axis=0, concat_axis=0, tiled=True)]
    pallas_call x0 -> x3, Pallas kernels: none -> 18.5 us  [the longest x1 9.07 us: body(): pl.pallas_call(tile_kernel, out_shape=jax.ShapeDtypeStruct((slot_total, T...]
  transfers between devices with their start and end apart: 4 -> 10, of which waited for: 4 -> 7; matrix products, arithmetic and copies ran while one was open for 2% -> 5% of each run, Pallas kernels for 0% -> 3%
where the time goes in v1:
time: 343 us; the launch traced here: 341 us
  waiting for transfers between devices  199 us (58%)
  starting transfers between devices  51.2 us (15%)
  blocking collectives  30.5 us (9%)
  Pallas kernels  18.5 us (5%)
  between operations  15 us (4%)
  local copies, waits for them, and re-layouts  13.7 us (4%)
  other arithmetic  13.2 us (4%)
    all_to_all x6, waiting for transfers between devices, exchange(): return lax.all_to_all(value, axis, split_axis=0, concat_axis=0, tiled=True)  127 us
    all_gather x1, waiting for transfers between devices, body(): delta_all = lax.all_gather(delta_y, 'z', axis=0, tiled=True)  72.5 us
    all_to_all x6, starting transfers between devices, exchange(): return lax.all_to_all(value, axis, split_axis=0, concat_axis=0, tiled=True)  31.9 us
    ppermute x3, starting transfers between devices, shift(): lax.ppermute(value, axis, [(i, (i + step) % size) for i in range(size)])  19.3 us
    all_to_all x2, blocking collectives, exchange(): return lax.all_to_all(value, axis, split_axis=0, concat_axis=0, tiled=True)  19.1 us
    all_gather x1, blocking collectives, body(): lax.all_gather(delta_value[0].astype(bf16), 'y', axis=0, tiled=True)  11.5 us
    pallas_call x1, Pallas kernels, body(): pl.pallas_call(tile_kernel, out_shape=jax.ShapeDtypeStruct((slot_total, T...  9.07 us
    pallas_call x1, Pallas kernels, body(): pl.pallas_call(contrib_kernel, out_shape=jax.ShapeDtypeStruct((tokens, wi...  8.94 us
  transfers between devices with their start and end apart: 10, of which 7 were waited for; matrix products, arithmetic and copies ran while one was open for 5% of the time, Pallas kernels for 3%

profile of v1, /device:TPU:1, one launch (start us, length us, event | category | flops | bytes accessed | tf_op | source)
XLA Modules:
  0.0 341.4 jit_solution(1719742962606440916)
XLA Ops:
  7.2 0.0 copy-start.5
  7.2 0.0 copy-start.6
  7.2 0.0 all-gather.4.cloned.1.call-start
  7.2 0.9 bitcast_convert_fusion
  8.2 11.5 %all-gather = bf16[1,8,128,128]{3,2,0,1:T(8,128)(2,1)} all-gather(bf16[1,2,128,128]{3,2,0,1:T(8,128)(2,1)S(1)} %bitcast_convert_fusion), channel_id=2, replica_groups=mesh['y'=4,'z'=16,'x'=4,'core'=2] {'y'}, dimensions={1}, use_global_device_ids=true | all-gather | bytes 327680 | tf_op jit(solution)/shard_map/all_gather | solution.py:155
  19.6 0.0 all-gather.4.cloned.1.call-update
  19.7 0.0 copy-start.2
  19.7 1.0 copy-done.2
  20.7 1.0 copy-done.3
  21.7 1.0 copy-done.4
  22.7 0.5 gate.1
  23.3 0.8 copy-done
  24.0 72.5 %all-gather.4.cloned.1.call-done = bf16[1,128,128,128]{3,2,0,1:T(8,128)(2,1)} async-done(((bf16[1,8,128,128]{3,2,0,1:T(8,128)(2,1)}), bf16[1,128,128,128]{3,2,0,1:T(8,128)(2,1)}) %all-gather.4.cloned.1.call-update) | async-done | bytes 4194320 | tf_op jit(solution)/shard_map/all_gather | solution.py:156
  96.5 0.0 copy-done.6
  96.6 8.9 %contribs.1 = bf16[128,8192]{1,0:T(8,128)(2,1)S(1)} custom-call(s32[1,112]{1,0:T(1,128)S(1)} %copy-done.5, s32[1,112]{1,0:T(1,128)S(1)} %copy-done.6, s32[1,64]{1,0:T(1,128)S(1)} %copy-done.7, bf16[14,128,128]{2,1,0:T(8,128)(2,1)S(1)} %get-tuple-element.6.grad_ref, bf16[128,128,128]{2,1,0:T(8,128)(2,1)} %bitcast.39), custom_call_target="tpu_custom_call" | custom-call | flops 469762048 | bytes 8388608 | tf_op jit(solution)/shard_map/contribs/pallas_call | solution.py:211
  105.5 0.0 copy-start.9
  105.5 1.1 constant_dynamic-slice_fusion.1
  106.6 11.5 %collective-permute-start = (bf16[64,8192]{1,0:T(8,128)(2,1)}, bf16[64,8192]{1,0:T(8,128)(2,1)}, u32[]{:S(2)}, u32[]{:S(2)}) collective-permute-start(bf16[64,8192]{1,0:T(8,128)(2,1)} %constant_dynamic-slice_fusion.1), channel_id=1, source_target_pairs={{0,1},{1,0},{2,3},{3,2},{4,5},{5,4},{6,7},{7,6},{8,9},{9,8},{10,11... | collective-permute-start | bytes 3145736 | tf_op jit(solution)/shard_map/ppermute | solution.py:20
  118.0 1.1 broadcast_in_dim.50
  119.2 4.0 %all-to-all-start.2 = ((bf16[4,128,1024]{2,1,0:T(8,128)(2,1)}), bf16[4,128,1024]{2,1,0:T(8,128)(2,1)S(1)}, u32[]{:S(2)}, u32[]{:S(2)}) async-start(bf16[4,128,1024]{2,1,0:T(8,128)(2,1)} %broadcast_in_dim.50), calls=%async_computation.2 | async-start | bytes 2097152 | tf_op jit(solution)/shard_map/all_to_all | solution.py:24
  123.1 14.9 %all-to-all-done.2.own_ref = bf16[4,128,1024]{2,1,0:T(8,128)(2,1)S(1)} async-done(((bf16[4,128,1024]{2,1,0:T(8,128)(2,1)}), bf16[4,128,1024]{2,1,0:T(8,128)(2,1)S(1)}, u32[]{:S(2)}, u32[]{:S(2)}) %all-to-all-start.2) | async-done | bytes 1048608 | tf_op jit(solution)/shard_map/all_to_all | solution.py:24
  138.1 3.0 collective-permute-start.2
  141.1 0.0 collective-permute-done
  141.1 2.4 add_convert_fusion
  143.5 3.6 %all-to-all-start = ((bf16[4,16,8192]{2,1,0:T(8,128)(2,1)}), bf16[4,16,8192]{2,1,0:T(8,128)(2,1)S(1)}, u32[]{:S(2)}, u32[]{:S(2)}) async-start(bf16[4,16,8192]{2,1,0:T(8,128)(2,1)} %bitcast.42), calls=%async_computation | async-start | bytes 2097152 | tf_op jit(solution)/shard_map/all_to_all | solution.py:24
  147.2 0.0 collective-permute-done.2.other_ref
  147.2 0.0 copy-done.1
  147.2 9.1 %tiles.1 = bf16[128,128,128]{2,1,0:T(8,128)(2,1)} custom-call(s32[1]{0:T(128)} %bitcast.5.core_ref, s32[1,112]{1,0:T(1,128)S(1)} %copy-done.5, s32[1,112]{1,0:T(1,128)S(1)} %copy-done.6, s32[1,64]{1,0:T(1,128)S(1)} %copy-done.7, bf16[4,128,1024]{2,1,0:T(8,128)(2,1)S(1)} %all-to-all-done.2.own_ref, bf16[4,128,1024]{2,1,0:T(8,128)(2,1)} %collective-permute-done.2.other_ref, ...), custom_call_target="tpu_custom_call" | custom-call | flops 469762048 | bytes 8388608 | tf_op jit(solution)/shard_map/tiles/pallas_call | solution.py:173
  156.3 6.1 %all-to-all-done = bf16[4,16,8192]{2,1,0:T(8,128)(2,1)S(1)} async-done(((bf16[4,16,8192]{2,1,0:T(8,128)(2,1)}), bf16[4,16,8192]{2,1,0:T(8,128)(2,1)S(1)}, u32[]{:S(2)}, u32[]{:S(2)}) %all-to-all-start) | async-done | bytes 1048608 | tf_op jit(solution)/shard_map/all_to_all | solution.py:24
  162.4 4.8 %all-to-all-start.3 = ((bf16[128,128,128]{2,1,0:T(8,128)(2,1)}), bf16[128,128,128]{2,1,0:T(8,128)(2,1)}, u32[]{:S(2)}, u32[]{:S(2)}) async-start(bf16[128,128,128]{2,1,0:T(8,128)(2,1)} %tiles.1), calls=%async_computation.3 | async-start | bytes 8388608 | tf_op jit(solution)/shard_map/all_to_all | solution.py:24
  167.3 0.3 reduce_sum.69
  167.5 47.9 %all-to-all-done.3 = bf16[128,128,128]{2,1,0:T(8,128)(2,1)} async-done(((bf16[128,128,128]{2,1,0:T(8,128)(2,1)}), bf16[128,128,128]{2,1,0:T(8,128)(2,1)}, u32[]{:S(2)}, u32[]{:S(2)}) %all-to-all-start.3) | async-done | bytes 4194336 | tf_op jit(solution)/shard_map/all_to_all | solution.py:24
  215.4 1.0 broadcast_in_dim.46
  216.4 3.5 %all-to-all-start.1 = ((bf16[4,16,8192]{2,1,0:T(8,128)(2,1)}), bf16[4,16,8192]{2,1,0:T(8,128)(2,1)S(1)}, u32[]{:S(2)}, u32[]{:S(2)}) async-start(bf16[4,16,8192]{2,1,0:T(8,128)(2,1)} %broadcast_in_dim.46), calls=%async_computation.1 | async-start | bytes 2097152 | tf_op jit(solution)/shard_map/all_to_all | solution.py:24
  220.0 4.3 %reduce_sum.70 = bf16[32,128,128]{2,1,0:T(8,128)(2,1)} reduce(bf16[4,32,128,128]{3,2,1,0:T(8,128)(2,1)} %bitcast.6, bf16[]{:T(256)} %constant.15.clone.1), dimensions={0}, to_apply=%region_1.0 | reduce | flops 1572864 | bytes 5242882 | tf_op jit(solution)/shard_map/reduce_sum | solution.py:191
  224.2 9.2 %all-to-all-done.1 = bf16[4,16,8192]{2,1,0:T(8,128)(2,1)S(1)} async-done(((bf16[4,16,8192]{2,1,0:T(8,128)(2,1)}), bf16[4,16,8192]{2,1,0:T(8,128)(2,1)S(1)}, u32[]{:S(2)}, u32[]{:S(2)}) %all-to-all-start.1) | async-done | bytes 1048608 | tf_op jit(solution)/shard_map/all_to_all | solution.py:24
  233.4 7.1 %all-to-all-start.4 = ((bf16[32,128,128]{2,1,0:T(8,128)(2,1)}), bf16[32,128,128]{2,1,0:T(8,128)(2,1)S(1)}, u32[]{:S(2)}, u32[]{:S(2)}) async-start(bf16[32,128,128]{2,1,0:T(8,128)(2,1)} %reduce_sum.70), calls=%async_computation.4 | async-start | bytes 2097152 | tf_op jit(solution)/shard_map/all_to_all | solution.py:24
  240.5 0.6 constant_dynamic-slice_fusion
  241.1 0.6 iota_compare_fusion
  241.8 4.8 %collective-permute-start.1 = (bf16[64,8192]{1,0:T(8,128)(2,1)S(1)}, bf16[64,8192]{1,0:T(8,128)(2,1)S(1)}, u32[]{:S(2)}, u32[]{:S(2)}) collective-permute-start(bf16[64,8192]{1,0:T(8,128)(2,1)S(1)} %bitcast.40), channel_id=1, source_target_pairs={{0,1},{1,0},{2,3},{3,2},{4,5},{5,4},{6,7},{7,6},{8,9},{9,8},{10,11... | collective-permute-start | bytes 3145736 | tf_op jit(solution)/shard_map/ppermute | solution.py:20
  246.6 38.3 %all-to-all-done.4 = bf16[32,128,128]{2,1,0:T(8,128)(2,1)S(1)} async-done(((bf16[32,128,128]{2,1,0:T(8,128)(2,1)}), bf16[32,128,128]{2,1,0:T(8,128)(2,1)S(1)}, u32[]{:S(2)}, u32[]{:S(2)}) %all-to-all-start.4) | async-done | bytes 1048608 | tf_op jit(solution)/shard_map/all_to_all | solution.py:24
  284.8 0.1 convert_reduce_fusion
  285.0 0.7 multiply_reduce_fusion
  285.7 0.6 broadcast_in_dim_broadcast_in_dim_broadcast_in_dim.6
  286.3 12.5 %all_to_all.44 = f32[8,8,128]{2,1,0:T(8,128)S(1)} all-to-all(f32[8,8,128]{2,1,0:T(8,128)S(1)} %broadcast_in_dim_broadcast_in_dim_broadcast_in_dim.6), channel_id=1, replica_groups=mesh['y'=4,'z'=16,'x'=4,'core'=2] {'x','core'}, dimensions={0} | all-to-all | bytes 65536 | tf_op jit(solution)/shard_map/all_to_all | solution.py:24
  298.9 0.6 slice_reduce_fusion.1
  299.5 0.6 broadcast_in_dim_broadcast_in_dim_broadcast_in_dim.7
  300.1 6.6 %all_to_all.45 = f32[4,8,128]{2,1,0:T(8,128)S(1)} all-to-all(f32[4,8,128]{2,1,0:T(8,128)S(1)} %broadcast_in_dim_broadcast_in_dim_broadcast_in_dim.7), channel_id=1, replica_groups=mesh['y'=4,'z'=16,'x'=4,'core'=2] {'y'}, dimensions={0} | all-to-all | bytes 32768 | tf_op jit(solution)/shard_map/all_to_all | solution.py:24
  306.7 0.6 slice_reduce_fusion.2
  307.3 1.3 broadcast_in_dim_broadcast_in_dim_broadcast_in_dim.8
  308.6 8.8 %all-to-all-start.7 = ((f32[16,8,128]{2,1,0:T(8,128)}), f32[16,8,128]{2,1,0:T(8,128)S(1)}, u32[]{:S(2)}, u32[]{:S(2)}) async-start(f32[16,8,128]{2,1,0:T(8,128)} %broadcast_in_dim_broadcast_in_dim_broadcast_in_dim.8), calls=%async_computation.7 | async-start | bytes 131072 | tf_op jit(solution)/shard_map/all_to_all | solution.py:24
  317.4 0.1 copy.33
  317.5 0.0 copy-done.10
  317.5 0.1 copy.27
  317.6 1.0 copy.31
  318.6 10.4 %all-to-all-done.7 = f32[16,8,128]{2,1,0:T(8,128)S(1)} async-done(((f32[16,8,128]{2,1,0:T(8,128)}), f32[16,8,128]{2,1,0:T(8,128)S(1)}, u32[]{:S(2)}, u32[]{:S(2)}) %all-to-all-start.7) | async-done | bytes 65568 | tf_op jit(solution)/shard_map/all_to_all | solution.py:24
  328.9 0.6 slice_reduce_fusion
  330.3 0.2 fusion.3
  330.5 0.8 copy.37
  331.2 0.8 copy.38
  332.0 0.8 copy.39
  332.7 0.0 collective-permute-done.1
  332.7 0.3 broadcast_select_fusion.1
  333.1 1.5 pad_maximum_fusion
  (11 shorter events, 0.0 us)
Async XLA Ops:
  7.2 89.4 %copy-start.5 = (s32[1,112]{1,0:T(1,128)S(1)}, s32[1,112]{1,0:T(1,128)}, u32[]{:S(2)}) copy-start(s32[1,112]{1,0:T(1,128)} %rows_ref.3) | copy-start | bytes 1348
  7.2 89.4 %copy-start.6 = (s32[1,112]{1,0:T(1,128)S(1)}, s32[1,112]{1,0:T(1,128)}, u32[]{:S(2)}) copy-start(s32[1,112]{1,0:T(1,128)} %cols_ref.3) | copy-start | bytes 1348
  7.2 89.4 %copy-start.7 = (s32[1,64]{1,0:T(1,128)S(1)}, s32[1,64]{1,0:T(1,128)}, u32[]{:S(2)}) copy-start(s32[1,64]{1,0:T(1,128)} %counts_ref.3) | copy-start | bytes 772
  7.2 89.3 %all-gather.4.cloned.1.call-start = ((), (), s32[]{:S(2)}) async-start(), calls=%async_computation.8 | async-start | bytes 4456448 | tf_op jit(solution)/shard_map/all_gather | solution.py:156
  19.7 1.0 copy-start.2
  20.7 1.0 copy-start.3
  21.7 1.0 copy-start.4
  23.3 0.8 copy-start
  105.5 12.5 %copy-start.9 = (bf16[128,1024]{1,0:T(8,128)(2,1)S(1)}, bf16[128,1024]{1,0:T(8,128)(2,1)}, u32[]{:S(2)}) copy-start(bf16[128,1024]{1,0:T(8,128)(2,1)} %param.10) | copy-start | bytes 786436
  106.6 34.5 %collective-permute-start = (bf16[64,8192]{1,0:T(8,128)(2,1)}, bf16[64,8192]{1,0:T(8,128)(2,1)}, u32[]{:S(2)}, u32[]{:S(2)}) collective-permute-start(bf16[64,8192]{1,0:T(8,128)(2,1)} %constant_dynamic-slice_fusion.1), channel_id=1, source_target_pairs={{0,1},{1,0},{2,3},{3,2},{4,5},{5,4},{6,7},{7,6},{8,9},{9,8},{10,11... | collective-permute-start | bytes 3145736 | tf_op jit(solution)/shard_map/ppermute | solution.py:20
  119.2 18.9 %all-to-all-start.2 = ((bf16[4,128,1024]{2,1,0:T(8,128)(2,1)}), bf16[4,128,1024]{2,1,0:T(8,128)(2,1)S(1)}, u32[]{:S(2)}, u32[]{:S(2)}) async-start(bf16[4,128,1024]{2,1,0:T(8,128)(2,1)} %broadcast_in_dim.50), calls=%async_computation.2 | async-start | bytes 2097152 | tf_op jit(solution)/shard_map/all_to_all | solution.py:24
  138.1 9.1 %collective-permute-start.2 = (bf16[4,128,1024]{2,1,0:T(8,128)(2,1)S(1)}, bf16[4,128,1024]{2,1,0:T(8,128)(2,1)}, u32[]{:S(2)}, u32[]{:S(2)}) collective-permute-start(bf16[4,128,1024]{2,1,0:T(8,128)(2,1)S(1)} %all-to-all-done.2.own_ref), channel_id=1, source_target_pairs={{0,1},{1,0},{2,3},{3,2},{4,5},{5,4},{6,7},{7,6},{8,9},{9,8},{10,11... | collective-permute-start | bytes 3145736 | tf_op jit(solution)/shard_map/ppermute | solution.py:20
  143.5 3.7 %copy-start.1 = (bf16[14,128,128]{2,1,0:T(8,128)(2,1)S(1)}, bf16[14,128,128]{2,1,0:T(8,128)(2,1)}, u32[]{:S(2)}) copy-start(bf16[14,128,128]{2,1,0:T(8,128)(2,1)} %copy-done) | copy-start | bytes 1376260
  143.5 18.9 %all-to-all-start = ((bf16[4,16,8192]{2,1,0:T(8,128)(2,1)}), bf16[4,16,8192]{2,1,0:T(8,128)(2,1)S(1)}, u32[]{:S(2)}, u32[]{:S(2)}) async-start(bf16[4,16,8192]{2,1,0:T(8,128)(2,1)} %bitcast.42), calls=%async_computation | async-start | bytes 2097152 | tf_op jit(solution)/shard_map/all_to_all | solution.py:24
  162.4 53.0 %all-to-all-start.3 = ((bf16[128,128,128]{2,1,0:T(8,128)(2,1)}), bf16[128,128,128]{2,1,0:T(8,128)(2,1)}, u32[]{:S(2)}, u32[]{:S(2)}) async-start(bf16[128,128,128]{2,1,0:T(8,128)(2,1)} %tiles.1), calls=%async_computation.3 | async-start | bytes 8388608 | tf_op jit(solution)/shard_map/all_to_all | solution.py:24
  216.4 16.9 %all-to-all-start.1 = ((bf16[4,16,8192]{2,1,0:T(8,128)(2,1)}), bf16[4,16,8192]{2,1,0:T(8,128)(2,1)S(1)}, u32[]{:S(2)}, u32[]{:S(2)}) async-start(bf16[4,16,8192]{2,1,0:T(8,128)(2,1)} %broadcast_in_dim.46), calls=%async_computation.1 | async-start | bytes 2097152 | tf_op jit(solution)/shard_map/all_to_all | solution.py:24
  224.2 93.2 %copy-start.8 = (f32[1,2,128,128]{3,2,1,0:T(8,128)S(1)}, f32[1,2,128,128]{3,2,1,0:T(8,128)}, u32[]{:S(2)}) copy-start(f32[1,2,128,128]{3,2,1,0:T(8,128)} %param.17) | copy-start | bytes 393220
  224.2 93.3 %copy-start.10 = (f32[1,2,128,128]{3,2,1,0:T(8,128)S(1)}, f32[1,2,128,128]{3,2,1,0:T(8,128)}, u32[]{:S(2)}) copy-start(f32[1,2,128,128]{3,2,1,0:T(8,128)} %param.18) | copy-start | bytes 393220
  233.4 51.5 %all-to-all-start.4 = ((bf16[32,128,128]{2,1,0:T(8,128)(2,1)}), bf16[32,128,128]{2,1,0:T(8,128)(2,1)S(1)}, u32[]{:S(2)}, u32[]{:S(2)}) async-start(bf16[32,128,128]{2,1,0:T(8,128)(2,1)} %reduce_sum.70), calls=%async_computation.4 | async-start | bytes 2097152 | tf_op jit(solution)/shard_map/all_to_all | solution.py:24
  241.8 91.0 %collective-permute-start.1 = (bf16[64,8192]{1,0:T(8,128)(2,1)S(1)}, bf16[64,8192]{1,0:T(8,128)(2,1)S(1)}, u32[]{:S(2)}, u32[]{:S(2)}) collective-permute-start(bf16[64,8192]{1,0:T(8,128)(2,1)S(1)} %bitcast.40), channel_id=1, source_target_pairs={{0,1},{1,0},{2,3},{3,2},{4,5},{5,4},{6,7},{7,6},{8,9},{9,8},{10,11... | collective-permute-start | bytes 3145736 | tf_op jit(solution)/shard_map/ppermute | solution.py:20
  308.6 20.4 %all-to-all-start.7 = ((f32[16,8,128]{2,1,0:T(8,128)}), f32[16,8,128]{2,1,0:T(8,128)S(1)}, u32[]{:S(2)}, u32[]{:S(2)}) async-start(f32[16,8,128]{2,1,0:T(8,128)} %broadcast_in_dim_broadcast_in_dim_broadcast_in_dim.8), calls=%async_computation.7 | async-start | bytes 131072 | tf_op jit(solution)/shard_map/all_to_all | solution.py:24
Sparse Core Ops, SparseCore 0:
  19.8 76.7 all-gather.3

commit v2 on v1

--- a/solution.py
+++ b/solution.py
@@ -141,7 +141,7 @@
     delta_value, moment_one, moment_two,
 ):
     ny, nz, nx = (lax.axis_size(name) for name in ("y", "z", "x"))
-    core = lax.axis_index("core")
+    x, core = lax.axis_index("x"), lax.axis_index("core")
     owner = lax.axis_index("y") * nz + lax.axis_index("z")
     tokens, hidden = gate_pre.shape
     col_tiles = hidden // TILE
@@ -152,11 +152,11 @@
     params = pltpu.CompilerParams(vmem_limit_bytes=VMEM_LIMIT)
     bf16 = jnp.bfloat16
 
-    delta_y = lax.all_gather(delta_value[0].astype(bf16), "y", axis=0, tiled=True)
-    delta_all = lax.all_gather(delta_y, "z", axis=0, tiled=True)
-
     own = spread(features, "x")
     other = shift(own, "core", 1)
+
+    delta_y = spread(delta_value[0].astype(bf16), "y").reshape(ny * slot_cap, TILE, TILE)
+    delta_all = lax.all_gather(delta_y, "z", axis=0, tiled=True)
 
     grads, turned = pl.pallas_call(
         gate_kernel,
@@ -189,24 +189,12 @@
 
     arrived = exchange(terms, "y").reshape(ny, nz * slot_cap, TILE, TILE)
     summed = jnp.sum(arrived.astype(jnp.float32), axis=0).astype(bf16)
+    summed, grads = lax.optimization_barrier((summed, grads))
     arrived = exchange(summed, "z").reshape(nz, slot_cap, TILE, TILE)
     own_grad = jnp.sum(arrived.astype(jnp.float32), axis=0)
     own_count = lax.dynamic_index_in_dim(owner_counts[0], owner, axis=0, keepdims=False)
     own_valid = (jnp.arange(slot_cap, dtype=jnp.int32) < own_count)[:, None, None]
     own_grad = jnp.where(own_valid, own_grad, 0.0)
-
-    squares = jnp.sum(own_grad * own_grad)
-    for axes in (("x", "core"), "y", "z"):
-        piece = jnp.broadcast_to(squares[None, None], (8, TILE))
-        squares = jnp.sum(spread(piece, axes)[:, 0, 0])
-    root_mean = jnp.sqrt(
-        squares / (nx * 2 * tile_total * TILE * TILE) + 1e-06
-    )
-    factor = jnp.minimum(1.0, 1.0 / root_mean)
-    new_delta, new_first, new_second = adam_update(
-        own_grad.transpose(0, 2, 1)[None], own_valid[None], delta_value, moment_one,
-        moment_two, factor,
-    )
 
     partial = pl.pallas_call(
         contrib_kernel,
@@ -215,23 +203,38 @@
         out_specs=VMEM,
         scratch_shapes=[pltpu.SMEM((tile_total + 8,), jnp.int32)],
         compiler_params=params,
-        cost_estimate=pl.CostEstimate(
-            flops=2 * tile_total * TILE**3, bytes_accessed=8 << 20, transcendentals=0
-        ),
+        cost_estimate=pl.CostEstimate(flops=0, bytes_accessed=1 << 16, transcendentals=0),
         name="contribs",
     )(tile_rows, tile_cols, owner_counts, grads, delta_all)
 
-    half = tokens // 2
-    keep = lax.dynamic_slice_in_dim(partial, core * half, half, axis=0)
-    give = lax.dynamic_slice_in_dim(partial, (1 - core) * half, half, axis=0)
+    rows = tokens // (2 * nx)
+    blocks = partial.reshape(nx, 2, rows, width)
+    keep = lax.dynamic_index_in_dim(blocks, core, axis=1, keepdims=False)
+    give = lax.dynamic_index_in_dim(blocks, 1 - core, axis=1, keepdims=False)
     taken = shift(give, "core", 1)
     pair = (keep.astype(jnp.float32) + taken.astype(jnp.float32)).astype(bf16)
-    quarters = exchange(pair, "x").reshape(nx, half // nx, width)
-    mine = jnp.sum(quarters.astype(jnp.float32), axis=0).astype(bf16)
-    near = spread(mine, "x").reshape(half, width)
-    far = shift(near, "core", 1)
-    input_grad = jnp.concatenate(
-        [jnp.where(core == 0, near, far), jnp.where(core == 0, far, near)], axis=0
+
+    def block(away):
+        return lax.dynamic_index_in_dim(pair, (x + away) % nx, axis=0, keepdims=False)
+
+    mine = block(0).astype(jnp.float32)
+    for away in range(1, nx):
+        mine = mine + shift(block(away), "x", away).astype(jnp.float32)
+    own_grad, mine = lax.optimization_barrier((own_grad, mine.astype(bf16)))
+    input_grad = lax.all_gather(mine, ("x", "core"), axis=0, tiled=True)
+
+    def total_over(value, axes):
+        return jnp.sum(spread(jnp.broadcast_to(value[None, None], (8, TILE)), axes)[:, 0, 0])
+
+    squares = total_over(jnp.sum(own_grad * own_grad), ("y", "x", "core"))
+    squares = total_over(squares, "z")
+    root_mean = jnp.sqrt(
+        squares / (nx * 2 * tile_total * TILE * TILE) + 1e-06
+    )
+    factor = jnp.minimum(1.0, 1.0 / root_mean)
+    new_delta, new_first, new_second = adam_update(
+        own_grad.transpose(0, 2, 1)[None], own_valid[None], delta_value, moment_one,
+        moment_two, factor,
     )
     return (input_grad, new_delta, new_first, new_second)
 

time: 343 us -> 226 us (0.66)
  waiting for transfers between devices: 199 us -> 81.7 us
  blocking collectives: 30.5 us -> 41.6 us
  starting transfers between devices: 51.2 us -> 46.8 us
    all_gather x1, waiting for transfers between devices: 72.5 us -> 0.02 us  [body(): delta_all = lax.all_gather(delta_y, 'z', axis=0, tiled=True)]
    all_to_all x6 -> x3, waiting for transfers between devices: 127 us -> 79.8 us  [exchange(): return lax.all_to_all(value, axis, split_axis=0, concat_axis=0, tiled=True)]
    all_to_all x2 -> x3, blocking collectives: 19.1 us -> 41.6 us  [exchange(): return lax.all_to_all(value, axis, split_axis=0, concat_axis=0, tiled=True)]
    all_gather x1 -> x0, blocking collectives: 11.5 us -> none  [body(): lax.all_gather(delta_value[0].astype(bf16), 'y', axis=0, tiled=True)]
    all_to_all x6 -> x3, starting transfers between devices: 31.9 us -> 27.5 us  [exchange(): return lax.all_to_all(value, axis, split_axis=0, concat_axis=0, tiled=True)]
    unnamed x28 -> x25, local copies, waits for them, and re-layouts: 7.31 us -> 6.71 us
    ppermute x3 -> x5, starting transfers between devices: 19.3 us -> 19.2 us  [shift(): lax.ppermute(value, axis, [(i, (i + step) % size) for i in range(size)])]
  transfers between devices with their start and end apart: 10 -> 10, of which waited for: 7 -> 5; matrix products, arithmetic and copies ran while one was open for 5% -> 7% of each run, Pallas kernels for 3% -> 8%
where the time goes in v2:
time: 226 us
  waiting for transfers between devices  81.7 us (36%)
  starting transfers between devices  46.8 us (21%)
  blocking collectives  41.6 us (18%)
  Pallas kernels  18.3 us (8%)
  between operations  15.1 us (7%)
  other arithmetic  11.6 us (5%)
  local copies, waits for them, and re-layouts  10.5 us (5%)
    all_to_all x3, waiting for transfers between devices, exchange(): return lax.all_to_all(value, axis, split_axis=0, concat_axis=0, tiled=True)  79.8 us
    all_to_all x3, blocking collectives, exchange(): return lax.all_to_all(value, axis, split_axis=0, concat_axis=0, tiled=True)  41.6 us
    all_to_all x3, starting transfers between devices, exchange(): return lax.all_to_all(value, axis, split_axis=0, concat_axis=0, tiled=True)  27.5 us
    ppermute x5, starting transfers between devices, shift(): lax.ppermute(value, axis, [(i, (i + step) % size) for i in range(size)])  19.2 us
    pallas_call x1, Pallas kernels, body(): pl.pallas_call(contrib_kernel, out_shape=jax.ShapeDtypeStruct((tokens, wi...  8.94 us
    pallas_call x1, Pallas kernels, body(): pl.pallas_call(tile_kernel, out_shape=jax.ShapeDtypeStruct((slot_total, T...  8.82 us
    unnamed x25, local copies, waits for them, and re-layouts  6.71 us
  transfers between devices with their start and end apart: 10, of which 5 were waited for; matrix products, arithmetic and copies ran while one was open for 7% of the time, Pallas kernels for 8%

profile of v2, /device:TPU:1, one launch (start us, length us, event | category | flops | bytes accessed | tf_op | source)
XLA Modules:
  0.0 225.6 jit_solution(2073699457196460890)
XLA Ops:
  7.2 0.0 all-gather.3.cloned.1.call-start
  7.2 0.9 convert_bitcast_fusion
  8.2 0.0 copy-start
  8.2 0.0 copy-start.1
  8.2 10.6 %all_to_all.30 = bf16[4,2,128,128]{3,2,1,0:T(8,128)(2,1)} all-to-all(bf16[4,2,128,128]{3,2,1,0:T(8,128)(2,1)S(1)} %broadcast_in_dim.52), channel_id=1, replica_groups=mesh['y'=4,'z'=16,'x'=4,'core'=2] {'y'}, dimensions={0} | all-to-all | bytes 524288 | tf_op jit(solution)/shard_map/all_to_all | solution.py:24
  18.8 0.0 all-gather.3.cloned.1.call-update
  18.8 0.0 copy-start.3
  18.8 0.0 copy-start.4
  18.8 0.0 copy-start.5
  18.8 1.1 broadcast_in_dim.49
  19.9 13.9 %all_to_all.31.own_ref = bf16[4,128,1024]{2,1,0:T(8,128)(2,1)S(1)} all-to-all(bf16[4,128,1024]{2,1,0:T(8,128)(2,1)S(1)} %broadcast_in_dim.49), channel_id=1, replica_groups=mesh['y'=4,'z'=16,'x'=4,'core'=2] {'x'}, dimensions={0} | all-to-all | bytes 2097152 | tf_op jit(solution)/shard_map/all_to_all | solution.py:24
  33.8 7.9 %collective-permute-start = (bf16[4,128,1024]{2,1,0:T(8,128)(2,1)S(1)}, bf16[4,128,1024]{2,1,0:T(8,128)(2,1)S(1)}, u32[]{:S(2)}, u32[]{:S(2)}) collective-permute-start(bf16[4,128,1024]{2,1,0:T(8,128)(2,1)S(1)} %all_to_all.31.own_ref), channel_id=1, source_target_pairs={{0,1},{1,0},{2,3},{3,2},{4,5},{5,4},{6,7},{7,6},{8,9},{9,8},{10,11... | collective-permute-start | bytes 3145736 | tf_op jit(solution)/shard_map/ppermute | solution.py:20
  41.7 0.0 copy-done
  41.7 0.0 copy-done.1
  41.7 0.0 copy-start.2
  41.8 1.0 copy-done.2
  42.8 0.5 gate.1
  43.3 0.7 collective-permute-done.other_ref
  44.0 0.0 copy-done.3
  44.0 0.0 copy-done.4
  44.0 8.8 %tiles.1 = bf16[128,128,128]{2,1,0:T(8,128)(2,1)} custom-call(s32[1]{0:T(128)} %bitcast.1.core_ref, s32[1,112]{1,0:T(1,128)S(1)} %copy-done.3, s32[1,112]{1,0:T(1,128)S(1)} %copy-done.4, s32[1,64]{1,0:T(1,128)S(1)} %copy-done.5, bf16[4,128,1024]{2,1,0:T(8,128)(2,1)S(1)} %all_to_all.31.own_ref, bf16[4,128,1024]{2,1,0:T(8,128)(2,1)S(1)} %collective-permute-done.other_ref, ...), custom_call_target="tpu_custom_call" | custom-call | flops 469762048 | bytes 8388608 | tf_op jit(solution)/shard_map/tiles/pallas_call | solution.py:173
  52.8 4.9 %all-to-all-start.1 = ((bf16[128,128,128]{2,1,0:T(8,128)(2,1)}), bf16[128,128,128]{2,1,0:T(8,128)(2,1)}, u32[]{:S(2)}, u32[]{:S(2)}) async-start(bf16[128,128,128]{2,1,0:T(8,128)(2,1)} %tiles.1), calls=%async_computation.1 | async-start | bytes 8388608 | tf_op jit(solution)/shard_map/all_to_all | solution.py:24
  57.7 48.6 %all-to-all-done.1 = bf16[128,128,128]{2,1,0:T(8,128)(2,1)} async-done(((bf16[128,128,128]{2,1,0:T(8,128)(2,1)}), bf16[128,128,128]{2,1,0:T(8,128)(2,1)}, u32[]{:S(2)}, u32[]{:S(2)}) %all-to-all-start.1) | async-done | bytes 4194336 | tf_op jit(solution)/shard_map/all_to_all | solution.py:24
  106.3 4.2 %reduce_sum.48 = bf16[32,128,128]{2,1,0:T(8,128)(2,1)} reduce(bf16[4,32,128,128]{3,2,1,0:T(8,128)(2,1)} %bitcast.2, bf16[]{:T(256)} %constant.84.clone.1), dimensions={0}, to_apply=%region_0.0 | reduce | flops 1572864 | bytes 5242882 | tf_op jit(solution)/shard_map/reduce_sum | solution.py:191
  110.6 15.0 %all-to-all-start.2 = ((bf16[32,128,128]{2,1,0:T(8,128)(2,1)}), bf16[32,128,128]{2,1,0:T(8,128)(2,1)}, u32[]{:S(2)}, u32[]{:S(2)}) async-start(bf16[32,128,128]{2,1,0:T(8,128)(2,1)} %reduce_sum.48), calls=%async_computation.2 | async-start | bytes 2097152 | tf_op jit(solution)/shard_map/all_to_all | solution.py:24
  125.5 0.0 all-gather.5.cloned.1.call-start
  125.6 0.0 all-gather.3.cloned.1.call-done.delta_ref
  125.6 8.9 %contribs.1 = bf16[128,8192]{1,0:T(8,128)(2,1)S(1)} custom-call(s32[1,112]{1,0:T(1,128)S(1)} %copy-done.3, s32[1,112]{1,0:T(1,128)S(1)} %copy-done.4, s32[1,64]{1,0:T(1,128)S(1)} %copy-done.5, bf16[14,128,128]{2,1,0:T(8,128)(2,1)S(1)} %get-tuple-element.13.grad_ref, bf16[128,128,128]{2,1,0:T(8,128)(2,1)} %all-gather.3.cloned.1.call-done.delta_ref), custom_call_target="tpu_custom_call" | custom-call | bytes 65536 | tf_op jit(solution)/shard_map/contribs/pallas_call | solution.py:199
  134.5 0.1 dynamic-slice_bitcast_fusion
  134.6 3.4 %collective-permute-start.1 = (bf16[4,16,8192]{2,1,0:T(8,128)(2,1)S(1)}, bf16[4,16,8192]{2,1,0:T(8,128)(2,1)}, u32[]{:S(2)}, u32[]{:S(2)}) collective-permute-start(bf16[4,16,8192]{2,1,0:T(8,128)(2,1)S(1)} %dynamic-slice_bitcast_fusion), channel_id=1, source_target_pairs={{0,1},{1,0},{2,3},{3,2},{4,5},{5,4},{6,7},{7,6},{8,9},{9,8},{10,11... | collective-permute-start | bytes 3145736 | tf_op jit(solution)/shard_map/ppermute | solution.py:20
  138.1 0.6 constant_dynamic-slice_fusion
  138.7 0.6 iota_compare_fusion
  139.3 1.1 collective-permute-done.1
  140.4 1.5 fusion
  141.9 0.1 dynamic-slice_bitcast_fusion.3
  142.0 0.0 copy-start.6
  142.0 0.0 copy-start.7
  142.0 2.9 %collective-permute-start.4 = (bf16[16,8192]{1,0:T(8,128)(2,1)S(1)}, bf16[16,8192]{1,0:T(8,128)(2,1)S(1)}, u32[]{:S(2)}, u32[]{:S(2)}) collective-permute-start(bf16[16,8192]{1,0:T(8,128)(2,1)S(1)} %get-tuple-element.25), channel_id=1, source_target_pairs={{0,6},{2,0},{4,2},{6,4},{1,7},{3,1},{5,3},{7,5},{8,14},{10,8},{12,... | collective-permute-start | bytes 786440 | tf_op jit(solution)/shard_map/ppermute | solution.py:20
  144.9 3.1 %collective-permute-start.3 = (bf16[16,8192]{1,0:T(8,128)(2,1)S(1)}, bf16[16,8192]{1,0:T(8,128)(2,1)S(1)}, u32[]{:S(2)}, u32[]{:S(2)}) collective-permute-start(bf16[16,8192]{1,0:T(8,128)(2,1)S(1)} %get-tuple-element.26), channel_id=1, source_target_pairs={{0,4},{2,6},{4,0},{6,2},{1,5},{3,7},{5,1},{7,3},{8,12},{10,14},{12... | collective-permute-start | bytes 786440 | tf_op jit(solution)/shard_map/ppermute | solution.py:20
  148.0 1.9 collective-permute-start.2
  150.0 20.0 %all-to-all-done.2 = bf16[32,128,128]{2,1,0:T(8,128)(2,1)} async-done(((bf16[32,128,128]{2,1,0:T(8,128)(2,1)}), bf16[32,128,128]{2,1,0:T(8,128)(2,1)}, u32[]{:S(2)}, u32[]{:S(2)}) %all-to-all-start.2) | async-done | bytes 1048608 | tf_op jit(solution)/shard_map/all_to_all | solution.py:24
  169.9 1.4 convert_reduce_fusion
  171.3 0.1 broadcast_select_fusion
  171.4 0.0 collective-permute-done.4
  171.4 0.0 collective-permute-done.3
  171.4 0.0 collective-permute-done.2
  171.4 0.8 fusion.3
  172.3 0.0 all-gather.5.cloned.1.call-update
  172.3 0.6 multiply_reduce_fusion
  172.9 0.7 broadcast_in_dim_broadcast_in_dim_broadcast_in_dim.4
  173.6 17.1 %all_to_all.32 = f32[32,8,128]{2,1,0:T(8,128)S(1)} all-to-all(f32[32,8,128]{2,1,0:T(8,128)S(1)} %broadcast_in_dim_broadcast_in_dim_broadcast_in_dim.4), channel_id=1, replica_groups=mesh['y'=4,'z'=16,'x'=4,'core'=2] {'y','x','core'}, dimensions={0} | all-to-all | bytes 262144 | tf_op jit(solution)/shard_map/all_to_all | solution.py:24
  190.7 0.6 slice_reduce_fusion
  191.4 1.3 broadcast_in_dim_broadcast_in_dim_broadcast_in_dim.5
  192.7 7.7 %all-to-all-start.5 = ((f32[16,8,128]{2,1,0:T(8,128)}), f32[16,8,128]{2,1,0:T(8,128)S(1)}, u32[]{:S(2)}, u32[]{:S(2)}) async-start(f32[16,8,128]{2,1,0:T(8,128)} %broadcast_in_dim_broadcast_in_dim_broadcast_in_dim.5), calls=%async_computation.5 | async-start | bytes 131072 | tf_op jit(solution)/shard_map/all_to_all | solution.py:24
  200.4 0.1 copy.33
  200.5 0.1 copy.31
  200.6 0.1 copy.28
  200.7 11.3 %all-to-all-done.5 = f32[16,8,128]{2,1,0:T(8,128)S(1)} async-done(((f32[16,8,128]{2,1,0:T(8,128)}), f32[16,8,128]{2,1,0:T(8,128)S(1)}, u32[]{:S(2)}, u32[]{:S(2)}) %all-to-all-start.5) | async-done | bytes 65568 | tf_op jit(solution)/shard_map/all_to_all | solution.py:24
  212.0 0.6 slice_reduce_fusion.1
  213.3 0.1 fusion.7
  213.4 0.8 copy.37
  214.2 0.8 copy.38
  214.9 0.8 copy.39
  215.7 3.1 %copy.44 = bf16[128,8192]{1,0:T(8,128)(2,1)} copy(bf16[128,8192]{1,0:T(8,128)(2,1)} %all-gather.5.cloned.1.call-done) | data formatting | bytes 4194304
  (7 shorter events, 0.0 us)
Async XLA Ops:
  7.2 118.4 %all-gather.3.cloned.1.call-start = ((), (), s32[]{:S(2)}) async-start(), calls=%async_computation.6 | async-start | bytes 4456448 | tf_op jit(solution)/shard_map/all_gather | solution.py:159
  8.2 33.6 %copy-start = (bf16[128,1792]{1,0:T(8,128)(2,1)S(1)}, bf16[128,1792]{1,0:T(8,128)(2,1)}, u32[]{:S(2)}) copy-start(bf16[128,1792]{1,0:T(8,128)(2,1)} %gate_ref.1) | copy-start | bytes 1376260
  8.2 33.6 %copy-start.1 = (bf16[128,1792]{1,0:T(8,128)(2,1)S(1)}, bf16[128,1792]{1,0:T(8,128)(2,1)}, u32[]{:S(2)}) copy-start(bf16[128,1792]{1,0:T(8,128)(2,1)} %up_ref.1) | copy-start | bytes 1376260
  18.8 25.2 %copy-start.3 = (s32[1,112]{1,0:T(1,128)S(1)}, s32[1,112]{1,0:T(1,128)}, u32[]{:S(2)}) copy-start(s32[1,112]{1,0:T(1,128)} %rows_ref.3) | copy-start | bytes 1348
  18.8 25.2 %copy-start.4 = (s32[1,112]{1,0:T(1,128)S(1)}, s32[1,112]{1,0:T(1,128)}, u32[]{:S(2)}) copy-start(s32[1,112]{1,0:T(1,128)} %cols_ref.3) | copy-start | bytes 1348
  18.8 25.2 %copy-start.5 = (s32[1,64]{1,0:T(1,128)S(1)}, s32[1,64]{1,0:T(1,128)}, u32[]{:S(2)}) copy-start(s32[1,64]{1,0:T(1,128)} %counts_ref.3) | copy-start | bytes 772
  33.8 10.2 %collective-permute-start = (bf16[4,128,1024]{2,1,0:T(8,128)(2,1)S(1)}, bf16[4,128,1024]{2,1,0:T(8,128)(2,1)S(1)}, u32[]{:S(2)}, u32[]{:S(2)}) collective-permute-start(bf16[4,128,1024]{2,1,0:T(8,128)(2,1)S(1)} %all_to_all.31.own_ref), channel_id=1, source_target_pairs={{0,1},{1,0},{2,3},{3,2},{4,5},{5,4},{6,7},{7,6},{8,9},{9,8},{10,11... | collective-permute-start | bytes 3145736 | tf_op jit(solution)/shard_map/ppermute | solution.py:20
  41.7 1.0 copy-start.2
  52.8 53.5 %all-to-all-start.1 = ((bf16[128,128,128]{2,1,0:T(8,128)(2,1)}), bf16[128,128,128]{2,1,0:T(8,128)(2,1)}, u32[]{:S(2)}, u32[]{:S(2)}) async-start(bf16[128,128,128]{2,1,0:T(8,128)(2,1)} %tiles.1), calls=%async_computation.1 | async-start | bytes 8388608 | tf_op jit(solution)/shard_map/all_to_all | solution.py:24
  110.6 59.4 %all-to-all-start.2 = ((bf16[32,128,128]{2,1,0:T(8,128)(2,1)}), bf16[32,128,128]{2,1,0:T(8,128)(2,1)}, u32[]{:S(2)}, u32[]{:S(2)}) async-start(bf16[32,128,128]{2,1,0:T(8,128)(2,1)} %reduce_sum.48), calls=%async_computation.2 | async-start | bytes 2097152 | tf_op jit(solution)/shard_map/all_to_all | solution.py:24
  125.5 90.2 %all-gather.5.cloned.1.call-start = ((), (), s32[]{:S(2)}) async-start(), calls=%async_computation.7 | async-start | bytes 2359296 | tf_op jit(solution)/shard_map/all_gather | solution.py:224
  134.6 5.8 %collective-permute-start.1 = (bf16[4,16,8192]{2,1,0:T(8,128)(2,1)S(1)}, bf16[4,16,8192]{2,1,0:T(8,128)(2,1)}, u32[]{:S(2)}, u32[]{:S(2)}) collective-permute-start(bf16[4,16,8192]{2,1,0:T(8,128)(2,1)S(1)} %dynamic-slice_bitcast_fusion), channel_id=1, source_target_pairs={{0,1},{1,0},{2,3},{3,2},{4,5},{5,4},{6,7},{7,6},{8,9},{9,8},{10,11... | collective-permute-start | bytes 3145736 | tf_op jit(solution)/shard_map/ppermute | solution.py:20
  142.0 58.4 %copy-start.6 = (f32[1,2,128,128]{3,2,1,0:T(8,128)S(1)}, f32[1,2,128,128]{3,2,1,0:T(8,128)}, u32[]{:S(2)}) copy-start(f32[1,2,128,128]{3,2,1,0:T(8,128)} %param.17) | copy-start | bytes 393220
  142.0 58.5 %copy-start.7 = (f32[1,2,128,128]{3,2,1,0:T(8,128)S(1)}, f32[1,2,128,128]{3,2,1,0:T(8,128)}, u32[]{:S(2)}) copy-start(f32[1,2,128,128]{3,2,1,0:T(8,128)} %param.19) | copy-start | bytes 393220
  142.0 29.4 %collective-permute-start.4 = (bf16[16,8192]{1,0:T(8,128)(2,1)S(1)}, bf16[16,8192]{1,0:T(8,128)(2,1)S(1)}, u32[]{:S(2)}, u32[]{:S(2)}) collective-permute-start(bf16[16,8192]{1,0:T(8,128)(2,1)S(1)} %get-tuple-element.25), channel_id=1, source_target_pairs={{0,6},{2,0},{4,2},{6,4},{1,7},{3,1},{5,3},{7,5},{8,14},{10,8},{12,... | collective-permute-start | bytes 786440 | tf_op jit(solution)/shard_map/ppermute | solution.py:20
  144.9 26.5 %collective-permute-start.3 = (bf16[16,8192]{1,0:T(8,128)(2,1)S(1)}, bf16[16,8192]{1,0:T(8,128)(2,1)S(1)}, u32[]{:S(2)}, u32[]{:S(2)}) collective-permute-start(bf16[16,8192]{1,0:T(8,128)(2,1)S(1)} %get-tuple-element.26), channel_id=1, source_target_pairs={{0,4},{2,6},{4,0},{6,2},{1,5},{3,7},{5,1},{7,3},{8,12},{10,14},{12... | collective-permute-start | bytes 786440 | tf_op jit(solution)/shard_map/ppermute | solution.py:20
  148.0 23.4 %collective-permute-start.2 = (bf16[16,8192]{1,0:T(8,128)(2,1)S(1)}, bf16[16,8192]{1,0:T(8,128)(2,1)S(1)}, u32[]{:S(2)}, u32[]{:S(2)}) collective-permute-start(bf16[16,8192]{1,0:T(8,128)(2,1)S(1)} %get-tuple-element.24), channel_id=1, source_target_pairs={{0,2},{2,4},{4,6},{6,0},{1,3},{3,5},{5,7},{7,1},{8,10},{10,12},{12... | collective-permute-start | bytes 786440 | tf_op jit(solution)/shard_map/ppermute | solution.py:20
  169.9 30.7 %copy-start.8 = (f32[1,2,128,128]{3,2,1,0:T(8,128)S(1)}, f32[1,2,128,128]{3,2,1,0:T(8,128)}, u32[]{:S(2)}) copy-start(f32[1,2,128,128]{3,2,1,0:T(8,128)} %param.18) | copy-start | bytes 393220
  192.7 19.3 %all-to-all-start.5 = ((f32[16,8,128]{2,1,0:T(8,128)}), f32[16,8,128]{2,1,0:T(8,128)S(1)}, u32[]{:S(2)}, u32[]{:S(2)}) async-start(f32[16,8,128]{2,1,0:T(8,128)} %broadcast_in_dim_broadcast_in_dim_broadcast_in_dim.5), calls=%async_computation.5 | async-start | bytes 131072 | tf_op jit(solution)/shard_map/all_to_all | solution.py:24
Sparse Core Ops, SparseCore 0:
  18.9 74.3 all-gather.2
  172.4 32.4 all-gather.4

commit v3 on v2

v3 whole, which is shorter than its diff:
```python
import jax
import jax.numpy as jnp
from jax import lax
from jax.experimental import pallas as pl
from jax.experimental.pallas import tpu as pltpu
from jax.sharding import Mesh, PartitionSpec as P

NY, NM, NX = 4, 8, 4
Z = ("m", "p")
TILE = 128
SLOT_CAP = 2
GROUP = 2 * NM * SLOT_CAP
BF16, F32 = jnp.bfloat16, jnp.float32
SMEM = pl.BlockSpec(memory_space=pltpu.SMEM)
VMEM = pl.BlockSpec(memory_space=pltpu.VMEM)
ANY = pl.BlockSpec(memory_space=pl.ANY)
SHAPE = jax.ShapeDtypeStruct


def kernel_call(kernel, name, outs, ins, out_specs, scratch=(), flops=0, moved=1 << 20):
    return pl.pallas_call(
        kernel,
        out_shape=outs,
        in_specs=ins,
        out_specs=out_specs,
        scratch_shapes=scratch,
        compiler_params=pltpu.CompilerParams(vmem_limit_bytes=48 * 1024 * 1024),
        cost_estimate=pl.CostEstimate(flops=flops, bytes_accessed=moved, transcendentals=0),
        name=name,
    )


def shift(value, axis, step):
    size = lax.axis_size(axis)
    return lax.ppermute(value, axis, [(i, (i + step) % size) for i in range(size)])


def exchange(value, axis):
    return lax.all_to_all(value, axis, split_axis=0, concat_axis=0, tiled=True)


def spread(value, axis):
    copies = jnp.broadcast_to(value[None], (lax.axis_size(axis),) + value.shape)
    return exchange(copies, axis)


def gate_kernel(ids_ref, gate_ref, up_ref, hidden_ref, grad_ref, turned_ref):
    blocks = 2 * NX
    rows = grad_ref.shape[1] // blocks
    core = ids_ref[3]
    for col in range(grad_ref.shape[0]):
        cut = slice(col * TILE, (col + 1) * TILE)
        gate = gate_ref[:, cut].astype(F32)
        sig = 1.0 / (1.0 + jnp.exp(-gate))
        value = (
            hidden_ref[:, cut].astype(F32)
            * up_ref[:, cut].astype(F32)
            * sig
            * (1.0 + gate * (1.0 - sig))
        )
        for block in range(blocks):
            place = pl.multiple_of((((block & 1) ^ core) * NX + (block >> 1)) * rows, rows)
            part = value[block * rows : (block + 1) * rows]
            grad_ref[col, pl.ds(place, rows)] = part.astype(BF16)
        turned_ref[col] = value.T.astype(BF16)


def load_features(own_ref, other_ref, features, sems, starts_ref, counts_ref):
    first = pltpu.make_async_copy(own_ref, features.at[0], sems.at[0])
    second = pltpu.make_async_copy(other_ref, features.at[1], sems.at[1])
    first.start()
    second.start()

    def owner_step(owner, start):
        starts_ref[owner] = start
        return start + counts_ref[0, owner]

    lax.fori_loop(0, counts_ref.shape[1], owner_step, 0)
    first.wait()
    second.wait()


def slot_products(group, owners, put, ids_ref, rows_ref, cols_ref, starts_ref, features, turned_ref):
    core = ids_ref[3]
    last = rows_ref.shape[1] - 1
    per_step = 4

    def step(index, carry):
        for part in range(per_step):
            owner = owners[0] + index * per_step + part
            start = starts_ref[group * 2 * NM + owner]
            for rank in range(SLOT_CAP):
                k = jnp.minimum(start + rank, last)
                row = rows_ref[0, k]
                lane = pl.multiple_of((row & 7) * TILE, TILE)
                x = features[((row >> 3) & 1) ^ core, row >> 4, :, pl.ds(lane, TILE)]
                term = jnp.dot(turned_ref[cols_ref[0, k]], x, preferred_element_type=F32)
                put((index * per_step + part) * SLOT_CAP + rank, term.astype(BF16))
        return carry

    lax.fori_loop(0, (owners[1] - owners[0]) // per_step, step, 0)


def far_kernel(
    ids_ref, rows_ref, cols_ref, counts_ref, own_ref, other_ref, turned_ref,
    low_ref, high_ref, features, starts_ref, sems,
):
    load_features(own_ref, other_ref, features, sems, starts_ref, counts_ref)
    group = (ids_ref[0] + 2) & (NY - 1)
    for ref, owners in ((low_ref, (0, NM)), (high_ref, (NM, 2 * NM))):

        def put(slot, term, ref=ref):
            ref[slot] = term

        slot_products(
            group, owners, put, ids_ref, rows_ref, cols_ref, starts_ref, features, turned_ref
        )


def near_kernel(
    ids_ref, rows_ref, cols_ref, counts_ref, own_ref, other_ref, turned_ref,
    up_ref, down_ref, mine_ref, features, starts_ref, sems,
):
    load_features(own_ref, other_ref, features, sems, starts_ref, counts_ref)
    for ref, away in ((up_ref, 1), (down_ref, 3), (mine_ref, 0)):

        def put(slot, term, ref=ref):
            ref[slot] = term

        slot_products(
            (ids_ref[0] + away) & (NY - 1), (0, 2 * NM), put,
            ids_ref, rows_ref, cols_ref, starts_ref, features, turned_ref,
        )


def passing_kernel(up_ref, low_ref, down_ref, high_ref, up_out, down_out):
    half = GROUP // 2
    up_out[:half] = (up_ref[:half].astype(F32) + low_ref[...].astype(F32)).astype(BF16)
    up_out[half:] = up_ref[half:]
    down_out[:half] = down_ref[:half]
    down_out[half:] = (down_ref[half:].astype(F32) + high_ref[...].astype(F32)).astype(BF16)


def y_sum_kernel(ids_ref, mine_ref, below_ref, above_ref, keep_ref, low_ref, high_ref):
    parity = ids_ref[1] & 1
    for m in range(NM):

        def total(side):
            return (
                mine_ref[m, side].astype(F32)
                + below_ref[m, side].astype(F32)
                + above_ref[m, side].astype(F32)
            ).astype(BF16)

        keep_ref[m] = total(parity)
        if m < NM // 2:
            low_ref[m] = total(1 - parity)
        else:
            high_ref[m - NM // 2] = total(1 - parity)


def pair_sum_kernel(keep_ref, low_ref, high_ref, out_ref):
    half = NM // 2
    out_ref[:half] = (keep_ref[:half].astype(F32) + low_ref[...].astype(F32)).astype(BF16)
    out_ref[half:] = (keep_ref[half:].astype(F32) + high_ref[...].astype(F32)).astype(BF16)


def own_grad_kernel(ids_ref, counts_ref, arrived_ref, grad_ref, squares_ref):
    count = counts_ref[0, ids_ref[0] * 2 * NM + ids_ref[1]]
    squares = jnp.zeros((TILE, TILE), F32)
    for rank in range(SLOT_CAP):
        total = arrived_ref[0, rank].astype(F32)
        for m in range(1, NM):
            total = total + arrived_ref[m, rank].astype(F32)
        total = jnp.where(rank < count, total, 0.0)
        grad_ref[rank] = total
        squares = squares + total * total
    squares_ref[...] = jnp.broadcast_to(jnp.sum(squares), squares_ref.shape)


def relay_kernel(arrived_ref, out_ref):
    total = jnp.sum(arrived_ref[...], axis=0, keepdims=True)
    out_ref[...] = jnp.broadcast_to(total, out_ref.shape)


def adam_kernel(
    count_all, ids_ref, counts_ref, arrived_ref, grad_ref, delta_ref, one_ref, two_ref,
    new_delta_ref, new_one_ref, new_two_ref,
):
    squares = jnp.sum(arrived_ref[...], axis=0)[0:1]
    factor = jnp.minimum(1.0, 1.0 / jnp.sqrt(squares / count_all + 1e-06))
    count = counts_ref[0, ids_ref[0] * 2 * NM + ids_ref[1]]
    for rank in range(SLOT_CAP):
        live = rank < count
        clipped = factor * grad_ref[rank].T
        delta, one, two = delta_ref[0, rank], one_ref[0, rank], two_ref[0, rank]
        first = 0.9 * one + 0.1 * clipped
        second = 0.95 * two + 0.05 * clipped * clipped
        size = first / (1.0 - 0.9**10) / (jnp.sqrt(second / (1.0 - 0.95**10)) + 1e-08)
        updated = delta - 0.02 * (size + 0.1 * delta)
        new_delta_ref[0, rank] = jnp.where(live, updated, delta)
        new_one_ref[0, rank] = jnp.where(live, first, one)
        new_two_ref[0, rank] = jnp.where(live, second, two)


def contrib_kernel(
    ids_ref, rows_ref, cols_ref, counts_ref, grad_ref, delta_ref, stay_ref, give_ref, places_ref
):
    stay_ref[...] = jnp.zeros_like(stay_ref)
    give_ref[...] = jnp.zeros_like(give_ref)
    half = stay_ref.shape[0]
    y = ids_ref[0]

    def owner_step(owner, start):
        place = ((owner & 15) * NY + (((owner >> 4) - y) & (NY - 1))) * SLOT_CAP
        places_ref[start] = place
        places_ref[start + 1] = place + 1
        return start + counts_ref[0, owner]

    lax.fori_loop(0, counts_ref.shape[1], owner_step, 0)
    per_step = 4

    def step(index, carry):
        last, total = carry
        for part in range(per_step):
            k = index * per_step + part
            row = rows_ref[0, k]
            product = lax.dot_general(
                grad_ref[cols_ref[0, k]], delta_ref[places_ref[k]],
                (((1,), (1,)), ((), ())), preferred_element_type=F32,
            )
            total = jnp.where(row == last, total, 0.0) + product
            lane = pl.multiple_of(row * TILE, TILE)
            stay_ref[:, pl.ds(lane, TILE)] = total[:half].astype(BF16)
            give_ref[:, pl.ds(lane, TILE)] = total[half:].astype(BF16)
            last = row
        return last, total

    lax.fori_loop(
        0, rows_ref.shape[1] // per_step, step,
        (jnp.int32(-1), jnp.zeros((TILE, TILE), F32)),
    )


def core_sum_kernel(ids_ref, stay_ref, taken_ref, *out_refs):
    for away, ref in enumerate(out_refs):
        at = (ids_ref[2] + away) & (NX - 1)
        ref[...] = (stay_ref[at].astype(F32) + taken_ref[at].astype(F32)).astype(BF16)


def copy_kernel(in_ref, out_ref, sem):
    copy = pltpu.make_async_copy(in_ref, out_ref, sem)
    copy.start()
    copy.wait()


def body(
    features, gate_pre, up_pre, hidden_grad, tile_rows, tile_cols, owner_counts,
    delta_value, moment_one, moment_two,
):
    ids = jnp.stack([lax.axis_index(name) for name in ("y", Z, "x", "core")]).astype(jnp.int32)
    tokens, hidden = gate_pre.shape
    shard_width = features.shape[1]
    width = shard_width * NX * 2
    tile_total = tile_rows.shape[1]
    lists = (tile_rows, tile_cols, owner_counts)

    own = spread(features, "x")
    other = shift(own, "core", 1)

    delta_half = delta_value[0].astype(BF16)
    delta_y = jnp.concatenate(
        [delta_half] + [shift(delta_half, "y", -away) for away in range(1, NY)], axis=0
    )
    _, delta_y = lax.optimization_barrier((own, delta_y))
    delta_all = lax.all_gather(delta_y, Z, axis=0, tiled=True)

    grads, turned = kernel_call(
        gate_kernel, "gate", [SHAPE((hidden // TILE, tokens, TILE), BF16)] * 2,
        [SMEM] + [VMEM] * 3, [VMEM] * 2, flops=tokens * hidden * 12, moved=tokens * hidden * 10,
    )(ids, gate_pre, up_pre, hidden_grad)

    tile_ins = [SMEM] * 4 + [ANY, ANY, VMEM]
    tile_scratch = [
        pltpu.VMEM((2, NX, tokens, shard_width), BF16),
        pltpu.SMEM((owner_counts.shape[1],), jnp.int32),
        pltpu.SemaphoreType.DMA((2,)),
    ]
    half = (GROUP // 2, TILE, TILE)
    whole = (GROUP, TILE, TILE)
    low, high = kernel_call(
        far_kernel, "tiles_far", [SHAPE(half, BF16)] * 2, tile_ins, [VMEM] * 2, tile_scratch,
        flops=2 * GROUP * TILE**3, moved=4 << 20,
    )(ids, *lists, own, other, turned)

    low = shift(low, "y", 1)
    high = shift(high, "y", -1)
    up, down, mine = kernel_call(
        near_kernel, "tiles_near", [SHAPE(whole, BF16)] * 3, tile_ins, [VMEM] * 3, tile_scratch,
        flops=6 * GROUP * TILE**3, moved=4 << 20,
    )(ids, *lists, own, other, turned)
    up, down = kernel_call(
        passing_kernel, "passing", [SHAPE(whole, BF16)] * 2, [VMEM] * 4, [VMEM] * 2
    )(up, low, down, high)
    below = shift(up, "y", 1)
    above = shift(down, "y", -1)
    parted = (NM, 2, SLOT_CAP, TILE, TILE)
    quarter = SHAPE((NM // 2, SLOT_CAP, TILE, TILE), BF16)
    kept = SHAPE((NM, SLOT_CAP, TILE, TILE), BF16)
    keep, low, high = kernel_call(
        y_sum_kernel, "y_sum", [kept, quarter, quarter], [SMEM] + [VMEM] * 3, [VMEM] * 3
    )(ids, mine.reshape(parted), below.reshape(parted), above.reshape(parted))

    low = shift(low, Z, 1)
    high = shift(high, Z, -1)
    pairs = kernel_call(pair_sum_kernel, "pair_sum", kept, [VMEM] * 3, VMEM)(keep, low, high)
    pairs, grads = lax.optimization_barrier((pairs, grads))
    arrived = exchange(pairs, "m")
    own_grad, squares = kernel_call(
        own_grad_kernel, "own_grad",
        [SHAPE((SLOT_CAP, TILE, TILE), F32), SHAPE((NY * NX * 2, 8, TILE), F32)],
        [SMEM, SMEM, VMEM], [VMEM] * 2,
    )(ids, owner_counts, arrived)

    stay, give = kernel_call(
        contrib_kernel, "contribs", [SHAPE((tokens // 2, width), BF16)] * 2,
        [SMEM] * 4 + [VMEM] * 2, [VMEM] * 2, [pltpu.SMEM((tile_total + 8,), jnp.int32)],
        moved=1 << 12,
    )(ids, *lists, grads, delta_all)

    rows = tokens // (2 * NX)
    taken = shift(give, "core", 1)
    share, *others = kernel_call(
        core_sum_kernel, "core_sum", [SHAPE((rows, width), BF16)] * NX,
        [SMEM] + [VMEM] * 2, [VMEM] * NX, moved=1 << 12,
    )(ids, stay.reshape(NX, rows, width), taken.reshape(NX, rows, width))
    share = share.astype(F32)
    for away, part in enumerate(others):
        share = share + shift(part, "x", away + 1).astype(F32)
    squares, share = lax.optimization_barrier((squares, share.astype(BF16)))
    gathered = lax.all_gather(share, ("x", "core"), axis=0, tiled=True)
    input_grad = kernel_call(
        copy_kernel, "result", SHAPE((tokens, width), BF16), [ANY], ANY,
        [pltpu.SemaphoreType.DMA], moved=4 << 20,
    )(gathered)

    squares = exchange(squares, ("y", "x", "core"))
    squares = kernel_call(relay_kernel, "relay", SHAPE((2 * NM, 8, TILE), F32), [VMEM], VMEM)(squares)
    squares = exchange(squares, Z)
    squares, input_grad = lax.optimization_barrier((squares, input_grad))
    count_all = float(NX * 2 * tile_total * TILE * TILE)

    def adam(*refs):
        adam_kernel(count_all, *refs)

    outs = kernel_call(
        adam, "adam", [SHAPE(delta_value.shape, F32)] * 3, [SMEM] * 2 + [VMEM] * 5, [VMEM] * 3
    )(ids, owner_counts, squares, own_grad, delta_value, moment_one, moment_two)
    return (input_grad, *outs)


def solution(mesh):
    grid = Mesh(mesh.devices.reshape(NY, NM, 2, NX, 2), ("y", "m", "p", "x", "core"))
    dp, tensor = ("y", "m", "p"), ("x", "core")
    tokens = P(dp, tensor)
    lists = P(tensor, None)
    slots = P(tensor, dp, None, None)
    return jax.shard_map(
        body,
        mesh=grid,
        in_specs=(tokens,) * 4 + (lists,) * 3 + (slots,) * 3,
        out_specs=(P(dp, None),) + (slots,) * 3,
        check_vma=False,
    )
```

time: 226 us -> 201 us (0.89)
  starting transfers between devices: 46.8 us -> 78.7 us
  blocking collectives: 41.6 us -> 12.8 us
  waiting for transfers between devices: 81.7 us -> 63.7 us
  other arithmetic: 11.6 us -> 1.68 us
  Pallas kernels: 18.3 us -> 23.2 us
  local copies, waits for them, and re-layouts: 10.5 us -> 5.77 us
    all_to_all x3, waiting for transfers between devices: 79.8 us -> 3.28 us  [exchange(): return lax.all_to_all(value, axis, split_axis=0, concat_axis=0, tiled=True)]
    ppermute x5 -> x14, waiting for transfers between devices: 1.78 us -> 53.3 us  [shift(): lax.ppermute(value, axis, [(i, (i + step) % size) for i in range(size)])]
    ppermute x5 -> x14, starting transfers between devices: 19.2 us -> 54 us  [shift(): lax.ppermute(value, axis, [(i, (i + step) % size) for i in range(size)])]
    all_to_all x3 -> x1, blocking collectives: 41.6 us -> 12.8 us  [exchange(): return lax.all_to_all(value, axis, split_axis=0, concat_axis=0, tiled=True)]
    reduce_sum x5 -> x0, other arithmetic: 7.55 us -> none  [the longest x1 4.25 us: body(): summed = jnp.sum(arrived.astype(jnp.float32), axis=0).astype(bf16)]
    all_gather x2, waiting for transfers between devices: 0.02 us -> 7.1 us  [the longest x1 7.08 us: body(): gathered = lax.all_gather(share, ('x', 'core'), axis=0, tiled=True)]
    pallas_call x3 -> x12, Pallas kernels: 18.3 us -> 23.2 us  [the longest x1 8.87 us: body(): kernel_call(contrib_kernel, 'contribs', [SHAPE((tokens // 2, width), BF16...]
    unnamed x25 -> x20, local copies, waits for them, and re-layouts: 6.71 us -> 3.66 us
  transfers between devices with their start and end apart: 10 -> 19, of which waited for: 5 -> 12; matrix products, arithmetic and copies ran while one was open for 7% -> 0% of each run, Pallas kernels for 8% -> 11%
where the time goes in v3:
time: 201 us; the launch traced here: 200 us
  starting transfers between devices  78.7 us (39%)
  waiting for transfers between devices  63.7 us (32%)
  Pallas kernels  23.2 us (12%)
  between operations  14.3 us (7%)
  blocking collectives  12.8 us (6%)
  local copies, waits for them, and re-layouts  5.77 us (3%)
    ppermute x14, starting transfers between devices, shift(): lax.ppermute(value, axis, [(i, (i + step) % size) for i in range(size)])  54 us
    ppermute x14, waiting for transfers between devices, shift(): lax.ppermute(value, axis, [(i, (i + step) % size) for i in range(size)])  53.3 us
    all_to_all x3, starting transfers between devices, exchange(): return lax.all_to_all(value, axis, split_axis=0, concat_axis=0, tiled=True)  24.6 us
    all_to_all x1, blocking collectives, exchange(): return lax.all_to_all(value, axis, split_axis=0, concat_axis=0, tiled=True)  12.8 us
    pallas_call x1, Pallas kernels, body(): kernel_call(contrib_kernel, 'contribs', [SHAPE((tokens // 2, width), BF16...  8.87 us
    all_gather x1, waiting for transfers between devices, body(): gathered = lax.all_gather(share, ('x', 'core'), axis=0, tiled=True)  7.08 us
    pallas_call x1, Pallas kernels, body(): kernel_call(near_kernel, 'tiles_near', [SHAPE(whole, BF16)] * 3, tile_ins...  4.04 us
  transfers between devices with their start and end apart: 19, of which 12 were waited for; matrix products, arithmetic and copies ran while one was open for 0% of the time, Pallas kernels for 11%

profile of v3, /device:TPU:1, one launch (start us, length us, event | category | flops | bytes accessed | tf_op | source)
XLA Modules:
  0.0 200.2 jit_solution(14834972779644481270)
XLA Ops:
  7.2 0.0 copy-start.1
  7.2 0.0 copy-start.2
  7.2 2.1 %broadcast_in_dim.2 = bf16[4,128,1024]{2,1,0:T(8,128)(2,1)} broadcast(bf16[128,1024]{1,0:T(8,128)(2,1)} %param.10), dimensions={1,2} | broadcast | bytes 1310720 | tf_op jit(solution)/shard_map/broadcast_in_dim | solution.py:43
  9.3 5.0 %all-to-all-start = ((bf16[4,128,1024]{2,1,0:T(8,128)(2,1)}), bf16[4,128,1024]{2,1,0:T(8,128)(2,1)S(1)}, u32[]{:S(2)}, u32[]{:S(2)}) async-start(bf16[4,128,1024]{2,1,0:T(8,128)(2,1)} %broadcast_in_dim.2), calls=%async_computation | async-start | bytes 2097152 | tf_op jit(solution)/shard_map/all_to_all | solution.py:39
  14.3 0.0 all-gather.3.cloned.1.call-start
  14.3 0.0 copy-done.1
  14.3 3.2 %collective-permute-start.9 = (bf16[2,128,128]{2,1,0:T(8,128)(2,1)S(1)}, bf16[2,128,128]{2,1,0:T(8,128)(2,1)S(1)}, u32[]{:S(2)}, u32[]{:S(2)}) collective-permute-start(bf16[2,128,128]{2,1,0:T(8,128)(2,1)S(1)} %convert_bitcast_fusion), channel_id=1, source_target_pairs={{0,128},{128,256},{256,384},{384,0},{1,129},{129,257},{257,385},{3... | collective-permute-start | bytes 196616 | tf_op jit(solution)/shard_map/ppermute | solution.py:35
  17.5 4.5 %collective-permute-start.8 = (bf16[2,128,128]{2,1,0:T(8,128)(2,1)S(1)}, bf16[2,128,128]{2,1,0:T(8,128)(2,1)S(1)}, u32[]{:S(2)}, u32[]{:S(2)}) collective-permute-start(bf16[2,128,128]{2,1,0:T(8,128)(2,1)S(1)} %convert_bitcast_fusion), channel_id=1, source_target_pairs={{0,256},{128,384},{256,0},{384,128},{1,257},{129,385},{257,1},{385... | collective-permute-start | bytes 196616 | tf_op jit(solution)/shard_map/ppermute | solution.py:35
  22.0 3.0 %collective-permute-start.7 = (bf16[2,128,128]{2,1,0:T(8,128)(2,1)S(1)}, bf16[2,128,128]{2,1,0:T(8,128)(2,1)S(1)}, u32[]{:S(2)}, u32[]{:S(2)}) collective-permute-start(bf16[2,128,128]{2,1,0:T(8,128)(2,1)S(1)} %convert_bitcast_fusion), channel_id=1, source_target_pairs={{0,384},{128,0},{256,128},{384,256},{1,385},{129,1},{257,129},{385... | collective-permute-start | bytes 196616 | tf_op jit(solution)/shard_map/ppermute | solution.py:35
  25.0 0.0 collective-permute-done.9
  25.0 0.0 collective-permute-done.8
  25.1 2.1 %collective-permute-done.7 = bf16[2,128,128]{2,1,0:T(8,128)(2,1)S(1)} collective-permute-done((bf16[2,128,128]{2,1,0:T(8,128)(2,1)S(1)}, bf16[2,128,128]{2,1,0:T(8,128)(2,1)S(1)}, u32[]{:S(2)}, u32[]{:S(2)}) %collective-permute-start.7) | collective-permute-done | bytes 65568 | tf_op jit(solution)/shard_map/ppermute | solution.py:35
  27.2 0.8 pad_maximum_fusion
  28.0 0.0 all-to-all-done.own_ref
  28.0 0.0 all-gather.3.cloned.1.call-update
  28.0 6.7 %collective-permute-start = (bf16[4,128,1024]{2,1,0:T(8,128)(2,1)S(1)}, bf16[4,128,1024]{2,1,0:T(8,128)(2,1)S(1)}, u32[]{:S(2)}, u32[]{:S(2)}) collective-permute-start(bf16[4,128,1024]{2,1,0:T(8,128)(2,1)S(1)} %all-to-all-done.own_ref), channel_id=1, source_target_pairs={{0,1},{1,0},{2,3},{3,2},{4,5},{5,4},{6,7},{7,6},{8,9},{9,8},{10,11... | collective-permute-start | bytes 3145736 | tf_op jit(solution)/shard_map/ppermute | solution.py:35
  34.7 0.1 pad_add_fusion.ids_ref.refs_0_
  34.8 1.0 copy-done.3
  35.8 1.0 copy-done.4
  36.8 1.1 gate.1
  37.9 0.0 collective-permute-done.other_ref
  38.0 2.1 %tiles_far.1 = (bf16[16,128,128]{2,1,0:T(8,128)(2,1)S(1)}, bf16[16,128,128]{2,1,0:T(8,128)(2,1)S(1)}) custom-call(s32[4]{0:T(128)S(1)} %pad_add_fusion.ids_ref.refs_0_, s32[1,112]{1,0:T(1,128)S(1)} %copy-done.8, s32[1,112]{1,0:T(1,128)S(1)} %copy-done.9, s32[1,64]{1,0:T(1,128)S(1)} %copy-done.7, bf16[4,128,1024]{2,1,0:T(8,128)(2,1)S(1)} %all-to-all-done.own_ref, ...), custom_call_target="tpu_custom_call" | custom-call | flops 134217728 | bytes 4194304 | tf_op jit(solution)/shard_map/tiles_far/pallas_call | solution.py:291
  40.1 3.7 %collective-permute-start.1 = (bf16[16,128,128]{2,1,0:T(8,128)(2,1)S(1)}, bf16[16,128,128]{2,1,0:T(8,128)(2,1)S(1)}, u32[]{:S(2)}, u32[]{:S(2)}) collective-permute-start(bf16[16,128,128]{2,1,0:T(8,128)(2,1)S(1)} %get-tuple-element.37), channel_id=1, source_target_pairs={{0,128},{128,256},{256,384},{384,0},{1,129},{129,257},{257,385},{3... | collective-permute-start | bytes 1572872 | tf_op jit(solution)/shard_map/ppermute | solution.py:35
  43.7 2.8 %collective-permute-start.2 = (bf16[16,128,128]{2,1,0:T(8,128)(2,1)S(1)}, bf16[16,128,128]{2,1,0:T(8,128)(2,1)S(1)}, u32[]{:S(2)}, u32[]{:S(2)}) collective-permute-start(bf16[16,128,128]{2,1,0:T(8,128)(2,1)S(1)} %get-tuple-element.39), channel_id=1, source_target_pairs={{0,384},{128,0},{256,128},{384,256},{1,385},{129,1},{257,129},{385... | collective-permute-start | bytes 1572872 | tf_op jit(solution)/shard_map/ppermute | solution.py:35
  46.6 4.0 %tiles_near.1 = (bf16[32,128,128]{2,1,0:T(8,128)(2,1)S(1)}, bf16[32,128,128]{2,1,0:T(8,128)(2,1)S(1)}, bf16[32,128,128]{2,1,0:T(8,128)(2,1)S(1)}) custom-call(s32[4]{0:T(128)S(1)} %pad_add_fusion.ids_ref.refs_0_, s32[1,112]{1,0:T(1,128)S(1)} %copy-done.8, s32[1,112]{1,0:T(1,128)S(1)} %copy-done.9, s32[1,64]{1,0:T(1,128)S(1)} %copy-done.7, ...), custom_call_target="tpu_custom_call" | custom-call | flops 402653184 | bytes 4194304 | tf_op jit(solution)/shard_map/tiles_near/pallas_call | solution.py:298
  50.6 6.2 %collective-permute-done.1.low_ref = bf16[16,128,128]{2,1,0:T(8,128)(2,1)S(1)} collective-permute-done((bf16[16,128,128]{2,1,0:T(8,128)(2,1)S(1)}, bf16[16,128,128]{2,1,0:T(8,128)(2,1)S(1)}, u32[]{:S(2)}, u32[]{:S(2)}) %collective-permute-start.1) | collective-permute-done | bytes 524320 | tf_op jit(solution)/shard_map/ppermute | solution.py:35
  56.8 2.1 %collective-permute-done.2.high_ref = bf16[16,128,128]{2,1,0:T(8,128)(2,1)S(1)} collective-permute-done((bf16[16,128,128]{2,1,0:T(8,128)(2,1)S(1)}, bf16[16,128,128]{2,1,0:T(8,128)(2,1)S(1)}, u32[]{:S(2)}, u32[]{:S(2)}) %collective-permute-start.2) | collective-permute-done | bytes 524320 | tf_op jit(solution)/shard_map/ppermute | solution.py:35
  59.0 0.3 passing.1
  59.2 2.2 %collective-permute-start.3 = (bf16[32,128,128]{2,1,0:T(8,128)(2,1)S(1)}, bf16[32,128,128]{2,1,0:T(8,128)(2,1)S(1)}, u32[]{:S(2)}, u32[]{:S(2)}) collective-permute-start(bf16[32,128,128]{2,1,0:T(8,128)(2,1)S(1)} %get-tuple-element.40), channel_id=1, source_target_pairs={{0,128},{128,256},{256,384},{384,0},{1,129},{129,257},{257,385},{3... | collective-permute-start | bytes 3145736 | tf_op jit(solution)/shard_map/ppermute | solution.py:35
  61.5 4.3 %collective-permute-start.4 = (bf16[32,128,128]{2,1,0:T(8,128)(2,1)S(1)}, bf16[32,128,128]{2,1,0:T(8,128)(2,1)S(1)}, u32[]{:S(2)}, u32[]{:S(2)}) collective-permute-start(bf16[32,128,128]{2,1,0:T(8,128)(2,1)S(1)} %get-tuple-element.41), channel_id=1, source_target_pairs={{0,384},{128,0},{256,128},{384,256},{1,385},{129,1},{257,129},{385... | collective-permute-start | bytes 3145736 | tf_op jit(solution)/shard_map/ppermute | solution.py:35
  65.7 20.4 %collective-permute-done.3 = bf16[32,128,128]{2,1,0:T(8,128)(2,1)S(1)} collective-permute-done((bf16[32,128,128]{2,1,0:T(8,128)(2,1)S(1)}, bf16[32,128,128]{2,1,0:T(8,128)(2,1)S(1)}, u32[]{:S(2)}, u32[]{:S(2)}) %collective-permute-start.3) | collective-permute-done | bytes 1048608 | tf_op jit(solution)/shard_map/ppermute | solution.py:35
  86.1 1.1 collective-permute-done.4
  87.2 1.0 y_sum.1
  88.1 1.9 collective-permute-start.5
  90.1 8.7 %collective-permute-start.6 = (bf16[4,2,128,128]{3,2,1,0:T(8,128)(2,1)S(1)}, bf16[4,2,128,128]{3,2,1,0:T(8,128)(2,1)S(1)}, u32[]{:S(2)}, u32[]{:S(2)}) collective-permute-start(bf16[4,2,128,128]{3,2,1,0:T(8,128)(2,1)S(1)} %get-tuple-element.44), channel_id=1, source_target_pairs={{0,120},{8,0},{16,8},{24,16},{32,24},{40,32},{48,40},{56,48},{64,5... | collective-permute-start | bytes 786440 | tf_op jit(solution)/shard_map/ppermute | solution.py:35
  98.8 9.3 %collective-permute-done.5.low_ref = bf16[4,2,128,128]{3,2,1,0:T(8,128)(2,1)S(1)} collective-permute-done((bf16[4,2,128,128]{3,2,1,0:T(8,128)(2,1)S(1)}, bf16[4,2,128,128]{3,2,1,0:T(8,128)(2,1)S(1)}, u32[]{:S(2)}, u32[]{:S(2)}) %collective-permute-start.5) | collective-permute-done | bytes 262176 | tf_op jit(solution)/shard_map/ppermute | solution.py:35
  108.1 0.0 collective-permute-done.6.high_ref
  108.1 0.9 pair_sum.1
  109.0 7.9 %all-to-all-start.1 = ((bf16[8,2,128,128]{3,2,1,0:T(8,128)(2,1)}), bf16[8,2,128,128]{3,2,1,0:T(8,128)(2,1)S(1)}, u32[]{:S(2)}, u32[]{:S(2)}) async-start(bf16[8,2,128,128]{3,2,1,0:T(8,128)(2,1)} %pair_sum.1), calls=%async_computation.1 | async-start | bytes 1048576 | tf_op jit(solution)/shard_map/all_to_all | solution.py:39
  116.9 0.0 all-gather.5.cloned.1.call-start
  116.9 0.0 all-gather.3.cloned.1.call-done.delta_ref
  117.0 8.9 %contribs.1 = (bf16[64,8192]{1,0:T(8,128)(2,1)S(1)}, bf16[64,8192]{1,0:T(8,128)(2,1)S(1)}) custom-call(s32[4]{0:T(128)S(1)} %pad_add_fusion.ids_ref.refs_0_, s32[1,112]{1,0:T(1,128)S(1)} %copy-done.8, s32[1,112]{1,0:T(1,128)S(1)} %copy-done.9, s32[1,64]{1,0:T(1,128)S(1)} %copy-done.7, bf16[14,128,128]{2,1,0:T(8,128)(2,1)S(1)} %get-tuple-element.48.grad_ref, ...), custom_call_target="tpu_custom_call" | custom-call | bytes 4096 | tf_op jit(solution)/shard_map/contribs/pallas_call | solution.py:325
  125.8 3.8 %collective-permute-start.10 = (bf16[64,8192]{1,0:T(8,128)(2,1)S(1)}, bf16[64,8192]{1,0:T(8,128)(2,1)S(1)}, u32[]{:S(2)}, u32[]{:S(2)}) collective-permute-start(bf16[64,8192]{1,0:T(8,128)(2,1)S(1)} %get-tuple-element.51), channel_id=1, source_target_pairs={{0,1},{1,0},{2,3},{3,2},{4,5},{5,4},{6,7},{7,6},{8,9},{9,8},{10,11... | collective-permute-start | bytes 3145736 | tf_op jit(solution)/shard_map/ppermute | solution.py:35
  129.6 2.3 %collective-permute-done.10 = bf16[64,8192]{1,0:T(8,128)(2,1)S(1)} collective-permute-done((bf16[64,8192]{1,0:T(8,128)(2,1)S(1)}, bf16[64,8192]{1,0:T(8,128)(2,1)S(1)}, u32[]{:S(2)}, u32[]{:S(2)}) %collective-permute-start.10) | collective-permute-done | bytes 1048608 | tf_op jit(solution)/shard_map/ppermute | solution.py:35
  131.9 0.8 core_sum.1
  132.7 4.2 %collective-permute-start.13 = (bf16[16,8192]{1,0:T(8,128)(2,1)S(1)}, bf16[16,8192]{1,0:T(8,128)(2,1)S(1)}, u32[]{:S(2)}, u32[]{:S(2)}) collective-permute-start(bf16[16,8192]{1,0:T(8,128)(2,1)S(1)} %get-tuple-element.55), channel_id=1, source_target_pairs={{0,6},{2,0},{4,2},{6,4},{1,7},{3,1},{5,3},{7,5},{8,14},{10,8},{12,... | collective-permute-start | bytes 786440 | tf_op jit(solution)/shard_map/ppermute | solution.py:35
  136.9 2.6 %collective-permute-start.12 = (bf16[16,8192]{1,0:T(8,128)(2,1)S(1)}, bf16[16,8192]{1,0:T(8,128)(2,1)S(1)}, u32[]{:S(2)}, u32[]{:S(2)}) collective-permute-start(bf16[16,8192]{1,0:T(8,128)(2,1)S(1)} %get-tuple-element.54), channel_id=1, source_target_pairs={{0,4},{2,6},{4,0},{6,2},{1,5},{3,7},{5,1},{7,3},{8,12},{10,14},{12... | collective-permute-start | bytes 786440 | tf_op jit(solution)/shard_map/ppermute | solution.py:35
  139.5 2.4 %collective-permute-start.11 = (bf16[16,8192]{1,0:T(8,128)(2,1)S(1)}, bf16[16,8192]{1,0:T(8,128)(2,1)S(1)}, u32[]{:S(2)}, u32[]{:S(2)}) collective-permute-start(bf16[16,8192]{1,0:T(8,128)(2,1)S(1)} %get-tuple-element.53), channel_id=1, source_target_pairs={{0,2},{2,4},{4,6},{6,0},{1,3},{3,5},{5,7},{7,1},{8,10},{10,12},{12... | collective-permute-start | bytes 786440 | tf_op jit(solution)/shard_map/ppermute | solution.py:35
  141.9 1.7 all-to-all-done.1.arrived_ref
  143.6 0.8 own_grad.1
  144.4 0.0 collective-permute-done.13
  144.4 3.2 %collective-permute-done.12 = bf16[16,8192]{1,0:T(8,128)(2,1)S(1)} collective-permute-done((bf16[16,8192]{1,0:T(8,128)(2,1)S(1)}, bf16[16,8192]{1,0:T(8,128)(2,1)S(1)}, u32[]{:S(2)}, u32[]{:S(2)}) %collective-permute-start.12) | collective-permute-done | bytes 262176 | tf_op jit(solution)/shard_map/ppermute | solution.py:35
  147.6 6.6 %collective-permute-done.11 = bf16[16,8192]{1,0:T(8,128)(2,1)S(1)} collective-permute-done((bf16[16,8192]{1,0:T(8,128)(2,1)S(1)}, bf16[16,8192]{1,0:T(8,128)(2,1)S(1)}, u32[]{:S(2)}, u32[]{:S(2)}) %collective-permute-start.11) | collective-permute-done | bytes 262176 | tf_op jit(solution)/shard_map/ppermute | solution.py:35
  154.2 0.8 add_convert_fusion
  155.0 0.0 all-gather.5.cloned.1.call-update
  155.0 12.8 %all_to_all.20.arrived_ref = f32[32,8,128]{2,1,0:T(8,128)S(1)} all-to-all(f32[32,8,128]{2,1,0:T(8,128)S(1)} %get-tuple-element.56), channel_id=1, replica_groups=mesh['y'=4,'m'=8,'p'=2,'x'=4,'core'=2] {'y','x','core'}, dimensions={0} | all-to-all | bytes 262144 | tf_op jit(solution)/shard_map/all_to_all | solution.py:39
  167.8 0.7 relay.1
  168.5 11.8 %all-to-all-start.3 = ((f32[16,8,128]{2,1,0:T(8,128)}), f32[16,8,128]{2,1,0:T(8,128)S(1)}, u32[]{:S(2)}, u32[]{:S(2)}) async-start(f32[16,8,128]{2,1,0:T(8,128)} %relay.1), calls=%async_computation.3 | async-start | bytes 131072 | tf_op jit(solution)/shard_map/all_to_all | solution.py:39
  180.3 7.1 %all-gather.5.cloned.1.call-done.in_ref = bf16[128,8192]{1,0:T(8,128)(2,1)} async-done(((bf16[16,8192]{1,0:T(8,128)(2,1)}), bf16[128,8192]{1,0:T(8,128)(2,1)}) %all-gather.5.cloned.1.call-update) | async-done | bytes 2097168 | tf_op jit(solution)/shard_map/all_gather | solution.py:341
  187.4 1.6 copy-done
  189.0 1.3 result.1
  190.3 1.6 all-to-all-done.3.refs_2_
  191.9 0.0 copy-done.5
  191.9 1.5 adam.1
  (14 shorter events, 0.0 us)
Async XLA Ops:
  7.2 7.1 %copy-start.1 = (f32[1,2,128,128]{3,2,1,0:T(8,128)S(1)}, f32[1,2,128,128]{3,2,1,0:T(8,128)}, u32[]{:S(2)}) copy-start(f32[1,2,128,128]{3,2,1,0:T(8,128)} %refs_4_.1) | copy-start | bytes 393220
  7.2 27.6 %copy-start.2 = (bf16[128,1792]{1,0:T(8,128)(2,1)S(1)}, bf16[128,1792]{1,0:T(8,128)(2,1)}, u32[]{:S(2)}) copy-start(bf16[128,1792]{1,0:T(8,128)(2,1)} %gate_ref.1) | copy-start | bytes 1376260
  9.3 28.7 %copy-start.7 = (s32[1,64]{1,0:T(1,128)S(1)}, s32[1,64]{1,0:T(1,128)}, u32[]{:S(2)}) copy-start(s32[1,64]{1,0:T(1,128)} %refs_1_.1) | copy-start | bytes 772
  9.3 28.7 %copy-start.8 = (s32[1,112]{1,0:T(1,128)S(1)}, s32[1,112]{1,0:T(1,128)}, u32[]{:S(2)}) copy-start(s32[1,112]{1,0:T(1,128)} %rows_ref.5) | copy-start | bytes 1348
  9.3 28.7 %copy-start.9 = (s32[1,112]{1,0:T(1,128)S(1)}, s32[1,112]{1,0:T(1,128)}, u32[]{:S(2)}) copy-start(s32[1,112]{1,0:T(1,128)} %cols_ref.5) | copy-start | bytes 1348
  9.3 18.7 %all-to-all-start = ((bf16[4,128,1024]{2,1,0:T(8,128)(2,1)}), bf16[4,128,1024]{2,1,0:T(8,128)(2,1)S(1)}, u32[]{:S(2)}, u32[]{:S(2)}) async-start(bf16[4,128,1024]{2,1,0:T(8,128)(2,1)} %broadcast_in_dim.2), calls=%async_computation | async-start | bytes 2097152 | tf_op jit(solution)/shard_map/all_to_all | solution.py:39
  14.3 102.7 %all-gather.3.cloned.1.call-start = ((), (), s32[]{:S(2)}) async-start(), calls=%async_computation.4 | async-start | bytes 4456448 | tf_op jit(solution)/shard_map/all_gather | solution.py:276
  14.3 10.7 %collective-permute-start.9 = (bf16[2,128,128]{2,1,0:T(8,128)(2,1)S(1)}, bf16[2,128,128]{2,1,0:T(8,128)(2,1)S(1)}, u32[]{:S(2)}, u32[]{:S(2)}) collective-permute-start(bf16[2,128,128]{2,1,0:T(8,128)(2,1)S(1)} %convert_bitcast_fusion), channel_id=1, source_target_pairs={{0,128},{128,256},{256,384},{384,0},{1,129},{129,257},{257,385},{3... | collective-permute-start | bytes 196616 | tf_op jit(solution)/shard_map/ppermute | solution.py:35
  17.5 7.5 %collective-permute-start.8 = (bf16[2,128,128]{2,1,0:T(8,128)(2,1)S(1)}, bf16[2,128,128]{2,1,0:T(8,128)(2,1)S(1)}, u32[]{:S(2)}, u32[]{:S(2)}) collective-permute-start(bf16[2,128,128]{2,1,0:T(8,128)(2,1)S(1)} %convert_bitcast_fusion), channel_id=1, source_target_pairs={{0,256},{128,384},{256,0},{384,128},{1,257},{129,385},{257,1},{385... | collective-permute-start | bytes 196616 | tf_op jit(solution)/shard_map/ppermute | solution.py:35
  22.0 5.2 %collective-permute-start.7 = (bf16[2,128,128]{2,1,0:T(8,128)(2,1)S(1)}, bf16[2,128,128]{2,1,0:T(8,128)(2,1)S(1)}, u32[]{:S(2)}, u32[]{:S(2)}) collective-permute-start(bf16[2,128,128]{2,1,0:T(8,128)(2,1)S(1)} %convert_bitcast_fusion), channel_id=1, source_target_pairs={{0,384},{128,0},{256,128},{384,256},{1,385},{129,1},{257,129},{385... | collective-permute-start | bytes 196616 | tf_op jit(solution)/shard_map/ppermute | solution.py:35
  28.0 10.0 %collective-permute-start = (bf16[4,128,1024]{2,1,0:T(8,128)(2,1)S(1)}, bf16[4,128,1024]{2,1,0:T(8,128)(2,1)S(1)}, u32[]{:S(2)}, u32[]{:S(2)}) collective-permute-start(bf16[4,128,1024]{2,1,0:T(8,128)(2,1)S(1)} %all-to-all-done.own_ref), channel_id=1, source_target_pairs={{0,1},{1,0},{2,3},{3,2},{4,5},{5,4},{6,7},{7,6},{8,9},{9,8},{10,11... | collective-permute-start | bytes 3145736 | tf_op jit(solution)/shard_map/ppermute | solution.py:35
  34.8 1.0 copy-start.3
  35.8 1.0 copy-start.4
  40.1 16.8 %collective-permute-start.1 = (bf16[16,128,128]{2,1,0:T(8,128)(2,1)S(1)}, bf16[16,128,128]{2,1,0:T(8,128)(2,1)S(1)}, u32[]{:S(2)}, u32[]{:S(2)}) collective-permute-start(bf16[16,128,128]{2,1,0:T(8,128)(2,1)S(1)} %get-tuple-element.37), channel_id=1, source_target_pairs={{0,128},{128,256},{256,384},{384,0},{1,129},{129,257},{257,385},{3... | collective-permute-start | bytes 1572872 | tf_op jit(solution)/shard_map/ppermute | solution.py:35
  43.7 15.2 %collective-permute-start.2 = (bf16[16,128,128]{2,1,0:T(8,128)(2,1)S(1)}, bf16[16,128,128]{2,1,0:T(8,128)(2,1)S(1)}, u32[]{:S(2)}, u32[]{:S(2)}) collective-permute-start(bf16[16,128,128]{2,1,0:T(8,128)(2,1)S(1)} %get-tuple-element.39), channel_id=1, source_target_pairs={{0,384},{128,0},{256,128},{384,256},{1,385},{129,1},{257,129},{385... | collective-permute-start | bytes 1572872 | tf_op jit(solution)/shard_map/ppermute | solution.py:35
  59.2 26.9 %collective-permute-start.3 = (bf16[32,128,128]{2,1,0:T(8,128)(2,1)S(1)}, bf16[32,128,128]{2,1,0:T(8,128)(2,1)S(1)}, u32[]{:S(2)}, u32[]{:S(2)}) collective-permute-start(bf16[32,128,128]{2,1,0:T(8,128)(2,1)S(1)} %get-tuple-element.40), channel_id=1, source_target_pairs={{0,128},{128,256},{256,384},{384,0},{1,129},{129,257},{257,385},{3... | collective-permute-start | bytes 3145736 | tf_op jit(solution)/shard_map/ppermute | solution.py:35
  61.5 25.7 %collective-permute-start.4 = (bf16[32,128,128]{2,1,0:T(8,128)(2,1)S(1)}, bf16[32,128,128]{2,1,0:T(8,128)(2,1)S(1)}, u32[]{:S(2)}, u32[]{:S(2)}) collective-permute-start(bf16[32,128,128]{2,1,0:T(8,128)(2,1)S(1)} %get-tuple-element.41), channel_id=1, source_target_pairs={{0,384},{128,0},{256,128},{384,256},{1,385},{129,1},{257,129},{385... | collective-permute-start | bytes 3145736 | tf_op jit(solution)/shard_map/ppermute | solution.py:35
  88.1 20.0 %collective-permute-start.5 = (bf16[4,2,128,128]{3,2,1,0:T(8,128)(2,1)S(1)}, bf16[4,2,128,128]{3,2,1,0:T(8,128)(2,1)S(1)}, u32[]{:S(2)}, u32[]{:S(2)}) collective-permute-start(bf16[4,2,128,128]{3,2,1,0:T(8,128)(2,1)S(1)} %get-tuple-element.43), channel_id=1, source_target_pairs={{0,8},{8,16},{16,24},{24,32},{32,40},{40,48},{48,56},{56,64},{64,7... | collective-permute-start | bytes 786440 | tf_op jit(solution)/shard_map/ppermute | solution.py:35
  90.1 18.1 %collective-permute-start.6 = (bf16[4,2,128,128]{3,2,1,0:T(8,128)(2,1)S(1)}, bf16[4,2,128,128]{3,2,1,0:T(8,128)(2,1)S(1)}, u32[]{:S(2)}, u32[]{:S(2)}) collective-permute-start(bf16[4,2,128,128]{3,2,1,0:T(8,128)(2,1)S(1)} %get-tuple-element.44), channel_id=1, source_target_pairs={{0,120},{8,0},{16,8},{24,16},{32,24},{40,32},{48,40},{56,48},{64,5... | collective-permute-start | bytes 786440 | tf_op jit(solution)/shard_map/ppermute | solution.py:35
  109.0 34.6 %all-to-all-start.1 = ((bf16[8,2,128,128]{3,2,1,0:T(8,128)(2,1)}), bf16[8,2,128,128]{3,2,1,0:T(8,128)(2,1)S(1)}, u32[]{:S(2)}, u32[]{:S(2)}) async-start(bf16[8,2,128,128]{3,2,1,0:T(8,128)(2,1)} %pair_sum.1), calls=%async_computation.1 | async-start | bytes 1048576 | tf_op jit(solution)/shard_map/all_to_all | solution.py:39
  116.9 70.5 %all-gather.5.cloned.1.call-start = ((), (), s32[]{:S(2)}) async-start(), calls=%async_computation.5 | async-start | bytes 2359296 | tf_op jit(solution)/shard_map/all_gather | solution.py:341
  125.8 6.1 %collective-permute-start.10 = (bf16[64,8192]{1,0:T(8,128)(2,1)S(1)}, bf16[64,8192]{1,0:T(8,128)(2,1)S(1)}, u32[]{:S(2)}, u32[]{:S(2)}) collective-permute-start(bf16[64,8192]{1,0:T(8,128)(2,1)S(1)} %get-tuple-element.51), channel_id=1, source_target_pairs={{0,1},{1,0},{2,3},{3,2},{4,5},{5,4},{6,7},{7,6},{8,9},{9,8},{10,11... | collective-permute-start | bytes 3145736 | tf_op jit(solution)/shard_map/ppermute | solution.py:35
  132.7 11.7 %collective-permute-start.13 = (bf16[16,8192]{1,0:T(8,128)(2,1)S(1)}, bf16[16,8192]{1,0:T(8,128)(2,1)S(1)}, u32[]{:S(2)}, u32[]{:S(2)}) collective-permute-start(bf16[16,8192]{1,0:T(8,128)(2,1)S(1)} %get-tuple-element.55), channel_id=1, source_target_pairs={{0,6},{2,0},{4,2},{6,4},{1,7},{3,1},{5,3},{7,5},{8,14},{10,8},{12,... | collective-permute-start | bytes 786440 | tf_op jit(solution)/shard_map/ppermute | solution.py:35
  136.9 10.6 %collective-permute-start.12 = (bf16[16,8192]{1,0:T(8,128)(2,1)S(1)}, bf16[16,8192]{1,0:T(8,128)(2,1)S(1)}, u32[]{:S(2)}, u32[]{:S(2)}) collective-permute-start(bf16[16,8192]{1,0:T(8,128)(2,1)S(1)} %get-tuple-element.54), channel_id=1, source_target_pairs={{0,4},{2,6},{4,0},{6,2},{1,5},{3,7},{5,1},{7,3},{8,12},{10,14},{12... | collective-permute-start | bytes 786440 | tf_op jit(solution)/shard_map/ppermute | solution.py:35
  139.5 14.7 %collective-permute-start.11 = (bf16[16,8192]{1,0:T(8,128)(2,1)S(1)}, bf16[16,8192]{1,0:T(8,128)(2,1)S(1)}, u32[]{:S(2)}, u32[]{:S(2)}) collective-permute-start(bf16[16,8192]{1,0:T(8,128)(2,1)S(1)} %get-tuple-element.53), channel_id=1, source_target_pairs={{0,2},{2,4},{4,6},{6,0},{1,3},{3,5},{5,7},{7,1},{8,10},{10,12},{12... | collective-permute-start | bytes 786440 | tf_op jit(solution)/shard_map/ppermute | solution.py:35
  168.5 23.4 %all-to-all-start.3 = ((f32[16,8,128]{2,1,0:T(8,128)}), f32[16,8,128]{2,1,0:T(8,128)S(1)}, u32[]{:S(2)}, u32[]{:S(2)}) async-start(f32[16,8,128]{2,1,0:T(8,128)} %relay.1), calls=%async_computation.3 | async-start | bytes 131072 | tf_op jit(solution)/shard_map/all_to_all | solution.py:39
  187.4 1.6 copy-start
  189.0 2.9 %copy-start.5 = (f32[1,2,128,128]{3,2,1,0:T(8,128)S(1)}, f32[1,2,128,128]{3,2,1,0:T(8,128)}, u32[]{:S(2)}) copy-start(f32[1,2,128,128]{3,2,1,0:T(8,128)} %refs_5_.1) | copy-start | bytes 393220
  189.0 2.9 %copy-start.6 = (f32[1,2,128,128]{3,2,1,0:T(8,128)S(1)}, f32[1,2,128,128]{3,2,1,0:T(8,128)}, u32[]{:S(2)}) copy-start(f32[1,2,128,128]{3,2,1,0:T(8,128)} %refs_6_.1) | copy-start | bytes 393220
Sparse Core Ops, SparseCore 0:
  28.1 80.7 all-gather.2
  155.2 32.1 all-gather.4

commit v4 on v3

v4 whole, which is shorter than its diff:
```python
import functools

import jax
import jax.numpy as jnp
from jax import lax
from jax.experimental import pallas as pl
from jax.experimental.pallas import tpu as pltpu
from jax.sharding import Mesh, PartitionSpec as P

NY, NM, NX = 4, 8, 4
Z = ("m", "p")
TILE = 128
SLOT_CAP = 2
BF16, F32 = jnp.bfloat16, jnp.float32
SMEM = pl.BlockSpec(memory_space=pltpu.SMEM)
VMEM = pl.BlockSpec(memory_space=pltpu.VMEM)
ANY = pl.BlockSpec(memory_space=pl.ANY)
SHAPE = jax.ShapeDtypeStruct


def kernel_call(
    kernel, name, outs, ins, out_specs, scratch=(), flops=0, moved=1 << 20, vmem=48
):
    return pl.pallas_call(
        kernel,
        out_shape=outs,
        in_specs=ins,
        out_specs=out_specs,
        scratch_shapes=scratch,
        compiler_params=pltpu.CompilerParams(vmem_limit_bytes=vmem * 1024 * 1024),
        cost_estimate=pl.CostEstimate(flops=flops, bytes_accessed=moved, transcendentals=0),
        name=name,
    )


def shift(value, axis, step):
    size = lax.axis_size(axis)
    return lax.ppermute(value, axis, [(i, (i + step) % size) for i in range(size)])


def exchange(value, axis):
    return lax.all_to_all(value, axis, split_axis=0, concat_axis=0, tiled=True)


def spread(value, axis):
    copies = jnp.broadcast_to(value[None], (lax.axis_size(axis),) + value.shape)
    return exchange(copies, axis)


def gate_kernel(ids_ref, gate_ref, up_ref, hidden_ref, grad_ref, turned_ref):
    blocks = 2 * NX
    rows = grad_ref.shape[2] // NX
    core = ids_ref[3]
    for col in range(turned_ref.shape[0]):
        cut = slice(col * TILE, (col + 1) * TILE)
        gate = gate_ref[:, cut].astype(F32)
        sig = 1.0 / (1.0 + jnp.exp(-gate))
        value = (
            hidden_ref[:, cut].astype(F32)
            * up_ref[:, cut].astype(F32)
            * sig
            * (1.0 + gate * (1.0 - sig))
        )
        for block in range(blocks):
            part = value[block * rows : (block + 1) * rows].astype(BF16)
            place = (block >> 1) * rows
            grad_ref[(block & 1) ^ core, col, place : place + rows] = part
        turned_ref[col] = value.T.astype(BF16)


def load_features(own_ref, other_ref, features, sems, starts_ref, counts_ref):
    first = pltpu.make_async_copy(own_ref, features.at[0], sems.at[0])
    second = pltpu.make_async_copy(other_ref, features.at[1], sems.at[1])
    first.start()
    second.start()

    def owner_step(owner, start):
        starts_ref[owner] = start
        return start + counts_ref[0, owner]

    lax.fori_loop(0, counts_ref.shape[1], owner_step, 0)
    first.wait()
    second.wait()


def slot_products(
    parity, away, span, put, ids_ref, rows_ref, cols_ref, starts_ref, features, turned_ref
):
    core = ids_ref[3]
    last = rows_ref.shape[1] - 1
    group = (ids_ref[0] + away) & (NY - 1)
    per_step = 4

    def step(index, carry):
        for part in range(per_step):
            m = span[0] + index * per_step + part
            start = starts_ref[(group * NM + m) * 2 + parity]
            for rank in range(SLOT_CAP):
                k = jnp.minimum(start + rank, last)
                row = rows_ref[0, k]
                lane = pl.multiple_of((row & 7) * TILE, TILE)
                x = features[((row >> 3) & 1) ^ core, row >> 4, :, pl.ds(lane, TILE)]
                term = jnp.dot(turned_ref[cols_ref[0, k]], x, preferred_element_type=F32)
                put(m - span[0], rank, term.astype(BF16))
        return carry

    lax.fori_loop(0, (span[1] - span[0]) // per_step, step, 0)


def give_kernel(
    ids_ref, rows_ref, cols_ref, counts_ref, own_ref, other_ref, turned_ref,
    low_ref, high_ref, features, starts_ref, sems,
):
    load_features(own_ref, other_ref, features, sems, starts_ref, counts_ref)
    parity = 1 - (ids_ref[1] & 1)
    for away in range(NY):
        for ref, span in ((low_ref, (0, NM // 2)), (high_ref, (NM // 2, NM))):

            def put(m, rank, term, ref=ref, away=away):
                ref[away, m, rank] = term

            slot_products(
                parity, away, span, put,
                ids_ref, rows_ref, cols_ref, starts_ref, features, turned_ref,
            )


def keep_kernel(
    ids_ref, rows_ref, cols_ref, counts_ref, own_ref, other_ref, turned_ref,
    keep_ref, features, starts_ref, sems,
):
    load_features(own_ref, other_ref, features, sems, starts_ref, counts_ref)
    parity = ids_ref[1] & 1
    for away in range(NY):

        def put(m, rank, term, away=away):
            keep_ref[away, m, rank] = term

        slot_products(
            parity, away, (0, NM), put,
            ids_ref, rows_ref, cols_ref, starts_ref, features, turned_ref,
        )


def pair_sum(keep_ref, low_ref, high_ref, away, m):
    half = NM // 2
    other = low_ref[away, m] if m < half else high_ref[away, m - half]
    return keep_ref[away, m].astype(F32) + other.astype(F32)


def far_kernel(keep_ref, low_ref, high_ref, far_low_ref, far_high_ref):
    half = NM // 2
    for m in range(NM):
        ref = far_low_ref if m < half else far_high_ref
        ref[m % half] = pair_sum(keep_ref, low_ref, high_ref, 2, m).astype(BF16)


def near_kernel(
    keep_ref, low_ref, high_ref, far_low_ref, far_high_ref, up_ref, down_ref
):
    half = NM // 2
    for m in range(NM):
        up = pair_sum(keep_ref, low_ref, high_ref, 1, m)
        down = pair_sum(keep_ref, low_ref, high_ref, 3, m)
        if m < half:
            up = up + far_low_ref[m].astype(F32)
        else:
            down = down + far_high_ref[m - half].astype(F32)
        up_ref[m] = up.astype(BF16)
        down_ref[m] = down.astype(BF16)


def y_sum_kernel(keep_ref, low_ref, high_ref, below_ref, above_ref, out_ref):
    for m in range(NM):
        total = pair_sum(keep_ref, low_ref, high_ref, 0, m)
        total = total + below_ref[m].astype(F32) + above_ref[m].astype(F32)
        out_ref[m] = total.astype(BF16)


def own_grad_kernel(ids_ref, counts_ref, arrived_ref, grad_ref, squares_ref):
    count = counts_ref[0, ids_ref[0] * 2 * NM + ids_ref[1]]
    squares = jnp.zeros((TILE, TILE), F32)
    for rank in range(SLOT_CAP):
        total = arrived_ref[0, rank].astype(F32)
        for m in range(1, NM):
            total = total + arrived_ref[m, rank].astype(F32)
        total = jnp.where(rank < count, total, 0.0)
        grad_ref[rank] = total
        squares = squares + total * total
    squares_ref[...] = jnp.broadcast_to(jnp.sum(squares), squares_ref.shape)


def relay_kernel(arrived_ref, out_ref):
    total = jnp.sum(arrived_ref[...], axis=0, keepdims=True)
    out_ref[...] = jnp.broadcast_to(total, out_ref.shape)


def adam_kernel(
    count_all, ids_ref, counts_ref, arrived_ref, grad_ref, delta_ref, one_ref, two_ref,
    new_delta_ref, new_one_ref, new_two_ref,
):
    squares = jnp.sum(arrived_ref[...], axis=0)[0:1]
    factor = jnp.minimum(1.0, 1.0 / jnp.sqrt(squares / count_all + 1e-06))
    count = counts_ref[0, ids_ref[0] * 2 * NM + ids_ref[1]]
    for rank in range(SLOT_CAP):
        live = rank < count
        clipped = factor * grad_ref[rank].T
        delta, one, two = delta_ref[0, rank], one_ref[0, rank], two_ref[0, rank]
        first = 0.9 * one + 0.1 * clipped
        second = 0.95 * two + 0.05 * clipped * clipped
        size = first / (1.0 - 0.9**10) / (jnp.sqrt(second / (1.0 - 0.95**10)) + 1e-08)
        updated = delta - 0.02 * (size + 0.1 * delta)
        new_delta_ref[0, rank] = jnp.where(live, updated, delta)
        new_one_ref[0, rank] = jnp.where(live, first, one)
        new_two_ref[0, rank] = jnp.where(live, second, two)


def contrib_kernel(
    side, ids_ref, rows_ref, cols_ref, counts_ref, grad_ref, delta_ref, out_ref, places_ref
):
    out_ref[...] = jnp.zeros_like(out_ref)
    y = ids_ref[0]

    def owner_step(owner, start):
        place = ((owner & 15) * NY + (((owner >> 4) - y) & (NY - 1))) * SLOT_CAP
        places_ref[start] = place
        places_ref[start + 1] = place + 1
        return start + counts_ref[0, owner]

    lax.fori_loop(0, counts_ref.shape[1], owner_step, 0)
    per_step = 4

    def step(index, carry):
        last, total = carry
        for part in range(per_step):
            k = index * per_step + part
            row = rows_ref[0, k]
            product = lax.dot_general(
                grad_ref[side, cols_ref[0, k]], delta_ref[places_ref[k]],
                (((1,), (1,)), ((), ())), preferred_element_type=F32,
            )
            total = jnp.where(row == last, total, 0.0) + product
            lane = pl.multiple_of(row * TILE, TILE)
            out_ref[:, pl.ds(lane, TILE)] = total.astype(BF16)
            last = row
        return last, total

    lax.fori_loop(
        0, rows_ref.shape[1] // per_step, step,
        (jnp.int32(-1), jnp.zeros((out_ref.shape[0], TILE), F32)),
    )


def core_sum_kernel(ids_ref, stay_ref, taken_ref, *out_refs):
    for away, ref in enumerate(out_refs):
        at = (ids_ref[2] + away) & (NX - 1)
        ref[...] = (stay_ref[at].astype(F32) + taken_ref[at].astype(F32)).astype(BF16)


def copy_kernel(in_ref, out_ref, sem):
    copy = pltpu.make_async_copy(in_ref, out_ref, sem)
    copy.start()
    copy.wait()


def body(
    features, gate_pre, up_pre, hidden_grad, tile_rows, tile_cols, owner_counts,
    delta_value, moment_one, moment_two,
):
    ids = jnp.stack([lax.axis_index(name) for name in ("y", Z, "x", "core")]).astype(jnp.int32)
    tokens, hidden = gate_pre.shape
    shard_width = features.shape[1]
    width = shard_width * NX * 2
    tile_total = tile_rows.shape[1]
    lists = (tile_rows, tile_cols, owner_counts)

    own = spread(features, "x")
    other = shift(own, "core", 1)

    delta_half = delta_value[0].astype(BF16)
    delta_y = jnp.concatenate(
        [delta_half] + [shift(delta_half, "y", -away) for away in range(1, NY)], axis=0
    )
    _, delta_y = lax.optimization_barrier((own, delta_y))
    delta_all = lax.all_gather(delta_y, Z, axis=0, tiled=True)

    grads, turned = kernel_call(
        gate_kernel, "gate",
        [
            SHAPE((2, hidden // TILE, tokens // 2, TILE), BF16),
            SHAPE((hidden // TILE, TILE, tokens), BF16),
        ],
        [SMEM] + [VMEM] * 3, [VMEM] * 2, flops=tokens * hidden * 12, moved=tokens * hidden * 10,
    )(ids, gate_pre, up_pre, hidden_grad)

    tile_ins = [SMEM] * 4 + [ANY, ANY, VMEM]
    tile_scratch = [
        pltpu.VMEM((2, NX, tokens, shard_width), BF16),
        pltpu.SMEM((owner_counts.shape[1],), jnp.int32),
        pltpu.SemaphoreType.DMA((2,)),
    ]
    half = SHAPE((NM // 2, SLOT_CAP, TILE, TILE), BF16)
    whole = SHAPE((NM, SLOT_CAP, TILE, TILE), BF16)
    halves = SHAPE((NY,) + half.shape, BF16)

    low, high = kernel_call(
        give_kernel, "give", [halves] * 2, tile_ins, [VMEM] * 2, tile_scratch,
        flops=tile_total * TILE**3, moved=4 << 20,
    )(ids, *lists, own, other, turned)
    low = shift(low, Z, 1)
    high = shift(high, Z, -1)
    keep = kernel_call(
        keep_kernel, "keep", SHAPE((NY,) + whole.shape, BF16), tile_ins, VMEM, tile_scratch,
        flops=tile_total * TILE**3, moved=4 << 20,
    )(ids, *lists, own, other, turned)

    far_low, far_high = kernel_call(far_kernel, "far", [half] * 2, [VMEM] * 3, [VMEM] * 2)(
        keep, low, high
    )
    far_low = shift(far_low, "y", 1)
    far_high = shift(far_high, "y", -1)
    up, down = kernel_call(near_kernel, "near", [whole] * 2, [VMEM] * 5, [VMEM] * 2)(
        keep, low, high, far_low, far_high
    )
    below = shift(up, "y", 1)
    above = shift(down, "y", -1)
    pairs = kernel_call(y_sum_kernel, "y_sum", whole, [VMEM] * 5, VMEM)(
        keep, low, high, below, above
    )

    pairs, grads = lax.optimization_barrier((pairs, grads))
    arrived = exchange(pairs, "m")
    own_grad, squares = kernel_call(
        own_grad_kernel, "own_grad",
        [SHAPE((SLOT_CAP, TILE, TILE), F32), SHAPE((NY * NX * 2, 8, TILE), F32)],
        [SMEM, SMEM, VMEM], [VMEM] * 2,
    )(ids, owner_counts, arrived)

    def contribs(side):
        return kernel_call(
            functools.partial(contrib_kernel, side), "contribs",
            SHAPE((tokens // 2, width), BF16), [SMEM] * 4 + [VMEM] * 2, VMEM,
            [pltpu.SMEM((tile_total + 8,), jnp.int32)], moved=1 << 12,
        )(ids, *lists, grads, delta_all)

    give, stay = contribs(1), contribs(0)

    rows = tokens // (2 * NX)
    taken = shift(give, "core", 1)
    share, *others = kernel_call(
        core_sum_kernel, "core_sum", [SHAPE((rows, width), BF16)] * NX,
        [SMEM] + [VMEM] * 2, [VMEM] * NX, moved=1 << 12,
    )(ids, stay.reshape(NX, rows, width), taken.reshape(NX, rows, width))
    others = [shift(part, "x", away + 1) for away, part in enumerate(others)]

    squares = exchange(squares, ("y", "x", "core"))
    squares = kernel_call(relay_kernel, "relay", SHAPE((2 * NM, 8, TILE), F32), [VMEM], VMEM)(squares)
    squares, share, *others = lax.optimization_barrier((squares, share, *others))
    for part in others:
        share = share.astype(F32) + part.astype(F32)
    gathered = lax.all_gather(share.astype(BF16), ("x", "core"), axis=0, tiled=True)
    input_grad = kernel_call(
        copy_kernel, "result", SHAPE((tokens, width), BF16), [ANY], ANY,
        [pltpu.SemaphoreType.DMA], moved=4 << 20, vmem=63,
    )(gathered)
    squares = exchange(squares, Z)
    squares, input_grad = lax.optimization_barrier((squares, input_grad))
    count_all = float(NX * 2 * tile_total * TILE * TILE)

    outs = kernel_call(
        functools.partial(adam_kernel, count_all), "adam", [SHAPE(delta_value.shape, F32)] * 3, [SMEM] * 2 + [VMEM] * 5, [VMEM] * 3
    )(ids, owner_counts, squares, own_grad, delta_value, moment_one, moment_two)
    return (input_grad, *outs)


def solution(mesh):
    grid = Mesh(mesh.devices.reshape(NY, NM, 2, NX, 2), ("y", "m", "p", "x", "core"))
    dp, tensor = ("y", "m", "p"), ("x", "core")
    tokens = P(dp, tensor)
    lists = P(tensor, None)
    slots = P(tensor, dp, None, None)
    return jax.shard_map(
        body,
        mesh=grid,
        in_specs=(tokens,) * 4 + (lists,) * 3 + (slots,) * 3,
        out_specs=(P(dp, None),) + (slots,) * 3,
        check_vma=False,
    )
```

time: 201 us -> 286 us (1.42)
  Pallas kernels: 23.2 us -> 89.6 us
  waiting for transfers between devices: 63.7 us -> 77.7 us
  starting transfers between devices: 78.7 us -> 82.1 us
    pallas_call x1, Pallas kernels: 1.33 us -> 64.6 us  [body(): kernel_call(copy_kernel, 'result', SHAPE((tokens, width), BF16), [ANY], A...]
    all_gather x1, waiting for transfers between devices: 7.08 us -> 19.7 us  [body(): lax.all_gather(share.astype(BF16), ('x', 'core'), axis=0, tiled=True)]
    ppermute x14, waiting for transfers between devices: 53.3 us -> 57.9 us  [shift(): lax.ppermute(value, axis, [(i, (i + step) % size) for i in range(size)])]
    all_to_all x3, waiting for transfers between devices: 3.28 us -> 0.01 us  [exchange(): return lax.all_to_all(value, axis, split_axis=0, concat_axis=0, tiled=True)]
    pallas_call x8 -> x9, Pallas kernels: 19.7 us -> 22.8 us  [the longest x2 13.7 us: contribs(): kernel_call(functools.partial(contrib_kernel, side), 'contribs', SHAPE((t...]
  transfers between devices with their start and end apart: 19 -> 19, of which waited for: 12 -> 9; matrix products, arithmetic and copies ran while one was open for 0% -> 0% of each run, Pallas kernels for 11% -> 31%
where the time goes in v4:
time: 286 us; the launch traced here: 285 us
  Pallas kernels  89.6 us (31%)
  starting transfers between devices  82.1 us (29%)
  waiting for transfers between devices  77.7 us (27%)
  between operations  14.4 us (5%)
  blocking collectives  13.6 us (5%)
  local copies, waits for them, and re-layouts  6.36 us (2%)
    pallas_call x1, Pallas kernels, body(): kernel_call(copy_kernel, 'result', SHAPE((tokens, width), BF16), [ANY], A...  64.6 us
    ppermute x14, waiting for transfers between devices, shift(): lax.ppermute(value, axis, [(i, (i + step) % size) for i in range(size)])  57.9 us
    ppermute x14, starting transfers between devices, shift(): lax.ppermute(value, axis, [(i, (i + step) % size) for i in range(size)])  56.7 us
    all_to_all x3, starting transfers between devices, exchange(): return lax.all_to_all(value, axis, split_axis=0, concat_axis=0, tiled=True)  25.4 us
    all_gather x1, waiting for transfers between devices, body(): lax.all_gather(share.astype(BF16), ('x', 'core'), axis=0, tiled=True)  19.7 us
    pallas_call x2, Pallas kernels, contribs(): kernel_call(functools.partial(contrib_kernel, side), 'contribs', SHAPE((t...  13.7 us
    all_to_all x1, blocking collectives, exchange(): return lax.all_to_all(value, axis, split_axis=0, concat_axis=0, tiled=True)  13.6 us
  transfers between devices with their start and end apart: 19, of which 9 were waited for; matrix products, arithmetic and copies ran while one was open for 0% of the time, Pallas kernels for 31%

profile of v4, /device:TPU:1, one launch (start us, length us, event | category | flops | bytes accessed | tf_op | source)
XLA Modules:
  0.0 285.4 jit_solution(16726249765042296539)
XLA Ops:
  7.2 2.1 broadcast_in_dim.2
  9.3 5.0 %all-to-all-start = ((bf16[4,128,1024]{2,1,0:T(8,128)(2,1)}), bf16[4,128,1024]{2,1,0:T(8,128)(2,1)S(1)}, u32[]{:S(2)}, u32[]{:S(2)}) async-start(bf16[4,128,1024]{2,1,0:T(8,128)(2,1)} %broadcast_in_dim.2), calls=%async_computation | async-start | bytes 2097152 | tf_op jit(solution)/shard_map/all_to_all | solution.py:42
  14.3 0.0 copy-done.1
  14.3 4.6 %collective-permute-start.7 = (bf16[2,128,128]{2,1,0:T(8,128)(2,1)S(1)}, bf16[2,128,128]{2,1,0:T(8,128)(2,1)S(1)}, u32[]{:S(2)}, u32[]{:S(2)}) collective-permute-start(bf16[2,128,128]{2,1,0:T(8,128)(2,1)S(1)} %convert_bitcast_fusion), channel_id=1, source_target_pairs={{0,384},{128,0},{256,128},{384,256},{1,385},{129,1},{257,129},{385... | collective-permute-start | bytes 196616 | tf_op jit(solution)/shard_map/ppermute | solution.py:38
  18.9 2.3 collective-permute-start.8
  21.2 2.6 collective-permute-start.9
  23.8 0.0 collective-permute-done.7
  23.8 1.6 collective-permute-done.8
  25.5 2.3 collective-permute-done.9
  27.7 0.7 pad_maximum_fusion
  28.5 0.0 all-to-all-done.own_ref
  28.5 0.0 all-gather.3.cloned.1.call-update
  28.5 6.8 %collective-permute-start = (bf16[4,128,1024]{2,1,0:T(8,128)(2,1)S(1)}, bf16[4,128,1024]{2,1,0:T(8,128)(2,1)S(1)}, u32[]{:S(2)}, u32[]{:S(2)}) collective-permute-start(bf16[4,128,1024]{2,1,0:T(8,128)(2,1)S(1)} %all-to-all-done.own_ref), channel_id=1, source_target_pairs={{0,1},{1,0},{2,3},{3,2},{4,5},{5,4},{6,7},{7,6},{8,9},{9,8},{10,11... | collective-permute-start | bytes 3145736 | tf_op jit(solution)/shard_map/ppermute | solution.py:38
  35.3 0.1 pad_add_fusion.ids_ref
  35.4 1.0 copy-done.3
  36.4 1.0 copy-done.4
  37.4 1.1 gate.1
  38.5 0.0 collective-permute-done.other_ref
  38.6 1.9 give.1
  40.5 1.9 collective-permute-start.1
  42.4 8.6 %collective-permute-start.2 = (bf16[4,4,2,128,128]{4,3,2,1,0:T(8,128)(2,1)S(1)}, bf16[4,4,2,128,128]{4,3,2,1,0:T(8,128)(2,1)S(1)}, u32[]{:S(2)}, u32[]{:S(2)}) collective-permute-start(bf16[4,4,2,128,128]{4,3,2,1,0:T(8,128)(2,1)S(1)} %get-tuple-element.33), channel_id=1, source_target_pairs={{0,120},{8,0},{16,8},{24,16},{32,24},{40,32},{48,40},{56,48},{64,5... | collective-permute-start | bytes 3145736 | tf_op jit(solution)/shard_map/ppermute | solution.py:38
  51.1 3.1 %keep.1.keep_ref = bf16[4,8,2,128,128]{4,3,2,1,0:T(8,128)(2,1)S(1)} custom-call(s32[4]{0:T(128)S(1)} %pad_add_fusion.ids_ref, s32[1,112]{1,0:T(1,128)S(1)} %copy-done.8, s32[1,112]{1,0:T(1,128)S(1)} %copy-done.9, s32[1,64]{1,0:T(1,128)S(1)} %copy-done.7, bf16[4,128,1024]{2,1,0:T(8,128)(2,1)S(1)} %all-to-all-done.own_ref, ...), custom_call_target="tpu_custom_call" | custom-call | flops 234881024 | bytes 4194304 | tf_op jit(solution)/shard_map/keep/pallas_call | solution.py:312
  54.1 36.3 %collective-permute-done.1.low_ref = bf16[4,4,2,128,128]{4,3,2,1,0:T(8,128)(2,1)S(1)} collective-permute-done((bf16[4,4,2,128,128]{4,3,2,1,0:T(8,128)(2,1)S(1)}, bf16[4,4,2,128,128]{4,3,2,1,0:T(8,128)(2,1)S(1)}, u32[]{:S(2)}, u32[]{:S(2)}) %collective-permute-start.1) | collective-permute-done | bytes 1048608 | tf_op jit(solution)/shard_map/ppermute | solution.py:38
  90.5 2.7 collective-permute-done.2.high_ref
  93.1 0.1 far.1
  93.3 3.4 %collective-permute-start.3 = (bf16[4,2,128,128]{3,2,1,0:T(8,128)(2,1)S(1)}, bf16[4,2,128,128]{3,2,1,0:T(8,128)(2,1)S(1)}, u32[]{:S(2)}, u32[]{:S(2)}) collective-permute-start(bf16[4,2,128,128]{3,2,1,0:T(8,128)(2,1)S(1)} %get-tuple-element.34), channel_id=1, source_target_pairs={{0,128},{128,256},{256,384},{384,0},{1,129},{129,257},{257,385},{3... | collective-permute-start | bytes 786440 | tf_op jit(solution)/shard_map/ppermute | solution.py:38
  96.7 3.1 %collective-permute-start.4 = (bf16[4,2,128,128]{3,2,1,0:T(8,128)(2,1)S(1)}, bf16[4,2,128,128]{3,2,1,0:T(8,128)(2,1)S(1)}, u32[]{:S(2)}, u32[]{:S(2)}) collective-permute-start(bf16[4,2,128,128]{3,2,1,0:T(8,128)(2,1)S(1)} %get-tuple-element.35), channel_id=1, source_target_pairs={{0,384},{128,0},{256,128},{384,256},{1,385},{129,1},{257,129},{385... | collective-permute-start | bytes 786440 | tf_op jit(solution)/shard_map/ppermute | solution.py:38
  99.8 3.6 %collective-permute-done.3.far_low_ref = bf16[4,2,128,128]{3,2,1,0:T(8,128)(2,1)S(1)} collective-permute-done((bf16[4,2,128,128]{3,2,1,0:T(8,128)(2,1)S(1)}, bf16[4,2,128,128]{3,2,1,0:T(8,128)(2,1)S(1)}, u32[]{:S(2)}, u32[]{:S(2)}) %collective-permute-start.3) | collective-permute-done | bytes 262176 | tf_op jit(solution)/shard_map/ppermute | solution.py:38
  103.4 1.9 collective-permute-done.4.far_high_ref
  105.3 0.3 near.1
  105.7 2.9 %collective-permute-start.5 = (bf16[8,2,128,128]{3,2,1,0:T(8,128)(2,1)S(1)}, bf16[8,2,128,128]{3,2,1,0:T(8,128)(2,1)S(1)}, u32[]{:S(2)}, u32[]{:S(2)}) collective-permute-start(bf16[8,2,128,128]{3,2,1,0:T(8,128)(2,1)S(1)} %get-tuple-element.36), channel_id=1, source_target_pairs={{0,128},{128,256},{256,384},{384,0},{1,129},{129,257},{257,385},{3... | collective-permute-start | bytes 1572872 | tf_op jit(solution)/shard_map/ppermute | solution.py:38
  108.6 3.6 %collective-permute-start.6 = (bf16[8,2,128,128]{3,2,1,0:T(8,128)(2,1)S(1)}, bf16[8,2,128,128]{3,2,1,0:T(8,128)(2,1)S(1)}, u32[]{:S(2)}, u32[]{:S(2)}) collective-permute-start(bf16[8,2,128,128]{3,2,1,0:T(8,128)(2,1)S(1)} %get-tuple-element.37), channel_id=1, source_target_pairs={{0,384},{128,0},{256,128},{384,256},{1,385},{129,1},{257,129},{385... | collective-permute-start | bytes 1572872 | tf_op jit(solution)/shard_map/ppermute | solution.py:38
  112.2 8.2 %collective-permute-done.5.below_ref = bf16[8,2,128,128]{3,2,1,0:T(8,128)(2,1)S(1)} collective-permute-done((bf16[8,2,128,128]{3,2,1,0:T(8,128)(2,1)S(1)}, bf16[8,2,128,128]{3,2,1,0:T(8,128)(2,1)S(1)}, u32[]{:S(2)}, u32[]{:S(2)}) %collective-permute-start.5) | collective-permute-done | bytes 524320 | tf_op jit(solution)/shard_map/ppermute | solution.py:38
  120.3 1.3 collective-permute-done.6.above_ref
  121.6 1.0 y_sum.1
  122.6 5.6 %all-to-all-start.1 = ((bf16[8,2,128,128]{3,2,1,0:T(8,128)(2,1)}), bf16[8,2,128,128]{3,2,1,0:T(8,128)(2,1)S(1)}, u32[]{:S(2)}, u32[]{:S(2)}) async-start(bf16[8,2,128,128]{3,2,1,0:T(8,128)(2,1)} %y_sum.1), calls=%async_computation.1 | async-start | bytes 1048576 | tf_op jit(solution)/shard_map/all_to_all | solution.py:42
  128.3 0.0 all-gather.5.cloned.1.call-start
  128.3 0.0 all-gather.3.cloned.1.call-done.delta_ref
  128.4 2.2 copy-done
  130.5 6.9 %contribs.3 = bf16[64,8192]{1,0:T(8,128)(2,1)S(1)} custom-call(s32[4]{0:T(128)S(1)} %pad_add_fusion.ids_ref, s32[1,112]{1,0:T(1,128)S(1)} %copy-done.8, s32[1,112]{1,0:T(1,128)S(1)} %copy-done.9, s32[1,64]{1,0:T(1,128)S(1)} %copy-done.7, bf16[2,14,64,128]{3,2,1,0:T(8,128)(2,1)S(1)} %get-tuple-element.41.grad_ref, bf16[128,128,128]{2,1,0:T(8,128)(2,1)S(1)} %copy-done), custom_call_target="tpu_custom_call" | custom-call | bytes 4096 | tf_op jit(solution)/shard_map/contribs/pallas_call | solution.py:340
  137.4 5.5 %collective-permute-start.10 = (bf16[64,8192]{1,0:T(8,128)(2,1)S(1)}, bf16[64,8192]{1,0:T(8,128)(2,1)S(1)}, u32[]{:S(2)}, u32[]{:S(2)}) collective-permute-start(bf16[64,8192]{1,0:T(8,128)(2,1)S(1)} %contribs.3), channel_id=1, source_target_pairs={{0,1},{1,0},{2,3},{3,2},{4,5},{5,4},{6,7},{7,6},{8,9},{9,8},{10,11... | collective-permute-start | bytes 3145736 | tf_op jit(solution)/shard_map/ppermute | solution.py:38
  142.9 6.9 %contribs.2 = bf16[64,8192]{1,0:T(8,128)(2,1)S(1)} custom-call(s32[4]{0:T(128)S(1)} %pad_add_fusion.ids_ref, s32[1,112]{1,0:T(1,128)S(1)} %copy-done.8, s32[1,112]{1,0:T(1,128)S(1)} %copy-done.9, s32[1,64]{1,0:T(1,128)S(1)} %copy-done.7, bf16[2,14,64,128]{3,2,1,0:T(8,128)(2,1)S(1)} %get-tuple-element.41.grad_ref, bf16[128,128,128]{2,1,0:T(8,128)(2,1)S(1)} %copy-done), custom_call_target="tpu_custom_call" | custom-call | bytes 4096 | tf_op jit(solution)/shard_map/contribs/pallas_call | solution.py:340
  149.8 0.0 collective-permute-done.10
  149.8 0.8 core_sum.1
  150.6 4.3 %collective-permute-start.11 = (bf16[16,8192]{1,0:T(8,128)(2,1)S(1)}, bf16[16,8192]{1,0:T(8,128)(2,1)S(1)}, u32[]{:S(2)}, u32[]{:S(2)}) collective-permute-start(bf16[16,8192]{1,0:T(8,128)(2,1)S(1)} %get-tuple-element.44), channel_id=1, source_target_pairs={{0,2},{2,4},{4,6},{6,0},{1,3},{3,5},{5,7},{7,1},{8,10},{10,12},{12... | collective-permute-start | bytes 786440 | tf_op jit(solution)/shard_map/ppermute | solution.py:38
  154.9 4.1 %collective-permute-start.12 = (bf16[16,8192]{1,0:T(8,128)(2,1)S(1)}, bf16[16,8192]{1,0:T(8,128)(2,1)S(1)}, u32[]{:S(2)}, u32[]{:S(2)}) collective-permute-start(bf16[16,8192]{1,0:T(8,128)(2,1)S(1)} %get-tuple-element.45), channel_id=1, source_target_pairs={{0,4},{2,6},{4,0},{6,2},{1,5},{3,7},{5,1},{7,3},{8,12},{10,14},{12... | collective-permute-start | bytes 786440 | tf_op jit(solution)/shard_map/ppermute | solution.py:38
  159.0 2.9 %collective-permute-start.13 = (bf16[16,8192]{1,0:T(8,128)(2,1)S(1)}, bf16[16,8192]{1,0:T(8,128)(2,1)S(1)}, u32[]{:S(2)}, u32[]{:S(2)}) collective-permute-start(bf16[16,8192]{1,0:T(8,128)(2,1)S(1)} %get-tuple-element.46), channel_id=1, source_target_pairs={{0,6},{2,0},{4,2},{6,4},{1,7},{3,1},{5,3},{7,5},{8,14},{10,8},{12,... | collective-permute-start | bytes 786440 | tf_op jit(solution)/shard_map/ppermute | solution.py:38
  161.9 0.0 all-to-all-done.1.arrived_ref
  162.0 0.8 own_grad.1
  162.7 13.6 %all_to_all.20.arrived_ref = f32[32,8,128]{2,1,0:T(8,128)S(1)} all-to-all(f32[32,8,128]{2,1,0:T(8,128)S(1)} %get-tuple-element.40), channel_id=1, replica_groups=mesh['y'=4,'m'=8,'p'=2,'x'=4,'core'=2] {'y','x','core'}, dimensions={0} | all-to-all | bytes 262144 | tf_op jit(solution)/shard_map/all_to_all | solution.py:42
  176.3 0.7 relay.1
  177.0 0.0 collective-permute-done.11
  177.0 0.0 collective-permute-done.12
  177.0 0.0 collective-permute-done.13
  177.0 0.8 add_convert_fusion
  177.8 0.0 all-gather.5.cloned.1.call-update
  177.8 14.8 %all-to-all-start.3 = ((f32[16,8,128]{2,1,0:T(8,128)}), f32[16,8,128]{2,1,0:T(8,128)S(1)}, u32[]{:S(2)}, u32[]{:S(2)}) async-start(f32[16,8,128]{2,1,0:T(8,128)} %relay.1), calls=%async_computation.3 | async-start | bytes 131072 | tf_op jit(solution)/shard_map/all_to_all | solution.py:42
  192.7 0.0 copy-start.5
  192.7 0.0 copy-start.6
  192.7 19.7 %all-gather.5.cloned.1.call-done.in_ref = bf16[128,8192]{1,0:T(8,128)(2,1)} async-done(((bf16[16,8192]{1,0:T(8,128)(2,1)}), bf16[128,8192]{1,0:T(8,128)(2,1)}) %all-gather.5.cloned.1.call-update) | async-done | bytes 2097168 | tf_op jit(solution)/shard_map/all_gather | solution.py:361
  212.4 64.6 %result.1 = bf16[128,8192]{1,0:T(8,128)(2,1)} custom-call(bf16[128,8192]{1,0:T(8,128)(2,1)} %all-gather.5.cloned.1.call-done.in_ref), custom_call_target="tpu_custom_call" | custom-call | bytes 4194304 | tf_op jit(solution)/shard_map/result/pallas_call | solution.py:362
  277.1 0.0 all-to-all-done.3.arrived_ref
  277.1 0.0 copy-done.5
  277.1 1.5 adam.1
  (15 shorter events, 0.0 us)
Async XLA Ops:
  7.2 7.1 %copy-start.1 = (f32[1,2,128,128]{3,2,1,0:T(8,128)S(1)}, f32[1,2,128,128]{3,2,1,0:T(8,128)}, u32[]{:S(2)}) copy-start(f32[1,2,128,128]{3,2,1,0:T(8,128)} %delta_ref.1) | copy-start | bytes 393220
  7.2 28.2 %copy-start.2 = (bf16[128,1792]{1,0:T(8,128)(2,1)S(1)}, bf16[128,1792]{1,0:T(8,128)(2,1)}, u32[]{:S(2)}) copy-start(bf16[128,1792]{1,0:T(8,128)(2,1)} %gate_ref.1) | copy-start | bytes 1376260
  9.3 29.3 %copy-start.7 = (s32[1,64]{1,0:T(1,128)S(1)}, s32[1,64]{1,0:T(1,128)}, u32[]{:S(2)}) copy-start(s32[1,64]{1,0:T(1,128)} %counts_ref.11) | copy-start | bytes 772
  9.3 29.3 %copy-start.8 = (s32[1,112]{1,0:T(1,128)S(1)}, s32[1,112]{1,0:T(1,128)}, u32[]{:S(2)}) copy-start(s32[1,112]{1,0:T(1,128)} %rows_ref.7) | copy-start | bytes 1348
  9.3 29.3 %copy-start.9 = (s32[1,112]{1,0:T(1,128)S(1)}, s32[1,112]{1,0:T(1,128)}, u32[]{:S(2)}) copy-start(s32[1,112]{1,0:T(1,128)} %cols_ref.7) | copy-start | bytes 1348
  9.3 19.2 %all-to-all-start = ((bf16[4,128,1024]{2,1,0:T(8,128)(2,1)}), bf16[4,128,1024]{2,1,0:T(8,128)(2,1)S(1)}, u32[]{:S(2)}, u32[]{:S(2)}) async-start(bf16[4,128,1024]{2,1,0:T(8,128)(2,1)} %broadcast_in_dim.2), calls=%async_computation | async-start | bytes 2097152 | tf_op jit(solution)/shard_map/all_to_all | solution.py:42
  14.3 114.1 %all-gather.3.cloned.1.call-start = ((), (), s32[]{:S(2)}) async-start(), calls=%async_computation.4 | async-start | bytes 4456448 | tf_op jit(solution)/shard_map/all_gather | solution.py:285
  14.3 9.5 %collective-permute-start.7 = (bf16[2,128,128]{2,1,0:T(8,128)(2,1)S(1)}, bf16[2,128,128]{2,1,0:T(8,128)(2,1)S(1)}, u32[]{:S(2)}, u32[]{:S(2)}) collective-permute-start(bf16[2,128,128]{2,1,0:T(8,128)(2,1)S(1)} %convert_bitcast_fusion), channel_id=1, source_target_pairs={{0,384},{128,0},{256,128},{384,256},{1,385},{129,1},{257,129},{385... | collective-permute-start | bytes 196616 | tf_op jit(solution)/shard_map/ppermute | solution.py:38
  18.9 6.5 %collective-permute-start.8 = (bf16[2,128,128]{2,1,0:T(8,128)(2,1)S(1)}, bf16[2,128,128]{2,1,0:T(8,128)(2,1)S(1)}, u32[]{:S(2)}, u32[]{:S(2)}) collective-permute-start(bf16[2,128,128]{2,1,0:T(8,128)(2,1)S(1)} %convert_bitcast_fusion), channel_id=1, source_target_pairs={{0,256},{128,384},{256,0},{384,128},{1,257},{129,385},{257,1},{385... | collective-permute-start | bytes 196616 | tf_op jit(solution)/shard_map/ppermute | solution.py:38
  21.2 6.5 %collective-permute-start.9 = (bf16[2,128,128]{2,1,0:T(8,128)(2,1)S(1)}, bf16[2,128,128]{2,1,0:T(8,128)(2,1)S(1)}, u32[]{:S(2)}, u32[]{:S(2)}) collective-permute-start(bf16[2,128,128]{2,1,0:T(8,128)(2,1)S(1)} %convert_bitcast_fusion), channel_id=1, source_target_pairs={{0,128},{128,256},{256,384},{384,0},{1,129},{129,257},{257,385},{3... | collective-permute-start | bytes 196616 | tf_op jit(solution)/shard_map/ppermute | solution.py:38
  28.5 10.0 %collective-permute-start = (bf16[4,128,1024]{2,1,0:T(8,128)(2,1)S(1)}, bf16[4,128,1024]{2,1,0:T(8,128)(2,1)S(1)}, u32[]{:S(2)}, u32[]{:S(2)}) collective-permute-start(bf16[4,128,1024]{2,1,0:T(8,128)(2,1)S(1)} %all-to-all-done.own_ref), channel_id=1, source_target_pairs={{0,1},{1,0},{2,3},{3,2},{4,5},{5,4},{6,7},{7,6},{8,9},{9,8},{10,11... | collective-permute-start | bytes 3145736 | tf_op jit(solution)/shard_map/ppermute | solution.py:38
  35.4 1.0 copy-start.3
  36.4 1.0 copy-start.4
  40.5 50.0 %collective-permute-start.1 = (bf16[4,4,2,128,128]{4,3,2,1,0:T(8,128)(2,1)S(1)}, bf16[4,4,2,128,128]{4,3,2,1,0:T(8,128)(2,1)S(1)}, u32[]{:S(2)}, u32[]{:S(2)}) collective-permute-start(bf16[4,4,2,128,128]{4,3,2,1,0:T(8,128)(2,1)S(1)} %get-tuple-element.32), channel_id=1, source_target_pairs={{0,8},{8,16},{16,24},{24,32},{32,40},{40,48},{48,56},{56,64},{64,7... | collective-permute-start | bytes 3145736 | tf_op jit(solution)/shard_map/ppermute | solution.py:38
  42.4 50.7 %collective-permute-start.2 = (bf16[4,4,2,128,128]{4,3,2,1,0:T(8,128)(2,1)S(1)}, bf16[4,4,2,128,128]{4,3,2,1,0:T(8,128)(2,1)S(1)}, u32[]{:S(2)}, u32[]{:S(2)}) collective-permute-start(bf16[4,4,2,128,128]{4,3,2,1,0:T(8,128)(2,1)S(1)} %get-tuple-element.33), channel_id=1, source_target_pairs={{0,120},{8,0},{16,8},{24,16},{32,24},{40,32},{48,40},{56,48},{64,5... | collective-permute-start | bytes 3145736 | tf_op jit(solution)/shard_map/ppermute | solution.py:38
  93.3 10.2 %collective-permute-start.3 = (bf16[4,2,128,128]{3,2,1,0:T(8,128)(2,1)S(1)}, bf16[4,2,128,128]{3,2,1,0:T(8,128)(2,1)S(1)}, u32[]{:S(2)}, u32[]{:S(2)}) collective-permute-start(bf16[4,2,128,128]{3,2,1,0:T(8,128)(2,1)S(1)} %get-tuple-element.34), channel_id=1, source_target_pairs={{0,128},{128,256},{256,384},{384,0},{1,129},{129,257},{257,385},{3... | collective-permute-start | bytes 786440 | tf_op jit(solution)/shard_map/ppermute | solution.py:38
  96.7 8.7 %collective-permute-start.4 = (bf16[4,2,128,128]{3,2,1,0:T(8,128)(2,1)S(1)}, bf16[4,2,128,128]{3,2,1,0:T(8,128)(2,1)S(1)}, u32[]{:S(2)}, u32[]{:S(2)}) collective-permute-start(bf16[4,2,128,128]{3,2,1,0:T(8,128)(2,1)S(1)} %get-tuple-element.35), channel_id=1, source_target_pairs={{0,384},{128,0},{256,128},{384,256},{1,385},{129,1},{257,129},{385... | collective-permute-start | bytes 786440 | tf_op jit(solution)/shard_map/ppermute | solution.py:38
  105.7 14.7 %collective-permute-start.5 = (bf16[8,2,128,128]{3,2,1,0:T(8,128)(2,1)S(1)}, bf16[8,2,128,128]{3,2,1,0:T(8,128)(2,1)S(1)}, u32[]{:S(2)}, u32[]{:S(2)}) collective-permute-start(bf16[8,2,128,128]{3,2,1,0:T(8,128)(2,1)S(1)} %get-tuple-element.36), channel_id=1, source_target_pairs={{0,128},{128,256},{256,384},{384,0},{1,129},{129,257},{257,385},{3... | collective-permute-start | bytes 1572872 | tf_op jit(solution)/shard_map/ppermute | solution.py:38
  108.6 13.0 %collective-permute-start.6 = (bf16[8,2,128,128]{3,2,1,0:T(8,128)(2,1)S(1)}, bf16[8,2,128,128]{3,2,1,0:T(8,128)(2,1)S(1)}, u32[]{:S(2)}, u32[]{:S(2)}) collective-permute-start(bf16[8,2,128,128]{3,2,1,0:T(8,128)(2,1)S(1)} %get-tuple-element.37), channel_id=1, source_target_pairs={{0,384},{128,0},{256,128},{384,256},{1,385},{129,1},{257,129},{385... | collective-permute-start | bytes 1572872 | tf_op jit(solution)/shard_map/ppermute | solution.py:38
  122.6 39.3 %all-to-all-start.1 = ((bf16[8,2,128,128]{3,2,1,0:T(8,128)(2,1)}), bf16[8,2,128,128]{3,2,1,0:T(8,128)(2,1)S(1)}, u32[]{:S(2)}, u32[]{:S(2)}) async-start(bf16[8,2,128,128]{3,2,1,0:T(8,128)(2,1)} %y_sum.1), calls=%async_computation.1 | async-start | bytes 1048576 | tf_op jit(solution)/shard_map/all_to_all | solution.py:42
  128.3 84.1 %all-gather.5.cloned.1.call-start = ((), (), s32[]{:S(2)}) async-start(), calls=%async_computation.5 | async-start | bytes 2359296 | tf_op jit(solution)/shard_map/all_gather | solution.py:361
  128.4 2.2 copy-start
  137.4 12.4 %collective-permute-start.10 = (bf16[64,8192]{1,0:T(8,128)(2,1)S(1)}, bf16[64,8192]{1,0:T(8,128)(2,1)S(1)}, u32[]{:S(2)}, u32[]{:S(2)}) collective-permute-start(bf16[64,8192]{1,0:T(8,128)(2,1)S(1)} %contribs.3), channel_id=1, source_target_pairs={{0,1},{1,0},{2,3},{3,2},{4,5},{5,4},{6,7},{7,6},{8,9},{9,8},{10,11... | collective-permute-start | bytes 3145736 | tf_op jit(solution)/shard_map/ppermute | solution.py:38
  150.6 26.4 %collective-permute-start.11 = (bf16[16,8192]{1,0:T(8,128)(2,1)S(1)}, bf16[16,8192]{1,0:T(8,128)(2,1)S(1)}, u32[]{:S(2)}, u32[]{:S(2)}) collective-permute-start(bf16[16,8192]{1,0:T(8,128)(2,1)S(1)} %get-tuple-element.44), channel_id=1, source_target_pairs={{0,2},{2,4},{4,6},{6,0},{1,3},{3,5},{5,7},{7,1},{8,10},{10,12},{12... | collective-permute-start | bytes 786440 | tf_op jit(solution)/shard_map/ppermute | solution.py:38
  154.9 22.1 %collective-permute-start.12 = (bf16[16,8192]{1,0:T(8,128)(2,1)S(1)}, bf16[16,8192]{1,0:T(8,128)(2,1)S(1)}, u32[]{:S(2)}, u32[]{:S(2)}) collective-permute-start(bf16[16,8192]{1,0:T(8,128)(2,1)S(1)} %get-tuple-element.45), channel_id=1, source_target_pairs={{0,4},{2,6},{4,0},{6,2},{1,5},{3,7},{5,1},{7,3},{8,12},{10,14},{12... | collective-permute-start | bytes 786440 | tf_op jit(solution)/shard_map/ppermute | solution.py:38
  159.0 18.0 %collective-permute-start.13 = (bf16[16,8192]{1,0:T(8,128)(2,1)S(1)}, bf16[16,8192]{1,0:T(8,128)(2,1)S(1)}, u32[]{:S(2)}, u32[]{:S(2)}) collective-permute-start(bf16[16,8192]{1,0:T(8,128)(2,1)S(1)} %get-tuple-element.46), channel_id=1, source_target_pairs={{0,6},{2,0},{4,2},{6,4},{1,7},{3,1},{5,3},{7,5},{8,14},{10,8},{12,... | collective-permute-start | bytes 786440 | tf_op jit(solution)/shard_map/ppermute | solution.py:38
  177.8 99.2 %all-to-all-start.3 = ((f32[16,8,128]{2,1,0:T(8,128)}), f32[16,8,128]{2,1,0:T(8,128)S(1)}, u32[]{:S(2)}, u32[]{:S(2)}) async-start(f32[16,8,128]{2,1,0:T(8,128)} %relay.1), calls=%async_computation.3 | async-start | bytes 131072 | tf_op jit(solution)/shard_map/all_to_all | solution.py:42
  192.7 84.4 %copy-start.5 = (f32[1,2,128,128]{3,2,1,0:T(8,128)S(1)}, f32[1,2,128,128]{3,2,1,0:T(8,128)}, u32[]{:S(2)}) copy-start(f32[1,2,128,128]{3,2,1,0:T(8,128)} %one_ref.1) | copy-start | bytes 393220
  192.7 84.4 %copy-start.6 = (f32[1,2,128,128]{3,2,1,0:T(8,128)S(1)}, f32[1,2,128,128]{3,2,1,0:T(8,128)}, u32[]{:S(2)}) copy-start(f32[1,2,128,128]{3,2,1,0:T(8,128)} %two_ref.1) | copy-start | bytes 393220
Sparse Core Ops, SparseCore 0:
  28.6 93.1 all-gather.2
  178.0 34.4 all-gather.4

commit v5 on v3

--- a/solution.py
+++ b/solution.py
@@ -1,3 +1,5 @@
+import functools
+
 import jax
 import jax.numpy as jnp
 from jax import lax
@@ -101,28 +103,12 @@
     lax.fori_loop(0, (owners[1] - owners[0]) // per_step, step, 0)
 
 
-def far_kernel(
-    ids_ref, rows_ref, cols_ref, counts_ref, own_ref, other_ref, turned_ref,
-    low_ref, high_ref, features, starts_ref, sems,
+def tile_kernel(
+    aways, ids_ref, rows_ref, cols_ref, counts_ref, own_ref, other_ref, turned_ref, *refs
 ):
+    features, starts_ref, sems = refs[len(aways) :]
     load_features(own_ref, other_ref, features, sems, starts_ref, counts_ref)
-    group = (ids_ref[0] + 2) & (NY - 1)
-    for ref, owners in ((low_ref, (0, NM)), (high_ref, (NM, 2 * NM))):
-
-        def put(slot, term, ref=ref):
-            ref[slot] = term
-
-        slot_products(
-            group, owners, put, ids_ref, rows_ref, cols_ref, starts_ref, features, turned_ref
-        )
-
-
-def near_kernel(
-    ids_ref, rows_ref, cols_ref, counts_ref, own_ref, other_ref, turned_ref,
-    up_ref, down_ref, mine_ref, features, starts_ref, sems,
-):
-    load_features(own_ref, other_ref, features, sems, starts_ref, counts_ref)
-    for ref, away in ((up_ref, 1), (down_ref, 3), (mine_ref, 0)):
+    for ref, away in zip(refs, aways):
 
         def put(slot, term, ref=ref):
             ref[slot] = term
@@ -133,15 +119,7 @@
         )
 
 
-def passing_kernel(up_ref, low_ref, down_ref, high_ref, up_out, down_out):
-    half = GROUP // 2
-    up_out[:half] = (up_ref[:half].astype(F32) + low_ref[...].astype(F32)).astype(BF16)
-    up_out[half:] = up_ref[half:]
-    down_out[:half] = down_ref[:half]
-    down_out[half:] = (down_ref[half:].astype(F32) + high_ref[...].astype(F32)).astype(BF16)
-
-
-def y_sum_kernel(ids_ref, mine_ref, below_ref, above_ref, keep_ref, low_ref, high_ref):
+def y_sum_kernel(ids_ref, mine_ref, below_ref, above_ref, far_ref, keep_ref, low_ref, high_ref):
     parity = ids_ref[1] & 1
     for m in range(NM):
 
@@ -150,6 +128,7 @@
                 mine_ref[m, side].astype(F32)
                 + below_ref[m, side].astype(F32)
                 + above_ref[m, side].astype(F32)
+                + far_ref[m, side].astype(F32)
             ).astype(BF16)
 
         keep_ref[m] = total(parity)
@@ -203,6 +182,11 @@
         new_two_ref[0, rank] = jnp.where(live, second, two)
 
 
+def turn_kernel(delta_ref, out_ref):
+    for rank in range(SLOT_CAP):
+        out_ref[rank] = delta_ref[0, rank].T.astype(BF16)
+
+
 def contrib_kernel(
     ids_ref, rows_ref, cols_ref, counts_ref, grad_ref, delta_ref, stay_ref, give_ref, places_ref
 ):
@@ -218,16 +202,15 @@
         return start + counts_ref[0, owner]
 
     lax.fori_loop(0, counts_ref.shape[1], owner_step, 0)
-    per_step = 4
+    per_step = 28
 
     def step(index, carry):
         last, total = carry
         for part in range(per_step):
             k = index * per_step + part
             row = rows_ref[0, k]
-            product = lax.dot_general(
-                grad_ref[cols_ref[0, k]], delta_ref[places_ref[k]],
-                (((1,), (1,)), ((), ())), preferred_element_type=F32,
+            product = jnp.dot(
+                grad_ref[cols_ref[0, k]], delta_ref[places_ref[k]], preferred_element_type=F32
             )
             total = jnp.where(row == last, total, 0.0) + product
             lane = pl.multiple_of(row * TILE, TILE)
@@ -268,7 +251,9 @@
     own = spread(features, "x")
     other = shift(own, "core", 1)
 
-    delta_half = delta_value[0].astype(BF16)
+    delta_half = kernel_call(
+        turn_kernel, "turn", SHAPE(delta_value.shape[1:], BF16), [VMEM], VMEM
+    )(delta_value)
     delta_y = jnp.concatenate(
         [delta_half] + [shift(delta_half, "y", -away) for away in range(1, NY)], axis=0
     )
@@ -286,30 +271,27 @@
         pltpu.SMEM((owner_counts.shape[1],), jnp.int32),
         pltpu.SemaphoreType.DMA((2,)),
     ]
-    half = (GROUP // 2, TILE, TILE)
-    whole = (GROUP, TILE, TILE)
-    low, high = kernel_call(
-        far_kernel, "tiles_far", [SHAPE(half, BF16)] * 2, tile_ins, [VMEM] * 2, tile_scratch,
-        flops=2 * GROUP * TILE**3, moved=4 << 20,
-    )(ids, *lists, own, other, turned)
-
-    low = shift(low, "y", 1)
-    high = shift(high, "y", -1)
-    up, down, mine = kernel_call(
-        near_kernel, "tiles_near", [SHAPE(whole, BF16)] * 3, tile_ins, [VMEM] * 3, tile_scratch,
-        flops=6 * GROUP * TILE**3, moved=4 << 20,
-    )(ids, *lists, own, other, turned)
-    up, down = kernel_call(
-        passing_kernel, "passing", [SHAPE(whole, BF16)] * 2, [VMEM] * 4, [VMEM] * 2
-    )(up, low, down, high)
+
+    def terms(*aways):
+        return kernel_call(
+            functools.partial(tile_kernel, aways), "tiles",
+            [SHAPE((GROUP, TILE, TILE), BF16)] * len(aways), tile_ins, [VMEM] * len(aways),
+            tile_scratch, flops=2 * len(aways) * GROUP * TILE**3, moved=4 << 20,
+        )(ids, *lists, own, other, turned)
+
+    (far,) = terms(2)
+    far, turned = lax.optimization_barrier((far, turned))
+    far = shift(far, "y", 2)
+    up, down = terms(1, 3)
     below = shift(up, "y", 1)
     above = shift(down, "y", -1)
+    (mine,) = terms(0)
     parted = (NM, 2, SLOT_CAP, TILE, TILE)
     quarter = SHAPE((NM // 2, SLOT_CAP, TILE, TILE), BF16)
     kept = SHAPE((NM, SLOT_CAP, TILE, TILE), BF16)
     keep, low, high = kernel_call(
-        y_sum_kernel, "y_sum", [kept, quarter, quarter], [SMEM] + [VMEM] * 3, [VMEM] * 3
-    )(ids, mine.reshape(parted), below.reshape(parted), above.reshape(parted))
+        y_sum_kernel, "y_sum", [kept, quarter, quarter], [SMEM] + [VMEM] * 4, [VMEM] * 3
+    )(ids, *(value.reshape(parted) for value in (mine, below, above, far)))
 
     low = shift(low, Z, 1)
     high = shift(high, Z, -1)

time: 201 us -> 203 us (level)
  waiting for transfers between devices: 63.7 us -> 71.5 us
  Pallas kernels: 23.2 us -> 20 us
  starting transfers between devices: 78.7 us -> 75.8 us
    all_to_all x3, waiting for transfers between devices: 3.28 us -> 11.1 us  [exchange(): return lax.all_to_all(value, axis, split_axis=0, concat_axis=0, tiled=True)]
    pallas_call x1, Pallas kernels: 8.87 us -> 4.58 us  [body(): kernel_call(contrib_kernel, 'contribs', [SHAPE((tokens // 2, width), BF16...]
    ppermute x14 -> x13, starting transfers between devices: 54 us -> 51 us  [shift(): lax.ppermute(value, axis, [(i, (i + step) % size) for i in range(size)])]
    pallas_call x3 -> x4, Pallas kernels: 6.38 us -> 7.31 us  [the longest x3 7.21 us: terms(): kernel_call(functools.partial(tile_kernel, aways), 'tiles', [SHAPE((GROUP...]
    ppermute x14 -> x13, waiting for transfers between devices: 53.3 us -> 53.3 us  [shift(): lax.ppermute(value, axis, [(i, (i + step) % size) for i in range(size)])]
  transfers between devices with their start and end apart: 19 -> 18, of which waited for: 12 -> 11; matrix products, arithmetic and copies ran while one was open for 0% -> 0% of each run, Pallas kernels for 11% -> 9%
where the time goes in v5:
time: 203 us; the launch traced here: 202 us
  starting transfers between devices  75.8 us (37%)
  waiting for transfers between devices  71.5 us (35%)
  Pallas kernels  20 us (10%)
  between operations  14.3 us (7%)
  blocking collectives  12.8 us (6%)
  local copies, waits for them, and re-layouts  5.77 us (3%)
    ppermute x13, waiting for transfers between devices, shift(): lax.ppermute(value, axis, [(i, (i + step) % size) for i in range(size)])  53.3 us
    ppermute x13, starting transfers between devices, shift(): lax.ppermute(value, axis, [(i, (i + step) % size) for i in range(size)])  51 us
    all_to_all x3, starting transfers between devices, exchange(): return lax.all_to_all(value, axis, split_axis=0, concat_axis=0, tiled=True)  24.8 us
    all_to_all x1, blocking collectives, exchange(): return lax.all_to_all(value, axis, split_axis=0, concat_axis=0, tiled=True)  12.8 us
    all_to_all x3, waiting for transfers between devices, exchange(): return lax.all_to_all(value, axis, split_axis=0, concat_axis=0, tiled=True)  11.1 us
    pallas_call x3, Pallas kernels, terms(): kernel_call(functools.partial(tile_kernel, aways), 'tiles', [SHAPE((GROUP...  7.21 us
    all_gather x1, waiting for transfers between devices, body(): gathered = lax.all_gather(share, ('x', 'core'), axis=0, tiled=True)  7.08 us
    pallas_call x1, Pallas kernels, body(): kernel_call(contrib_kernel, 'contribs', [SHAPE((tokens // 2, width), BF16...  4.58 us
  transfers between devices with their start and end apart: 18, of which 11 were waited for; matrix products, arithmetic and copies ran while one was open for 0% of the time, Pallas kernels for 9%

profile of v5, /device:TPU:1, one launch (start us, length us, event | category | flops | bytes accessed | tf_op | source)
XLA Modules:
  0.0 201.9 jit_solution(747058412624850060)
XLA Ops:
  7.2 0.0 copy-start.1
  7.2 2.1 %broadcast_in_dim.2 = bf16[4,128,1024]{2,1,0:T(8,128)(2,1)} broadcast(bf16[128,1024]{1,0:T(8,128)(2,1)} %param.10), dimensions={1,2} | broadcast | bytes 1310720 | tf_op jit(solution)/shard_map/broadcast_in_dim | solution.py:45
  9.3 5.0 %all-to-all-start = ((bf16[4,128,1024]{2,1,0:T(8,128)(2,1)}), bf16[4,128,1024]{2,1,0:T(8,128)(2,1)S(1)}, u32[]{:S(2)}, u32[]{:S(2)}) async-start(bf16[4,128,1024]{2,1,0:T(8,128)(2,1)} %broadcast_in_dim.2), calls=%async_computation | async-start | bytes 2097152 | tf_op jit(solution)/shard_map/all_to_all | solution.py:41
  14.3 0.0 copy-done.1
  14.3 0.1 turn.1
  14.4 3.2 %collective-permute-start.8 = (bf16[2,128,128]{2,1,0:T(8,128)(2,1)S(1)}, bf16[2,128,128]{2,1,0:T(8,128)(2,1)S(1)}, u32[]{:S(2)}, u32[]{:S(2)}) collective-permute-start(bf16[2,128,128]{2,1,0:T(8,128)(2,1)S(1)} %turn.1), channel_id=1, source_target_pairs={{0,128},{128,256},{256,384},{384,0},{1,129},{129,257},{257,385},{3... | collective-permute-start | bytes 196616 | tf_op jit(solution)/shard_map/ppermute | solution.py:37
  17.6 4.5 %collective-permute-start.7 = (bf16[2,128,128]{2,1,0:T(8,128)(2,1)S(1)}, bf16[2,128,128]{2,1,0:T(8,128)(2,1)S(1)}, u32[]{:S(2)}, u32[]{:S(2)}) collective-permute-start(bf16[2,128,128]{2,1,0:T(8,128)(2,1)S(1)} %turn.1), channel_id=1, source_target_pairs={{0,256},{128,384},{256,0},{384,128},{1,257},{129,385},{257,1},{385... | collective-permute-start | bytes 196616 | tf_op jit(solution)/shard_map/ppermute | solution.py:37
  22.1 3.0 %collective-permute-start.6 = (bf16[2,128,128]{2,1,0:T(8,128)(2,1)S(1)}, bf16[2,128,128]{2,1,0:T(8,128)(2,1)S(1)}, u32[]{:S(2)}, u32[]{:S(2)}) collective-permute-start(bf16[2,128,128]{2,1,0:T(8,128)(2,1)S(1)} %turn.1), channel_id=1, source_target_pairs={{0,384},{128,0},{256,128},{384,256},{1,385},{129,1},{257,129},{385... | collective-permute-start | bytes 196616 | tf_op jit(solution)/shard_map/ppermute | solution.py:37
  25.1 0.0 collective-permute-done.8
  25.1 0.0 collective-permute-done.7
  25.1 2.1 %collective-permute-done.6 = bf16[2,128,128]{2,1,0:T(8,128)(2,1)S(1)} collective-permute-done((bf16[2,128,128]{2,1,0:T(8,128)(2,1)S(1)}, bf16[2,128,128]{2,1,0:T(8,128)(2,1)S(1)}, u32[]{:S(2)}, u32[]{:S(2)}) %collective-permute-start.6) | collective-permute-done | bytes 65568 | tf_op jit(solution)/shard_map/ppermute | solution.py:37
  27.2 0.7 pad_maximum_fusion
  27.9 0.0 all-to-all-done.own_ref
  27.9 0.0 all-gather.3.cloned.1.call-update
  28.0 6.8 %collective-permute-start = (bf16[4,128,1024]{2,1,0:T(8,128)(2,1)S(1)}, bf16[4,128,1024]{2,1,0:T(8,128)(2,1)S(1)}, u32[]{:S(2)}, u32[]{:S(2)}) collective-permute-start(bf16[4,128,1024]{2,1,0:T(8,128)(2,1)S(1)} %all-to-all-done.own_ref), channel_id=1, source_target_pairs={{0,1},{1,0},{2,3},{3,2},{4,5},{5,4},{6,7},{7,6},{8,9},{9,8},{10,11... | collective-permute-start | bytes 3145736 | tf_op jit(solution)/shard_map/ppermute | solution.py:37
  34.8 0.1 pad_add_fusion.ids_ref.refs_0_
  34.8 1.0 copy-done.3
  35.9 1.0 copy-done.4
  36.9 1.1 gate.1
  38.0 0.0 collective-permute-done.other_ref
  38.0 0.0 copy-done.7
  38.0 0.0 copy-done.8
  38.0 0.0 copy-done.9
  38.0 2.1 %tiles.3 = bf16[32,128,128]{2,1,0:T(8,128)(2,1)S(1)} custom-call(s32[4]{0:T(128)S(1)} %pad_add_fusion.ids_ref.refs_0_, s32[1,112]{1,0:T(1,128)S(1)} %copy-done.8, s32[1,112]{1,0:T(1,128)S(1)} %copy-done.9, s32[1,64]{1,0:T(1,128)S(1)} %copy-done.7, bf16[4,128,1024]{2,1,0:T(8,128)(2,1)S(1)} %all-to-all-done.own_ref, ...), custom_call_target="tpu_custom_call" | custom-call | flops 134217728 | bytes 4194304 | tf_op jit(solution)/shard_map/tiles/pallas_call | solution.py:276
  40.1 3.1 %tiles.5 = (bf16[32,128,128]{2,1,0:T(8,128)(2,1)S(1)}, bf16[32,128,128]{2,1,0:T(8,128)(2,1)S(1)}) custom-call(s32[4]{0:T(128)S(1)} %pad_add_fusion.ids_ref.refs_0_, s32[1,112]{1,0:T(1,128)S(1)} %copy-done.8, s32[1,112]{1,0:T(1,128)S(1)} %copy-done.9, s32[1,64]{1,0:T(1,128)S(1)} %copy-done.7, bf16[4,128,1024]{2,1,0:T(8,128)(2,1)S(1)} %all-to-all-done.own_ref, ...), custom_call_target="tpu_custom_call" | custom-call | flops 268435456 | bytes 4194304 | tf_op jit(solution)/shard_map/tiles/pallas_call | solution.py:276
  43.2 3.6 %collective-permute-start.1 = (bf16[32,128,128]{2,1,0:T(8,128)(2,1)S(1)}, bf16[32,128,128]{2,1,0:T(8,128)(2,1)S(1)}, u32[]{:S(2)}, u32[]{:S(2)}) collective-permute-start(bf16[32,128,128]{2,1,0:T(8,128)(2,1)S(1)} %get-tuple-element.33), channel_id=1, source_target_pairs={{0,128},{128,256},{256,384},{384,0},{1,129},{129,257},{257,385},{3... | collective-permute-start | bytes 3145736 | tf_op jit(solution)/shard_map/ppermute | solution.py:37
  46.8 2.9 %collective-permute-start.2 = (bf16[32,128,128]{2,1,0:T(8,128)(2,1)S(1)}, bf16[32,128,128]{2,1,0:T(8,128)(2,1)S(1)}, u32[]{:S(2)}, u32[]{:S(2)}) collective-permute-start(bf16[32,128,128]{2,1,0:T(8,128)(2,1)S(1)} %get-tuple-element.34), channel_id=1, source_target_pairs={{0,384},{128,0},{256,128},{384,256},{1,385},{129,1},{257,129},{385... | collective-permute-start | bytes 3145736 | tf_op jit(solution)/shard_map/ppermute | solution.py:37
  49.7 2.8 %collective-permute-start.3 = (bf16[32,128,128]{2,1,0:T(8,128)(2,1)S(1)}, bf16[32,128,128]{2,1,0:T(8,128)(2,1)S(1)}, u32[]{:S(2)}, u32[]{:S(2)}) collective-permute-start(bf16[32,128,128]{2,1,0:T(8,128)(2,1)S(1)} %tiles.3), channel_id=1, source_target_pairs={{0,256},{128,384},{256,0},{384,128},{1,257},{129,385},{257,1},{385... | collective-permute-start | bytes 3145736 | tf_op jit(solution)/shard_map/ppermute | solution.py:37
  52.5 2.1 %tiles.4 = bf16[32,128,128]{2,1,0:T(8,128)(2,1)S(1)} custom-call(s32[4]{0:T(128)S(1)} %pad_add_fusion.ids_ref.refs_0_, s32[1,112]{1,0:T(1,128)S(1)} %copy-done.8, s32[1,112]{1,0:T(1,128)S(1)} %copy-done.9, s32[1,64]{1,0:T(1,128)S(1)} %copy-done.7, bf16[4,128,1024]{2,1,0:T(8,128)(2,1)S(1)} %all-to-all-done.own_ref, ...), custom_call_target="tpu_custom_call" | custom-call | flops 134217728 | bytes 4194304 | tf_op jit(solution)/shard_map/tiles/pallas_call | solution.py:276
  54.6 16.5 %collective-permute-done.1 = bf16[32,128,128]{2,1,0:T(8,128)(2,1)S(1)} collective-permute-done((bf16[32,128,128]{2,1,0:T(8,128)(2,1)S(1)}, bf16[32,128,128]{2,1,0:T(8,128)(2,1)S(1)}, u32[]{:S(2)}, u32[]{:S(2)}) %collective-permute-start.1) | collective-permute-done | bytes 1048608 | tf_op jit(solution)/shard_map/ppermute | solution.py:37
  71.1 2.2 %collective-permute-done.2 = bf16[32,128,128]{2,1,0:T(8,128)(2,1)S(1)} collective-permute-done((bf16[32,128,128]{2,1,0:T(8,128)(2,1)S(1)}, bf16[32,128,128]{2,1,0:T(8,128)(2,1)S(1)}, u32[]{:S(2)}, u32[]{:S(2)}) %collective-permute-start.2) | collective-permute-done | bytes 1048608 | tf_op jit(solution)/shard_map/ppermute | solution.py:37
  73.3 20.9 %collective-permute-done.3 = bf16[32,128,128]{2,1,0:T(8,128)(2,1)S(1)} collective-permute-done((bf16[32,128,128]{2,1,0:T(8,128)(2,1)S(1)}, bf16[32,128,128]{2,1,0:T(8,128)(2,1)S(1)}, u32[]{:S(2)}, u32[]{:S(2)}) %collective-permute-start.3) | collective-permute-done | bytes 1048608 | tf_op jit(solution)/shard_map/ppermute | solution.py:37
  94.1 1.1 y_sum.1
  95.2 1.9 collective-permute-start.4
  97.1 9.3 %collective-permute-start.5 = (bf16[4,2,128,128]{3,2,1,0:T(8,128)(2,1)S(1)}, bf16[4,2,128,128]{3,2,1,0:T(8,128)(2,1)S(1)}, u32[]{:S(2)}, u32[]{:S(2)}) collective-permute-start(bf16[4,2,128,128]{3,2,1,0:T(8,128)(2,1)S(1)} %get-tuple-element.38), channel_id=1, source_target_pairs={{0,120},{8,0},{16,8},{24,16},{32,24},{40,32},{48,40},{56,48},{64,5... | collective-permute-start | bytes 786440 | tf_op jit(solution)/shard_map/ppermute | solution.py:37
  106.4 6.1 %collective-permute-done.4.low_ref = bf16[4,2,128,128]{3,2,1,0:T(8,128)(2,1)S(1)} collective-permute-done((bf16[4,2,128,128]{3,2,1,0:T(8,128)(2,1)S(1)}, bf16[4,2,128,128]{3,2,1,0:T(8,128)(2,1)S(1)}, u32[]{:S(2)}, u32[]{:S(2)}) %collective-permute-start.4) | collective-permute-done | bytes 262176 | tf_op jit(solution)/shard_map/ppermute | solution.py:37
  112.5 1.3 collective-permute-done.5.high_ref
  113.8 0.9 pair_sum.1
  114.7 8.1 %all-to-all-start.1 = ((bf16[8,2,128,128]{3,2,1,0:T(8,128)(2,1)}), bf16[8,2,128,128]{3,2,1,0:T(8,128)(2,1)S(1)}, u32[]{:S(2)}, u32[]{:S(2)}) async-start(bf16[8,2,128,128]{3,2,1,0:T(8,128)(2,1)} %pair_sum.1), calls=%async_computation.1 | async-start | bytes 1048576 | tf_op jit(solution)/shard_map/all_to_all | solution.py:41
  122.8 0.0 all-gather.5.cloned.1.call-start
  122.9 0.0 all-gather.3.cloned.1.call-done.delta_ref
  122.9 4.6 %contribs.1 = (bf16[64,8192]{1,0:T(8,128)(2,1)S(1)}, bf16[64,8192]{1,0:T(8,128)(2,1)S(1)}) custom-call(s32[4]{0:T(128)S(1)} %pad_add_fusion.ids_ref.refs_0_, s32[1,112]{1,0:T(1,128)S(1)} %copy-done.8, s32[1,112]{1,0:T(1,128)S(1)} %copy-done.9, s32[1,64]{1,0:T(1,128)S(1)} %copy-done.7, bf16[14,128,128]{2,1,0:T(8,128)(2,1)S(1)} %get-tuple-element.42.grad_ref, ...), custom_call_target="tpu_custom_call" | custom-call | bytes 4096 | tf_op jit(solution)/shard_map/contribs/pallas_call | solution.py:307
  127.5 3.5 %collective-permute-start.9 = (bf16[64,8192]{1,0:T(8,128)(2,1)S(1)}, bf16[64,8192]{1,0:T(8,128)(2,1)S(1)}, u32[]{:S(2)}, u32[]{:S(2)}) collective-permute-start(bf16[64,8192]{1,0:T(8,128)(2,1)S(1)} %get-tuple-element.45), channel_id=1, source_target_pairs={{0,1},{1,0},{2,3},{3,2},{4,5},{5,4},{6,7},{7,6},{8,9},{9,8},{10,11... | collective-permute-start | bytes 3145736 | tf_op jit(solution)/shard_map/ppermute | solution.py:37
  131.0 2.3 %collective-permute-done.9 = bf16[64,8192]{1,0:T(8,128)(2,1)S(1)} collective-permute-done((bf16[64,8192]{1,0:T(8,128)(2,1)S(1)}, bf16[64,8192]{1,0:T(8,128)(2,1)S(1)}, u32[]{:S(2)}, u32[]{:S(2)}) %collective-permute-start.9) | collective-permute-done | bytes 1048608 | tf_op jit(solution)/shard_map/ppermute | solution.py:37
  133.2 0.8 core_sum.1
  134.0 4.6 %collective-permute-start.12 = (bf16[16,8192]{1,0:T(8,128)(2,1)S(1)}, bf16[16,8192]{1,0:T(8,128)(2,1)S(1)}, u32[]{:S(2)}, u32[]{:S(2)}) collective-permute-start(bf16[16,8192]{1,0:T(8,128)(2,1)S(1)} %get-tuple-element.49), channel_id=1, source_target_pairs={{0,6},{2,0},{4,2},{6,4},{1,7},{3,1},{5,3},{7,5},{8,14},{10,8},{12,... | collective-permute-start | bytes 786440 | tf_op jit(solution)/shard_map/ppermute | solution.py:37
  138.6 2.5 %collective-permute-start.11 = (bf16[16,8192]{1,0:T(8,128)(2,1)S(1)}, bf16[16,8192]{1,0:T(8,128)(2,1)S(1)}, u32[]{:S(2)}, u32[]{:S(2)}) collective-permute-start(bf16[16,8192]{1,0:T(8,128)(2,1)S(1)} %get-tuple-element.48), channel_id=1, source_target_pairs={{0,4},{2,6},{4,0},{6,2},{1,5},{3,7},{5,1},{7,3},{8,12},{10,14},{12... | collective-permute-start | bytes 786440 | tf_op jit(solution)/shard_map/ppermute | solution.py:37
  141.1 2.5 %collective-permute-start.10 = (bf16[16,8192]{1,0:T(8,128)(2,1)S(1)}, bf16[16,8192]{1,0:T(8,128)(2,1)S(1)}, u32[]{:S(2)}, u32[]{:S(2)}) collective-permute-start(bf16[16,8192]{1,0:T(8,128)(2,1)S(1)} %get-tuple-element.47), channel_id=1, source_target_pairs={{0,2},{2,4},{4,6},{6,0},{1,3},{3,5},{5,7},{7,1},{8,10},{10,12},{12... | collective-permute-start | bytes 786440 | tf_op jit(solution)/shard_map/ppermute | solution.py:37
  143.6 9.5 %all-to-all-done.1.arrived_ref = bf16[8,2,128,128]{3,2,1,0:T(8,128)(2,1)S(1)} async-done(((bf16[8,2,128,128]{3,2,1,0:T(8,128)(2,1)}), bf16[8,2,128,128]{3,2,1,0:T(8,128)(2,1)S(1)}, u32[]{:S(2)}, u32[]{:S(2)}) %all-to-all-start.1) | async-done | bytes 524320 | tf_op jit(solution)/shard_map/all_to_all | solution.py:41
  153.1 0.8 own_grad.1
  153.8 0.0 collective-permute-done.12
  153.8 0.0 collective-permute-done.11
  153.9 2.0 collective-permute-done.10
  155.9 0.8 add_convert_fusion
  156.7 0.0 all-gather.5.cloned.1.call-update
  156.7 12.8 %all_to_all.20.arrived_ref = f32[32,8,128]{2,1,0:T(8,128)S(1)} all-to-all(f32[32,8,128]{2,1,0:T(8,128)S(1)} %get-tuple-element.50), channel_id=1, replica_groups=mesh['y'=4,'m'=8,'p'=2,'x'=4,'core'=2] {'y','x','core'}, dimensions={0} | all-to-all | bytes 262144 | tf_op jit(solution)/shard_map/all_to_all | solution.py:41
  169.5 0.7 relay.1
  170.2 11.8 %all-to-all-start.3 = ((f32[16,8,128]{2,1,0:T(8,128)}), f32[16,8,128]{2,1,0:T(8,128)S(1)}, u32[]{:S(2)}, u32[]{:S(2)}) async-start(f32[16,8,128]{2,1,0:T(8,128)} %relay.1), calls=%async_computation.3 | async-start | bytes 131072 | tf_op jit(solution)/shard_map/all_to_all | solution.py:41
  182.0 7.1 %all-gather.5.cloned.1.call-done.in_ref = bf16[128,8192]{1,0:T(8,128)(2,1)} async-done(((bf16[16,8192]{1,0:T(8,128)(2,1)}), bf16[128,8192]{1,0:T(8,128)(2,1)}) %all-gather.5.cloned.1.call-update) | async-done | bytes 2097168 | tf_op jit(solution)/shard_map/all_gather | solution.py:323
  189.1 1.6 copy-done
  190.7 1.3 result.1
  192.0 1.6 all-to-all-done.3.refs_2_
  193.6 0.0 copy-done.5
  193.6 1.5 adam.1
  (12 shorter events, 0.0 us)
Async XLA Ops:
  7.2 7.1 %copy-start.1 = (f32[1,2,128,128]{3,2,1,0:T(8,128)S(1)}, f32[1,2,128,128]{3,2,1,0:T(8,128)}, u32[]{:S(2)}) copy-start(f32[1,2,128,128]{3,2,1,0:T(8,128)} %refs_4_.1) | copy-start | bytes 393220
  7.2 27.7 %copy-start.2 = (bf16[128,1792]{1,0:T(8,128)(2,1)S(1)}, bf16[128,1792]{1,0:T(8,128)(2,1)}, u32[]{:S(2)}) copy-start(bf16[128,1792]{1,0:T(8,128)(2,1)} %gate_ref.1) | copy-start | bytes 1376260
  9.3 28.7 %copy-start.7 = (s32[1,64]{1,0:T(1,128)S(1)}, s32[1,64]{1,0:T(1,128)}, u32[]{:S(2)}) copy-start(s32[1,64]{1,0:T(1,128)} %refs_1_.1) | copy-start | bytes 772
  9.3 28.7 %copy-start.8 = (s32[1,112]{1,0:T(1,128)S(1)}, s32[1,112]{1,0:T(1,128)}, u32[]{:S(2)}) copy-start(s32[1,112]{1,0:T(1,128)} %rows_ref.7) | copy-start | bytes 1348
  9.3 28.7 %copy-start.9 = (s32[1,112]{1,0:T(1,128)S(1)}, s32[1,112]{1,0:T(1,128)}, u32[]{:S(2)}) copy-start(s32[1,112]{1,0:T(1,128)} %cols_ref.7) | copy-start | bytes 1348
  9.3 18.6 %all-to-all-start = ((bf16[4,128,1024]{2,1,0:T(8,128)(2,1)}), bf16[4,128,1024]{2,1,0:T(8,128)(2,1)S(1)}, u32[]{:S(2)}, u32[]{:S(2)}) async-start(bf16[4,128,1024]{2,1,0:T(8,128)(2,1)} %broadcast_in_dim.2), calls=%async_computation | async-start | bytes 2097152 | tf_op jit(solution)/shard_map/all_to_all | solution.py:41
  14.3 108.6 %all-gather.3.cloned.1.call-start = ((), (), s32[]{:S(2)}) async-start(), calls=%async_computation.4 | async-start | bytes 4456448 | tf_op jit(solution)/shard_map/all_gather | solution.py:261
  14.4 10.7 %collective-permute-start.8 = (bf16[2,128,128]{2,1,0:T(8,128)(2,1)S(1)}, bf16[2,128,128]{2,1,0:T(8,128)(2,1)S(1)}, u32[]{:S(2)}, u32[]{:S(2)}) collective-permute-start(bf16[2,128,128]{2,1,0:T(8,128)(2,1)S(1)} %turn.1), channel_id=1, source_target_pairs={{0,128},{128,256},{256,384},{384,0},{1,129},{129,257},{257,385},{3... | collective-permute-start | bytes 196616 | tf_op jit(solution)/shard_map/ppermute | solution.py:37
  17.6 7.5 %collective-permute-start.7 = (bf16[2,128,128]{2,1,0:T(8,128)(2,1)S(1)}, bf16[2,128,128]{2,1,0:T(8,128)(2,1)S(1)}, u32[]{:S(2)}, u32[]{:S(2)}) collective-permute-start(bf16[2,128,128]{2,1,0:T(8,128)(2,1)S(1)} %turn.1), channel_id=1, source_target_pairs={{0,256},{128,384},{256,0},{384,128},{1,257},{129,385},{257,1},{385... | collective-permute-start | bytes 196616 | tf_op jit(solution)/shard_map/ppermute | solution.py:37
  22.1 5.1 %collective-permute-start.6 = (bf16[2,128,128]{2,1,0:T(8,128)(2,1)S(1)}, bf16[2,128,128]{2,1,0:T(8,128)(2,1)S(1)}, u32[]{:S(2)}, u32[]{:S(2)}) collective-permute-start(bf16[2,128,128]{2,1,0:T(8,128)(2,1)S(1)} %turn.1), channel_id=1, source_target_pairs={{0,384},{128,0},{256,128},{384,256},{1,385},{129,1},{257,129},{385... | collective-permute-start | bytes 196616 | tf_op jit(solution)/shard_map/ppermute | solution.py:37
  28.0 10.0 %collective-permute-start = (bf16[4,128,1024]{2,1,0:T(8,128)(2,1)S(1)}, bf16[4,128,1024]{2,1,0:T(8,128)(2,1)S(1)}, u32[]{:S(2)}, u32[]{:S(2)}) collective-permute-start(bf16[4,128,1024]{2,1,0:T(8,128)(2,1)S(1)} %all-to-all-done.own_ref), channel_id=1, source_target_pairs={{0,1},{1,0},{2,3},{3,2},{4,5},{5,4},{6,7},{7,6},{8,9},{9,8},{10,11... | collective-permute-start | bytes 3145736 | tf_op jit(solution)/shard_map/ppermute | solution.py:37
  34.8 1.0 copy-start.3
  35.9 1.0 copy-start.4
  43.2 27.9 %collective-permute-start.1 = (bf16[32,128,128]{2,1,0:T(8,128)(2,1)S(1)}, bf16[32,128,128]{2,1,0:T(8,128)(2,1)S(1)}, u32[]{:S(2)}, u32[]{:S(2)}) collective-permute-start(bf16[32,128,128]{2,1,0:T(8,128)(2,1)S(1)} %get-tuple-element.33), channel_id=1, source_target_pairs={{0,128},{128,256},{256,384},{384,0},{1,129},{129,257},{257,385},{3... | collective-permute-start | bytes 3145736 | tf_op jit(solution)/shard_map/ppermute | solution.py:37
  46.8 26.4 %collective-permute-start.2 = (bf16[32,128,128]{2,1,0:T(8,128)(2,1)S(1)}, bf16[32,128,128]{2,1,0:T(8,128)(2,1)S(1)}, u32[]{:S(2)}, u32[]{:S(2)}) collective-permute-start(bf16[32,128,128]{2,1,0:T(8,128)(2,1)S(1)} %get-tuple-element.34), channel_id=1, source_target_pairs={{0,384},{128,0},{256,128},{384,256},{1,385},{129,1},{257,129},{385... | collective-permute-start | bytes 3145736 | tf_op jit(solution)/shard_map/ppermute | solution.py:37
  49.7 44.4 %collective-permute-start.3 = (bf16[32,128,128]{2,1,0:T(8,128)(2,1)S(1)}, bf16[32,128,128]{2,1,0:T(8,128)(2,1)S(1)}, u32[]{:S(2)}, u32[]{:S(2)}) collective-permute-start(bf16[32,128,128]{2,1,0:T(8,128)(2,1)S(1)} %tiles.3), channel_id=1, source_target_pairs={{0,256},{128,384},{256,0},{384,128},{1,257},{129,385},{257,1},{385... | collective-permute-start | bytes 3145736 | tf_op jit(solution)/shard_map/ppermute | solution.py:37
  95.2 17.3 %collective-permute-start.4 = (bf16[4,2,128,128]{3,2,1,0:T(8,128)(2,1)S(1)}, bf16[4,2,128,128]{3,2,1,0:T(8,128)(2,1)S(1)}, u32[]{:S(2)}, u32[]{:S(2)}) collective-permute-start(bf16[4,2,128,128]{3,2,1,0:T(8,128)(2,1)S(1)} %get-tuple-element.37), channel_id=1, source_target_pairs={{0,8},{8,16},{16,24},{24,32},{32,40},{40,48},{48,56},{56,64},{64,7... | collective-permute-start | bytes 786440 | tf_op jit(solution)/shard_map/ppermute | solution.py:37
  97.1 16.7 %collective-permute-start.5 = (bf16[4,2,128,128]{3,2,1,0:T(8,128)(2,1)S(1)}, bf16[4,2,128,128]{3,2,1,0:T(8,128)(2,1)S(1)}, u32[]{:S(2)}, u32[]{:S(2)}) collective-permute-start(bf16[4,2,128,128]{3,2,1,0:T(8,128)(2,1)S(1)} %get-tuple-element.38), channel_id=1, source_target_pairs={{0,120},{8,0},{16,8},{24,16},{32,24},{40,32},{48,40},{56,48},{64,5... | collective-permute-start | bytes 786440 | tf_op jit(solution)/shard_map/ppermute | solution.py:37
  114.7 38.3 %all-to-all-start.1 = ((bf16[8,2,128,128]{3,2,1,0:T(8,128)(2,1)}), bf16[8,2,128,128]{3,2,1,0:T(8,128)(2,1)S(1)}, u32[]{:S(2)}, u32[]{:S(2)}) async-start(bf16[8,2,128,128]{3,2,1,0:T(8,128)(2,1)} %pair_sum.1), calls=%async_computation.1 | async-start | bytes 1048576 | tf_op jit(solution)/shard_map/all_to_all | solution.py:41
  122.8 66.2 %all-gather.5.cloned.1.call-start = ((), (), s32[]{:S(2)}) async-start(), calls=%async_computation.5 | async-start | bytes 2359296 | tf_op jit(solution)/shard_map/all_gather | solution.py:323
  127.5 5.8 %collective-permute-start.9 = (bf16[64,8192]{1,0:T(8,128)(2,1)S(1)}, bf16[64,8192]{1,0:T(8,128)(2,1)S(1)}, u32[]{:S(2)}, u32[]{:S(2)}) collective-permute-start(bf16[64,8192]{1,0:T(8,128)(2,1)S(1)} %get-tuple-element.45), channel_id=1, source_target_pairs={{0,1},{1,0},{2,3},{3,2},{4,5},{5,4},{6,7},{7,6},{8,9},{9,8},{10,11... | collective-permute-start | bytes 3145736 | tf_op jit(solution)/shard_map/ppermute | solution.py:37
  134.0 19.8 %collective-permute-start.12 = (bf16[16,8192]{1,0:T(8,128)(2,1)S(1)}, bf16[16,8192]{1,0:T(8,128)(2,1)S(1)}, u32[]{:S(2)}, u32[]{:S(2)}) collective-permute-start(bf16[16,8192]{1,0:T(8,128)(2,1)S(1)} %get-tuple-element.49), channel_id=1, source_target_pairs={{0,6},{2,0},{4,2},{6,4},{1,7},{3,1},{5,3},{7,5},{8,14},{10,8},{12,... | collective-permute-start | bytes 786440 | tf_op jit(solution)/shard_map/ppermute | solution.py:37
  138.6 15.2 %collective-permute-start.11 = (bf16[16,8192]{1,0:T(8,128)(2,1)S(1)}, bf16[16,8192]{1,0:T(8,128)(2,1)S(1)}, u32[]{:S(2)}, u32[]{:S(2)}) collective-permute-start(bf16[16,8192]{1,0:T(8,128)(2,1)S(1)} %get-tuple-element.48), channel_id=1, source_target_pairs={{0,4},{2,6},{4,0},{6,2},{1,5},{3,7},{5,1},{7,3},{8,12},{10,14},{12... | collective-permute-start | bytes 786440 | tf_op jit(solution)/shard_map/ppermute | solution.py:37
  141.1 14.8 %collective-permute-start.10 = (bf16[16,8192]{1,0:T(8,128)(2,1)S(1)}, bf16[16,8192]{1,0:T(8,128)(2,1)S(1)}, u32[]{:S(2)}, u32[]{:S(2)}) collective-permute-start(bf16[16,8192]{1,0:T(8,128)(2,1)S(1)} %get-tuple-element.47), channel_id=1, source_target_pairs={{0,2},{2,4},{4,6},{6,0},{1,3},{3,5},{5,7},{7,1},{8,10},{10,12},{12... | collective-permute-start | bytes 786440 | tf_op jit(solution)/shard_map/ppermute | solution.py:37
  170.2 23.4 %all-to-all-start.3 = ((f32[16,8,128]{2,1,0:T(8,128)}), f32[16,8,128]{2,1,0:T(8,128)S(1)}, u32[]{:S(2)}, u32[]{:S(2)}) async-start(f32[16,8,128]{2,1,0:T(8,128)} %relay.1), calls=%async_computation.3 | async-start | bytes 131072 | tf_op jit(solution)/shard_map/all_to_all | solution.py:41
  189.1 1.6 copy-start
  190.6 2.9 %copy-start.5 = (f32[1,2,128,128]{3,2,1,0:T(8,128)S(1)}, f32[1,2,128,128]{3,2,1,0:T(8,128)}, u32[]{:S(2)}) copy-start(f32[1,2,128,128]{3,2,1,0:T(8,128)} %refs_5_.1) | copy-start | bytes 393220
  190.7 2.9 %copy-start.6 = (f32[1,2,128,128]{3,2,1,0:T(8,128)S(1)}, f32[1,2,128,128]{3,2,1,0:T(8,128)}, u32[]{:S(2)}) copy-start(f32[1,2,128,128]{3,2,1,0:T(8,128)} %refs_6_.1) | copy-start | bytes 393220
Sparse Core Ops, SparseCore 0:
  28.1 77.9 all-gather.2
  156.8 32.1 all-gather.4

commit v6 on v5

--- a/solution.py
+++ b/solution.py
@@ -7,11 +7,12 @@
 from jax.experimental.pallas import tpu as pltpu
 from jax.sharding import Mesh, PartitionSpec as P
 
-NY, NM, NX = 4, 8, 4
-Z = ("m", "p")
+NY, NQ, NC, NX = 4, 4, 4, 4
+NZ = NQ * NC
+Z = ("q", "c")
 TILE = 128
 SLOT_CAP = 2
-GROUP = 2 * NM * SLOT_CAP
+LOW, HIGH = (0, NZ // 2), (NZ // 2, NZ)
 BF16, F32 = jnp.bfloat16, jnp.float32
 SMEM = pl.BlockSpec(memory_space=pltpu.SMEM)
 VMEM = pl.BlockSpec(memory_space=pltpu.VMEM)
@@ -90,7 +91,7 @@
     def step(index, carry):
         for part in range(per_step):
             owner = owners[0] + index * per_step + part
-            start = starts_ref[group * 2 * NM + owner]
+            start = starts_ref[group * NZ + owner]
             for rank in range(SLOT_CAP):
                 k = jnp.minimum(start + rank, last)
                 row = rows_ref[0, k]
@@ -104,53 +105,64 @@
 
 
 def tile_kernel(
-    aways, ids_ref, rows_ref, cols_ref, counts_ref, own_ref, other_ref, turned_ref, *refs
-):
-    features, starts_ref, sems = refs[len(aways) :]
+    parts, ids_ref, rows_ref, cols_ref, counts_ref, own_ref, other_ref, turned_ref, *refs
+):
+    features, starts_ref, sems = refs[len(parts) :]
     load_features(own_ref, other_ref, features, sems, starts_ref, counts_ref)
-    for ref, away in zip(refs, aways):
+    for ref, (away, owners) in zip(refs, parts):
 
         def put(slot, term, ref=ref):
             ref[slot] = term
 
         slot_products(
-            (ids_ref[0] + away) & (NY - 1), (0, 2 * NM), put,
+            (ids_ref[0] + away) & (NY - 1), owners, put,
             ids_ref, rows_ref, cols_ref, starts_ref, features, turned_ref,
         )
 
 
-def y_sum_kernel(ids_ref, mine_ref, below_ref, above_ref, far_ref, keep_ref, low_ref, high_ref):
-    parity = ids_ref[1] & 1
-    for m in range(NM):
-
-        def total(side):
+def passing_kernel(up_ref, far_low_ref, down_ref, far_high_ref, up_out, down_out):
+    up_out[...] = (up_ref[...].astype(F32) + far_low_ref[...].astype(F32)).astype(BF16)
+    down_out[...] = (down_ref[...].astype(F32) + far_high_ref[...].astype(F32)).astype(BF16)
+
+
+def y_sum_kernel(
+    ids_ref, mine_ref, below_low_ref, above_low_ref, below_high_ref, above_high_ref,
+    keep_ref, up_ref, down_ref, up_two_ref, down_two_ref,
+):
+    mine_class = ids_ref[1] & (NC - 1)
+    half = NQ // 2
+    for q in range(NQ):
+        below, above = (below_low_ref, above_low_ref) if q < half else (below_high_ref, above_high_ref)
+
+        def total(step):
+            side = (mine_class + step) & (NC - 1)
             return (
-                mine_ref[m, side].astype(F32)
-                + below_ref[m, side].astype(F32)
-                + above_ref[m, side].astype(F32)
-                + far_ref[m, side].astype(F32)
+                mine_ref[q, side].astype(F32)
+                + below[q % half, side].astype(F32)
+                + above[q % half, side].astype(F32)
             ).astype(BF16)
 
-        keep_ref[m] = total(parity)
-        if m < NM // 2:
-            low_ref[m] = total(1 - parity)
-        else:
-            high_ref[m - NM // 2] = total(1 - parity)
-
-
-def pair_sum_kernel(keep_ref, low_ref, high_ref, out_ref):
-    half = NM // 2
-    out_ref[:half] = (keep_ref[:half].astype(F32) + low_ref[...].astype(F32)).astype(BF16)
-    out_ref[half:] = (keep_ref[half:].astype(F32) + high_ref[...].astype(F32)).astype(BF16)
+        keep_ref[q] = total(0)
+        up_ref[q] = total(1)
+        down_ref[q] = total(3)
+        (up_two_ref if q < half else down_two_ref)[q % half] = total(2)
+
+
+def class_sum_kernel(keep_ref, one_ref, other_ref, low_ref, high_ref, out_ref):
+    half = NQ // 2
+    for q in range(NQ):
+        two = low_ref[q] if q < half else high_ref[q - half]
+        total = keep_ref[q].astype(F32) + one_ref[q].astype(F32)
+        out_ref[q] = (total + other_ref[q].astype(F32) + two.astype(F32)).astype(BF16)
 
 
 def own_grad_kernel(ids_ref, counts_ref, arrived_ref, grad_ref, squares_ref):
-    count = counts_ref[0, ids_ref[0] * 2 * NM + ids_ref[1]]
+    count = counts_ref[0, ids_ref[0] * NZ + ids_ref[1]]
     squares = jnp.zeros((TILE, TILE), F32)
     for rank in range(SLOT_CAP):
         total = arrived_ref[0, rank].astype(F32)
-        for m in range(1, NM):
-            total = total + arrived_ref[m, rank].astype(F32)
+        for q in range(1, NQ):
+            total = total + arrived_ref[q, rank].astype(F32)
         total = jnp.where(rank < count, total, 0.0)
         grad_ref[rank] = total
         squares = squares + total * total
@@ -168,7 +180,7 @@
 ):
     squares = jnp.sum(arrived_ref[...], axis=0)[0:1]
     factor = jnp.minimum(1.0, 1.0 / jnp.sqrt(squares / count_all + 1e-06))
-    count = counts_ref[0, ids_ref[0] * 2 * NM + ids_ref[1]]
+    count = counts_ref[0, ids_ref[0] * NZ + ids_ref[1]]
     for rank in range(SLOT_CAP):
         live = rank < count
         clipped = factor * grad_ref[rank].T
@@ -188,15 +200,14 @@
 
 
 def contrib_kernel(
-    ids_ref, rows_ref, cols_ref, counts_ref, grad_ref, delta_ref, stay_ref, give_ref, places_ref
+    rows_ref, cols_ref, counts_ref, grad_ref, delta_ref, stay_ref, give_ref, places_ref
 ):
     stay_ref[...] = jnp.zeros_like(stay_ref)
     give_ref[...] = jnp.zeros_like(give_ref)
     half = stay_ref.shape[0]
-    y = ids_ref[0]
 
     def owner_step(owner, start):
-        place = ((owner & 15) * NY + (((owner >> 4) - y) & (NY - 1))) * SLOT_CAP
+        place = ((owner & (NZ - 1)) * NY + owner // NZ) * SLOT_CAP
         places_ref[start] = place
         places_ref[start + 1] = place + 1
         return start + counts_ref[0, owner]
@@ -254,10 +265,7 @@
     delta_half = kernel_call(
         turn_kernel, "turn", SHAPE(delta_value.shape[1:], BF16), [VMEM], VMEM
     )(delta_value)
-    delta_y = jnp.concatenate(
-        [delta_half] + [shift(delta_half, "y", -away) for away in range(1, NY)], axis=0
-    )
-    _, delta_y = lax.optimization_barrier((own, delta_y))
+    delta_y = spread(delta_half, "y").reshape(NY * SLOT_CAP, TILE, TILE)
     delta_all = lax.all_gather(delta_y, Z, axis=0, tiled=True)
 
     grads, turned = kernel_call(
@@ -272,32 +280,39 @@
         pltpu.SemaphoreType.DMA((2,)),
     ]
 
-    def terms(*aways):
-        return kernel_call(
-            functools.partial(tile_kernel, aways), "tiles",
-            [SHAPE((GROUP, TILE, TILE), BF16)] * len(aways), tile_ins, [VMEM] * len(aways),
-            tile_scratch, flops=2 * len(aways) * GROUP * TILE**3, moved=4 << 20,
-        )(ids, *lists, own, other, turned)
-
-    (far,) = terms(2)
-    far, turned = lax.optimization_barrier((far, turned))
-    far = shift(far, "y", 2)
-    up, down = terms(1, 3)
-    below = shift(up, "y", 1)
-    above = shift(down, "y", -1)
-    (mine,) = terms(0)
-    parted = (NM, 2, SLOT_CAP, TILE, TILE)
-    quarter = SHAPE((NM // 2, SLOT_CAP, TILE, TILE), BF16)
-    kept = SHAPE((NM, SLOT_CAP, TILE, TILE), BF16)
-    keep, low, high = kernel_call(
-        y_sum_kernel, "y_sum", [kept, quarter, quarter], [SMEM] + [VMEM] * 4, [VMEM] * 3
-    )(ids, *(value.reshape(parted) for value in (mine, below, above, far)))
-
-    low = shift(low, Z, 1)
-    high = shift(high, Z, -1)
-    pairs = kernel_call(pair_sum_kernel, "pair_sum", kept, [VMEM] * 3, VMEM)(keep, low, high)
-    pairs, grads = lax.optimization_barrier((pairs, grads))
-    arrived = exchange(pairs, "m")
+    def terms(turned, *parts):
+        *values, turned = lax.optimization_barrier((*kernel_call(
+            functools.partial(tile_kernel, parts), "tiles",
+            [SHAPE(((last - first) * SLOT_CAP, TILE, TILE), BF16) for _, (first, last) in parts],
+            tile_ins, [VMEM] * len(parts), tile_scratch,
+            flops=2 * tile_total * TILE**3 // 4, moved=2 << 20,
+        )(ids, *lists, own, other, turned), turned))
+        return values, turned
+
+    (far_low, far_high), turned = terms(turned, (2, LOW), (2, HIGH))
+    far_low, far_high = shift(far_low, "y", 1), shift(far_high, "y", -1)
+    (up_high, down_low), turned = terms(turned, (1, HIGH), (3, LOW))
+    below_high, above_low = shift(up_high, "y", 1), shift(down_low, "y", -1)
+    (up_low, down_high, mine), turned = terms(turned, (1, LOW), (3, HIGH), (0, (0, NZ)))
+    half = SHAPE(up_low.shape, BF16)
+    up_low, down_high = kernel_call(
+        passing_kernel, "passing", [half] * 2, [VMEM] * 4, [VMEM] * 2
+    )(up_low, far_low, down_high, far_high)
+    below_low, above_high = shift(up_low, "y", 1), shift(down_high, "y", -1)
+
+    def parted(value):
+        return value.reshape(-1, NC, SLOT_CAP, TILE, TILE)
+
+    four = SHAPE((NQ, SLOT_CAP, TILE, TILE), BF16)
+    two = SHAPE((NQ // 2, SLOT_CAP, TILE, TILE), BF16)
+    keep, up, down, up_two, down_two = kernel_call(
+        y_sum_kernel, "y_sum", [four, four, four, two, two], [SMEM] + [VMEM] * 5, [VMEM] * 5
+    )(ids, *map(parted, (mine, below_low, above_low, below_high, above_high)))
+
+    moved = [shift(up, Z, 1), shift(down, Z, -1), shift(up_two, Z, 2), shift(down_two, Z, -2)]
+    *moved, grads = lax.optimization_barrier((*moved, grads))
+    pairs = kernel_call(class_sum_kernel, "class_sum", four, [VMEM] * 5, VMEM)(keep, *moved)
+    arrived = exchange(pairs, "q")
     own_grad, squares = kernel_call(
         own_grad_kernel, "own_grad",
         [SHAPE((SLOT_CAP, TILE, TILE), F32), SHAPE((NY * NX * 2, 8, TILE), F32)],
@@ -306,9 +321,9 @@
 
     stay, give = kernel_call(
         contrib_kernel, "contribs", [SHAPE((tokens // 2, width), BF16)] * 2,
-        [SMEM] * 4 + [VMEM] * 2, [VMEM] * 2, [pltpu.SMEM((tile_total + 8,), jnp.int32)],
+        [SMEM] * 3 + [VMEM] * 2, [VMEM] * 2, [pltpu.SMEM((tile_total + 8,), jnp.int32)],
         moved=1 << 12,
-    )(ids, *lists, grads, delta_all)
+    )(*lists, grads, delta_all)
 
     rows = tokens // (2 * NX)
     taken = shift(give, "core", 1)
@@ -327,7 +342,7 @@
     )(gathered)
 
     squares = exchange(squares, ("y", "x", "core"))
-    squares = kernel_call(relay_kernel, "relay", SHAPE((2 * NM, 8, TILE), F32), [VMEM], VMEM)(squares)
+    squares = kernel_call(relay_kernel, "relay", SHAPE((NZ, 8, TILE), F32), [VMEM], VMEM)(squares)
     squares = exchange(squares, Z)
     squares, input_grad = lax.optimization_barrier((squares, input_grad))
     count_all = float(NX * 2 * tile_total * TILE * TILE)
@@ -342,8 +357,8 @@
 
 
 def solution(mesh):
-    grid = Mesh(mesh.devices.reshape(NY, NM, 2, NX, 2), ("y", "m", "p", "x", "core"))
-    dp, tensor = ("y", "m", "p"), ("x", "core")
+    grid = Mesh(mesh.devices.reshape(NY, NQ, NC, NX, 2), ("y", "q", "c", "x", "core"))
+    dp, tensor = ("y", "q", "c"), ("x", "core")
     tokens = P(dp, tensor)
     lists = P(tensor, None)
     slots = P(tensor, dp, None, None)

time: 203 us -> 200 us (0.985)
  waiting for transfers between devices: 71.5 us -> 40.8 us
  blocking collectives: 12.8 us -> 37.1 us
  starting transfers between devices: 75.8 us -> 81.2 us
  local copies, waits for them, and re-layouts: 5.77 us -> 3.66 us
    ppermute x13 -> x15, waiting for transfers between devices: 53.3 us -> 24.4 us  [shift(): lax.ppermute(value, axis, [(i, (i + step) % size) for i in range(size)])]
    all_to_all x1 -> x3, blocking collectives: 12.8 us -> 37.1 us  [exchange(): return lax.all_to_all(value, axis, split_axis=0, concat_axis=0, tiled=True)]
    ppermute x13 -> x15, starting transfers between devices: 51 us -> 59.5 us  [shift(): lax.ppermute(value, axis, [(i, (i + step) % size) for i in range(size)])]
    all_to_all x3 -> x2, starting transfers between devices: 24.8 us -> 21.7 us  [exchange(): return lax.all_to_all(value, axis, split_axis=0, concat_axis=0, tiled=True)]
    all_to_all x3 -> x2, waiting for transfers between devices: 11.1 us -> 9.31 us  [exchange(): return lax.all_to_all(value, axis, split_axis=0, concat_axis=0, tiled=True)]
    pallas_call x6 -> x7, Pallas kernels: 9.84 us -> 9.86 us  [the longest x3 7.19 us: terms(): kernel_call(functools.partial(tile_kernel, parts), 'tiles', [SHAPE(((last...]
  transfers between devices with their start and end apart: 18 -> 19, of which waited for: 11 -> 11; matrix products, arithmetic and copies ran while one was open for 0% -> 1% of each run, Pallas kernels for 9% -> 7%
where the time goes in v6:
time: 200 us; the launch traced here: 199 us
  starting transfers between devices  81.2 us (41%)
  waiting for transfers between devices  40.8 us (20%)
  blocking collectives  37.1 us (19%)
  Pallas kernels  21.2 us (11%)
  between operations  14.4 us (7%)
  local copies, waits for them, and re-layouts  3.66 us (2%)
    ppermute x15, starting transfers between devices, shift(): lax.ppermute(value, axis, [(i, (i + step) % size) for i in range(size)])  59.5 us
    all_to_all x3, blocking collectives, exchange(): return lax.all_to_all(value, axis, split_axis=0, concat_axis=0, tiled=True)  37.1 us
    ppermute x15, waiting for transfers between devices, shift(): lax.ppermute(value, axis, [(i, (i + step) % size) for i in range(size)])  24.4 us
    all_to_all x2, starting transfers between devices, exchange(): return lax.all_to_all(value, axis, split_axis=0, concat_axis=0, tiled=True)  21.7 us
    all_to_all x2, waiting for transfers between devices, exchange(): return lax.all_to_all(value, axis, split_axis=0, concat_axis=0, tiled=True)  9.31 us
    pallas_call x3, Pallas kernels, terms(): kernel_call(functools.partial(tile_kernel, parts), 'tiles', [SHAPE(((last...  7.19 us
    all_gather x1, waiting for transfers between devices, body(): gathered = lax.all_gather(share, ('x', 'core'), axis=0, tiled=True)  7.08 us
    pallas_call x1, Pallas kernels, body(): kernel_call(contrib_kernel, 'contribs', [SHAPE((tokens // 2, width), BF16...  5.8 us
  transfers between devices with their start and end apart: 19, of which 11 were waited for; matrix products, arithmetic and copies ran while one was open for 1% of the time, Pallas kernels for 7%

profile of v6, /device:TPU:1, one launch (start us, length us, event | category | flops | bytes accessed | tf_op | source)
XLA Modules:
  0.0 199.3 jit_solution(1420040408831709116)
XLA Ops:
  7.2 0.0 all-gather.3.cloned.1.call-start
  7.2 0.0 copy-start.1
  7.2 0.9 copy-done.1
  8.1 0.1 turn.1
  8.3 0.0 copy-start.3
  8.3 0.0 copy-start.4
  8.3 0.0 copy-start.5
  8.3 10.6 %all_to_all.25 = bf16[4,2,128,128]{3,2,1,0:T(8,128)(2,1)} all-to-all(bf16[4,2,128,128]{3,2,1,0:T(8,128)(2,1)S(1)} %broadcast_in_dim.5), channel_id=1, replica_groups=mesh['y'=4,'q'=4,'c'=4,'x'=4,'core'=2] {'y'}, dimensions={0} | all-to-all | bytes 524288 | tf_op jit(solution)/shard_map/all_to_all | solution.py:42
  18.9 0.0 all-gather.3.cloned.1.call-update
  18.9 0.0 copy-start.10
  18.9 0.0 copy-start.11
  18.9 0.0 copy-start.12
  18.9 1.1 broadcast_in_dim.4
  20.0 13.9 %all_to_all.26.own_ref = bf16[4,128,1024]{2,1,0:T(8,128)(2,1)S(1)} all-to-all(bf16[4,128,1024]{2,1,0:T(8,128)(2,1)S(1)} %broadcast_in_dim.4), channel_id=1, replica_groups=mesh['y'=4,'q'=4,'c'=4,'x'=4,'core'=2] {'x'}, dimensions={0} | all-to-all | bytes 2097152 | tf_op jit(solution)/shard_map/all_to_all | solution.py:42
  34.0 7.9 %collective-permute-start = (bf16[4,128,1024]{2,1,0:T(8,128)(2,1)S(1)}, bf16[4,128,1024]{2,1,0:T(8,128)(2,1)S(1)}, u32[]{:S(2)}, u32[]{:S(2)}) collective-permute-start(bf16[4,128,1024]{2,1,0:T(8,128)(2,1)S(1)} %all_to_all.26.own_ref), channel_id=1, source_target_pairs={{0,1},{1,0},{2,3},{3,2},{4,5},{5,4},{6,7},{7,6},{8,9},{9,8},{10,11... | collective-permute-start | bytes 3145736 | tf_op jit(solution)/shard_map/ppermute | solution.py:38
  41.8 0.1 pad_add_fusion.ids_ref.refs_0_
  41.9 1.1 gate.1
  43.1 1.0 collective-permute-done.other_ref
  44.1 2.1 %tiles.3 = (bf16[16,128,128]{2,1,0:T(8,128)(2,1)S(1)}, bf16[16,128,128]{2,1,0:T(8,128)(2,1)S(1)}) custom-call(s32[4]{0:T(128)S(1)} %pad_add_fusion.ids_ref.refs_0_, s32[1,112]{1,0:T(1,128)S(1)} %copy-done.11, s32[1,112]{1,0:T(1,128)S(1)} %copy-done.12, s32[1,64]{1,0:T(1,128)S(1)} %copy-done.10, bf16[4,128,1024]{2,1,0:T(8,128)(2,1)S(1)} %all_to_all.26.own_ref, ...), custom_call_target="tpu_custom_call" | custom-call | flops 117440512 | bytes 2097152 | tf_op jit(solution)/shard_map/tiles/pallas_call | solution.py:284
  46.2 2.3 %collective-permute-start.1 = (bf16[16,128,128]{2,1,0:T(8,128)(2,1)S(1)}, bf16[16,128,128]{2,1,0:T(8,128)(2,1)S(1)}, u32[]{:S(2)}, u32[]{:S(2)}) collective-permute-start(bf16[16,128,128]{2,1,0:T(8,128)(2,1)S(1)} %get-tuple-element.61), channel_id=1, source_target_pairs={{0,128},{128,256},{256,384},{384,0},{1,129},{129,257},{257,385},{3... | collective-permute-start | bytes 1572872 | tf_op jit(solution)/shard_map/ppermute | solution.py:38
  48.5 4.2 %collective-permute-start.2 = (bf16[16,128,128]{2,1,0:T(8,128)(2,1)S(1)}, bf16[16,128,128]{2,1,0:T(8,128)(2,1)S(1)}, u32[]{:S(2)}, u32[]{:S(2)}) collective-permute-start(bf16[16,128,128]{2,1,0:T(8,128)(2,1)S(1)} %get-tuple-element.63), channel_id=1, source_target_pairs={{0,384},{128,0},{256,128},{384,256},{1,385},{129,1},{257,129},{385... | collective-permute-start | bytes 1572872 | tf_op jit(solution)/shard_map/ppermute | solution.py:38
  52.7 2.1 %tiles.4 = (bf16[16,128,128]{2,1,0:T(8,128)(2,1)S(1)}, bf16[16,128,128]{2,1,0:T(8,128)(2,1)S(1)}) custom-call(s32[4]{0:T(128)S(1)} %pad_add_fusion.ids_ref.refs_0_, s32[1,112]{1,0:T(1,128)S(1)} %copy-done.11, s32[1,112]{1,0:T(1,128)S(1)} %copy-done.12, s32[1,64]{1,0:T(1,128)S(1)} %copy-done.10, bf16[4,128,1024]{2,1,0:T(8,128)(2,1)S(1)} %all_to_all.26.own_ref, ...), custom_call_target="tpu_custom_call" | custom-call | flops 117440512 | bytes 2097152 | tf_op jit(solution)/shard_map/tiles/pallas_call | solution.py:284
  54.8 3.1 %tiles.5 = (bf16[16,128,128]{2,1,0:T(8,128)(2,1)S(1)}, bf16[16,128,128]{2,1,0:T(8,128)(2,1)S(1)}, bf16[32,128,128]{2,1,0:T(8,128)(2,1)S(1)}) custom-call(s32[4]{0:T(128)S(1)} %pad_add_fusion.ids_ref.refs_0_, s32[1,112]{1,0:T(1,128)S(1)} %copy-done.11, s32[1,112]{1,0:T(1,128)S(1)} %copy-done.12, s32[1,64]{1,0:T(1,128)S(1)} %copy-done.10, ...), custom_call_target="tpu_custom_call" | custom-call | flops 117440512 | bytes 2097152 | tf_op jit(solution)/shard_map/tiles/pallas_call | solution.py:284
  57.8 1.9 collective-permute-start.4
  59.8 3.4 %collective-permute-start.5 = (bf16[16,128,128]{2,1,0:T(8,128)(2,1)S(1)}, bf16[16,128,128]{2,1,0:T(8,128)(2,1)S(1)}, u32[]{:S(2)}, u32[]{:S(2)}) collective-permute-start(bf16[16,128,128]{2,1,0:T(8,128)(2,1)S(1)} %get-tuple-element.66), channel_id=1, source_target_pairs={{0,128},{128,256},{256,384},{384,0},{1,129},{129,257},{257,385},{3... | collective-permute-start | bytes 1572872 | tf_op jit(solution)/shard_map/ppermute | solution.py:38
  63.1 0.0 collective-permute-done.1.far_low_ref
  63.1 0.1 collective-permute-done.2.far_high_ref
  63.3 0.2 passing.1
  63.5 0.0 copy-start.7
  63.5 2.1 %collective-permute-start.3 = (bf16[16,128,128]{2,1,0:T(8,128)(2,1)S(1)}, bf16[16,128,128]{2,1,0:T(8,128)(2,1)S(1)}, u32[]{:S(2)}, u32[]{:S(2)}) collective-permute-start(bf16[16,128,128]{2,1,0:T(8,128)(2,1)S(1)} %get-tuple-element.64), channel_id=1, source_target_pairs={{0,128},{128,256},{256,384},{384,0},{1,129},{129,257},{257,385},{3... | collective-permute-start | bytes 1572872 | tf_op jit(solution)/shard_map/ppermute | solution.py:38
  65.7 5.2 %collective-permute-start.6 = (bf16[16,128,128]{2,1,0:T(8,128)(2,1)S(1)}, bf16[16,128,128]{2,1,0:T(8,128)(2,1)S(1)}, u32[]{:S(2)}, u32[]{:S(2)}) collective-permute-start(bf16[16,128,128]{2,1,0:T(8,128)(2,1)S(1)} %get-tuple-element.67), channel_id=1, source_target_pairs={{0,384},{128,0},{256,128},{384,256},{1,385},{129,1},{257,129},{385... | collective-permute-start | bytes 1572872 | tf_op jit(solution)/shard_map/ppermute | solution.py:38
  70.9 3.6 %collective-permute-done.4 = bf16[16,128,128]{2,1,0:T(8,128)(2,1)S(1)} collective-permute-done((bf16[16,128,128]{2,1,0:T(8,128)(2,1)S(1)}, bf16[16,128,128]{2,1,0:T(8,128)(2,1)S(1)}, u32[]{:S(2)}, u32[]{:S(2)}) %collective-permute-start.4) | collective-permute-done | bytes 524320 | tf_op jit(solution)/shard_map/ppermute | solution.py:38
  74.5 0.9 collective-permute-done.5
  75.5 11.2 %collective-permute-done.3 = bf16[16,128,128]{2,1,0:T(8,128)(2,1)S(1)} collective-permute-done((bf16[16,128,128]{2,1,0:T(8,128)(2,1)S(1)}, bf16[16,128,128]{2,1,0:T(8,128)(2,1)S(1)}, u32[]{:S(2)}, u32[]{:S(2)}) %collective-permute-start.3) | collective-permute-done | bytes 524320 | tf_op jit(solution)/shard_map/ppermute | solution.py:38
  86.7 0.0 collective-permute-done.6
  86.7 0.9 y_sum.1
  87.6 3.4 %collective-permute-start.7 = (bf16[4,2,128,128]{3,2,1,0:T(8,128)(2,1)S(1)}, bf16[4,2,128,128]{3,2,1,0:T(8,128)(2,1)S(1)}, u32[]{:S(2)}, u32[]{:S(2)}) collective-permute-start(bf16[4,2,128,128]{3,2,1,0:T(8,128)(2,1)S(1)} %get-tuple-element.69), channel_id=1, source_target_pairs={{0,8},{8,16},{16,24},{24,32},{32,40},{40,48},{48,56},{56,64},{64,7... | collective-permute-start | bytes 786440 | tf_op jit(solution)/shard_map/ppermute | solution.py:38
  91.1 9.5 %collective-permute-start.8 = (bf16[4,2,128,128]{3,2,1,0:T(8,128)(2,1)S(1)}, bf16[4,2,128,128]{3,2,1,0:T(8,128)(2,1)S(1)}, u32[]{:S(2)}, u32[]{:S(2)}) collective-permute-start(bf16[4,2,128,128]{3,2,1,0:T(8,128)(2,1)S(1)} %get-tuple-element.70), channel_id=1, source_target_pairs={{0,120},{8,0},{16,8},{24,16},{32,24},{40,32},{48,40},{56,48},{64,5... | collective-permute-start | bytes 786440 | tf_op jit(solution)/shard_map/ppermute | solution.py:38
  100.6 1.9 collective-permute-start.9
  102.5 5.5 %collective-permute-start.10 = (bf16[2,2,128,128]{3,2,1,0:T(8,128)(2,1)S(1)}, bf16[2,2,128,128]{3,2,1,0:T(8,128)(2,1)S(1)}, u32[]{:S(2)}, u32[]{:S(2)}) collective-permute-start(bf16[2,2,128,128]{3,2,1,0:T(8,128)(2,1)S(1)} %get-tuple-element.72), channel_id=1, source_target_pairs={{0,112},{8,120},{16,0},{24,8},{32,16},{40,24},{48,32},{56,40},{64,... | collective-permute-start | bytes 393224 | tf_op jit(solution)/shard_map/ppermute | solution.py:38
  108.0 1.0 collective-permute-done.9.low_ref
  109.0 2.9 %collective-permute-done.10.high_ref = bf16[2,2,128,128]{3,2,1,0:T(8,128)(2,1)S(1)} collective-permute-done((bf16[2,2,128,128]{3,2,1,0:T(8,128)(2,1)S(1)}, bf16[2,2,128,128]{3,2,1,0:T(8,128)(2,1)S(1)}, u32[]{:S(2)}, u32[]{:S(2)}) %collective-permute-start.10) | collective-permute-done | bytes 131104 | tf_op jit(solution)/shard_map/ppermute | solution.py:38
  111.9 0.0 collective-permute-done.7.one_ref
  111.9 5.8 %contribs.1 = (bf16[64,8192]{1,0:T(8,128)(2,1)S(1)}, bf16[64,8192]{1,0:T(8,128)(2,1)}) custom-call(s32[1,112]{1,0:T(1,128)S(1)} %copy-done.11, s32[1,112]{1,0:T(1,128)S(1)} %copy-done.12, s32[1,64]{1,0:T(1,128)S(1)} %copy-done.10, bf16[14,128,128]{2,1,0:T(8,128)(2,1)S(1)} %copy-done.7, bf16[128,128,128]{2,1,0:T(8,128)(2,1)} %all-gather.3.cloned.1.call-done.delta_ref), custom_call_target="tpu_custom_call" | custom-call | bytes 4096 | tf_op jit(solution)/shard_map/contribs/pallas_call | solution.py:322
  117.7 4.4 %collective-permute-start.11 = (bf16[64,8192]{1,0:T(8,128)(2,1)}, bf16[64,8192]{1,0:T(8,128)(2,1)S(1)}, u32[]{:S(2)}, u32[]{:S(2)}) collective-permute-start(bf16[64,8192]{1,0:T(8,128)(2,1)} %get-tuple-element.81), channel_id=1, source_target_pairs={{0,1},{1,0},{2,3},{3,2},{4,5},{5,4},{6,7},{7,6},{8,9},{9,8},{10,11... | collective-permute-start | bytes 3145736 | tf_op jit(solution)/shard_map/ppermute | solution.py:38
  122.1 0.8 class_sum.1
  122.9 8.6 %all-to-all-start.1 = ((bf16[4,2,128,128]{3,2,1,0:T(8,128)(2,1)}), bf16[4,2,128,128]{3,2,1,0:T(8,128)(2,1)S(1)}, u32[]{:S(2)}, u32[]{:S(2)}) async-start(bf16[4,2,128,128]{3,2,1,0:T(8,128)(2,1)} %class_sum.1), calls=%async_computation.1 | async-start | bytes 524288 | tf_op jit(solution)/shard_map/all_to_all | solution.py:42
  131.5 0.8 core_sum.1
  132.3 2.6 %collective-permute-start.14 = (bf16[16,8192]{1,0:T(8,128)(2,1)S(1)}, bf16[16,8192]{1,0:T(8,128)(2,1)S(1)}, u32[]{:S(2)}, u32[]{:S(2)}) collective-permute-start(bf16[16,8192]{1,0:T(8,128)(2,1)S(1)} %get-tuple-element.85), channel_id=1, source_target_pairs={{0,6},{2,0},{4,2},{6,4},{1,7},{3,1},{5,3},{7,5},{8,14},{10,8},{12,... | collective-permute-start | bytes 786440 | tf_op jit(solution)/shard_map/ppermute | solution.py:38
  134.9 3.3 %collective-permute-start.13 = (bf16[16,8192]{1,0:T(8,128)(2,1)S(1)}, bf16[16,8192]{1,0:T(8,128)(2,1)S(1)}, u32[]{:S(2)}, u32[]{:S(2)}) collective-permute-start(bf16[16,8192]{1,0:T(8,128)(2,1)S(1)} %get-tuple-element.84), channel_id=1, source_target_pairs={{0,4},{2,6},{4,0},{6,2},{1,5},{3,7},{5,1},{7,3},{8,12},{10,14},{12... | collective-permute-start | bytes 786440 | tf_op jit(solution)/shard_map/ppermute | solution.py:38
  138.2 1.9 collective-permute-start.12
  140.1 7.7 %all-to-all-done.1.arrived_ref = bf16[4,2,128,128]{3,2,1,0:T(8,128)(2,1)S(1)} async-done(((bf16[4,2,128,128]{3,2,1,0:T(8,128)(2,1)}), bf16[4,2,128,128]{3,2,1,0:T(8,128)(2,1)S(1)}, u32[]{:S(2)}, u32[]{:S(2)}) %all-to-all-start.1) | async-done | bytes 262176 | tf_op jit(solution)/shard_map/all_to_all | solution.py:42
  147.8 0.7 own_grad.1
  148.6 3.5 %collective-permute-done.12 = bf16[16,8192]{1,0:T(8,128)(2,1)S(1)} collective-permute-done((bf16[16,8192]{1,0:T(8,128)(2,1)S(1)}, bf16[16,8192]{1,0:T(8,128)(2,1)S(1)}, u32[]{:S(2)}, u32[]{:S(2)}) %collective-permute-start.12) | collective-permute-done | bytes 262176 | tf_op jit(solution)/shard_map/ppermute | solution.py:38
  152.1 0.8 add_convert_fusion
  152.9 0.0 all-gather.5.cloned.1.call-update
  153.0 12.6 %all_to_all.27.arrived_ref = f32[32,8,128]{2,1,0:T(8,128)S(1)} all-to-all(f32[32,8,128]{2,1,0:T(8,128)S(1)} %get-tuple-element.86), channel_id=1, replica_groups=mesh['y'=4,'q'=4,'c'=4,'x'=4,'core'=2] {'y','x','core'}, dimensions={0} | all-to-all | bytes 262144 | tf_op jit(solution)/shard_map/all_to_all | solution.py:42
  165.5 0.7 relay.1
  166.2 13.1 %all-to-all-start.4 = ((f32[16,8,128]{2,1,0:T(8,128)}), f32[16,8,128]{2,1,0:T(8,128)S(1)}, u32[]{:S(2)}, u32[]{:S(2)}) async-start(f32[16,8,128]{2,1,0:T(8,128)} %relay.1), calls=%async_computation.4 | async-start | bytes 131072 | tf_op jit(solution)/shard_map/all_to_all | solution.py:42
  179.4 7.1 %all-gather.5.cloned.1.call-done.in_ref = bf16[128,8192]{1,0:T(8,128)(2,1)} async-done(((bf16[16,8192]{1,0:T(8,128)(2,1)}), bf16[128,8192]{1,0:T(8,128)(2,1)}) %all-gather.5.cloned.1.call-update) | async-done | bytes 2097168 | tf_op jit(solution)/shard_map/all_gather | solution.py:338
  186.4 1.6 copy-done
  188.0 1.3 result.1
  189.4 1.6 all-to-all-done.4.refs_2_
  191.0 1.5 adam.1
  (23 shorter events, 0.1 us)
Async XLA Ops:
  7.2 104.7 %all-gather.3.cloned.1.call-start = ((), (), s32[]{:S(2)}) async-start(), calls=%async_computation.5 | async-start | bytes 4456448 | tf_op jit(solution)/shard_map/all_gather | solution.py:269
  7.2 0.9 copy-start.1
  8.3 33.7 %copy-start.3 = (bf16[128,1792]{1,0:T(8,128)(2,1)S(1)}, bf16[128,1792]{1,0:T(8,128)(2,1)}, u32[]{:S(2)}) copy-start(bf16[128,1792]{1,0:T(8,128)(2,1)} %gate_ref.1) | copy-start | bytes 1376260
  8.3 33.6 %copy-start.4 = (bf16[128,1792]{1,0:T(8,128)(2,1)S(1)}, bf16[128,1792]{1,0:T(8,128)(2,1)}, u32[]{:S(2)}) copy-start(bf16[128,1792]{1,0:T(8,128)(2,1)} %up_ref.1) | copy-start | bytes 1376260
  8.3 33.6 %copy-start.5 = (bf16[128,1792]{1,0:T(8,128)(2,1)S(1)}, bf16[128,1792]{1,0:T(8,128)(2,1)}, u32[]{:S(2)}) copy-start(bf16[128,1792]{1,0:T(8,128)(2,1)} %hidden_ref.1) | copy-start | bytes 1376260
  18.9 25.2 %copy-start.10 = (s32[1,64]{1,0:T(1,128)S(1)}, s32[1,64]{1,0:T(1,128)}, u32[]{:S(2)}) copy-start(s32[1,64]{1,0:T(1,128)} %refs_1_.1) | copy-start | bytes 772
  18.9 25.2 %copy-start.11 = (s32[1,112]{1,0:T(1,128)S(1)}, s32[1,112]{1,0:T(1,128)}, u32[]{:S(2)}) copy-start(s32[1,112]{1,0:T(1,128)} %rows_ref.7) | copy-start | bytes 1348
  18.9 25.2 %copy-start.12 = (s32[1,112]{1,0:T(1,128)S(1)}, s32[1,112]{1,0:T(1,128)}, u32[]{:S(2)}) copy-start(s32[1,112]{1,0:T(1,128)} %cols_ref.7) | copy-start | bytes 1348
  34.0 10.1 %collective-permute-start = (bf16[4,128,1024]{2,1,0:T(8,128)(2,1)S(1)}, bf16[4,128,1024]{2,1,0:T(8,128)(2,1)S(1)}, u32[]{:S(2)}, u32[]{:S(2)}) collective-permute-start(bf16[4,128,1024]{2,1,0:T(8,128)(2,1)S(1)} %all_to_all.26.own_ref), channel_id=1, source_target_pairs={{0,1},{1,0},{2,3},{3,2},{4,5},{5,4},{6,7},{7,6},{8,9},{9,8},{10,11... | collective-permute-start | bytes 3145736 | tf_op jit(solution)/shard_map/ppermute | solution.py:38
  43.0 11.7 %copy-start.6 = (bf16[14,128,128]{2,1,0:T(8,128)(2,1)}, bf16[14,128,128]{2,1,0:T(8,128)(2,1)S(1)}, u32[]{:S(2)}) copy-start(bf16[14,128,128]{2,1,0:T(8,128)(2,1)S(1)} %get-tuple-element.79.grad_ref) | copy-start | bytes 1376260
  46.2 17.0 %collective-permute-start.1 = (bf16[16,128,128]{2,1,0:T(8,128)(2,1)S(1)}, bf16[16,128,128]{2,1,0:T(8,128)(2,1)S(1)}, u32[]{:S(2)}, u32[]{:S(2)}) collective-permute-start(bf16[16,128,128]{2,1,0:T(8,128)(2,1)S(1)} %get-tuple-element.61), channel_id=1, source_target_pairs={{0,128},{128,256},{256,384},{384,0},{1,129},{129,257},{257,385},{3... | collective-permute-start | bytes 1572872 | tf_op jit(solution)/shard_map/ppermute | solution.py:38
  48.5 14.8 %collective-permute-start.2 = (bf16[16,128,128]{2,1,0:T(8,128)(2,1)S(1)}, bf16[16,128,128]{2,1,0:T(8,128)(2,1)S(1)}, u32[]{:S(2)}, u32[]{:S(2)}) collective-permute-start(bf16[16,128,128]{2,1,0:T(8,128)(2,1)S(1)} %get-tuple-element.63), channel_id=1, source_target_pairs={{0,384},{128,0},{256,128},{384,256},{1,385},{129,1},{257,129},{385... | collective-permute-start | bytes 1572872 | tf_op jit(solution)/shard_map/ppermute | solution.py:38
  57.8 16.7 %collective-permute-start.4 = (bf16[16,128,128]{2,1,0:T(8,128)(2,1)S(1)}, bf16[16,128,128]{2,1,0:T(8,128)(2,1)S(1)}, u32[]{:S(2)}, u32[]{:S(2)}) collective-permute-start(bf16[16,128,128]{2,1,0:T(8,128)(2,1)S(1)} %get-tuple-element.65), channel_id=1, source_target_pairs={{0,384},{128,0},{256,128},{384,256},{1,385},{129,1},{257,129},{385... | collective-permute-start | bytes 1572872 | tf_op jit(solution)/shard_map/ppermute | solution.py:38
  59.8 15.7 %collective-permute-start.5 = (bf16[16,128,128]{2,1,0:T(8,128)(2,1)S(1)}, bf16[16,128,128]{2,1,0:T(8,128)(2,1)S(1)}, u32[]{:S(2)}, u32[]{:S(2)}) collective-permute-start(bf16[16,128,128]{2,1,0:T(8,128)(2,1)S(1)} %get-tuple-element.66), channel_id=1, source_target_pairs={{0,128},{128,256},{256,384},{384,0},{1,129},{129,257},{257,385},{3... | collective-permute-start | bytes 1572872 | tf_op jit(solution)/shard_map/ppermute | solution.py:38
  63.5 48.3 %copy-start.7 = (bf16[14,128,128]{2,1,0:T(8,128)(2,1)S(1)}, bf16[14,128,128]{2,1,0:T(8,128)(2,1)}, u32[]{:S(2)}) copy-start(bf16[14,128,128]{2,1,0:T(8,128)(2,1)} %copy-done.6) | copy-start | bytes 1376260
  63.5 23.2 %collective-permute-start.3 = (bf16[16,128,128]{2,1,0:T(8,128)(2,1)S(1)}, bf16[16,128,128]{2,1,0:T(8,128)(2,1)S(1)}, u32[]{:S(2)}, u32[]{:S(2)}) collective-permute-start(bf16[16,128,128]{2,1,0:T(8,128)(2,1)S(1)} %get-tuple-element.64), channel_id=1, source_target_pairs={{0,128},{128,256},{256,384},{384,0},{1,129},{129,257},{257,385},{3... | collective-permute-start | bytes 1572872 | tf_op jit(solution)/shard_map/ppermute | solution.py:38
  65.7 21.0 %collective-permute-start.6 = (bf16[16,128,128]{2,1,0:T(8,128)(2,1)S(1)}, bf16[16,128,128]{2,1,0:T(8,128)(2,1)S(1)}, u32[]{:S(2)}, u32[]{:S(2)}) collective-permute-start(bf16[16,128,128]{2,1,0:T(8,128)(2,1)S(1)} %get-tuple-element.67), channel_id=1, source_target_pairs={{0,384},{128,0},{256,128},{384,256},{1,385},{129,1},{257,129},{385... | collective-permute-start | bytes 1572872 | tf_op jit(solution)/shard_map/ppermute | solution.py:38
  87.6 24.2 %collective-permute-start.7 = (bf16[4,2,128,128]{3,2,1,0:T(8,128)(2,1)S(1)}, bf16[4,2,128,128]{3,2,1,0:T(8,128)(2,1)S(1)}, u32[]{:S(2)}, u32[]{:S(2)}) collective-permute-start(bf16[4,2,128,128]{3,2,1,0:T(8,128)(2,1)S(1)} %get-tuple-element.69), channel_id=1, source_target_pairs={{0,8},{8,16},{16,24},{24,32},{32,40},{40,48},{48,56},{56,64},{64,7... | collective-permute-start | bytes 786440 | tf_op jit(solution)/shard_map/ppermute | solution.py:38
  91.1 20.8 %collective-permute-start.8 = (bf16[4,2,128,128]{3,2,1,0:T(8,128)(2,1)S(1)}, bf16[4,2,128,128]{3,2,1,0:T(8,128)(2,1)S(1)}, u32[]{:S(2)}, u32[]{:S(2)}) collective-permute-start(bf16[4,2,128,128]{3,2,1,0:T(8,128)(2,1)S(1)} %get-tuple-element.70), channel_id=1, source_target_pairs={{0,120},{8,0},{16,8},{24,16},{32,24},{40,32},{48,40},{56,48},{64,5... | collective-permute-start | bytes 786440 | tf_op jit(solution)/shard_map/ppermute | solution.py:38
  100.6 8.4 %collective-permute-start.9 = (bf16[2,2,128,128]{3,2,1,0:T(8,128)(2,1)S(1)}, bf16[2,2,128,128]{3,2,1,0:T(8,128)(2,1)S(1)}, u32[]{:S(2)}, u32[]{:S(2)}) collective-permute-start(bf16[2,2,128,128]{3,2,1,0:T(8,128)(2,1)S(1)} %get-tuple-element.71), channel_id=1, source_target_pairs={{0,16},{8,24},{16,32},{24,40},{32,48},{40,56},{48,64},{56,72},{64,... | collective-permute-start | bytes 393224 | tf_op jit(solution)/shard_map/ppermute | solution.py:38
  102.5 9.4 %collective-permute-start.10 = (bf16[2,2,128,128]{3,2,1,0:T(8,128)(2,1)S(1)}, bf16[2,2,128,128]{3,2,1,0:T(8,128)(2,1)S(1)}, u32[]{:S(2)}, u32[]{:S(2)}) collective-permute-start(bf16[2,2,128,128]{3,2,1,0:T(8,128)(2,1)S(1)} %get-tuple-element.72), channel_id=1, source_target_pairs={{0,112},{8,120},{16,0},{24,8},{32,16},{40,24},{48,32},{56,40},{64,... | collective-permute-start | bytes 393224 | tf_op jit(solution)/shard_map/ppermute | solution.py:38
  117.7 13.8 %collective-permute-start.11 = (bf16[64,8192]{1,0:T(8,128)(2,1)}, bf16[64,8192]{1,0:T(8,128)(2,1)S(1)}, u32[]{:S(2)}, u32[]{:S(2)}) collective-permute-start(bf16[64,8192]{1,0:T(8,128)(2,1)} %get-tuple-element.81), channel_id=1, source_target_pairs={{0,1},{1,0},{2,3},{3,2},{4,5},{5,4},{6,7},{7,6},{8,9},{9,8},{10,11... | collective-permute-start | bytes 3145736 | tf_op jit(solution)/shard_map/ppermute | solution.py:38
  122.9 24.9 %all-to-all-start.1 = ((bf16[4,2,128,128]{3,2,1,0:T(8,128)(2,1)}), bf16[4,2,128,128]{3,2,1,0:T(8,128)(2,1)S(1)}, u32[]{:S(2)}, u32[]{:S(2)}) async-start(bf16[4,2,128,128]{3,2,1,0:T(8,128)(2,1)} %class_sum.1), calls=%async_computation.1 | async-start | bytes 524288 | tf_op jit(solution)/shard_map/all_to_all | solution.py:42
  131.5 55.0 %all-gather.5.cloned.1.call-start = ((), (), s32[]{:S(2)}) async-start(), calls=%async_computation.6 | async-start | bytes 2359296 | tf_op jit(solution)/shard_map/all_gather | solution.py:338
  132.3 16.3 %collective-permute-start.14 = (bf16[16,8192]{1,0:T(8,128)(2,1)S(1)}, bf16[16,8192]{1,0:T(8,128)(2,1)S(1)}, u32[]{:S(2)}, u32[]{:S(2)}) collective-permute-start(bf16[16,8192]{1,0:T(8,128)(2,1)S(1)} %get-tuple-element.85), channel_id=1, source_target_pairs={{0,6},{2,0},{4,2},{6,4},{1,7},{3,1},{5,3},{7,5},{8,14},{10,8},{12,... | collective-permute-start | bytes 786440 | tf_op jit(solution)/shard_map/ppermute | solution.py:38
  134.9 13.7 %collective-permute-start.13 = (bf16[16,8192]{1,0:T(8,128)(2,1)S(1)}, bf16[16,8192]{1,0:T(8,128)(2,1)S(1)}, u32[]{:S(2)}, u32[]{:S(2)}) collective-permute-start(bf16[16,8192]{1,0:T(8,128)(2,1)S(1)} %get-tuple-element.84), channel_id=1, source_target_pairs={{0,4},{2,6},{4,0},{6,2},{1,5},{3,7},{5,1},{7,3},{8,12},{10,14},{12... | collective-permute-start | bytes 786440 | tf_op jit(solution)/shard_map/ppermute | solution.py:38
  138.2 13.9 %collective-permute-start.12 = (bf16[16,8192]{1,0:T(8,128)(2,1)S(1)}, bf16[16,8192]{1,0:T(8,128)(2,1)S(1)}, u32[]{:S(2)}, u32[]{:S(2)}) collective-permute-start(bf16[16,8192]{1,0:T(8,128)(2,1)S(1)} %get-tuple-element.83), channel_id=1, source_target_pairs={{0,2},{2,4},{4,6},{6,0},{1,3},{3,5},{5,7},{7,1},{8,10},{10,12},{12... | collective-permute-start | bytes 786440 | tf_op jit(solution)/shard_map/ppermute | solution.py:38
  166.2 24.7 %all-to-all-start.4 = ((f32[16,8,128]{2,1,0:T(8,128)}), f32[16,8,128]{2,1,0:T(8,128)S(1)}, u32[]{:S(2)}, u32[]{:S(2)}) async-start(f32[16,8,128]{2,1,0:T(8,128)} %relay.1), calls=%async_computation.4 | async-start | bytes 131072 | tf_op jit(solution)/shard_map/all_to_all | solution.py:42
  186.4 1.6 copy-start
  188.0 2.9 %copy-start.2 = (f32[1,2,128,128]{3,2,1,0:T(8,128)S(1)}, f32[1,2,128,128]{3,2,1,0:T(8,128)}, u32[]{:S(2)}) copy-start(f32[1,2,128,128]{3,2,1,0:T(8,128)} %refs_4_.1) | copy-start | bytes 393220
  188.0 2.9 %copy-start.8 = (f32[1,2,128,128]{3,2,1,0:T(8,128)S(1)}, f32[1,2,128,128]{3,2,1,0:T(8,128)}, u32[]{:S(2)}) copy-start(f32[1,2,128,128]{3,2,1,0:T(8,128)} %refs_5_.1) | copy-start | bytes 393220
  188.0 2.9 %copy-start.9 = (f32[1,2,128,128]{3,2,1,0:T(8,128)S(1)}, f32[1,2,128,128]{3,2,1,0:T(8,128)}, u32[]{:S(2)}) copy-start(f32[1,2,128,128]{3,2,1,0:T(8,128)} %refs_6_.1) | copy-start | bytes 393220
Sparse Core Ops, SparseCore 0:
  19.0 73.7 all-gather.2
  153.1 33.3 all-gather.4

commit v7 on v6

--- a/solution.py
+++ b/solution.py
@@ -7,9 +7,9 @@
 from jax.experimental.pallas import tpu as pltpu
 from jax.sharding import Mesh, PartitionSpec as P
 
-NY, NQ, NC, NX = 4, 4, 4, 4
-NZ = NQ * NC
-Z = ("q", "c")
+NY, NZ, NX = 4, 16, 4
+NM = NZ // 2
+Z = ("q", "d", "p")
 TILE = 128
 SLOT_CAP = 2
 LOW, HIGH = (0, NZ // 2), (NZ // 2, NZ)
@@ -127,33 +127,28 @@
 
 def y_sum_kernel(
     ids_ref, mine_ref, below_low_ref, above_low_ref, below_high_ref, above_high_ref,
-    keep_ref, up_ref, down_ref, up_two_ref, down_two_ref,
-):
-    mine_class = ids_ref[1] & (NC - 1)
-    half = NQ // 2
-    for q in range(NQ):
-        below, above = (below_low_ref, above_low_ref) if q < half else (below_high_ref, above_high_ref)
-
-        def total(step):
-            side = (mine_class + step) & (NC - 1)
+    keep_ref, low_ref, high_ref,
+):
+    parity = ids_ref[1] & 1
+    half = NM // 2
+    for m in range(NM):
+        below, above = (below_low_ref, above_low_ref) if m < half else (below_high_ref, above_high_ref)
+
+        def total(side):
             return (
-                mine_ref[q, side].astype(F32)
-                + below[q % half, side].astype(F32)
-                + above[q % half, side].astype(F32)
+                mine_ref[m, side].astype(F32)
+                + below[m % half, side].astype(F32)
+                + above[m % half, side].astype(F32)
             ).astype(BF16)
 
-        keep_ref[q] = total(0)
-        up_ref[q] = total(1)
-        down_ref[q] = total(3)
-        (up_two_ref if q < half else down_two_ref)[q % half] = total(2)
-
-
-def class_sum_kernel(keep_ref, one_ref, other_ref, low_ref, high_ref, out_ref):
-    half = NQ // 2
-    for q in range(NQ):
-        two = low_ref[q] if q < half else high_ref[q - half]
-        total = keep_ref[q].astype(F32) + one_ref[q].astype(F32)
-        out_ref[q] = (total + other_ref[q].astype(F32) + two.astype(F32)).astype(BF16)
+        keep_ref[m] = total(parity)
+        (low_ref if m < half else high_ref)[m % half] = total(1 - parity)
+
+
+def pair_sum_kernel(keep_ref, low_ref, high_ref, out_ref):
+    half = NM // 2
+    out_ref[:half] = (keep_ref[:half].astype(F32) + low_ref[...].astype(F32)).astype(BF16)
+    out_ref[half:] = (keep_ref[half:].astype(F32) + high_ref[...].astype(F32)).astype(BF16)
 
 
 def own_grad_kernel(ids_ref, counts_ref, arrived_ref, grad_ref, squares_ref):
@@ -161,8 +156,8 @@
     squares = jnp.zeros((TILE, TILE), F32)
     for rank in range(SLOT_CAP):
         total = arrived_ref[0, rank].astype(F32)
-        for q in range(1, NQ):
-            total = total + arrived_ref[q, rank].astype(F32)
+        for m in range(1, NM):
+            total = total + arrived_ref[m, rank].astype(F32)
         total = jnp.where(rank < count, total, 0.0)
         grad_ref[rank] = total
         squares = squares + total * total
@@ -301,21 +296,22 @@
     below_low, above_high = shift(up_low, "y", 1), shift(down_high, "y", -1)
 
     def parted(value):
-        return value.reshape(-1, NC, SLOT_CAP, TILE, TILE)
-
-    four = SHAPE((NQ, SLOT_CAP, TILE, TILE), BF16)
-    two = SHAPE((NQ // 2, SLOT_CAP, TILE, TILE), BF16)
-    keep, up, down, up_two, down_two = kernel_call(
-        y_sum_kernel, "y_sum", [four, four, four, two, two], [SMEM] + [VMEM] * 5, [VMEM] * 5
+        return value.reshape(-1, 2, SLOT_CAP, TILE, TILE)
+
+    eight = SHAPE((NM, SLOT_CAP, TILE, TILE), BF16)
+    four = SHAPE((NM // 2, SLOT_CAP, TILE, TILE), BF16)
+    keep, low, high = kernel_call(
+        y_sum_kernel, "y_sum", [eight, four, four], [SMEM] + [VMEM] * 5, [VMEM] * 3
     )(ids, *map(parted, (mine, below_low, above_low, below_high, above_high)))
 
-    moved = [shift(up, Z, 1), shift(down, Z, -1), shift(up_two, Z, 2), shift(down_two, Z, -2)]
-    *moved, grads = lax.optimization_barrier((*moved, grads))
-    pairs = kernel_call(class_sum_kernel, "class_sum", four, [VMEM] * 5, VMEM)(keep, *moved)
-    arrived = exchange(pairs, "q")
+    pairs = kernel_call(pair_sum_kernel, "pair_sum", eight, [VMEM] * 3, VMEM)(
+        keep, shift(low, Z, 1), shift(high, Z, -1)
+    )
+    pairs, grads = lax.optimization_barrier((pairs, grads))
+    arrived = exchange(pairs, ("q", "d"))
     own_grad, squares = kernel_call(
         own_grad_kernel, "own_grad",
-        [SHAPE((SLOT_CAP, TILE, TILE), F32), SHAPE((NY * NX * 2, 8, TILE), F32)],
+        [SHAPE((SLOT_CAP, TILE, TILE), F32), SHAPE((NY * NZ // 4, 8, TILE), F32)],
         [SMEM, SMEM, VMEM], [VMEM] * 2,
     )(ids, owner_counts, arrived)
 
@@ -341,9 +337,9 @@
         [pltpu.SemaphoreType.DMA], moved=4 << 20,
     )(gathered)
 
-    squares = exchange(squares, ("y", "x", "core"))
-    squares = kernel_call(relay_kernel, "relay", SHAPE((NZ, 8, TILE), F32), [VMEM], VMEM)(squares)
-    squares = exchange(squares, Z)
+    squares = exchange(squares, ("y", "d", "p"))
+    squares = kernel_call(relay_kernel, "relay", SHAPE((NZ // 4 * NX * 2, 8, TILE), F32), [VMEM], VMEM)(squares)
+    squares = exchange(squares, ("q", "x", "core"))
     squares, input_grad = lax.optimization_barrier((squares, input_grad))
     count_all = float(NX * 2 * tile_total * TILE * TILE)
 
@@ -357,8 +353,8 @@
 
 
 def solution(mesh):
-    grid = Mesh(mesh.devices.reshape(NY, NQ, NC, NX, 2), ("y", "q", "c", "x", "core"))
-    dp, tensor = ("y", "q", "c"), ("x", "core")
+    grid = Mesh(mesh.devices.reshape(NY, 4, 2, 2, NX, 2), ("y", "q", "d", "p", "x", "core"))
+    dp, tensor = ("y", "q", "d", "p"), ("x", "core")
     tokens = P(dp, tensor)
     lists = P(tensor, None)
     slots = P(tensor, dp, None, None)

time: 200 us -> 201 us (level)
  starting transfers between devices: 81.2 us -> 73.7 us
  waiting for transfers between devices: 40.8 us -> 47.8 us
    ppermute x15 -> x13, waiting for transfers between devices: 24.4 us -> 34.7 us  [shift(): lax.ppermute(value, axis, [(i, (i + step) % size) for i in range(size)])]
    ppermute x15 -> x13, starting transfers between devices: 59.5 us -> 53 us  [shift(): lax.ppermute(value, axis, [(i, (i + step) % size) for i in range(size)])]
  transfers between devices with their start and end apart: 19 -> 17, of which waited for: 11 -> 12; matrix products, arithmetic and copies ran while one was open for 1% -> 1% of each run, Pallas kernels for 7% -> 9%
where the time goes in v7:
time: 201 us; the launch traced here: 199 us
  starting transfers between devices  73.7 us (37%)
  waiting for transfers between devices  47.8 us (24%)
  blocking collectives  38.4 us (19%)
  Pallas kernels  20.3 us (10%)
  between operations  14.4 us (7%)
  local copies, waits for them, and re-layouts  3.66 us (2%)
    ppermute x13, starting transfers between devices, shift(): lax.ppermute(value, axis, [(i, (i + step) % size) for i in range(size)])  53 us
    all_to_all x3, blocking collectives, exchange(): return lax.all_to_all(value, axis, split_axis=0, concat_axis=0, tiled=True)  38.4 us
    ppermute x13, waiting for transfers between devices, shift(): lax.ppermute(value, axis, [(i, (i + step) % size) for i in range(size)])  34.7 us
    all_to_all x2, starting transfers between devices, exchange(): return lax.all_to_all(value, axis, split_axis=0, concat_axis=0, tiled=True)  20.7 us
    all_to_all x2, waiting for transfers between devices, exchange(): return lax.all_to_all(value, axis, split_axis=0, concat_axis=0, tiled=True)  7.61 us
    pallas_call x3, Pallas kernels, terms(): kernel_call(functools.partial(tile_kernel, parts), 'tiles', [SHAPE(((last...  7.2 us
    all_gather x1, waiting for transfers between devices, body(): gathered = lax.all_gather(share, ('x', 'core'), axis=0, tiled=True)  5.38 us
    pallas_call x1, Pallas kernels, body(): kernel_call(contrib_kernel, 'contribs', [SHAPE((tokens // 2, width), BF16...  4.81 us
  transfers between devices with their start and end apart: 17, of which 12 were waited for; matrix products, arithmetic and copies ran while one was open for 1% of the time, Pallas kernels for 9%

profile of v7, /device:TPU:1, one launch (start us, length us, event | category | flops | bytes accessed | tf_op | source)
XLA Modules:
  0.0 199.2 jit_solution(17884297157133535672)
XLA Ops:
  7.2 0.0 all-gather.3.cloned.1.call-start
  7.2 0.0 copy-start.1
  7.2 0.9 copy-done.1
  8.1 0.1 turn.1
  8.3 0.0 copy-start.3
  8.3 0.0 copy-start.4
  8.3 0.0 copy-start.5
  8.3 10.6 %all_to_all.25 = bf16[4,2,128,128]{3,2,1,0:T(8,128)(2,1)} all-to-all(bf16[4,2,128,128]{3,2,1,0:T(8,128)(2,1)S(1)} %broadcast_in_dim.5), channel_id=1, replica_groups=mesh['y'=4,'q'=4,'d'=2,'p'=2,'x'=4,'core'=2] {'y'}, dimensions={0} | all-to-all | bytes 524288 | tf_op jit(solution)/shard_map/all_to_all | solution.py:42
  18.9 0.0 all-gather.3.cloned.1.call-update
  18.9 0.0 copy-start.10
  18.9 0.0 copy-start.11
  18.9 0.0 copy-start.12
  18.9 1.1 broadcast_in_dim.4
  20.0 13.9 %all_to_all.26.own_ref = bf16[4,128,1024]{2,1,0:T(8,128)(2,1)S(1)} all-to-all(bf16[4,128,1024]{2,1,0:T(8,128)(2,1)S(1)} %broadcast_in_dim.4), channel_id=1, replica_groups=mesh['y'=4,'q'=4,'d'=2,'p'=2,'x'=4,'core'=2] {'x'}, dimensions={0} | all-to-all | bytes 2097152 | tf_op jit(solution)/shard_map/all_to_all | solution.py:42
  34.0 7.9 %collective-permute-start = (bf16[4,128,1024]{2,1,0:T(8,128)(2,1)S(1)}, bf16[4,128,1024]{2,1,0:T(8,128)(2,1)S(1)}, u32[]{:S(2)}, u32[]{:S(2)}) collective-permute-start(bf16[4,128,1024]{2,1,0:T(8,128)(2,1)S(1)} %all_to_all.26.own_ref), channel_id=1, source_target_pairs={{0,1},{1,0},{2,3},{3,2},{4,5},{5,4},{6,7},{7,6},{8,9},{9,8},{10,11... | collective-permute-start | bytes 3145736 | tf_op jit(solution)/shard_map/ppermute | solution.py:38
  41.8 0.1 pad_add_fusion.ids_ref.refs_0_
  41.9 1.1 gate.1
  43.1 1.0 collective-permute-done.other_ref
  44.1 2.1 %tiles.3 = (bf16[16,128,128]{2,1,0:T(8,128)(2,1)S(1)}, bf16[16,128,128]{2,1,0:T(8,128)(2,1)S(1)}) custom-call(s32[4]{0:T(128)S(1)} %pad_add_fusion.ids_ref.refs_0_, s32[1,112]{1,0:T(1,128)S(1)} %copy-done.11, s32[1,112]{1,0:T(1,128)S(1)} %copy-done.12, s32[1,64]{1,0:T(1,128)S(1)} %copy-done.10, bf16[4,128,1024]{2,1,0:T(8,128)(2,1)S(1)} %all_to_all.26.own_ref, ...), custom_call_target="tpu_custom_call" | custom-call | flops 117440512 | bytes 2097152 | tf_op jit(solution)/shard_map/tiles/pallas_call | solution.py:279
  46.2 2.3 %collective-permute-start.1 = (bf16[16,128,128]{2,1,0:T(8,128)(2,1)S(1)}, bf16[16,128,128]{2,1,0:T(8,128)(2,1)S(1)}, u32[]{:S(2)}, u32[]{:S(2)}) collective-permute-start(bf16[16,128,128]{2,1,0:T(8,128)(2,1)S(1)} %get-tuple-element.56), channel_id=1, source_target_pairs={{0,128},{128,256},{256,384},{384,0},{1,129},{129,257},{257,385},{3... | collective-permute-start | bytes 1572872 | tf_op jit(solution)/shard_map/ppermute | solution.py:38
  48.5 4.2 %collective-permute-start.2 = (bf16[16,128,128]{2,1,0:T(8,128)(2,1)S(1)}, bf16[16,128,128]{2,1,0:T(8,128)(2,1)S(1)}, u32[]{:S(2)}, u32[]{:S(2)}) collective-permute-start(bf16[16,128,128]{2,1,0:T(8,128)(2,1)S(1)} %get-tuple-element.58), channel_id=1, source_target_pairs={{0,384},{128,0},{256,128},{384,256},{1,385},{129,1},{257,129},{385... | collective-permute-start | bytes 1572872 | tf_op jit(solution)/shard_map/ppermute | solution.py:38
  52.7 2.1 %tiles.4 = (bf16[16,128,128]{2,1,0:T(8,128)(2,1)S(1)}, bf16[16,128,128]{2,1,0:T(8,128)(2,1)S(1)}) custom-call(s32[4]{0:T(128)S(1)} %pad_add_fusion.ids_ref.refs_0_, s32[1,112]{1,0:T(1,128)S(1)} %copy-done.11, s32[1,112]{1,0:T(1,128)S(1)} %copy-done.12, s32[1,64]{1,0:T(1,128)S(1)} %copy-done.10, bf16[4,128,1024]{2,1,0:T(8,128)(2,1)S(1)} %all_to_all.26.own_ref, ...), custom_call_target="tpu_custom_call" | custom-call | flops 117440512 | bytes 2097152 | tf_op jit(solution)/shard_map/tiles/pallas_call | solution.py:279
  54.8 3.0 %tiles.5 = (bf16[16,128,128]{2,1,0:T(8,128)(2,1)S(1)}, bf16[16,128,128]{2,1,0:T(8,128)(2,1)S(1)}, bf16[32,128,128]{2,1,0:T(8,128)(2,1)S(1)}) custom-call(s32[4]{0:T(128)S(1)} %pad_add_fusion.ids_ref.refs_0_, s32[1,112]{1,0:T(1,128)S(1)} %copy-done.11, s32[1,112]{1,0:T(1,128)S(1)} %copy-done.12, s32[1,64]{1,0:T(1,128)S(1)} %copy-done.10, ...), custom_call_target="tpu_custom_call" | custom-call | flops 117440512 | bytes 2097152 | tf_op jit(solution)/shard_map/tiles/pallas_call | solution.py:279
  57.8 1.9 collective-permute-start.4
  59.8 3.4 %collective-permute-start.5 = (bf16[16,128,128]{2,1,0:T(8,128)(2,1)S(1)}, bf16[16,128,128]{2,1,0:T(8,128)(2,1)S(1)}, u32[]{:S(2)}, u32[]{:S(2)}) collective-permute-start(bf16[16,128,128]{2,1,0:T(8,128)(2,1)S(1)} %get-tuple-element.61), channel_id=1, source_target_pairs={{0,128},{128,256},{256,384},{384,0},{1,129},{129,257},{257,385},{3... | collective-permute-start | bytes 1572872 | tf_op jit(solution)/shard_map/ppermute | solution.py:38
  63.1 0.0 collective-permute-done.1.far_low_ref
  63.1 0.1 collective-permute-done.2.far_high_ref
  63.3 0.2 passing.1
  63.5 2.0 %collective-permute-start.3 = (bf16[16,128,128]{2,1,0:T(8,128)(2,1)S(1)}, bf16[16,128,128]{2,1,0:T(8,128)(2,1)S(1)}, u32[]{:S(2)}, u32[]{:S(2)}) collective-permute-start(bf16[16,128,128]{2,1,0:T(8,128)(2,1)S(1)} %get-tuple-element.59), channel_id=1, source_target_pairs={{0,128},{128,256},{256,384},{384,0},{1,129},{129,257},{257,385},{3... | collective-permute-start | bytes 1572872 | tf_op jit(solution)/shard_map/ppermute | solution.py:38
  65.6 5.2 %collective-permute-start.6 = (bf16[16,128,128]{2,1,0:T(8,128)(2,1)S(1)}, bf16[16,128,128]{2,1,0:T(8,128)(2,1)S(1)}, u32[]{:S(2)}, u32[]{:S(2)}) collective-permute-start(bf16[16,128,128]{2,1,0:T(8,128)(2,1)S(1)} %get-tuple-element.62), channel_id=1, source_target_pairs={{0,384},{128,0},{256,128},{384,256},{1,385},{129,1},{257,129},{385... | collective-permute-start | bytes 1572872 | tf_op jit(solution)/shard_map/ppermute | solution.py:38
  70.8 3.7 %collective-permute-done.4 = bf16[16,128,128]{2,1,0:T(8,128)(2,1)S(1)} collective-permute-done((bf16[16,128,128]{2,1,0:T(8,128)(2,1)S(1)}, bf16[16,128,128]{2,1,0:T(8,128)(2,1)S(1)}, u32[]{:S(2)}, u32[]{:S(2)}) %collective-permute-start.4) | collective-permute-done | bytes 524320 | tf_op jit(solution)/shard_map/ppermute | solution.py:38
  74.5 1.0 collective-permute-done.5
  75.5 11.2 %collective-permute-done.3 = bf16[16,128,128]{2,1,0:T(8,128)(2,1)S(1)} collective-permute-done((bf16[16,128,128]{2,1,0:T(8,128)(2,1)S(1)}, bf16[16,128,128]{2,1,0:T(8,128)(2,1)S(1)}, u32[]{:S(2)}, u32[]{:S(2)}) %collective-permute-start.3) | collective-permute-done | bytes 524320 | tf_op jit(solution)/shard_map/ppermute | solution.py:38
  86.7 0.0 collective-permute-done.6
  86.7 0.9 y_sum.1
  87.7 3.6 %collective-permute-start.7 = (bf16[4,2,128,128]{3,2,1,0:T(8,128)(2,1)S(1)}, bf16[4,2,128,128]{3,2,1,0:T(8,128)(2,1)S(1)}, u32[]{:S(2)}, u32[]{:S(2)}) collective-permute-start(bf16[4,2,128,128]{3,2,1,0:T(8,128)(2,1)S(1)} %get-tuple-element.64), channel_id=1, source_target_pairs={{0,8},{8,16},{16,24},{24,32},{32,40},{40,48},{48,56},{56,64},{64,7... | collective-permute-start | bytes 786440 | tf_op jit(solution)/shard_map/ppermute | solution.py:38
  91.2 9.5 %collective-permute-start.8 = (bf16[4,2,128,128]{3,2,1,0:T(8,128)(2,1)S(1)}, bf16[4,2,128,128]{3,2,1,0:T(8,128)(2,1)S(1)}, u32[]{:S(2)}, u32[]{:S(2)}) collective-permute-start(bf16[4,2,128,128]{3,2,1,0:T(8,128)(2,1)S(1)} %get-tuple-element.65), channel_id=1, source_target_pairs={{0,120},{8,0},{16,8},{24,16},{32,24},{40,32},{48,40},{56,48},{64,5... | collective-permute-start | bytes 786440 | tf_op jit(solution)/shard_map/ppermute | solution.py:38
  100.8 3.9 %collective-permute-done.7.low_ref = bf16[4,2,128,128]{3,2,1,0:T(8,128)(2,1)S(1)} collective-permute-done((bf16[4,2,128,128]{3,2,1,0:T(8,128)(2,1)S(1)}, bf16[4,2,128,128]{3,2,1,0:T(8,128)(2,1)S(1)}, u32[]{:S(2)}, u32[]{:S(2)}) %collective-permute-start.7) | collective-permute-done | bytes 262176 | tf_op jit(solution)/shard_map/ppermute | solution.py:38
  104.7 0.0 collective-permute-done.8.high_ref
  104.7 0.9 pair_sum.1
  105.6 8.1 %all-to-all-start.1 = ((bf16[8,2,128,128]{3,2,1,0:T(8,128)(2,1)}), bf16[8,2,128,128]{3,2,1,0:T(8,128)(2,1)S(1)}, u32[]{:S(2)}, u32[]{:S(2)}) async-start(bf16[8,2,128,128]{3,2,1,0:T(8,128)(2,1)} %pair_sum.1), calls=%async_computation.1 | async-start | bytes 1048576 | tf_op jit(solution)/shard_map/all_to_all | solution.py:42
  113.7 0.0 all-gather.5.cloned.1.call-start
  113.7 0.0 all-gather.3.cloned.1.call-done.delta_ref
  113.7 4.8 %contribs.1 = (bf16[64,8192]{1,0:T(8,128)(2,1)S(1)}, bf16[64,8192]{1,0:T(8,128)(2,1)S(1)}) custom-call(s32[1,112]{1,0:T(1,128)S(1)} %copy-done.11, s32[1,112]{1,0:T(1,128)S(1)} %copy-done.12, s32[1,64]{1,0:T(1,128)S(1)} %copy-done.10, bf16[14,128,128]{2,1,0:T(8,128)(2,1)S(1)} %copy-done.7, bf16[128,128,128]{2,1,0:T(8,128)(2,1)} %all-gather.3.cloned.1.call-done.delta_ref), custom_call_target="tpu_custom_call" | custom-call | bytes 4096 | tf_op jit(solution)/shard_map/contribs/pallas_call | solution.py:318
  118.5 5.2 %collective-permute-start.9 = (bf16[64,8192]{1,0:T(8,128)(2,1)S(1)}, bf16[64,8192]{1,0:T(8,128)(2,1)S(1)}, u32[]{:S(2)}, u32[]{:S(2)}) collective-permute-start(bf16[64,8192]{1,0:T(8,128)(2,1)S(1)} %get-tuple-element.71), channel_id=1, source_target_pairs={{0,1},{1,0},{2,3},{3,2},{4,5},{5,4},{6,7},{7,6},{8,9},{9,8},{10,11... | collective-permute-start | bytes 3145736 | tf_op jit(solution)/shard_map/ppermute | solution.py:38
  123.8 2.3 %collective-permute-done.9 = bf16[64,8192]{1,0:T(8,128)(2,1)S(1)} collective-permute-done((bf16[64,8192]{1,0:T(8,128)(2,1)S(1)}, bf16[64,8192]{1,0:T(8,128)(2,1)S(1)}, u32[]{:S(2)}, u32[]{:S(2)}) %collective-permute-start.9) | collective-permute-done | bytes 1048608 | tf_op jit(solution)/shard_map/ppermute | solution.py:38
  126.1 0.8 core_sum.1
  126.9 2.8 %collective-permute-start.12 = (bf16[16,8192]{1,0:T(8,128)(2,1)S(1)}, bf16[16,8192]{1,0:T(8,128)(2,1)S(1)}, u32[]{:S(2)}, u32[]{:S(2)}) collective-permute-start(bf16[16,8192]{1,0:T(8,128)(2,1)S(1)} %get-tuple-element.75), channel_id=1, source_target_pairs={{0,6},{2,0},{4,2},{6,4},{1,7},{3,1},{5,3},{7,5},{8,14},{10,8},{12,... | collective-permute-start | bytes 786440 | tf_op jit(solution)/shard_map/ppermute | solution.py:38
  129.6 3.1 %collective-permute-start.11 = (bf16[16,8192]{1,0:T(8,128)(2,1)S(1)}, bf16[16,8192]{1,0:T(8,128)(2,1)S(1)}, u32[]{:S(2)}, u32[]{:S(2)}) collective-permute-start(bf16[16,8192]{1,0:T(8,128)(2,1)S(1)} %get-tuple-element.74), channel_id=1, source_target_pairs={{0,4},{2,6},{4,0},{6,2},{1,5},{3,7},{5,1},{7,3},{8,12},{10,14},{12... | collective-permute-start | bytes 786440 | tf_op jit(solution)/shard_map/ppermute | solution.py:38
  132.7 1.9 collective-permute-start.10
  134.7 0.8 own_grad.1
  135.4 0.9 collective-permute-done.12
  136.3 4.0 %collective-permute-done.11 = bf16[16,8192]{1,0:T(8,128)(2,1)S(1)} collective-permute-done((bf16[16,8192]{1,0:T(8,128)(2,1)S(1)}, bf16[16,8192]{1,0:T(8,128)(2,1)S(1)}, u32[]{:S(2)}, u32[]{:S(2)}) %collective-permute-start.11) | collective-permute-done | bytes 262176 | tf_op jit(solution)/shard_map/ppermute | solution.py:38
  140.2 6.6 %collective-permute-done.10 = bf16[16,8192]{1,0:T(8,128)(2,1)S(1)} collective-permute-done((bf16[16,8192]{1,0:T(8,128)(2,1)S(1)}, bf16[16,8192]{1,0:T(8,128)(2,1)S(1)}, u32[]{:S(2)}, u32[]{:S(2)}) %collective-permute-start.10) | collective-permute-done | bytes 262176 | tf_op jit(solution)/shard_map/ppermute | solution.py:38
  146.9 0.8 add_convert_fusion
  147.7 0.0 all-gather.5.cloned.1.call-update
  147.7 13.9 %all_to_all.27.arrived_ref = f32[16,8,128]{2,1,0:T(8,128)S(1)} all-to-all(f32[16,8,128]{2,1,0:T(8,128)S(1)} %get-tuple-element.76), channel_id=1, replica_groups=mesh['y'=4,'q'=4,'d'=2,'p'=2,'x'=4,'core'=2] {'y','d','p'}, dimensions={0} | all-to-all | bytes 131072 | tf_op jit(solution)/shard_map/all_to_all | solution.py:42
  161.6 0.7 relay.1
  162.3 12.6 %all-to-all-start.4 = ((f32[32,8,128]{2,1,0:T(8,128)}), f32[32,8,128]{2,1,0:T(8,128)S(1)}, u32[]{:S(2)}, u32[]{:S(2)}) async-start(f32[32,8,128]{2,1,0:T(8,128)} %relay.1), calls=%async_computation.4 | async-start | bytes 262144 | tf_op jit(solution)/shard_map/all_to_all | solution.py:42
  174.9 5.4 %all-gather.5.cloned.1.call-done.in_ref = bf16[128,8192]{1,0:T(8,128)(2,1)} async-done(((bf16[16,8192]{1,0:T(8,128)(2,1)}), bf16[128,8192]{1,0:T(8,128)(2,1)}) %all-gather.5.cloned.1.call-update) | async-done | bytes 2097168 | tf_op jit(solution)/shard_map/all_gather | solution.py:334
  180.3 1.6 copy-done
  181.9 1.3 result.1
  183.2 7.6 %all-to-all-done.4.refs_2_ = f32[32,8,128]{2,1,0:T(8,128)S(1)} async-done(((f32[32,8,128]{2,1,0:T(8,128)}), f32[32,8,128]{2,1,0:T(8,128)S(1)}, u32[]{:S(2)}, u32[]{:S(2)}) %all-to-all-start.4) | async-done | bytes 131104 | tf_op jit(solution)/shard_map/all_to_all | solution.py:42
  190.9 1.5 adam.1
  (19 shorter events, 0.1 us)
Async XLA Ops:
  7.2 106.5 %all-gather.3.cloned.1.call-start = ((), (), s32[]{:S(2)}) async-start(), calls=%async_computation.5 | async-start | bytes 4456448 | tf_op jit(solution)/shard_map/all_gather | solution.py:264
  7.2 0.9 copy-start.1
  8.3 33.7 %copy-start.3 = (bf16[128,1792]{1,0:T(8,128)(2,1)S(1)}, bf16[128,1792]{1,0:T(8,128)(2,1)}, u32[]{:S(2)}) copy-start(bf16[128,1792]{1,0:T(8,128)(2,1)} %gate_ref.1) | copy-start | bytes 1376260
  8.3 33.6 %copy-start.4 = (bf16[128,1792]{1,0:T(8,128)(2,1)S(1)}, bf16[128,1792]{1,0:T(8,128)(2,1)}, u32[]{:S(2)}) copy-start(bf16[128,1792]{1,0:T(8,128)(2,1)} %up_ref.1) | copy-start | bytes 1376260
  8.3 33.6 %copy-start.5 = (bf16[128,1792]{1,0:T(8,128)(2,1)S(1)}, bf16[128,1792]{1,0:T(8,128)(2,1)}, u32[]{:S(2)}) copy-start(bf16[128,1792]{1,0:T(8,128)(2,1)} %hidden_ref.1) | copy-start | bytes 1376260
  18.9 25.2 %copy-start.10 = (s32[1,64]{1,0:T(1,128)S(1)}, s32[1,64]{1,0:T(1,128)}, u32[]{:S(2)}) copy-start(s32[1,64]{1,0:T(1,128)} %refs_1_.1) | copy-start | bytes 772
  18.9 25.2 %copy-start.11 = (s32[1,112]{1,0:T(1,128)S(1)}, s32[1,112]{1,0:T(1,128)}, u32[]{:S(2)}) copy-start(s32[1,112]{1,0:T(1,128)} %rows_ref.7) | copy-start | bytes 1348
  18.9 25.2 %copy-start.12 = (s32[1,112]{1,0:T(1,128)S(1)}, s32[1,112]{1,0:T(1,128)}, u32[]{:S(2)}) copy-start(s32[1,112]{1,0:T(1,128)} %cols_ref.7) | copy-start | bytes 1348
  34.0 10.1 %collective-permute-start = (bf16[4,128,1024]{2,1,0:T(8,128)(2,1)S(1)}, bf16[4,128,1024]{2,1,0:T(8,128)(2,1)S(1)}, u32[]{:S(2)}, u32[]{:S(2)}) collective-permute-start(bf16[4,128,1024]{2,1,0:T(8,128)(2,1)S(1)} %all_to_all.26.own_ref), channel_id=1, source_target_pairs={{0,1},{1,0},{2,3},{3,2},{4,5},{5,4},{6,7},{7,6},{8,9},{9,8},{10,11... | collective-permute-start | bytes 3145736 | tf_op jit(solution)/shard_map/ppermute | solution.py:38
  43.0 11.7 %copy-start.6 = (bf16[14,128,128]{2,1,0:T(8,128)(2,1)}, bf16[14,128,128]{2,1,0:T(8,128)(2,1)S(1)}, u32[]{:S(2)}) copy-start(bf16[14,128,128]{2,1,0:T(8,128)(2,1)S(1)} %get-tuple-element.69.grad_ref) | copy-start | bytes 1376260
  46.2 17.0 %collective-permute-start.1 = (bf16[16,128,128]{2,1,0:T(8,128)(2,1)S(1)}, bf16[16,128,128]{2,1,0:T(8,128)(2,1)S(1)}, u32[]{:S(2)}, u32[]{:S(2)}) collective-permute-start(bf16[16,128,128]{2,1,0:T(8,128)(2,1)S(1)} %get-tuple-element.56), channel_id=1, source_target_pairs={{0,128},{128,256},{256,384},{384,0},{1,129},{129,257},{257,385},{3... | collective-permute-start | bytes 1572872 | tf_op jit(solution)/shard_map/ppermute | solution.py:38
  48.5 14.8 %collective-permute-start.2 = (bf16[16,128,128]{2,1,0:T(8,128)(2,1)S(1)}, bf16[16,128,128]{2,1,0:T(8,128)(2,1)S(1)}, u32[]{:S(2)}, u32[]{:S(2)}) collective-permute-start(bf16[16,128,128]{2,1,0:T(8,128)(2,1)S(1)} %get-tuple-element.58), channel_id=1, source_target_pairs={{0,384},{128,0},{256,128},{384,256},{1,385},{129,1},{257,129},{385... | collective-permute-start | bytes 1572872 | tf_op jit(solution)/shard_map/ppermute | solution.py:38
  57.8 16.7 %collective-permute-start.4 = (bf16[16,128,128]{2,1,0:T(8,128)(2,1)S(1)}, bf16[16,128,128]{2,1,0:T(8,128)(2,1)S(1)}, u32[]{:S(2)}, u32[]{:S(2)}) collective-permute-start(bf16[16,128,128]{2,1,0:T(8,128)(2,1)S(1)} %get-tuple-element.60), channel_id=1, source_target_pairs={{0,384},{128,0},{256,128},{384,256},{1,385},{129,1},{257,129},{385... | collective-permute-start | bytes 1572872 | tf_op jit(solution)/shard_map/ppermute | solution.py:38
  59.8 15.7 %collective-permute-start.5 = (bf16[16,128,128]{2,1,0:T(8,128)(2,1)S(1)}, bf16[16,128,128]{2,1,0:T(8,128)(2,1)S(1)}, u32[]{:S(2)}, u32[]{:S(2)}) collective-permute-start(bf16[16,128,128]{2,1,0:T(8,128)(2,1)S(1)} %get-tuple-element.61), channel_id=1, source_target_pairs={{0,128},{128,256},{256,384},{384,0},{1,129},{129,257},{257,385},{3... | collective-permute-start | bytes 1572872 | tf_op jit(solution)/shard_map/ppermute | solution.py:38
  63.5 23.2 %collective-permute-start.3 = (bf16[16,128,128]{2,1,0:T(8,128)(2,1)S(1)}, bf16[16,128,128]{2,1,0:T(8,128)(2,1)S(1)}, u32[]{:S(2)}, u32[]{:S(2)}) collective-permute-start(bf16[16,128,128]{2,1,0:T(8,128)(2,1)S(1)} %get-tuple-element.59), channel_id=1, source_target_pairs={{0,128},{128,256},{256,384},{384,0},{1,129},{129,257},{257,385},{3... | collective-permute-start | bytes 1572872 | tf_op jit(solution)/shard_map/ppermute | solution.py:38
  65.6 21.2 %collective-permute-start.6 = (bf16[16,128,128]{2,1,0:T(8,128)(2,1)S(1)}, bf16[16,128,128]{2,1,0:T(8,128)(2,1)S(1)}, u32[]{:S(2)}, u32[]{:S(2)}) collective-permute-start(bf16[16,128,128]{2,1,0:T(8,128)(2,1)S(1)} %get-tuple-element.62), channel_id=1, source_target_pairs={{0,384},{128,0},{256,128},{384,256},{1,385},{129,1},{257,129},{385... | collective-permute-start | bytes 1572872 | tf_op jit(solution)/shard_map/ppermute | solution.py:38
  87.7 26.1 %copy-start.7 = (bf16[14,128,128]{2,1,0:T(8,128)(2,1)S(1)}, bf16[14,128,128]{2,1,0:T(8,128)(2,1)}, u32[]{:S(2)}) copy-start(bf16[14,128,128]{2,1,0:T(8,128)(2,1)} %copy-done.6) | copy-start | bytes 1376260
  87.7 17.0 %collective-permute-start.7 = (bf16[4,2,128,128]{3,2,1,0:T(8,128)(2,1)S(1)}, bf16[4,2,128,128]{3,2,1,0:T(8,128)(2,1)S(1)}, u32[]{:S(2)}, u32[]{:S(2)}) collective-permute-start(bf16[4,2,128,128]{3,2,1,0:T(8,128)(2,1)S(1)} %get-tuple-element.64), channel_id=1, source_target_pairs={{0,8},{8,16},{16,24},{24,32},{32,40},{40,48},{48,56},{56,64},{64,7... | collective-permute-start | bytes 786440 | tf_op jit(solution)/shard_map/ppermute | solution.py:38
  91.2 13.4 %collective-permute-start.8 = (bf16[4,2,128,128]{3,2,1,0:T(8,128)(2,1)S(1)}, bf16[4,2,128,128]{3,2,1,0:T(8,128)(2,1)S(1)}, u32[]{:S(2)}, u32[]{:S(2)}) collective-permute-start(bf16[4,2,128,128]{3,2,1,0:T(8,128)(2,1)S(1)} %get-tuple-element.65), channel_id=1, source_target_pairs={{0,120},{8,0},{16,8},{24,16},{32,24},{40,32},{48,40},{56,48},{64,5... | collective-permute-start | bytes 786440 | tf_op jit(solution)/shard_map/ppermute | solution.py:38
  105.6 29.1 %all-to-all-start.1 = ((bf16[8,2,128,128]{3,2,1,0:T(8,128)(2,1)}), bf16[8,2,128,128]{3,2,1,0:T(8,128)(2,1)S(1)}, u32[]{:S(2)}, u32[]{:S(2)}) async-start(bf16[8,2,128,128]{3,2,1,0:T(8,128)(2,1)} %pair_sum.1), calls=%async_computation.1 | async-start | bytes 1048576 | tf_op jit(solution)/shard_map/all_to_all | solution.py:42
  113.7 66.7 %all-gather.5.cloned.1.call-start = ((), (), s32[]{:S(2)}) async-start(), calls=%async_computation.6 | async-start | bytes 2359296 | tf_op jit(solution)/shard_map/all_gather | solution.py:334
  118.5 7.5 %collective-permute-start.9 = (bf16[64,8192]{1,0:T(8,128)(2,1)S(1)}, bf16[64,8192]{1,0:T(8,128)(2,1)S(1)}, u32[]{:S(2)}, u32[]{:S(2)}) collective-permute-start(bf16[64,8192]{1,0:T(8,128)(2,1)S(1)} %get-tuple-element.71), channel_id=1, source_target_pairs={{0,1},{1,0},{2,3},{3,2},{4,5},{5,4},{6,7},{7,6},{8,9},{9,8},{10,11... | collective-permute-start | bytes 3145736 | tf_op jit(solution)/shard_map/ppermute | solution.py:38
  126.9 9.4 %collective-permute-start.12 = (bf16[16,8192]{1,0:T(8,128)(2,1)S(1)}, bf16[16,8192]{1,0:T(8,128)(2,1)S(1)}, u32[]{:S(2)}, u32[]{:S(2)}) collective-permute-start(bf16[16,8192]{1,0:T(8,128)(2,1)S(1)} %get-tuple-element.75), channel_id=1, source_target_pairs={{0,6},{2,0},{4,2},{6,4},{1,7},{3,1},{5,3},{7,5},{8,14},{10,8},{12,... | collective-permute-start | bytes 786440 | tf_op jit(solution)/shard_map/ppermute | solution.py:38
  129.6 10.6 %collective-permute-start.11 = (bf16[16,8192]{1,0:T(8,128)(2,1)S(1)}, bf16[16,8192]{1,0:T(8,128)(2,1)S(1)}, u32[]{:S(2)}, u32[]{:S(2)}) collective-permute-start(bf16[16,8192]{1,0:T(8,128)(2,1)S(1)} %get-tuple-element.74), channel_id=1, source_target_pairs={{0,4},{2,6},{4,0},{6,2},{1,5},{3,7},{5,1},{7,3},{8,12},{10,14},{12... | collective-permute-start | bytes 786440 | tf_op jit(solution)/shard_map/ppermute | solution.py:38
  132.7 14.2 %collective-permute-start.10 = (bf16[16,8192]{1,0:T(8,128)(2,1)S(1)}, bf16[16,8192]{1,0:T(8,128)(2,1)S(1)}, u32[]{:S(2)}, u32[]{:S(2)}) collective-permute-start(bf16[16,8192]{1,0:T(8,128)(2,1)S(1)} %get-tuple-element.73), channel_id=1, source_target_pairs={{0,2},{2,4},{4,6},{6,0},{1,3},{3,5},{5,7},{7,1},{8,10},{10,12},{12... | collective-permute-start | bytes 786440 | tf_op jit(solution)/shard_map/ppermute | solution.py:38
  162.3 28.5 %all-to-all-start.4 = ((f32[32,8,128]{2,1,0:T(8,128)}), f32[32,8,128]{2,1,0:T(8,128)S(1)}, u32[]{:S(2)}, u32[]{:S(2)}) async-start(f32[32,8,128]{2,1,0:T(8,128)} %relay.1), calls=%async_computation.4 | async-start | bytes 262144 | tf_op jit(solution)/shard_map/all_to_all | solution.py:42
  180.3 1.6 copy-start
  181.9 8.9 %copy-start.2 = (f32[1,2,128,128]{3,2,1,0:T(8,128)S(1)}, f32[1,2,128,128]{3,2,1,0:T(8,128)}, u32[]{:S(2)}) copy-start(f32[1,2,128,128]{3,2,1,0:T(8,128)} %refs_4_.1) | copy-start | bytes 393220
  181.9 8.9 %copy-start.8 = (f32[1,2,128,128]{3,2,1,0:T(8,128)S(1)}, f32[1,2,128,128]{3,2,1,0:T(8,128)}, u32[]{:S(2)}) copy-start(f32[1,2,128,128]{3,2,1,0:T(8,128)} %refs_5_.1) | copy-start | bytes 393220
  181.9 8.9 %copy-start.9 = (f32[1,2,128,128]{3,2,1,0:T(8,128)S(1)}, f32[1,2,128,128]{3,2,1,0:T(8,128)}, u32[]{:S(2)}) copy-start(f32[1,2,128,128]{3,2,1,0:T(8,128)} %refs_6_.1) | copy-start | bytes 393220
Sparse Core Ops, SparseCore 0:
  19.0 73.7 all-gather.2
  147.8 32.4 all-gather.4

commit v8 on v7

--- a/solution.py
+++ b/solution.py
@@ -7,9 +7,9 @@
 from jax.experimental.pallas import tpu as pltpu
 from jax.sharding import Mesh, PartitionSpec as P
 
-NY, NZ, NX = 4, 16, 4
-NM = NZ // 2
-Z = ("q", "d", "p")
+NY, NM, NX = 4, 8, 4
+NZ = 2 * NM
+Z = ("m", "p")
 TILE = 128
 SLOT_CAP = 2
 LOW, HIGH = (0, NZ // 2), (NZ // 2, NZ)
@@ -20,14 +20,16 @@
 SHAPE = jax.ShapeDtypeStruct
 
 
-def kernel_call(kernel, name, outs, ins, out_specs, scratch=(), flops=0, moved=1 << 20):
+def kernel_call(
+    kernel, name, outs, ins, out_specs, scratch=(), flops=0, moved=1 << 20, vmem=48
+):
     return pl.pallas_call(
         kernel,
         out_shape=outs,
         in_specs=ins,
         out_specs=out_specs,
         scratch_shapes=scratch,
-        compiler_params=pltpu.CompilerParams(vmem_limit_bytes=48 * 1024 * 1024),
+        compiler_params=pltpu.CompilerParams(vmem_limit_bytes=vmem * 1024 * 1024),
         cost_estimate=pl.CostEstimate(flops=flops, bytes_accessed=moved, transcendentals=0),
         name=name,
     )
@@ -127,7 +129,7 @@
 
 def y_sum_kernel(
     ids_ref, mine_ref, below_low_ref, above_low_ref, below_high_ref, above_high_ref,
-    keep_ref, low_ref, high_ref,
+    keep_ref, give_ref,
 ):
     parity = ids_ref[1] & 1
     half = NM // 2
@@ -142,13 +144,11 @@
             ).astype(BF16)
 
         keep_ref[m] = total(parity)
-        (low_ref if m < half else high_ref)[m % half] = total(1 - parity)
-
-
-def pair_sum_kernel(keep_ref, low_ref, high_ref, out_ref):
-    half = NM // 2
-    out_ref[:half] = (keep_ref[:half].astype(F32) + low_ref[...].astype(F32)).astype(BF16)
-    out_ref[half:] = (keep_ref[half:].astype(F32) + high_ref[...].astype(F32)).astype(BF16)
+        give_ref[m] = total(1 - parity)
+
+
+def pair_sum_kernel(keep_ref, taken_ref, out_ref):
+    out_ref[...] = (keep_ref[...].astype(F32) + taken_ref[...].astype(F32)).astype(BF16)
 
 
 def own_grad_kernel(ids_ref, counts_ref, arrived_ref, grad_ref, squares_ref):
@@ -237,10 +237,26 @@
         ref[...] = (stay_ref[at].astype(F32) + taken_ref[at].astype(F32)).astype(BF16)
 
 
-def copy_kernel(in_ref, out_ref, sem):
-    copy = pltpu.make_async_copy(in_ref, out_ref, sem)
-    copy.start()
-    copy.wait()
+def copy_kernel(in_ref, out_ref, held, sems):
+    chunks = held.shape[0]
+    rows = in_ref.shape[0] // chunks
+
+    def part(ref, chunk):
+        return ref.at[pl.ds(chunk * rows, rows)]
+
+    loads = [
+        pltpu.make_async_copy(part(in_ref, i), held.at[i], sems.at[0, i]) for i in range(chunks)
+    ]
+    stores = [
+        pltpu.make_async_copy(held.at[i], part(out_ref, i), sems.at[1, i]) for i in range(chunks)
+    ]
+    for load in loads:
+        load.start()
+    for load, store in zip(loads, stores):
+        load.wait()
+        store.start()
+    for store in stores:
+        store.wait()
 
 
 def body(
@@ -299,47 +315,49 @@
         return value.reshape(-1, 2, SLOT_CAP, TILE, TILE)
 
     eight = SHAPE((NM, SLOT_CAP, TILE, TILE), BF16)
-    four = SHAPE((NM // 2, SLOT_CAP, TILE, TILE), BF16)
-    keep, low, high = kernel_call(
-        y_sum_kernel, "y_sum", [eight, four, four], [SMEM] + [VMEM] * 5, [VMEM] * 3
+    keep, give = kernel_call(
+        y_sum_kernel, "y_sum", [eight] * 2, [SMEM] + [VMEM] * 5, [VMEM] * 2
     )(ids, *map(parted, (mine, below_low, above_low, below_high, above_high)))
 
-    pairs = kernel_call(pair_sum_kernel, "pair_sum", eight, [VMEM] * 3, VMEM)(
-        keep, shift(low, Z, 1), shift(high, Z, -1)
-    )
-    pairs, grads = lax.optimization_barrier((pairs, grads))
-    arrived = exchange(pairs, ("q", "d"))
-    own_grad, squares = kernel_call(
-        own_grad_kernel, "own_grad",
-        [SHAPE((SLOT_CAP, TILE, TILE), F32), SHAPE((NY * NZ // 4, 8, TILE), F32)],
-        [SMEM, SMEM, VMEM], [VMEM] * 2,
-    )(ids, owner_counts, arrived)
-
+    keep, grads = lax.optimization_barrier((keep, grads))
+    partner = shift(give, "p", 1)
     stay, give = kernel_call(
         contrib_kernel, "contribs", [SHAPE((tokens // 2, width), BF16)] * 2,
         [SMEM] * 3 + [VMEM] * 2, [VMEM] * 2, [pltpu.SMEM((tile_total + 8,), jnp.int32)],
         moved=1 << 12,
     )(*lists, grads, delta_all)
+    partner, give = lax.optimization_barrier((partner, give))
+    pairs = kernel_call(pair_sum_kernel, "pair_sum", eight, [VMEM] * 2, VMEM)(keep, partner)
+    arrived = exchange(pairs, "m")
+    own_grad, squares = kernel_call(
+        own_grad_kernel, "own_grad",
+        [SHAPE((SLOT_CAP, TILE, TILE), F32), SHAPE((NY * NX * 2, 8, TILE), F32)],
+        [SMEM, SMEM, VMEM], [VMEM] * 2,
+    )(ids, owner_counts, arrived)
+
 
     rows = tokens // (2 * NX)
+    _, give = lax.optimization_barrier((pairs, give))
     taken = shift(give, "core", 1)
     share, *others = kernel_call(
         core_sum_kernel, "core_sum", [SHAPE((rows, width), BF16)] * NX,
         [SMEM] + [VMEM] * 2, [VMEM] * NX, moved=1 << 12,
     )(ids, stay.reshape(NX, rows, width), taken.reshape(NX, rows, width))
+    others = [shift(part, "x", away + 1) for away, part in enumerate(others)]
+    squares, share, *others = lax.optimization_barrier((squares, share, *others))
     share = share.astype(F32)
-    for away, part in enumerate(others):
-        share = share + shift(part, "x", away + 1).astype(F32)
-    squares, share = lax.optimization_barrier((squares, share.astype(BF16)))
-    gathered = lax.all_gather(share, ("x", "core"), axis=0, tiled=True)
+    for part in others:
+        share = share + part.astype(F32)
+    gathered = lax.all_gather(share.astype(BF16), ("x", "core"), axis=0, tiled=True)
     input_grad = kernel_call(
         copy_kernel, "result", SHAPE((tokens, width), BF16), [ANY], ANY,
-        [pltpu.SemaphoreType.DMA], moved=4 << 20,
+        [pltpu.VMEM((4, tokens // 4, width), BF16), pltpu.SemaphoreType.DMA((2, 4))],
+        moved=4 << 20, vmem=63,
     )(gathered)
 
-    squares = exchange(squares, ("y", "d", "p"))
-    squares = kernel_call(relay_kernel, "relay", SHAPE((NZ // 4 * NX * 2, 8, TILE), F32), [VMEM], VMEM)(squares)
-    squares = exchange(squares, ("q", "x", "core"))
+    squares = exchange(squares, ("y", "x", "core"))
+    squares = kernel_call(relay_kernel, "relay", SHAPE((NZ, 8, TILE), F32), [VMEM], VMEM)(squares)
+    squares = exchange(squares, Z)
     squares, input_grad = lax.optimization_barrier((squares, input_grad))
     count_all = float(NX * 2 * tile_total * TILE * TILE)
 
@@ -353,8 +371,8 @@
 
 
 def solution(mesh):
-    grid = Mesh(mesh.devices.reshape(NY, 4, 2, 2, NX, 2), ("y", "q", "d", "p", "x", "core"))
-    dp, tensor = ("y", "q", "d", "p"), ("x", "core")
+    grid = Mesh(mesh.devices.reshape(NY, NM, 2, NX, 2), ("y", "m", "p", "x", "core"))
+    dp, tensor = ("y", "m", "p"), ("x", "core")
     tokens = P(dp, tensor)
     lists = P(tensor, None)
     slots = P(tensor, dp, None, None)

time: 201 us -> 193 us (0.960)
  starting transfers between devices: 73.7 us -> 60.7 us
  blocking collectives: 38.4 us -> 45.8 us
    ppermute x13 -> x12, starting transfers between devices: 53 us -> 44.2 us  [shift(): lax.ppermute(value, axis, [(i, (i + step) % size) for i in range(size)])]
    all_to_all x3, blocking collectives: 38.4 us -> 45.8 us  [exchange(): return lax.all_to_all(value, axis, split_axis=0, concat_axis=0, tiled=True)]
    ppermute x13 -> x12, waiting for transfers between devices: 34.7 us -> 27.9 us  [shift(): lax.ppermute(value, axis, [(i, (i + step) % size) for i in range(size)])]
    all_to_all x2, starting transfers between devices: 20.7 us -> 16.5 us  [exchange(): return lax.all_to_all(value, axis, split_axis=0, concat_axis=0, tiled=True)]
  transfers between devices with their start and end apart: 17 -> 16, of which waited for: 12 -> 12; matrix products, arithmetic and copies ran while one was open for 1% -> 1% of each run, Pallas kernels for 9% -> 10%
where the time goes in v8:
time: 193 us; the launch traced here: 192 us
  starting transfers between devices  60.7 us (31%)
  waiting for transfers between devices  45.9 us (24%)
  blocking collectives  45.8 us (24%)
  Pallas kernels  21.4 us (11%)
  between operations  14.4 us (7%)
  local copies, waits for them, and re-layouts  3.05 us (2%)
    all_to_all x3, blocking collectives, exchange(): return lax.all_to_all(value, axis, split_axis=0, concat_axis=0, tiled=True)  45.8 us
    ppermute x12, starting transfers between devices, shift(): lax.ppermute(value, axis, [(i, (i + step) % size) for i in range(size)])  44.2 us
    ppermute x12, waiting for transfers between devices, shift(): lax.ppermute(value, axis, [(i, (i + step) % size) for i in range(size)])  27.9 us
    all_to_all x2, starting transfers between devices, exchange(): return lax.all_to_all(value, axis, split_axis=0, concat_axis=0, tiled=True)  16.5 us
    all_to_all x2, waiting for transfers between devices, exchange(): return lax.all_to_all(value, axis, split_axis=0, concat_axis=0, tiled=True)  9.23 us
    pallas_call x3, Pallas kernels, terms(): kernel_call(functools.partial(tile_kernel, parts), 'tiles', [SHAPE(((last...  7.18 us
    all_gather x1, waiting for transfers between devices, body(): lax.all_gather(share.astype(BF16), ('x', 'core'), axis=0, tiled=True)  7.04 us
    pallas_call x1, Pallas kernels, body(): kernel_call(contrib_kernel, 'contribs', [SHAPE((tokens // 2, width), BF16...  4.81 us
  transfers between devices with their start and end apart: 16, of which 12 were waited for; matrix products, arithmetic and copies ran while one was open for 1% of the time, Pallas kernels for 10%

profile of v8, /device:TPU:1, one launch (start us, length us, event | category | flops | bytes accessed | tf_op | source)
XLA Modules:
  0.0 192.2 jit_solution(11816456825750093142)
XLA Ops:
  7.2 0.0 all-gather.3.cloned.1.call-start
  7.2 0.0 copy-start
  7.2 0.9 copy-done
  8.1 0.1 turn.1
  8.3 0.0 copy-start.2
  8.3 0.0 copy-start.3
  8.3 0.0 copy-start.4
  8.3 10.6 %all_to_all.25 = bf16[4,2,128,128]{3,2,1,0:T(8,128)(2,1)} all-to-all(bf16[4,2,128,128]{3,2,1,0:T(8,128)(2,1)S(1)} %broadcast_in_dim.5), channel_id=1, replica_groups=mesh['y'=4,'m'=8,'p'=2,'x'=4,'core'=2] {'y'}, dimensions={0} | all-to-all | bytes 524288 | tf_op jit(solution)/shard_map/all_to_all | solution.py:44
  18.9 0.0 all-gather.3.cloned.1.call-update
  18.9 0.0 copy-start.9
  18.9 0.0 copy-start.10
  18.9 0.0 copy-start.11
  18.9 1.1 broadcast_in_dim.4
  20.0 13.9 %all_to_all.26.own_ref = bf16[4,128,1024]{2,1,0:T(8,128)(2,1)S(1)} all-to-all(bf16[4,128,1024]{2,1,0:T(8,128)(2,1)S(1)} %broadcast_in_dim.4), channel_id=1, replica_groups=mesh['y'=4,'m'=8,'p'=2,'x'=4,'core'=2] {'x'}, dimensions={0} | all-to-all | bytes 2097152 | tf_op jit(solution)/shard_map/all_to_all | solution.py:44
  34.0 7.9 %collective-permute-start = (bf16[4,128,1024]{2,1,0:T(8,128)(2,1)S(1)}, bf16[4,128,1024]{2,1,0:T(8,128)(2,1)S(1)}, u32[]{:S(2)}, u32[]{:S(2)}) collective-permute-start(bf16[4,128,1024]{2,1,0:T(8,128)(2,1)S(1)} %all_to_all.26.own_ref), channel_id=1, source_target_pairs={{0,1},{1,0},{2,3},{3,2},{4,5},{5,4},{6,7},{7,6},{8,9},{9,8},{10,11... | collective-permute-start | bytes 3145736 | tf_op jit(solution)/shard_map/ppermute | solution.py:40
  41.8 0.1 pad_add_fusion.ids_ref.refs_0_
  41.9 1.1 gate.1
  43.1 1.0 collective-permute-done.other_ref
  44.1 2.1 %tiles.3 = (bf16[16,128,128]{2,1,0:T(8,128)(2,1)S(1)}, bf16[16,128,128]{2,1,0:T(8,128)(2,1)S(1)}) custom-call(s32[4]{0:T(128)S(1)} %pad_add_fusion.ids_ref.refs_0_, s32[1,112]{1,0:T(1,128)S(1)} %copy-done.10, s32[1,112]{1,0:T(1,128)S(1)} %copy-done.11, s32[1,64]{1,0:T(1,128)S(1)} %copy-done.9, bf16[4,128,1024]{2,1,0:T(8,128)(2,1)S(1)} %all_to_all.26.own_ref, ...), custom_call_target="tpu_custom_call" | custom-call | flops 117440512 | bytes 2097152 | tf_op jit(solution)/shard_map/tiles/pallas_call | solution.py:295
  46.2 2.3 %collective-permute-start.1 = (bf16[16,128,128]{2,1,0:T(8,128)(2,1)S(1)}, bf16[16,128,128]{2,1,0:T(8,128)(2,1)S(1)}, u32[]{:S(2)}, u32[]{:S(2)}) collective-permute-start(bf16[16,128,128]{2,1,0:T(8,128)(2,1)S(1)} %get-tuple-element.61), channel_id=1, source_target_pairs={{0,128},{128,256},{256,384},{384,0},{1,129},{129,257},{257,385},{3... | collective-permute-start | bytes 1572872 | tf_op jit(solution)/shard_map/ppermute | solution.py:40
  48.5 4.2 %collective-permute-start.2 = (bf16[16,128,128]{2,1,0:T(8,128)(2,1)S(1)}, bf16[16,128,128]{2,1,0:T(8,128)(2,1)S(1)}, u32[]{:S(2)}, u32[]{:S(2)}) collective-permute-start(bf16[16,128,128]{2,1,0:T(8,128)(2,1)S(1)} %get-tuple-element.63), channel_id=1, source_target_pairs={{0,384},{128,0},{256,128},{384,256},{1,385},{129,1},{257,129},{385... | collective-permute-start | bytes 1572872 | tf_op jit(solution)/shard_map/ppermute | solution.py:40
  52.7 2.1 %tiles.4 = (bf16[16,128,128]{2,1,0:T(8,128)(2,1)S(1)}, bf16[16,128,128]{2,1,0:T(8,128)(2,1)S(1)}) custom-call(s32[4]{0:T(128)S(1)} %pad_add_fusion.ids_ref.refs_0_, s32[1,112]{1,0:T(1,128)S(1)} %copy-done.10, s32[1,112]{1,0:T(1,128)S(1)} %copy-done.11, s32[1,64]{1,0:T(1,128)S(1)} %copy-done.9, bf16[4,128,1024]{2,1,0:T(8,128)(2,1)S(1)} %all_to_all.26.own_ref, ...), custom_call_target="tpu_custom_call" | custom-call | flops 117440512 | bytes 2097152 | tf_op jit(solution)/shard_map/tiles/pallas_call | solution.py:295
  54.8 3.0 %tiles.5 = (bf16[16,128,128]{2,1,0:T(8,128)(2,1)S(1)}, bf16[16,128,128]{2,1,0:T(8,128)(2,1)S(1)}, bf16[32,128,128]{2,1,0:T(8,128)(2,1)S(1)}) custom-call(s32[4]{0:T(128)S(1)} %pad_add_fusion.ids_ref.refs_0_, s32[1,112]{1,0:T(1,128)S(1)} %copy-done.10, s32[1,112]{1,0:T(1,128)S(1)} %copy-done.11, s32[1,64]{1,0:T(1,128)S(1)} %copy-done.9, ...), custom_call_target="tpu_custom_call" | custom-call | flops 117440512 | bytes 2097152 | tf_op jit(solution)/shard_map/tiles/pallas_call | solution.py:295
  57.8 1.9 collective-permute-start.4
  59.7 3.4 %collective-permute-start.5 = (bf16[16,128,128]{2,1,0:T(8,128)(2,1)S(1)}, bf16[16,128,128]{2,1,0:T(8,128)(2,1)S(1)}, u32[]{:S(2)}, u32[]{:S(2)}) collective-permute-start(bf16[16,128,128]{2,1,0:T(8,128)(2,1)S(1)} %get-tuple-element.66), channel_id=1, source_target_pairs={{0,128},{128,256},{256,384},{384,0},{1,129},{129,257},{257,385},{3... | collective-permute-start | bytes 1572872 | tf_op jit(solution)/shard_map/ppermute | solution.py:40
  63.1 0.1 collective-permute-done.2.far_high_ref
  63.3 0.2 passing.1
  63.5 0.0 copy-start.6
  63.5 2.2 %collective-permute-start.3 = (bf16[16,128,128]{2,1,0:T(8,128)(2,1)S(1)}, bf16[16,128,128]{2,1,0:T(8,128)(2,1)S(1)}, u32[]{:S(2)}, u32[]{:S(2)}) collective-permute-start(bf16[16,128,128]{2,1,0:T(8,128)(2,1)S(1)} %get-tuple-element.64), channel_id=1, source_target_pairs={{0,128},{128,256},{256,384},{384,0},{1,129},{129,257},{257,385},{3... | collective-permute-start | bytes 1572872 | tf_op jit(solution)/shard_map/ppermute | solution.py:40
  65.7 5.2 %collective-permute-start.6 = (bf16[16,128,128]{2,1,0:T(8,128)(2,1)S(1)}, bf16[16,128,128]{2,1,0:T(8,128)(2,1)S(1)}, u32[]{:S(2)}, u32[]{:S(2)}) collective-permute-start(bf16[16,128,128]{2,1,0:T(8,128)(2,1)S(1)} %get-tuple-element.67), channel_id=1, source_target_pairs={{0,384},{128,0},{256,128},{384,256},{1,385},{129,1},{257,129},{385... | collective-permute-start | bytes 1572872 | tf_op jit(solution)/shard_map/ppermute | solution.py:40
  70.9 3.6 %collective-permute-done.4 = bf16[16,128,128]{2,1,0:T(8,128)(2,1)S(1)} collective-permute-done((bf16[16,128,128]{2,1,0:T(8,128)(2,1)S(1)}, bf16[16,128,128]{2,1,0:T(8,128)(2,1)S(1)}, u32[]{:S(2)}, u32[]{:S(2)}) %collective-permute-start.4) | collective-permute-done | bytes 524320 | tf_op jit(solution)/shard_map/ppermute | solution.py:40
  74.5 0.9 collective-permute-done.5
  75.4 11.2 %collective-permute-done.3 = bf16[16,128,128]{2,1,0:T(8,128)(2,1)S(1)} collective-permute-done((bf16[16,128,128]{2,1,0:T(8,128)(2,1)S(1)}, bf16[16,128,128]{2,1,0:T(8,128)(2,1)S(1)}, u32[]{:S(2)}, u32[]{:S(2)}) %collective-permute-start.3) | collective-permute-done | bytes 524320 | tf_op jit(solution)/shard_map/ppermute | solution.py:40
  86.7 0.9 y_sum.1
  87.6 3.4 %collective-permute-start.7 = (bf16[8,2,128,128]{3,2,1,0:T(8,128)(2,1)S(1)}, bf16[8,2,128,128]{3,2,1,0:T(8,128)(2,1)S(1)}, u32[]{:S(2)}, u32[]{:S(2)}) collective-permute-start(bf16[8,2,128,128]{3,2,1,0:T(8,128)(2,1)S(1)} %get-tuple-element.71), channel_id=1, source_target_pairs={{0,8},{8,0},{1,9},{9,1},{2,10},{10,2},{3,11},{11,3},{4,12},{12,4},... | collective-permute-start | bytes 1572872 | tf_op jit(solution)/shard_map/ppermute | solution.py:40
  91.0 1.8 all-gather.3.cloned.1.call-done.delta_ref
  92.8 4.8 %contribs.1 = (bf16[64,8192]{1,0:T(8,128)(2,1)S(1)}, bf16[64,8192]{1,0:T(8,128)(2,1)S(1)}) custom-call(s32[1,112]{1,0:T(1,128)S(1)} %copy-done.10, s32[1,112]{1,0:T(1,128)S(1)} %copy-done.11, s32[1,64]{1,0:T(1,128)S(1)} %copy-done.9, bf16[14,128,128]{2,1,0:T(8,128)(2,1)S(1)} %copy-done.6, bf16[128,128,128]{2,1,0:T(8,128)(2,1)} %all-gather.3.cloned.1.call-done.delta_ref), custom_call_target="tpu_custom_call" | custom-call | bytes 4096 | tf_op jit(solution)/shard_map/contribs/pallas_call | solution.py:324
  97.6 0.0 copy-start.12
  97.6 1.0 copy-done.12
  98.6 7.3 %collective-permute-done.7.taken_ref = bf16[8,2,128,128]{3,2,1,0:T(8,128)(2,1)S(1)} collective-permute-done((bf16[8,2,128,128]{3,2,1,0:T(8,128)(2,1)S(1)}, bf16[8,2,128,128]{3,2,1,0:T(8,128)(2,1)S(1)}, u32[]{:S(2)}, u32[]{:S(2)}) %collective-permute-start.7) | collective-permute-done | bytes 524320 | tf_op jit(solution)/shard_map/ppermute | solution.py:40
  105.9 0.9 pair_sum.1
  106.8 10.6 %all-to-all-start.2 = ((bf16[8,2,128,128]{3,2,1,0:T(8,128)(2,1)}), bf16[8,2,128,128]{3,2,1,0:T(8,128)(2,1)S(1)}, u32[]{:S(2)}, u32[]{:S(2)}) async-start(bf16[8,2,128,128]{3,2,1,0:T(8,128)(2,1)} %pair_sum.1), calls=%async_computation.2 | async-start | bytes 1048576 | tf_op jit(solution)/shard_map/all_to_all | solution.py:44
  117.3 0.0 all-gather.5.cloned.1.call-start
  117.4 4.6 %collective-permute-start.8 = (bf16[64,8192]{1,0:T(8,128)(2,1)S(1)}, bf16[64,8192]{1,0:T(8,128)(2,1)S(1)}, u32[]{:S(2)}, u32[]{:S(2)}) collective-permute-start(bf16[64,8192]{1,0:T(8,128)(2,1)S(1)} %copy-done.13), channel_id=1, source_target_pairs={{0,1},{1,0},{2,3},{3,2},{4,5},{5,4},{6,7},{7,6},{8,9},{9,8},{10,11... | collective-permute-start | bytes 3145736 | tf_op jit(solution)/shard_map/ppermute | solution.py:40
  122.0 2.3 %collective-permute-done.8 = bf16[64,8192]{1,0:T(8,128)(2,1)S(1)} collective-permute-done((bf16[64,8192]{1,0:T(8,128)(2,1)S(1)}, bf16[64,8192]{1,0:T(8,128)(2,1)S(1)}, u32[]{:S(2)}, u32[]{:S(2)}) %collective-permute-start.8) | collective-permute-done | bytes 1048608 | tf_op jit(solution)/shard_map/ppermute | solution.py:40
  124.3 0.8 core_sum.1
  125.1 2.6 %collective-permute-start.9 = (bf16[16,8192]{1,0:T(8,128)(2,1)S(1)}, bf16[16,8192]{1,0:T(8,128)(2,1)S(1)}, u32[]{:S(2)}, u32[]{:S(2)}) collective-permute-start(bf16[16,8192]{1,0:T(8,128)(2,1)S(1)} %get-tuple-element.80), channel_id=1, source_target_pairs={{0,2},{2,4},{4,6},{6,0},{1,3},{3,5},{5,7},{7,1},{8,10},{10,12},{12... | collective-permute-start | bytes 786440 | tf_op jit(solution)/shard_map/ppermute | solution.py:40
  127.7 3.9 %collective-permute-start.10 = (bf16[16,8192]{1,0:T(8,128)(2,1)S(1)}, bf16[16,8192]{1,0:T(8,128)(2,1)S(1)}, u32[]{:S(2)}, u32[]{:S(2)}) collective-permute-start(bf16[16,8192]{1,0:T(8,128)(2,1)S(1)} %get-tuple-element.81), channel_id=1, source_target_pairs={{0,4},{2,6},{4,0},{6,2},{1,5},{3,7},{5,1},{7,3},{8,12},{10,14},{12... | collective-permute-start | bytes 786440 | tf_op jit(solution)/shard_map/ppermute | solution.py:40
  131.7 2.6 %collective-permute-start.11 = (bf16[16,8192]{1,0:T(8,128)(2,1)S(1)}, bf16[16,8192]{1,0:T(8,128)(2,1)S(1)}, u32[]{:S(2)}, u32[]{:S(2)}) collective-permute-start(bf16[16,8192]{1,0:T(8,128)(2,1)S(1)} %get-tuple-element.82), channel_id=1, source_target_pairs={{0,6},{2,0},{4,2},{6,4},{1,7},{3,1},{5,3},{7,5},{8,14},{10,8},{12,... | collective-permute-start | bytes 786440 | tf_op jit(solution)/shard_map/ppermute | solution.py:40
  134.3 7.1 %all-to-all-done.2.arrived_ref = bf16[8,2,128,128]{3,2,1,0:T(8,128)(2,1)S(1)} async-done(((bf16[8,2,128,128]{3,2,1,0:T(8,128)(2,1)}), bf16[8,2,128,128]{3,2,1,0:T(8,128)(2,1)S(1)}, u32[]{:S(2)}, u32[]{:S(2)}) %all-to-all-start.2) | async-done | bytes 524320 | tf_op jit(solution)/shard_map/all_to_all | solution.py:44
  141.4 0.8 own_grad.1
  142.2 1.4 collective-permute-done.11
  143.6 0.8 add_convert_fusion
  144.4 0.0 all-gather.5.cloned.1.call-update
  144.4 21.3 %all_to_all.27.arrived_ref = f32[32,8,128]{2,1,0:T(8,128)S(1)} all-to-all(f32[32,8,128]{2,1,0:T(8,128)S(1)} %get-tuple-element.83), channel_id=1, replica_groups=mesh['y'=4,'m'=8,'p'=2,'x'=4,'core'=2] {'y','x','core'}, dimensions={0} | all-to-all | bytes 262144 | tf_op jit(solution)/shard_map/all_to_all | solution.py:44
  165.7 0.7 relay.1
  166.4 5.9 %all-to-all-start.4 = ((f32[16,8,128]{2,1,0:T(8,128)}), f32[16,8,128]{2,1,0:T(8,128)S(1)}, u32[]{:S(2)}, u32[]{:S(2)}) async-start(f32[16,8,128]{2,1,0:T(8,128)} %relay.1), calls=%async_computation.4 | async-start | bytes 131072 | tf_op jit(solution)/shard_map/all_to_all | solution.py:44
  172.3 0.0 copy-start.1
  172.3 0.0 copy-start.7
  172.4 0.0 copy-start.8
  172.4 7.0 %all-gather.5.cloned.1.call-done.in_ref = bf16[128,8192]{1,0:T(8,128)(2,1)} async-done(((bf16[16,8192]{1,0:T(8,128)(2,1)}), bf16[128,8192]{1,0:T(8,128)(2,1)}) %all-gather.5.cloned.1.call-update) | async-done | bytes 2097168 | tf_op jit(solution)/shard_map/all_gather | solution.py:351
  179.4 2.4 %result.1 = bf16[128,8192]{1,0:T(8,128)(2,1)} custom-call(bf16[128,8192]{1,0:T(8,128)(2,1)} %all-gather.5.cloned.1.call-done.in_ref), custom_call_target="tpu_custom_call" | custom-call | bytes 4194304 | tf_op jit(solution)/shard_map/result/pallas_call | solution.py:352
  181.8 2.1 %all-to-all-done.4.refs_2_ = f32[16,8,128]{2,1,0:T(8,128)S(1)} async-done(((f32[16,8,128]{2,1,0:T(8,128)}), f32[16,8,128]{2,1,0:T(8,128)S(1)}, u32[]{:S(2)}, u32[]{:S(2)}) %all-to-all-start.4) | async-done | bytes 65568 | tf_op jit(solution)/shard_map/all_to_all | solution.py:44
  183.9 1.5 adam.1
  (19 shorter events, 0.1 us)
Async XLA Ops:
  7.2 85.6 %all-gather.3.cloned.1.call-start = ((), (), s32[]{:S(2)}) async-start(), calls=%async_computation.5 | async-start | bytes 4456448 | tf_op jit(solution)/shard_map/all_gather | solution.py:280
  7.2 0.9 copy-start
  8.3 33.7 %copy-start.2 = (bf16[128,1792]{1,0:T(8,128)(2,1)S(1)}, bf16[128,1792]{1,0:T(8,128)(2,1)}, u32[]{:S(2)}) copy-start(bf16[128,1792]{1,0:T(8,128)(2,1)} %gate_ref.1) | copy-start | bytes 1376260
  8.3 33.6 %copy-start.3 = (bf16[128,1792]{1,0:T(8,128)(2,1)S(1)}, bf16[128,1792]{1,0:T(8,128)(2,1)}, u32[]{:S(2)}) copy-start(bf16[128,1792]{1,0:T(8,128)(2,1)} %up_ref.1) | copy-start | bytes 1376260
  8.3 33.6 %copy-start.4 = (bf16[128,1792]{1,0:T(8,128)(2,1)S(1)}, bf16[128,1792]{1,0:T(8,128)(2,1)}, u32[]{:S(2)}) copy-start(bf16[128,1792]{1,0:T(8,128)(2,1)} %hidden_ref.1) | copy-start | bytes 1376260
  18.9 25.2 %copy-start.9 = (s32[1,64]{1,0:T(1,128)S(1)}, s32[1,64]{1,0:T(1,128)}, u32[]{:S(2)}) copy-start(s32[1,64]{1,0:T(1,128)} %refs_1_.1) | copy-start | bytes 772
  18.9 25.2 %copy-start.10 = (s32[1,112]{1,0:T(1,128)S(1)}, s32[1,112]{1,0:T(1,128)}, u32[]{:S(2)}) copy-start(s32[1,112]{1,0:T(1,128)} %rows_ref.7) | copy-start | bytes 1348
  18.9 25.2 %copy-start.11 = (s32[1,112]{1,0:T(1,128)S(1)}, s32[1,112]{1,0:T(1,128)}, u32[]{:S(2)}) copy-start(s32[1,112]{1,0:T(1,128)} %cols_ref.7) | copy-start | bytes 1348
  34.0 10.1 %collective-permute-start = (bf16[4,128,1024]{2,1,0:T(8,128)(2,1)S(1)}, bf16[4,128,1024]{2,1,0:T(8,128)(2,1)S(1)}, u32[]{:S(2)}, u32[]{:S(2)}) collective-permute-start(bf16[4,128,1024]{2,1,0:T(8,128)(2,1)S(1)} %all_to_all.26.own_ref), channel_id=1, source_target_pairs={{0,1},{1,0},{2,3},{3,2},{4,5},{5,4},{6,7},{7,6},{8,9},{9,8},{10,11... | collective-permute-start | bytes 3145736 | tf_op jit(solution)/shard_map/ppermute | solution.py:40
  43.0 11.7 %copy-start.5 = (bf16[14,128,128]{2,1,0:T(8,128)(2,1)}, bf16[14,128,128]{2,1,0:T(8,128)(2,1)S(1)}, u32[]{:S(2)}) copy-start(bf16[14,128,128]{2,1,0:T(8,128)(2,1)S(1)} %get-tuple-element.72.grad_ref) | copy-start | bytes 1376260
  46.2 16.9 %collective-permute-start.1 = (bf16[16,128,128]{2,1,0:T(8,128)(2,1)S(1)}, bf16[16,128,128]{2,1,0:T(8,128)(2,1)S(1)}, u32[]{:S(2)}, u32[]{:S(2)}) collective-permute-start(bf16[16,128,128]{2,1,0:T(8,128)(2,1)S(1)} %get-tuple-element.61), channel_id=1, source_target_pairs={{0,128},{128,256},{256,384},{384,0},{1,129},{129,257},{257,385},{3... | collective-permute-start | bytes 1572872 | tf_op jit(solution)/shard_map/ppermute | solution.py:40
  48.5 14.8 %collective-permute-start.2 = (bf16[16,128,128]{2,1,0:T(8,128)(2,1)S(1)}, bf16[16,128,128]{2,1,0:T(8,128)(2,1)S(1)}, u32[]{:S(2)}, u32[]{:S(2)}) collective-permute-start(bf16[16,128,128]{2,1,0:T(8,128)(2,1)S(1)} %get-tuple-element.63), channel_id=1, source_target_pairs={{0,384},{128,0},{256,128},{384,256},{1,385},{129,1},{257,129},{385... | collective-permute-start | bytes 1572872 | tf_op jit(solution)/shard_map/ppermute | solution.py:40
  57.8 16.7 %collective-permute-start.4 = (bf16[16,128,128]{2,1,0:T(8,128)(2,1)S(1)}, bf16[16,128,128]{2,1,0:T(8,128)(2,1)S(1)}, u32[]{:S(2)}, u32[]{:S(2)}) collective-permute-start(bf16[16,128,128]{2,1,0:T(8,128)(2,1)S(1)} %get-tuple-element.65), channel_id=1, source_target_pairs={{0,384},{128,0},{256,128},{384,256},{1,385},{129,1},{257,129},{385... | collective-permute-start | bytes 1572872 | tf_op jit(solution)/shard_map/ppermute | solution.py:40
  59.7 15.7 %collective-permute-start.5 = (bf16[16,128,128]{2,1,0:T(8,128)(2,1)S(1)}, bf16[16,128,128]{2,1,0:T(8,128)(2,1)S(1)}, u32[]{:S(2)}, u32[]{:S(2)}) collective-permute-start(bf16[16,128,128]{2,1,0:T(8,128)(2,1)S(1)} %get-tuple-element.66), channel_id=1, source_target_pairs={{0,128},{128,256},{256,384},{384,0},{1,129},{129,257},{257,385},{3... | collective-permute-start | bytes 1572872 | tf_op jit(solution)/shard_map/ppermute | solution.py:40
  63.5 29.3 %copy-start.6 = (bf16[14,128,128]{2,1,0:T(8,128)(2,1)S(1)}, bf16[14,128,128]{2,1,0:T(8,128)(2,1)}, u32[]{:S(2)}) copy-start(bf16[14,128,128]{2,1,0:T(8,128)(2,1)} %copy-done.5) | copy-start | bytes 1376260
  63.5 23.2 %collective-permute-start.3 = (bf16[16,128,128]{2,1,0:T(8,128)(2,1)S(1)}, bf16[16,128,128]{2,1,0:T(8,128)(2,1)S(1)}, u32[]{:S(2)}, u32[]{:S(2)}) collective-permute-start(bf16[16,128,128]{2,1,0:T(8,128)(2,1)S(1)} %get-tuple-element.64), channel_id=1, source_target_pairs={{0,128},{128,256},{256,384},{384,0},{1,129},{129,257},{257,385},{3... | collective-permute-start | bytes 1572872 | tf_op jit(solution)/shard_map/ppermute | solution.py:40
  65.7 21.0 %collective-permute-start.6 = (bf16[16,128,128]{2,1,0:T(8,128)(2,1)S(1)}, bf16[16,128,128]{2,1,0:T(8,128)(2,1)S(1)}, u32[]{:S(2)}, u32[]{:S(2)}) collective-permute-start(bf16[16,128,128]{2,1,0:T(8,128)(2,1)S(1)} %get-tuple-element.67), channel_id=1, source_target_pairs={{0,384},{128,0},{256,128},{384,256},{1,385},{129,1},{257,129},{385... | collective-permute-start | bytes 1572872 | tf_op jit(solution)/shard_map/ppermute | solution.py:40
  87.6 18.3 %collective-permute-start.7 = (bf16[8,2,128,128]{3,2,1,0:T(8,128)(2,1)S(1)}, bf16[8,2,128,128]{3,2,1,0:T(8,128)(2,1)S(1)}, u32[]{:S(2)}, u32[]{:S(2)}) collective-permute-start(bf16[8,2,128,128]{3,2,1,0:T(8,128)(2,1)S(1)} %get-tuple-element.71), channel_id=1, source_target_pairs={{0,8},{8,0},{1,9},{9,1},{2,10},{10,2},{3,11},{11,3},{4,12},{12,4},... | collective-permute-start | bytes 1572872 | tf_op jit(solution)/shard_map/ppermute | solution.py:40
  97.6 1.0 copy-start.12
  105.9 11.5 %copy-start.13 = (bf16[64,8192]{1,0:T(8,128)(2,1)S(1)}, bf16[64,8192]{1,0:T(8,128)(2,1)}, u32[]{:S(2)}) copy-start(bf16[64,8192]{1,0:T(8,128)(2,1)} %copy-done.12) | copy-start | bytes 3145732
  106.8 34.6 %all-to-all-start.2 = ((bf16[8,2,128,128]{3,2,1,0:T(8,128)(2,1)}), bf16[8,2,128,128]{3,2,1,0:T(8,128)(2,1)S(1)}, u32[]{:S(2)}, u32[]{:S(2)}) async-start(bf16[8,2,128,128]{3,2,1,0:T(8,128)(2,1)} %pair_sum.1), calls=%async_computation.2 | async-start | bytes 1048576 | tf_op jit(solution)/shard_map/all_to_all | solution.py:44
  117.3 62.1 %all-gather.5.cloned.1.call-start = ((), (), s32[]{:S(2)}) async-start(), calls=%async_computation.6 | async-start | bytes 2359296 | tf_op jit(solution)/shard_map/all_gather | solution.py:351
  117.4 6.9 %collective-permute-start.8 = (bf16[64,8192]{1,0:T(8,128)(2,1)S(1)}, bf16[64,8192]{1,0:T(8,128)(2,1)S(1)}, u32[]{:S(2)}, u32[]{:S(2)}) collective-permute-start(bf16[64,8192]{1,0:T(8,128)(2,1)S(1)} %copy-done.13), channel_id=1, source_target_pairs={{0,1},{1,0},{2,3},{3,2},{4,5},{5,4},{6,7},{7,6},{8,9},{9,8},{10,11... | collective-permute-start | bytes 3145736 | tf_op jit(solution)/shard_map/ppermute | solution.py:40
  125.1 17.1 %collective-permute-start.9 = (bf16[16,8192]{1,0:T(8,128)(2,1)S(1)}, bf16[16,8192]{1,0:T(8,128)(2,1)S(1)}, u32[]{:S(2)}, u32[]{:S(2)}) collective-permute-start(bf16[16,8192]{1,0:T(8,128)(2,1)S(1)} %get-tuple-element.80), channel_id=1, source_target_pairs={{0,2},{2,4},{4,6},{6,0},{1,3},{3,5},{5,7},{7,1},{8,10},{10,12},{12... | collective-permute-start | bytes 786440 | tf_op jit(solution)/shard_map/ppermute | solution.py:40
  127.7 14.5 %collective-permute-start.10 = (bf16[16,8192]{1,0:T(8,128)(2,1)S(1)}, bf16[16,8192]{1,0:T(8,128)(2,1)S(1)}, u32[]{:S(2)}, u32[]{:S(2)}) collective-permute-start(bf16[16,8192]{1,0:T(8,128)(2,1)S(1)} %get-tuple-element.81), channel_id=1, source_target_pairs={{0,4},{2,6},{4,0},{6,2},{1,5},{3,7},{5,1},{7,3},{8,12},{10,14},{12... | collective-permute-start | bytes 786440 | tf_op jit(solution)/shard_map/ppermute | solution.py:40
  131.7 11.9 %collective-permute-start.11 = (bf16[16,8192]{1,0:T(8,128)(2,1)S(1)}, bf16[16,8192]{1,0:T(8,128)(2,1)S(1)}, u32[]{:S(2)}, u32[]{:S(2)}) collective-permute-start(bf16[16,8192]{1,0:T(8,128)(2,1)S(1)} %get-tuple-element.82), channel_id=1, source_target_pairs={{0,6},{2,0},{4,2},{6,4},{1,7},{3,1},{5,3},{7,5},{8,14},{10,8},{12,... | collective-permute-start | bytes 786440 | tf_op jit(solution)/shard_map/ppermute | solution.py:40
  166.4 17.5 %all-to-all-start.4 = ((f32[16,8,128]{2,1,0:T(8,128)}), f32[16,8,128]{2,1,0:T(8,128)S(1)}, u32[]{:S(2)}, u32[]{:S(2)}) async-start(f32[16,8,128]{2,1,0:T(8,128)} %relay.1), calls=%async_computation.4 | async-start | bytes 131072 | tf_op jit(solution)/shard_map/all_to_all | solution.py:44
  172.3 11.6 %copy-start.1 = (f32[1,2,128,128]{3,2,1,0:T(8,128)S(1)}, f32[1,2,128,128]{3,2,1,0:T(8,128)}, u32[]{:S(2)}) copy-start(f32[1,2,128,128]{3,2,1,0:T(8,128)} %refs_4_.1) | copy-start | bytes 393220
  172.3 11.6 %copy-start.7 = (f32[1,2,128,128]{3,2,1,0:T(8,128)S(1)}, f32[1,2,128,128]{3,2,1,0:T(8,128)}, u32[]{:S(2)}) copy-start(f32[1,2,128,128]{3,2,1,0:T(8,128)} %refs_5_.1) | copy-start | bytes 393220
  172.4 11.6 %copy-start.8 = (f32[1,2,128,128]{3,2,1,0:T(8,128)S(1)}, f32[1,2,128,128]{3,2,1,0:T(8,128)}, u32[]{:S(2)}) copy-start(f32[1,2,128,128]{3,2,1,0:T(8,128)} %refs_6_.1) | copy-start | bytes 393220
Sparse Core Ops, SparseCore 0:
  19.0 73.7 all-gather.2
  144.6 34.8 all-gather.4

commit v9 on v8

--- a/solution.py
+++ b/solution.py
@@ -195,14 +195,15 @@
 
 
 def contrib_kernel(
-    rows_ref, cols_ref, counts_ref, grad_ref, delta_ref, stay_ref, give_ref, places_ref
+    ids_ref, rows_ref, cols_ref, counts_ref, grad_ref, delta_ref, stay_ref, give_ref, places_ref
 ):
     stay_ref[...] = jnp.zeros_like(stay_ref)
     give_ref[...] = jnp.zeros_like(give_ref)
     half = stay_ref.shape[0]
+    y = ids_ref[0]
 
     def owner_step(owner, start):
-        place = ((owner & (NZ - 1)) * NY + owner // NZ) * SLOT_CAP
+        place = ((owner & (NZ - 1)) * NY + ((owner // NZ - y) & (NY - 1))) * SLOT_CAP
         places_ref[start] = place
         places_ref[start + 1] = place + 1
         return start + counts_ref[0, owner]
@@ -276,7 +277,10 @@
     delta_half = kernel_call(
         turn_kernel, "turn", SHAPE(delta_value.shape[1:], BF16), [VMEM], VMEM
     )(delta_value)
-    delta_y = spread(delta_half, "y").reshape(NY * SLOT_CAP, TILE, TILE)
+    delta_y = jnp.concatenate(
+        [delta_half] + [shift(delta_half, "y", -away) for away in range(1, NY)], axis=0
+    )
+    _, delta_y = lax.optimization_barrier((own, delta_y))
     delta_all = lax.all_gather(delta_y, Z, axis=0, tiled=True)
 
     grads, turned = kernel_call(
@@ -319,15 +323,9 @@
         y_sum_kernel, "y_sum", [eight] * 2, [SMEM] + [VMEM] * 5, [VMEM] * 2
     )(ids, *map(parted, (mine, below_low, above_low, below_high, above_high)))
 
-    keep, grads = lax.optimization_barrier((keep, grads))
     partner = shift(give, "p", 1)
-    stay, give = kernel_call(
-        contrib_kernel, "contribs", [SHAPE((tokens // 2, width), BF16)] * 2,
-        [SMEM] * 3 + [VMEM] * 2, [VMEM] * 2, [pltpu.SMEM((tile_total + 8,), jnp.int32)],
-        moved=1 << 12,
-    )(*lists, grads, delta_all)
-    partner, give = lax.optimization_barrier((partner, give))
     pairs = kernel_call(pair_sum_kernel, "pair_sum", eight, [VMEM] * 2, VMEM)(keep, partner)
+    pairs, grads = lax.optimization_barrier((pairs, grads))
     arrived = exchange(pairs, "m")
     own_grad, squares = kernel_call(
         own_grad_kernel, "own_grad",
@@ -336,8 +334,13 @@
     )(ids, owner_counts, arrived)
 
 
+    stay, give = kernel_call(
+        contrib_kernel, "contribs", [SHAPE((tokens // 2, width), BF16)] * 2,
+        [SMEM] * 4 + [VMEM] * 2, [VMEM] * 2, [pltpu.SMEM((tile_total + 8,), jnp.int32)],
+        moved=1 << 12,
+    )(ids, *lists, grads, delta_all)
+
     rows = tokens // (2 * NX)
-    _, give = lax.optimization_barrier((pairs, give))
     taken = shift(give, "core", 1)
     share, *others = kernel_call(
         core_sum_kernel, "core_sum", [SHAPE((rows, width), BF16)] * NX,

time: 193 us -> 201 us (1.041)
  blocking collectives: 45.8 us -> 15.5 us
  starting transfers between devices: 60.7 us -> 81.2 us
  waiting for transfers between devices: 45.9 us -> 62.3 us
    all_to_all x3 -> x1, blocking collectives: 45.8 us -> 15.5 us  [exchange(): return lax.all_to_all(value, axis, split_axis=0, concat_axis=0, tiled=True)]
    ppermute x12 -> x15, waiting for transfers between devices: 27.9 us -> 49.6 us  [shift(): lax.ppermute(value, axis, [(i, (i + step) % size) for i in range(size)])]
    all_to_all x2 -> x3, starting transfers between devices: 16.5 us -> 29 us  [exchange(): return lax.all_to_all(value, axis, split_axis=0, concat_axis=0, tiled=True)]
    ppermute x12 -> x15, starting transfers between devices: 44.2 us -> 52.1 us  [shift(): lax.ppermute(value, axis, [(i, (i + step) % size) for i in range(size)])]
    all_to_all x2 -> x3, waiting for transfers between devices: 9.23 us -> 5.6 us  [exchange(): return lax.all_to_all(value, axis, split_axis=0, concat_axis=0, tiled=True)]
  transfers between devices with their start and end apart: 16 -> 20, of which waited for: 12 -> 12; matrix products, arithmetic and copies ran while one was open for 1% -> 0% of each run, Pallas kernels for 10% -> 10%
where the time goes in v9:
time: 201 us; the launch traced here: 200 us
  starting transfers between devices  81.2 us (40%)
  waiting for transfers between devices  62.3 us (31%)
  Pallas kernels  21.3 us (11%)
  blocking collectives  15.5 us (8%)
  between operations  14.4 us (7%)
  local copies, waits for them, and re-layouts  4.18 us (2%)
    ppermute x15, starting transfers between devices, shift(): lax.ppermute(value, axis, [(i, (i + step) % size) for i in range(size)])  52.1 us
    ppermute x15, waiting for transfers between devices, shift(): lax.ppermute(value, axis, [(i, (i + step) % size) for i in range(size)])  49.6 us
    all_to_all x3, starting transfers between devices, exchange(): return lax.all_to_all(value, axis, split_axis=0, concat_axis=0, tiled=True)  29 us
    all_to_all x1, blocking collectives, exchange(): return lax.all_to_all(value, axis, split_axis=0, concat_axis=0, tiled=True)  15.5 us
    pallas_call x3, Pallas kernels, terms(): kernel_call(functools.partial(tile_kernel, parts), 'tiles', [SHAPE(((last...  7.19 us
    all_gather x1, waiting for transfers between devices, body(): lax.all_gather(share.astype(BF16), ('x', 'core'), axis=0, tiled=True)  7.05 us
    all_to_all x3, waiting for transfers between devices, exchange(): return lax.all_to_all(value, axis, split_axis=0, concat_axis=0, tiled=True)  5.6 us
    pallas_call x1, Pallas kernels, body(): kernel_call(contrib_kernel, 'contribs', [SHAPE((tokens // 2, width), BF16...  4.72 us
  transfers between devices with their start and end apart: 20, of which 12 were waited for; matrix products, arithmetic and copies ran while one was open for 0% of the time, Pallas kernels for 10%

profile of v9, /device:TPU:1, one launch (start us, length us, event | category | flops | bytes accessed | tf_op | source)
XLA Modules:
  0.0 200.4 jit_solution(16845506602213992382)
XLA Ops:
  7.2 2.1 %broadcast_in_dim.2 = bf16[4,128,1024]{2,1,0:T(8,128)(2,1)} broadcast(bf16[128,1024]{1,0:T(8,128)(2,1)} %param.10), dimensions={1,2} | broadcast | bytes 1310720 | tf_op jit(solution)/shard_map/broadcast_in_dim | solution.py:48
  9.3 5.0 %all-to-all-start = ((bf16[4,128,1024]{2,1,0:T(8,128)(2,1)}), bf16[4,128,1024]{2,1,0:T(8,128)(2,1)S(1)}, u32[]{:S(2)}, u32[]{:S(2)}) async-start(bf16[4,128,1024]{2,1,0:T(8,128)(2,1)} %broadcast_in_dim.2), calls=%async_computation | async-start | bytes 2097152 | tf_op jit(solution)/shard_map/all_to_all | solution.py:44
  14.3 0.1 turn.1
  14.4 3.2 %collective-permute-start.10 = (bf16[2,128,128]{2,1,0:T(8,128)(2,1)S(1)}, bf16[2,128,128]{2,1,0:T(8,128)(2,1)S(1)}, u32[]{:S(2)}, u32[]{:S(2)}) collective-permute-start(bf16[2,128,128]{2,1,0:T(8,128)(2,1)S(1)} %turn.1), channel_id=1, source_target_pairs={{0,128},{128,256},{256,384},{384,0},{1,129},{129,257},{257,385},{3... | collective-permute-start | bytes 196616 | tf_op jit(solution)/shard_map/ppermute | solution.py:40
  17.6 4.5 %collective-permute-start.9 = (bf16[2,128,128]{2,1,0:T(8,128)(2,1)S(1)}, bf16[2,128,128]{2,1,0:T(8,128)(2,1)S(1)}, u32[]{:S(2)}, u32[]{:S(2)}) collective-permute-start(bf16[2,128,128]{2,1,0:T(8,128)(2,1)S(1)} %turn.1), channel_id=1, source_target_pairs={{0,256},{128,384},{256,0},{384,128},{1,257},{129,385},{257,1},{385... | collective-permute-start | bytes 196616 | tf_op jit(solution)/shard_map/ppermute | solution.py:40
  22.1 3.0 %collective-permute-start.8 = (bf16[2,128,128]{2,1,0:T(8,128)(2,1)S(1)}, bf16[2,128,128]{2,1,0:T(8,128)(2,1)S(1)}, u32[]{:S(2)}, u32[]{:S(2)}) collective-permute-start(bf16[2,128,128]{2,1,0:T(8,128)(2,1)S(1)} %turn.1), channel_id=1, source_target_pairs={{0,384},{128,0},{256,128},{384,256},{1,385},{129,1},{257,129},{385... | collective-permute-start | bytes 196616 | tf_op jit(solution)/shard_map/ppermute | solution.py:40
  25.1 0.0 collective-permute-done.10
  25.1 0.0 collective-permute-done.9
  25.1 2.1 %collective-permute-done.8 = bf16[2,128,128]{2,1,0:T(8,128)(2,1)S(1)} collective-permute-done((bf16[2,128,128]{2,1,0:T(8,128)(2,1)S(1)}, bf16[2,128,128]{2,1,0:T(8,128)(2,1)S(1)}, u32[]{:S(2)}, u32[]{:S(2)}) %collective-permute-start.8) | collective-permute-done | bytes 65568 | tf_op jit(solution)/shard_map/ppermute | solution.py:40
  27.2 0.7 pad_maximum_fusion
  27.9 0.0 all-to-all-done.own_ref
  27.9 0.0 all-gather.3.cloned.1.call-update
  28.0 6.8 %collective-permute-start = (bf16[4,128,1024]{2,1,0:T(8,128)(2,1)S(1)}, bf16[4,128,1024]{2,1,0:T(8,128)(2,1)S(1)}, u32[]{:S(2)}, u32[]{:S(2)}) collective-permute-start(bf16[4,128,1024]{2,1,0:T(8,128)(2,1)S(1)} %all-to-all-done.own_ref), channel_id=1, source_target_pairs={{0,1},{1,0},{2,3},{3,2},{4,5},{5,4},{6,7},{7,6},{8,9},{9,8},{10,11... | collective-permute-start | bytes 3145736 | tf_op jit(solution)/shard_map/ppermute | solution.py:40
  34.8 0.1 pad_add_fusion.ids_ref.refs_0_
  34.9 1.0 copy-done.2
  35.9 1.0 copy-done.3
  36.9 1.1 gate.1
  38.0 0.0 collective-permute-done.other_ref
  38.1 2.1 %tiles.3 = (bf16[16,128,128]{2,1,0:T(8,128)(2,1)S(1)}, bf16[16,128,128]{2,1,0:T(8,128)(2,1)S(1)}) custom-call(s32[4]{0:T(128)S(1)} %pad_add_fusion.ids_ref.refs_0_, s32[1,112]{1,0:T(1,128)S(1)} %copy-done.7, s32[1,112]{1,0:T(1,128)S(1)} %copy-done.8, s32[1,64]{1,0:T(1,128)S(1)} %copy-done.6, bf16[4,128,1024]{2,1,0:T(8,128)(2,1)S(1)} %all-to-all-done.own_ref, ...), custom_call_target="tpu_custom_call" | custom-call | flops 117440512 | bytes 2097152 | tf_op jit(solution)/shard_map/tiles/pallas_call | solution.py:299
  40.1 3.6 %collective-permute-start.1 = (bf16[16,128,128]{2,1,0:T(8,128)(2,1)S(1)}, bf16[16,128,128]{2,1,0:T(8,128)(2,1)S(1)}, u32[]{:S(2)}, u32[]{:S(2)}) collective-permute-start(bf16[16,128,128]{2,1,0:T(8,128)(2,1)S(1)} %get-tuple-element.59), channel_id=1, source_target_pairs={{0,128},{128,256},{256,384},{384,0},{1,129},{129,257},{257,385},{3... | collective-permute-start | bytes 1572872 | tf_op jit(solution)/shard_map/ppermute | solution.py:40
  43.8 2.8 %collective-permute-start.2 = (bf16[16,128,128]{2,1,0:T(8,128)(2,1)S(1)}, bf16[16,128,128]{2,1,0:T(8,128)(2,1)S(1)}, u32[]{:S(2)}, u32[]{:S(2)}) collective-permute-start(bf16[16,128,128]{2,1,0:T(8,128)(2,1)S(1)} %get-tuple-element.61), channel_id=1, source_target_pairs={{0,384},{128,0},{256,128},{384,256},{1,385},{129,1},{257,129},{385... | collective-permute-start | bytes 1572872 | tf_op jit(solution)/shard_map/ppermute | solution.py:40
  46.6 2.1 %tiles.4 = (bf16[16,128,128]{2,1,0:T(8,128)(2,1)S(1)}, bf16[16,128,128]{2,1,0:T(8,128)(2,1)S(1)}) custom-call(s32[4]{0:T(128)S(1)} %pad_add_fusion.ids_ref.refs_0_, s32[1,112]{1,0:T(1,128)S(1)} %copy-done.7, s32[1,112]{1,0:T(1,128)S(1)} %copy-done.8, s32[1,64]{1,0:T(1,128)S(1)} %copy-done.6, bf16[4,128,1024]{2,1,0:T(8,128)(2,1)S(1)} %all-to-all-done.own_ref, ...), custom_call_target="tpu_custom_call" | custom-call | flops 117440512 | bytes 2097152 | tf_op jit(solution)/shard_map/tiles/pallas_call | solution.py:299
  48.7 3.1 %tiles.5 = (bf16[16,128,128]{2,1,0:T(8,128)(2,1)S(1)}, bf16[16,128,128]{2,1,0:T(8,128)(2,1)S(1)}, bf16[32,128,128]{2,1,0:T(8,128)(2,1)S(1)}) custom-call(s32[4]{0:T(128)S(1)} %pad_add_fusion.ids_ref.refs_0_, s32[1,112]{1,0:T(1,128)S(1)} %copy-done.7, s32[1,112]{1,0:T(1,128)S(1)} %copy-done.8, s32[1,64]{1,0:T(1,128)S(1)} %copy-done.6, ...), custom_call_target="tpu_custom_call" | custom-call | flops 117440512 | bytes 2097152 | tf_op jit(solution)/shard_map/tiles/pallas_call | solution.py:299
  51.8 2.8 %collective-permute-start.4 = (bf16[16,128,128]{2,1,0:T(8,128)(2,1)S(1)}, bf16[16,128,128]{2,1,0:T(8,128)(2,1)S(1)}, u32[]{:S(2)}, u32[]{:S(2)}) collective-permute-start(bf16[16,128,128]{2,1,0:T(8,128)(2,1)S(1)} %get-tuple-element.63), channel_id=1, source_target_pairs={{0,384},{128,0},{256,128},{384,256},{1,385},{129,1},{257,129},{385... | collective-permute-start | bytes 1572872 | tf_op jit(solution)/shard_map/ppermute | solution.py:40
  54.6 2.5 %collective-permute-start.5 = (bf16[16,128,128]{2,1,0:T(8,128)(2,1)S(1)}, bf16[16,128,128]{2,1,0:T(8,128)(2,1)S(1)}, u32[]{:S(2)}, u32[]{:S(2)}) collective-permute-start(bf16[16,128,128]{2,1,0:T(8,128)(2,1)S(1)} %get-tuple-element.64), channel_id=1, source_target_pairs={{0,128},{128,256},{256,384},{384,0},{1,129},{129,257},{257,385},{3... | collective-permute-start | bytes 1572872 | tf_op jit(solution)/shard_map/ppermute | solution.py:40
  57.1 0.0 collective-permute-done.1.far_low_ref
  57.1 1.9 collective-permute-done.2.far_high_ref
  59.0 0.2 passing.1
  59.3 2.2 %collective-permute-start.3 = (bf16[16,128,128]{2,1,0:T(8,128)(2,1)S(1)}, bf16[16,128,128]{2,1,0:T(8,128)(2,1)S(1)}, u32[]{:S(2)}, u32[]{:S(2)}) collective-permute-start(bf16[16,128,128]{2,1,0:T(8,128)(2,1)S(1)} %get-tuple-element.62), channel_id=1, source_target_pairs={{0,128},{128,256},{256,384},{384,0},{1,129},{129,257},{257,385},{3... | collective-permute-start | bytes 1572872 | tf_op jit(solution)/shard_map/ppermute | solution.py:40
  61.5 4.3 %collective-permute-start.6 = (bf16[16,128,128]{2,1,0:T(8,128)(2,1)S(1)}, bf16[16,128,128]{2,1,0:T(8,128)(2,1)S(1)}, u32[]{:S(2)}, u32[]{:S(2)}) collective-permute-start(bf16[16,128,128]{2,1,0:T(8,128)(2,1)S(1)} %get-tuple-element.65), channel_id=1, source_target_pairs={{0,384},{128,0},{256,128},{384,256},{1,385},{129,1},{257,129},{385... | collective-permute-start | bytes 1572872 | tf_op jit(solution)/shard_map/ppermute | solution.py:40
  65.8 4.4 %collective-permute-done.4 = bf16[16,128,128]{2,1,0:T(8,128)(2,1)S(1)} collective-permute-done((bf16[16,128,128]{2,1,0:T(8,128)(2,1)S(1)}, bf16[16,128,128]{2,1,0:T(8,128)(2,1)S(1)}, u32[]{:S(2)}, u32[]{:S(2)}) %collective-permute-start.4) | collective-permute-done | bytes 524320 | tf_op jit(solution)/shard_map/ppermute | solution.py:40
  70.2 0.2 collective-permute-done.5
  70.3 11.3 %collective-permute-done.3 = bf16[16,128,128]{2,1,0:T(8,128)(2,1)S(1)} collective-permute-done((bf16[16,128,128]{2,1,0:T(8,128)(2,1)S(1)}, bf16[16,128,128]{2,1,0:T(8,128)(2,1)S(1)}, u32[]{:S(2)}, u32[]{:S(2)}) %collective-permute-start.3) | collective-permute-done | bytes 524320 | tf_op jit(solution)/shard_map/ppermute | solution.py:40
  81.7 0.0 collective-permute-done.6
  81.7 0.9 y_sum.1
  82.6 1.9 collective-permute-start.7
  84.5 23.9 %collective-permute-done.7.taken_ref = bf16[8,2,128,128]{3,2,1,0:T(8,128)(2,1)S(1)} collective-permute-done((bf16[8,2,128,128]{3,2,1,0:T(8,128)(2,1)S(1)}, bf16[8,2,128,128]{3,2,1,0:T(8,128)(2,1)S(1)}, u32[]{:S(2)}, u32[]{:S(2)}) %collective-permute-start.7) | collective-permute-done | bytes 524320 | tf_op jit(solution)/shard_map/ppermute | solution.py:40
  108.4 0.9 pair_sum.1
  109.3 12.3 %all-to-all-start.1 = ((bf16[8,2,128,128]{3,2,1,0:T(8,128)(2,1)}), bf16[8,2,128,128]{3,2,1,0:T(8,128)(2,1)S(1)}, u32[]{:S(2)}, u32[]{:S(2)}) async-start(bf16[8,2,128,128]{3,2,1,0:T(8,128)(2,1)} %pair_sum.1), calls=%async_computation.1 | async-start | bytes 1048576 | tf_op jit(solution)/shard_map/all_to_all | solution.py:44
  121.6 0.0 all-gather.5.cloned.1.call-start
  121.7 0.0 all-gather.3.cloned.1.call-done.delta_ref
  121.7 4.7 %contribs.1 = (bf16[64,8192]{1,0:T(8,128)(2,1)S(1)}, bf16[64,8192]{1,0:T(8,128)(2,1)S(1)}) custom-call(s32[4]{0:T(128)S(1)} %pad_add_fusion.ids_ref.refs_0_, s32[1,112]{1,0:T(1,128)S(1)} %copy-done.7, s32[1,112]{1,0:T(1,128)S(1)} %copy-done.8, s32[1,64]{1,0:T(1,128)S(1)} %copy-done.6, bf16[14,128,128]{2,1,0:T(8,128)(2,1)S(1)} %get-tuple-element.71.grad_ref, ...), custom_call_target="tpu_custom_call" | custom-call | bytes 4096 | tf_op jit(solution)/shard_map/contribs/pallas_call | solution.py:337
  126.4 3.9 %collective-permute-start.11 = (bf16[64,8192]{1,0:T(8,128)(2,1)S(1)}, bf16[64,8192]{1,0:T(8,128)(2,1)S(1)}, u32[]{:S(2)}, u32[]{:S(2)}) collective-permute-start(bf16[64,8192]{1,0:T(8,128)(2,1)S(1)} %get-tuple-element.74), channel_id=1, source_target_pairs={{0,1},{1,0},{2,3},{3,2},{4,5},{5,4},{6,7},{7,6},{8,9},{9,8},{10,11... | collective-permute-start | bytes 3145736 | tf_op jit(solution)/shard_map/ppermute | solution.py:40
  130.3 2.3 %collective-permute-done.11 = bf16[64,8192]{1,0:T(8,128)(2,1)S(1)} collective-permute-done((bf16[64,8192]{1,0:T(8,128)(2,1)S(1)}, bf16[64,8192]{1,0:T(8,128)(2,1)S(1)}, u32[]{:S(2)}, u32[]{:S(2)}) %collective-permute-start.11) | collective-permute-done | bytes 1048608 | tf_op jit(solution)/shard_map/ppermute | solution.py:40
  132.6 0.8 core_sum.1
  133.4 3.3 %collective-permute-start.12 = (bf16[16,8192]{1,0:T(8,128)(2,1)S(1)}, bf16[16,8192]{1,0:T(8,128)(2,1)S(1)}, u32[]{:S(2)}, u32[]{:S(2)}) collective-permute-start(bf16[16,8192]{1,0:T(8,128)(2,1)S(1)} %get-tuple-element.76), channel_id=1, source_target_pairs={{0,2},{2,4},{4,6},{6,0},{1,3},{3,5},{5,7},{7,1},{8,10},{10,12},{12... | collective-permute-start | bytes 786440 | tf_op jit(solution)/shard_map/ppermute | solution.py:40
  136.7 4.3 %collective-permute-start.13 = (bf16[16,8192]{1,0:T(8,128)(2,1)S(1)}, bf16[16,8192]{1,0:T(8,128)(2,1)S(1)}, u32[]{:S(2)}, u32[]{:S(2)}) collective-permute-start(bf16[16,8192]{1,0:T(8,128)(2,1)S(1)} %get-tuple-element.77), channel_id=1, source_target_pairs={{0,4},{2,6},{4,0},{6,2},{1,5},{3,7},{5,1},{7,3},{8,12},{10,14},{12... | collective-permute-start | bytes 786440 | tf_op jit(solution)/shard_map/ppermute | solution.py:40
  141.0 2.9 %collective-permute-start.14 = (bf16[16,8192]{1,0:T(8,128)(2,1)S(1)}, bf16[16,8192]{1,0:T(8,128)(2,1)S(1)}, u32[]{:S(2)}, u32[]{:S(2)}) collective-permute-start(bf16[16,8192]{1,0:T(8,128)(2,1)S(1)} %get-tuple-element.78), channel_id=1, source_target_pairs={{0,6},{2,0},{4,2},{6,4},{1,7},{3,1},{5,3},{7,5},{8,14},{10,8},{12,... | collective-permute-start | bytes 786440 | tf_op jit(solution)/shard_map/ppermute | solution.py:40
  143.9 3.5 %all-to-all-done.1.arrived_ref = bf16[8,2,128,128]{3,2,1,0:T(8,128)(2,1)S(1)} async-done(((bf16[8,2,128,128]{3,2,1,0:T(8,128)(2,1)}), bf16[8,2,128,128]{3,2,1,0:T(8,128)(2,1)S(1)}, u32[]{:S(2)}, u32[]{:S(2)}) %all-to-all-start.1) | async-done | bytes 524320 | tf_op jit(solution)/shard_map/all_to_all | solution.py:44
  147.4 0.8 own_grad.1
  148.2 0.0 collective-permute-done.12
  148.2 2.5 %collective-permute-done.13 = bf16[16,8192]{1,0:T(8,128)(2,1)S(1)} collective-permute-done((bf16[16,8192]{1,0:T(8,128)(2,1)S(1)}, bf16[16,8192]{1,0:T(8,128)(2,1)S(1)}, u32[]{:S(2)}, u32[]{:S(2)}) %collective-permute-start.13) | collective-permute-done | bytes 262176 | tf_op jit(solution)/shard_map/ppermute | solution.py:40
  150.8 1.0 collective-permute-done.14
  151.8 0.8 add_convert_fusion
  152.6 0.0 all-gather.5.cloned.1.call-update
  152.6 15.5 %all_to_all.20.arrived_ref = f32[32,8,128]{2,1,0:T(8,128)S(1)} all-to-all(f32[32,8,128]{2,1,0:T(8,128)S(1)} %get-tuple-element.79), channel_id=1, replica_groups=mesh['y'=4,'m'=8,'p'=2,'x'=4,'core'=2] {'y','x','core'}, dimensions={0} | all-to-all | bytes 262144 | tf_op jit(solution)/shard_map/all_to_all | solution.py:44
  168.1 0.7 relay.1
  168.8 11.8 %all-to-all-start.3 = ((f32[16,8,128]{2,1,0:T(8,128)}), f32[16,8,128]{2,1,0:T(8,128)S(1)}, u32[]{:S(2)}, u32[]{:S(2)}) async-start(f32[16,8,128]{2,1,0:T(8,128)} %relay.1), calls=%async_computation.3 | async-start | bytes 131072 | tf_op jit(solution)/shard_map/all_to_all | solution.py:44
  180.5 0.0 copy-start.4
  180.5 0.0 copy-start.5
  180.6 7.1 %all-gather.5.cloned.1.call-done.in_ref = bf16[128,8192]{1,0:T(8,128)(2,1)} async-done(((bf16[16,8192]{1,0:T(8,128)(2,1)}), bf16[128,8192]{1,0:T(8,128)(2,1)}) %all-gather.5.cloned.1.call-update) | async-done | bytes 2097168 | tf_op jit(solution)/shard_map/all_gather | solution.py:354
  187.6 2.4 %result.1 = bf16[128,8192]{1,0:T(8,128)(2,1)} custom-call(bf16[128,8192]{1,0:T(8,128)(2,1)} %all-gather.5.cloned.1.call-done.in_ref), custom_call_target="tpu_custom_call" | custom-call | bytes 4194304 | tf_op jit(solution)/shard_map/result/pallas_call | solution.py:355
  190.0 2.1 %all-to-all-done.3.refs_2_ = f32[16,8,128]{2,1,0:T(8,128)S(1)} async-done(((f32[16,8,128]{2,1,0:T(8,128)}), f32[16,8,128]{2,1,0:T(8,128)S(1)}, u32[]{:S(2)}, u32[]{:S(2)}) %all-to-all-start.3) | async-done | bytes 65568 | tf_op jit(solution)/shard_map/all_to_all | solution.py:44
  192.1 1.5 adam.1
  (15 shorter events, 0.0 us)
Async XLA Ops:
  7.2 7.1 %copy-start = (f32[1,2,128,128]{3,2,1,0:T(8,128)S(1)}, f32[1,2,128,128]{3,2,1,0:T(8,128)}, u32[]{:S(2)}) copy-start(f32[1,2,128,128]{3,2,1,0:T(8,128)} %refs_4_.1) | copy-start | bytes 393220
  7.2 27.7 %copy-start.1 = (bf16[128,1792]{1,0:T(8,128)(2,1)S(1)}, bf16[128,1792]{1,0:T(8,128)(2,1)}, u32[]{:S(2)}) copy-start(bf16[128,1792]{1,0:T(8,128)(2,1)} %gate_ref.1) | copy-start | bytes 1376260
  9.3 28.7 %copy-start.6 = (s32[1,64]{1,0:T(1,128)S(1)}, s32[1,64]{1,0:T(1,128)}, u32[]{:S(2)}) copy-start(s32[1,64]{1,0:T(1,128)} %refs_1_.1) | copy-start | bytes 772
  9.3 28.7 %copy-start.7 = (s32[1,112]{1,0:T(1,128)S(1)}, s32[1,112]{1,0:T(1,128)}, u32[]{:S(2)}) copy-start(s32[1,112]{1,0:T(1,128)} %rows_ref.7) | copy-start | bytes 1348
  9.3 28.7 %copy-start.8 = (s32[1,112]{1,0:T(1,128)S(1)}, s32[1,112]{1,0:T(1,128)}, u32[]{:S(2)}) copy-start(s32[1,112]{1,0:T(1,128)} %cols_ref.7) | copy-start | bytes 1348
  9.3 18.6 %all-to-all-start = ((bf16[4,128,1024]{2,1,0:T(8,128)(2,1)}), bf16[4,128,1024]{2,1,0:T(8,128)(2,1)S(1)}, u32[]{:S(2)}, u32[]{:S(2)}) async-start(bf16[4,128,1024]{2,1,0:T(8,128)(2,1)} %broadcast_in_dim.2), calls=%async_computation | async-start | bytes 2097152 | tf_op jit(solution)/shard_map/all_to_all | solution.py:44
  14.3 107.4 %all-gather.3.cloned.1.call-start = ((), (), s32[]{:S(2)}) async-start(), calls=%async_computation.4 | async-start | bytes 4456448 | tf_op jit(solution)/shard_map/all_gather | solution.py:284
  14.4 10.7 %collective-permute-start.10 = (bf16[2,128,128]{2,1,0:T(8,128)(2,1)S(1)}, bf16[2,128,128]{2,1,0:T(8,128)(2,1)S(1)}, u32[]{:S(2)}, u32[]{:S(2)}) collective-permute-start(bf16[2,128,128]{2,1,0:T(8,128)(2,1)S(1)} %turn.1), channel_id=1, source_target_pairs={{0,128},{128,256},{256,384},{384,0},{1,129},{129,257},{257,385},{3... | collective-permute-start | bytes 196616 | tf_op jit(solution)/shard_map/ppermute | solution.py:40
  17.6 7.5 %collective-permute-start.9 = (bf16[2,128,128]{2,1,0:T(8,128)(2,1)S(1)}, bf16[2,128,128]{2,1,0:T(8,128)(2,1)S(1)}, u32[]{:S(2)}, u32[]{:S(2)}) collective-permute-start(bf16[2,128,128]{2,1,0:T(8,128)(2,1)S(1)} %turn.1), channel_id=1, source_target_pairs={{0,256},{128,384},{256,0},{384,128},{1,257},{129,385},{257,1},{385... | collective-permute-start | bytes 196616 | tf_op jit(solution)/shard_map/ppermute | solution.py:40
  22.1 5.1 %collective-permute-start.8 = (bf16[2,128,128]{2,1,0:T(8,128)(2,1)S(1)}, bf16[2,128,128]{2,1,0:T(8,128)(2,1)S(1)}, u32[]{:S(2)}, u32[]{:S(2)}) collective-permute-start(bf16[2,128,128]{2,1,0:T(8,128)(2,1)S(1)} %turn.1), channel_id=1, source_target_pairs={{0,384},{128,0},{256,128},{384,256},{1,385},{129,1},{257,129},{385... | collective-permute-start | bytes 196616 | tf_op jit(solution)/shard_map/ppermute | solution.py:40
  28.0 10.0 %collective-permute-start = (bf16[4,128,1024]{2,1,0:T(8,128)(2,1)S(1)}, bf16[4,128,1024]{2,1,0:T(8,128)(2,1)S(1)}, u32[]{:S(2)}, u32[]{:S(2)}) collective-permute-start(bf16[4,128,1024]{2,1,0:T(8,128)(2,1)S(1)} %all-to-all-done.own_ref), channel_id=1, source_target_pairs={{0,1},{1,0},{2,3},{3,2},{4,5},{5,4},{6,7},{7,6},{8,9},{9,8},{10,11... | collective-permute-start | bytes 3145736 | tf_op jit(solution)/shard_map/ppermute | solution.py:40
  34.9 1.0 copy-start.2
  35.9 1.0 copy-start.3
  40.1 16.9 %collective-permute-start.1 = (bf16[16,128,128]{2,1,0:T(8,128)(2,1)S(1)}, bf16[16,128,128]{2,1,0:T(8,128)(2,1)S(1)}, u32[]{:S(2)}, u32[]{:S(2)}) collective-permute-start(bf16[16,128,128]{2,1,0:T(8,128)(2,1)S(1)} %get-tuple-element.59), channel_id=1, source_target_pairs={{0,128},{128,256},{256,384},{384,0},{1,129},{129,257},{257,385},{3... | collective-permute-start | bytes 1572872 | tf_op jit(solution)/shard_map/ppermute | solution.py:40
  43.8 15.2 %collective-permute-start.2 = (bf16[16,128,128]{2,1,0:T(8,128)(2,1)S(1)}, bf16[16,128,128]{2,1,0:T(8,128)(2,1)S(1)}, u32[]{:S(2)}, u32[]{:S(2)}) collective-permute-start(bf16[16,128,128]{2,1,0:T(8,128)(2,1)S(1)} %get-tuple-element.61), channel_id=1, source_target_pairs={{0,384},{128,0},{256,128},{384,256},{1,385},{129,1},{257,129},{385... | collective-permute-start | bytes 1572872 | tf_op jit(solution)/shard_map/ppermute | solution.py:40
  51.8 18.4 %collective-permute-start.4 = (bf16[16,128,128]{2,1,0:T(8,128)(2,1)S(1)}, bf16[16,128,128]{2,1,0:T(8,128)(2,1)S(1)}, u32[]{:S(2)}, u32[]{:S(2)}) collective-permute-start(bf16[16,128,128]{2,1,0:T(8,128)(2,1)S(1)} %get-tuple-element.63), channel_id=1, source_target_pairs={{0,384},{128,0},{256,128},{384,256},{1,385},{129,1},{257,129},{385... | collective-permute-start | bytes 1572872 | tf_op jit(solution)/shard_map/ppermute | solution.py:40
  54.6 15.7 %collective-permute-start.5 = (bf16[16,128,128]{2,1,0:T(8,128)(2,1)S(1)}, bf16[16,128,128]{2,1,0:T(8,128)(2,1)S(1)}, u32[]{:S(2)}, u32[]{:S(2)}) collective-permute-start(bf16[16,128,128]{2,1,0:T(8,128)(2,1)S(1)} %get-tuple-element.64), channel_id=1, source_target_pairs={{0,128},{128,256},{256,384},{384,0},{1,129},{129,257},{257,385},{3... | collective-permute-start | bytes 1572872 | tf_op jit(solution)/shard_map/ppermute | solution.py:40
  59.3 22.4 %collective-permute-start.3 = (bf16[16,128,128]{2,1,0:T(8,128)(2,1)S(1)}, bf16[16,128,128]{2,1,0:T(8,128)(2,1)S(1)}, u32[]{:S(2)}, u32[]{:S(2)}) collective-permute-start(bf16[16,128,128]{2,1,0:T(8,128)(2,1)S(1)} %get-tuple-element.62), channel_id=1, source_target_pairs={{0,128},{128,256},{256,384},{384,0},{1,129},{129,257},{257,385},{3... | collective-permute-start | bytes 1572872 | tf_op jit(solution)/shard_map/ppermute | solution.py:40
  61.5 20.1 %collective-permute-start.6 = (bf16[16,128,128]{2,1,0:T(8,128)(2,1)S(1)}, bf16[16,128,128]{2,1,0:T(8,128)(2,1)S(1)}, u32[]{:S(2)}, u32[]{:S(2)}) collective-permute-start(bf16[16,128,128]{2,1,0:T(8,128)(2,1)S(1)} %get-tuple-element.65), channel_id=1, source_target_pairs={{0,384},{128,0},{256,128},{384,256},{1,385},{129,1},{257,129},{385... | collective-permute-start | bytes 1572872 | tf_op jit(solution)/shard_map/ppermute | solution.py:40
  82.6 25.8 %collective-permute-start.7 = (bf16[8,2,128,128]{3,2,1,0:T(8,128)(2,1)S(1)}, bf16[8,2,128,128]{3,2,1,0:T(8,128)(2,1)S(1)}, u32[]{:S(2)}, u32[]{:S(2)}) collective-permute-start(bf16[8,2,128,128]{3,2,1,0:T(8,128)(2,1)S(1)} %get-tuple-element.67), channel_id=1, source_target_pairs={{0,8},{8,0},{1,9},{9,1},{2,10},{10,2},{3,11},{11,3},{4,12},{12,4},... | collective-permute-start | bytes 1572872 | tf_op jit(solution)/shard_map/ppermute | solution.py:40
  109.3 38.1 %all-to-all-start.1 = ((bf16[8,2,128,128]{3,2,1,0:T(8,128)(2,1)}), bf16[8,2,128,128]{3,2,1,0:T(8,128)(2,1)S(1)}, u32[]{:S(2)}, u32[]{:S(2)}) async-start(bf16[8,2,128,128]{3,2,1,0:T(8,128)(2,1)} %pair_sum.1), calls=%async_computation.1 | async-start | bytes 1048576 | tf_op jit(solution)/shard_map/all_to_all | solution.py:44
  121.6 66.0 %all-gather.5.cloned.1.call-start = ((), (), s32[]{:S(2)}) async-start(), calls=%async_computation.5 | async-start | bytes 2359296 | tf_op jit(solution)/shard_map/all_gather | solution.py:354
  126.4 6.2 %collective-permute-start.11 = (bf16[64,8192]{1,0:T(8,128)(2,1)S(1)}, bf16[64,8192]{1,0:T(8,128)(2,1)S(1)}, u32[]{:S(2)}, u32[]{:S(2)}) collective-permute-start(bf16[64,8192]{1,0:T(8,128)(2,1)S(1)} %get-tuple-element.74), channel_id=1, source_target_pairs={{0,1},{1,0},{2,3},{3,2},{4,5},{5,4},{6,7},{7,6},{8,9},{9,8},{10,11... | collective-permute-start | bytes 3145736 | tf_op jit(solution)/shard_map/ppermute | solution.py:40
  133.4 14.8 %collective-permute-start.12 = (bf16[16,8192]{1,0:T(8,128)(2,1)S(1)}, bf16[16,8192]{1,0:T(8,128)(2,1)S(1)}, u32[]{:S(2)}, u32[]{:S(2)}) collective-permute-start(bf16[16,8192]{1,0:T(8,128)(2,1)S(1)} %get-tuple-element.76), channel_id=1, source_target_pairs={{0,2},{2,4},{4,6},{6,0},{1,3},{3,5},{5,7},{7,1},{8,10},{10,12},{12... | collective-permute-start | bytes 786440 | tf_op jit(solution)/shard_map/ppermute | solution.py:40
  136.7 14.1 %collective-permute-start.13 = (bf16[16,8192]{1,0:T(8,128)(2,1)S(1)}, bf16[16,8192]{1,0:T(8,128)(2,1)S(1)}, u32[]{:S(2)}, u32[]{:S(2)}) collective-permute-start(bf16[16,8192]{1,0:T(8,128)(2,1)S(1)} %get-tuple-element.77), channel_id=1, source_target_pairs={{0,4},{2,6},{4,0},{6,2},{1,5},{3,7},{5,1},{7,3},{8,12},{10,14},{12... | collective-permute-start | bytes 786440 | tf_op jit(solution)/shard_map/ppermute | solution.py:40
  141.0 10.7 %collective-permute-start.14 = (bf16[16,8192]{1,0:T(8,128)(2,1)S(1)}, bf16[16,8192]{1,0:T(8,128)(2,1)S(1)}, u32[]{:S(2)}, u32[]{:S(2)}) collective-permute-start(bf16[16,8192]{1,0:T(8,128)(2,1)S(1)} %get-tuple-element.78), channel_id=1, source_target_pairs={{0,6},{2,0},{4,2},{6,4},{1,7},{3,1},{5,3},{7,5},{8,14},{10,8},{12,... | collective-permute-start | bytes 786440 | tf_op jit(solution)/shard_map/ppermute | solution.py:40
  168.8 23.4 %all-to-all-start.3 = ((f32[16,8,128]{2,1,0:T(8,128)}), f32[16,8,128]{2,1,0:T(8,128)S(1)}, u32[]{:S(2)}, u32[]{:S(2)}) async-start(f32[16,8,128]{2,1,0:T(8,128)} %relay.1), calls=%async_computation.3 | async-start | bytes 131072 | tf_op jit(solution)/shard_map/all_to_all | solution.py:44
  180.5 11.6 %copy-start.4 = (f32[1,2,128,128]{3,2,1,0:T(8,128)S(1)}, f32[1,2,128,128]{3,2,1,0:T(8,128)}, u32[]{:S(2)}) copy-start(f32[1,2,128,128]{3,2,1,0:T(8,128)} %refs_5_.1) | copy-start | bytes 393220
  180.5 11.6 %copy-start.5 = (f32[1,2,128,128]{3,2,1,0:T(8,128)S(1)}, f32[1,2,128,128]{3,2,1,0:T(8,128)}, u32[]{:S(2)}) copy-start(f32[1,2,128,128]{3,2,1,0:T(8,128)} %refs_6_.1) | copy-start | bytes 393220
Sparse Core Ops, SparseCore 0:
  28.1 85.5 all-gather.2
  152.8 34.8 all-gather.4

commit v10 on v8

--- a/solution.py
+++ b/solution.py
@@ -147,7 +147,7 @@
         give_ref[m] = total(1 - parity)
 
 
-def pair_sum_kernel(keep_ref, taken_ref, out_ref):
+def pair_sum_kernel(keep_ref, taken_ref, _, out_ref):
     out_ref[...] = (keep_ref[...].astype(F32) + taken_ref[...].astype(F32)).astype(BF16)
 
 
@@ -326,12 +326,13 @@
         [SMEM] * 3 + [VMEM] * 2, [VMEM] * 2, [pltpu.SMEM((tile_total + 8,), jnp.int32)],
         moved=1 << 12,
     )(*lists, grads, delta_all)
-    partner, give = lax.optimization_barrier((partner, give))
-    pairs = kernel_call(pair_sum_kernel, "pair_sum", eight, [VMEM] * 2, VMEM)(keep, partner)
+    pairs = kernel_call(pair_sum_kernel, "pair_sum", eight, [VMEM] * 2 + [ANY], VMEM)(
+        keep, partner, give
+    )
     arrived = exchange(pairs, "m")
     own_grad, squares = kernel_call(
         own_grad_kernel, "own_grad",
-        [SHAPE((SLOT_CAP, TILE, TILE), F32), SHAPE((NY * NX * 2, 8, TILE), F32)],
+        [SHAPE((SLOT_CAP, TILE, TILE), F32), SHAPE((NZ, 8, TILE), F32)],
         [SMEM, SMEM, VMEM], [VMEM] * 2,
     )(ids, owner_counts, arrived)
 
@@ -355,9 +356,10 @@
         moved=4 << 20, vmem=63,
     )(gathered)
 
+    squares = exchange(squares, Z)
+    near = SHAPE((NY * NX * 2, 8, TILE), F32)
+    squares = kernel_call(relay_kernel, "relay", near, [VMEM], VMEM)(squares)
     squares = exchange(squares, ("y", "x", "core"))
-    squares = kernel_call(relay_kernel, "relay", SHAPE((NZ, 8, TILE), F32), [VMEM], VMEM)(squares)
-    squares = exchange(squares, Z)
     squares, input_grad = lax.optimization_barrier((squares, input_grad))
     count_all = float(NX * 2 * tile_total * TILE * TILE)
 

time: 193 us -> 195 us (1.010)
  waiting for transfers between devices: 45.9 us -> 41.8 us
  starting transfers between devices: 60.7 us -> 64.6 us
    all_gather x1, waiting for transfers between devices: 7.04 us -> 1.35 us  [body(): lax.all_gather(share.astype(BF16), ('x', 'core'), axis=0, tiled=True)]
    all_to_all x2, starting transfers between devices: 16.5 us -> 20.1 us  [exchange(): return lax.all_to_all(value, axis, split_axis=0, concat_axis=0, tiled=True)]
  transfers between devices with their start and end apart: 16 -> 16, of which waited for: 12 -> 13; matrix products, arithmetic and copies ran while one was open for 1% -> 1% of each run, Pallas kernels for 10% -> 10%
where the time goes in v10:
time: 195 us
  starting transfers between devices  64.6 us (33%)
  blocking collectives  47.7 us (24%)
  waiting for transfers between devices  41.8 us (21%)
  Pallas kernels  22.1 us (11%)
  between operations  14.4 us (7%)
  local copies, waits for them, and re-layouts  3.09 us (2%)
    all_to_all x3, blocking collectives, exchange(): return lax.all_to_all(value, axis, split_axis=0, concat_axis=0, tiled=True)  47.7 us
    ppermute x12, starting transfers between devices, shift(): lax.ppermute(value, axis, [(i, (i + step) % size) for i in range(size)])  44.4 us
    ppermute x12, waiting for transfers between devices, shift(): lax.ppermute(value, axis, [(i, (i + step) % size) for i in range(size)])  29.6 us
    all_to_all x2, starting transfers between devices, exchange(): return lax.all_to_all(value, axis, split_axis=0, concat_axis=0, tiled=True)  20.1 us
    all_to_all x2, waiting for transfers between devices, exchange(): return lax.all_to_all(value, axis, split_axis=0, concat_axis=0, tiled=True)  9.9 us
    pallas_call x3, Pallas kernels, terms(): kernel_call(functools.partial(tile_kernel, parts), 'tiles', [SHAPE(((last...  7.19 us
    pallas_call x1, Pallas kernels, body(): kernel_call(contrib_kernel, 'contribs', [SHAPE((tokens // 2, width), BF16...  4.8 us
  transfers between devices with their start and end apart: 16, of which 13 were waited for; matrix products, arithmetic and copies ran while one was open for 1% of the time, Pallas kernels for 10%

profile of v10, /device:TPU:1, one launch (start us, length us, event | category | flops | bytes accessed | tf_op | source)
XLA Modules:
  0.0 194.5 jit_solution(18331915123105376222)
XLA Ops:
  7.2 0.0 all-gather.3.cloned.1.call-start
  7.2 0.0 copy-start
  7.2 0.9 copy-done
  8.1 0.1 turn.1
  8.3 0.0 copy-start.2
  8.3 0.0 copy-start.3
  8.3 0.0 copy-start.4
  8.3 10.6 %all_to_all.25 = bf16[4,2,128,128]{3,2,1,0:T(8,128)(2,1)} all-to-all(bf16[4,2,128,128]{3,2,1,0:T(8,128)(2,1)S(1)} %broadcast_in_dim.5), channel_id=1, replica_groups=mesh['y'=4,'m'=8,'p'=2,'x'=4,'core'=2] {'y'}, dimensions={0} | all-to-all | bytes 524288 | tf_op jit(solution)/shard_map/all_to_all | solution.py:44
  18.9 0.0 all-gather.3.cloned.1.call-update
  18.9 0.0 copy-start.9
  18.9 0.0 copy-start.10
  18.9 0.0 copy-start.11
  18.9 1.1 broadcast_in_dim.4
  20.0 13.9 %all_to_all.26.own_ref = bf16[4,128,1024]{2,1,0:T(8,128)(2,1)S(1)} all-to-all(bf16[4,128,1024]{2,1,0:T(8,128)(2,1)S(1)} %broadcast_in_dim.4), channel_id=1, replica_groups=mesh['y'=4,'m'=8,'p'=2,'x'=4,'core'=2] {'x'}, dimensions={0} | all-to-all | bytes 2097152 | tf_op jit(solution)/shard_map/all_to_all | solution.py:44
  34.0 7.9 %collective-permute-start = (bf16[4,128,1024]{2,1,0:T(8,128)(2,1)S(1)}, bf16[4,128,1024]{2,1,0:T(8,128)(2,1)S(1)}, u32[]{:S(2)}, u32[]{:S(2)}) collective-permute-start(bf16[4,128,1024]{2,1,0:T(8,128)(2,1)S(1)} %all_to_all.26.own_ref), channel_id=1, source_target_pairs={{0,1},{1,0},{2,3},{3,2},{4,5},{5,4},{6,7},{7,6},{8,9},{9,8},{10,11... | collective-permute-start | bytes 3145736 | tf_op jit(solution)/shard_map/ppermute | solution.py:40
  41.8 0.1 pad_add_fusion.ids_ref.refs_0_
  41.9 1.1 gate.1
  43.1 1.0 collective-permute-done.other_ref
  44.1 2.1 %tiles.3 = (bf16[16,128,128]{2,1,0:T(8,128)(2,1)S(1)}, bf16[16,128,128]{2,1,0:T(8,128)(2,1)S(1)}) custom-call(s32[4]{0:T(128)S(1)} %pad_add_fusion.ids_ref.refs_0_, s32[1,112]{1,0:T(1,128)S(1)} %copy-done.10, s32[1,112]{1,0:T(1,128)S(1)} %copy-done.11, s32[1,64]{1,0:T(1,128)S(1)} %copy-done.9, bf16[4,128,1024]{2,1,0:T(8,128)(2,1)S(1)} %all_to_all.26.own_ref, ...), custom_call_target="tpu_custom_call" | custom-call | flops 117440512 | bytes 2097152 | tf_op jit(solution)/shard_map/tiles/pallas_call | solution.py:295
  46.2 2.3 %collective-permute-start.1 = (bf16[16,128,128]{2,1,0:T(8,128)(2,1)S(1)}, bf16[16,128,128]{2,1,0:T(8,128)(2,1)S(1)}, u32[]{:S(2)}, u32[]{:S(2)}) collective-permute-start(bf16[16,128,128]{2,1,0:T(8,128)(2,1)S(1)} %get-tuple-element.59), channel_id=1, source_target_pairs={{0,128},{128,256},{256,384},{384,0},{1,129},{129,257},{257,385},{3... | collective-permute-start | bytes 1572872 | tf_op jit(solution)/shard_map/ppermute | solution.py:40
  48.5 4.2 %collective-permute-start.2 = (bf16[16,128,128]{2,1,0:T(8,128)(2,1)S(1)}, bf16[16,128,128]{2,1,0:T(8,128)(2,1)S(1)}, u32[]{:S(2)}, u32[]{:S(2)}) collective-permute-start(bf16[16,128,128]{2,1,0:T(8,128)(2,1)S(1)} %get-tuple-element.61), channel_id=1, source_target_pairs={{0,384},{128,0},{256,128},{384,256},{1,385},{129,1},{257,129},{385... | collective-permute-start | bytes 1572872 | tf_op jit(solution)/shard_map/ppermute | solution.py:40
  52.7 2.1 %tiles.4 = (bf16[16,128,128]{2,1,0:T(8,128)(2,1)S(1)}, bf16[16,128,128]{2,1,0:T(8,128)(2,1)S(1)}) custom-call(s32[4]{0:T(128)S(1)} %pad_add_fusion.ids_ref.refs_0_, s32[1,112]{1,0:T(1,128)S(1)} %copy-done.10, s32[1,112]{1,0:T(1,128)S(1)} %copy-done.11, s32[1,64]{1,0:T(1,128)S(1)} %copy-done.9, bf16[4,128,1024]{2,1,0:T(8,128)(2,1)S(1)} %all_to_all.26.own_ref, ...), custom_call_target="tpu_custom_call" | custom-call | flops 117440512 | bytes 2097152 | tf_op jit(solution)/shard_map/tiles/pallas_call | solution.py:295
  54.8 3.0 %tiles.5 = (bf16[16,128,128]{2,1,0:T(8,128)(2,1)S(1)}, bf16[16,128,128]{2,1,0:T(8,128)(2,1)S(1)}, bf16[32,128,128]{2,1,0:T(8,128)(2,1)S(1)}) custom-call(s32[4]{0:T(128)S(1)} %pad_add_fusion.ids_ref.refs_0_, s32[1,112]{1,0:T(1,128)S(1)} %copy-done.10, s32[1,112]{1,0:T(1,128)S(1)} %copy-done.11, s32[1,64]{1,0:T(1,128)S(1)} %copy-done.9, ...), custom_call_target="tpu_custom_call" | custom-call | flops 117440512 | bytes 2097152 | tf_op jit(solution)/shard_map/tiles/pallas_call | solution.py:295
  57.8 1.9 collective-permute-start.4
  59.8 3.4 %collective-permute-start.5 = (bf16[16,128,128]{2,1,0:T(8,128)(2,1)S(1)}, bf16[16,128,128]{2,1,0:T(8,128)(2,1)S(1)}, u32[]{:S(2)}, u32[]{:S(2)}) collective-permute-start(bf16[16,128,128]{2,1,0:T(8,128)(2,1)S(1)} %get-tuple-element.64), channel_id=1, source_target_pairs={{0,128},{128,256},{256,384},{384,0},{1,129},{129,257},{257,385},{3... | collective-permute-start | bytes 1572872 | tf_op jit(solution)/shard_map/ppermute | solution.py:40
  63.1 0.1 collective-permute-done.2.far_high_ref
  63.3 0.2 passing.1
  63.5 2.0 %collective-permute-start.3 = (bf16[16,128,128]{2,1,0:T(8,128)(2,1)S(1)}, bf16[16,128,128]{2,1,0:T(8,128)(2,1)S(1)}, u32[]{:S(2)}, u32[]{:S(2)}) collective-permute-start(bf16[16,128,128]{2,1,0:T(8,128)(2,1)S(1)} %get-tuple-element.62), channel_id=1, source_target_pairs={{0,128},{128,256},{256,384},{384,0},{1,129},{129,257},{257,385},{3... | collective-permute-start | bytes 1572872 | tf_op jit(solution)/shard_map/ppermute | solution.py:40
  65.5 5.2 %collective-permute-start.6 = (bf16[16,128,128]{2,1,0:T(8,128)(2,1)S(1)}, bf16[16,128,128]{2,1,0:T(8,128)(2,1)S(1)}, u32[]{:S(2)}, u32[]{:S(2)}) collective-permute-start(bf16[16,128,128]{2,1,0:T(8,128)(2,1)S(1)} %get-tuple-element.65), channel_id=1, source_target_pairs={{0,384},{128,0},{256,128},{384,256},{1,385},{129,1},{257,129},{385... | collective-permute-start | bytes 1572872 | tf_op jit(solution)/shard_map/ppermute | solution.py:40
  70.8 3.7 %collective-permute-done.4 = bf16[16,128,128]{2,1,0:T(8,128)(2,1)S(1)} collective-permute-done((bf16[16,128,128]{2,1,0:T(8,128)(2,1)S(1)}, bf16[16,128,128]{2,1,0:T(8,128)(2,1)S(1)}, u32[]{:S(2)}, u32[]{:S(2)}) %collective-permute-start.4) | collective-permute-done | bytes 524320 | tf_op jit(solution)/shard_map/ppermute | solution.py:40
  74.5 0.9 collective-permute-done.5
  75.5 11.2 %collective-permute-done.3 = bf16[16,128,128]{2,1,0:T(8,128)(2,1)S(1)} collective-permute-done((bf16[16,128,128]{2,1,0:T(8,128)(2,1)S(1)}, bf16[16,128,128]{2,1,0:T(8,128)(2,1)S(1)}, u32[]{:S(2)}, u32[]{:S(2)}) %collective-permute-start.3) | collective-permute-done | bytes 524320 | tf_op jit(solution)/shard_map/ppermute | solution.py:40
  86.7 0.0 collective-permute-done.6
  86.7 1.6 y_sum.1
  88.3 3.5 %collective-permute-start.7 = (bf16[8,2,128,128]{3,2,1,0:T(8,128)(2,1)}, bf16[8,2,128,128]{3,2,1,0:T(8,128)(2,1)S(1)}, u32[]{:S(2)}, u32[]{:S(2)}) collective-permute-start(bf16[8,2,128,128]{3,2,1,0:T(8,128)(2,1)} %get-tuple-element.69), channel_id=1, source_target_pairs={{0,8},{8,0},{1,9},{9,1},{2,10},{10,2},{3,11},{11,3},{4,12},{12,4},... | collective-permute-start | bytes 1572872 | tf_op jit(solution)/shard_map/ppermute | solution.py:40
  91.8 1.0 all-gather.3.cloned.1.call-done.delta_ref
  92.8 1.0 copy-done.6
  93.8 4.8 %contribs.1 = (bf16[64,8192]{1,0:T(8,128)(2,1)S(1)}, bf16[64,8192]{1,0:T(8,128)(2,1)S(1)}) custom-call(s32[1,112]{1,0:T(1,128)S(1)} %copy-done.10, s32[1,112]{1,0:T(1,128)S(1)} %copy-done.11, s32[1,64]{1,0:T(1,128)S(1)} %copy-done.9, bf16[14,128,128]{2,1,0:T(8,128)(2,1)S(1)} %copy-done.6, bf16[128,128,128]{2,1,0:T(8,128)(2,1)} %all-gather.3.cloned.1.call-done.delta_ref), custom_call_target="tpu_custom_call" | custom-call | bytes 4096 | tf_op jit(solution)/shard_map/contribs/pallas_call | solution.py:324
  98.6 7.7 %collective-permute-done.7.taken_ref = bf16[8,2,128,128]{3,2,1,0:T(8,128)(2,1)S(1)} collective-permute-done((bf16[8,2,128,128]{3,2,1,0:T(8,128)(2,1)}, bf16[8,2,128,128]{3,2,1,0:T(8,128)(2,1)S(1)}, u32[]{:S(2)}, u32[]{:S(2)}) %collective-permute-start.7) | collective-permute-done | bytes 524320 | tf_op jit(solution)/shard_map/ppermute | solution.py:40
  106.3 0.9 pair_sum.1
  107.2 10.4 %all-to-all-start.2 = ((bf16[8,2,128,128]{3,2,1,0:T(8,128)(2,1)}), bf16[8,2,128,128]{3,2,1,0:T(8,128)(2,1)S(1)}, u32[]{:S(2)}, u32[]{:S(2)}) async-start(bf16[8,2,128,128]{3,2,1,0:T(8,128)(2,1)} %pair_sum.1), calls=%async_computation.2 | async-start | bytes 1048576 | tf_op jit(solution)/shard_map/all_to_all | solution.py:44
  117.7 0.0 all-gather.5.cloned.1.call-start
  117.7 4.9 %collective-permute-start.8 = (bf16[64,8192]{1,0:T(8,128)(2,1)S(1)}, bf16[64,8192]{1,0:T(8,128)(2,1)S(1)}, u32[]{:S(2)}, u32[]{:S(2)}) collective-permute-start(bf16[64,8192]{1,0:T(8,128)(2,1)S(1)} %get-tuple-element.74._), channel_id=1, source_target_pairs={{0,1},{1,0},{2,3},{3,2},{4,5},{5,4},{6,7},{7,6},{8,9},{9,8},{10,11... | collective-permute-start | bytes 3145736 | tf_op jit(solution)/shard_map/ppermute | solution.py:40
  122.7 2.3 %collective-permute-done.8 = bf16[64,8192]{1,0:T(8,128)(2,1)S(1)} collective-permute-done((bf16[64,8192]{1,0:T(8,128)(2,1)S(1)}, bf16[64,8192]{1,0:T(8,128)(2,1)S(1)}, u32[]{:S(2)}, u32[]{:S(2)}) %collective-permute-start.8) | collective-permute-done | bytes 1048608 | tf_op jit(solution)/shard_map/ppermute | solution.py:40
  124.9 0.8 core_sum.1
  125.8 2.5 %collective-permute-start.9 = (bf16[16,8192]{1,0:T(8,128)(2,1)S(1)}, bf16[16,8192]{1,0:T(8,128)(2,1)S(1)}, u32[]{:S(2)}, u32[]{:S(2)}) collective-permute-start(bf16[16,8192]{1,0:T(8,128)(2,1)S(1)} %get-tuple-element.76), channel_id=1, source_target_pairs={{0,2},{2,4},{4,6},{6,0},{1,3},{3,5},{5,7},{7,1},{8,10},{10,12},{12... | collective-permute-start | bytes 786440 | tf_op jit(solution)/shard_map/ppermute | solution.py:40
  128.3 4.0 %collective-permute-start.10 = (bf16[16,8192]{1,0:T(8,128)(2,1)S(1)}, bf16[16,8192]{1,0:T(8,128)(2,1)S(1)}, u32[]{:S(2)}, u32[]{:S(2)}) collective-permute-start(bf16[16,8192]{1,0:T(8,128)(2,1)S(1)} %get-tuple-element.77), channel_id=1, source_target_pairs={{0,4},{2,6},{4,0},{6,2},{1,5},{3,7},{5,1},{7,3},{8,12},{10,14},{12... | collective-permute-start | bytes 786440 | tf_op jit(solution)/shard_map/ppermute | solution.py:40
  132.3 2.5 %collective-permute-start.11 = (bf16[16,8192]{1,0:T(8,128)(2,1)S(1)}, bf16[16,8192]{1,0:T(8,128)(2,1)S(1)}, u32[]{:S(2)}, u32[]{:S(2)}) collective-permute-start(bf16[16,8192]{1,0:T(8,128)(2,1)S(1)} %get-tuple-element.78), channel_id=1, source_target_pairs={{0,6},{2,0},{4,2},{6,4},{1,7},{3,1},{5,3},{7,5},{8,14},{10,8},{12,... | collective-permute-start | bytes 786440 | tf_op jit(solution)/shard_map/ppermute | solution.py:40
  134.9 6.1 %all-to-all-done.2.arrived_ref = bf16[8,2,128,128]{3,2,1,0:T(8,128)(2,1)S(1)} async-done(((bf16[8,2,128,128]{3,2,1,0:T(8,128)(2,1)}), bf16[8,2,128,128]{3,2,1,0:T(8,128)(2,1)S(1)}, u32[]{:S(2)}, u32[]{:S(2)}) %all-to-all-start.2) | async-done | bytes 524320 | tf_op jit(solution)/shard_map/all_to_all | solution.py:44
  140.9 0.8 own_grad.1
  141.7 0.3 collective-permute-done.10
  142.1 2.1 %collective-permute-done.11 = bf16[16,8192]{1,0:T(8,128)(2,1)S(1)} collective-permute-done((bf16[16,8192]{1,0:T(8,128)(2,1)S(1)}, bf16[16,8192]{1,0:T(8,128)(2,1)S(1)}, u32[]{:S(2)}, u32[]{:S(2)}) %collective-permute-start.11) | collective-permute-done | bytes 262176 | tf_op jit(solution)/shard_map/ppermute | solution.py:40
  144.2 0.8 add_convert_fusion
  145.0 0.0 all-gather.5.cloned.1.call-update
  145.1 23.2 %all_to_all.27.arrived_ref = f32[16,8,128]{2,1,0:T(8,128)S(1)} all-to-all(f32[16,8,128]{2,1,0:T(8,128)S(1)} %get-tuple-element.79), channel_id=1, replica_groups=mesh['y'=4,'m'=8,'p'=2,'x'=4,'core'=2] {'m','p'}, dimensions={0} | all-to-all | bytes 131072 | tf_op jit(solution)/shard_map/all_to_all | solution.py:44
  168.2 0.7 relay.1
  168.9 9.7 %all-to-all-start.4 = ((f32[32,8,128]{2,1,0:T(8,128)}), f32[32,8,128]{2,1,0:T(8,128)S(1)}, u32[]{:S(2)}, u32[]{:S(2)}) async-start(f32[32,8,128]{2,1,0:T(8,128)} %relay.1), calls=%async_computation.4 | async-start | bytes 262144 | tf_op jit(solution)/shard_map/all_to_all | solution.py:44
  178.6 0.0 copy-start.1
  178.6 0.0 copy-start.7
  178.6 0.0 copy-start.8
  178.6 1.4 all-gather.5.cloned.1.call-done.in_ref
  180.0 2.4 %result.1 = bf16[128,8192]{1,0:T(8,128)(2,1)} custom-call(bf16[128,8192]{1,0:T(8,128)(2,1)} %all-gather.5.cloned.1.call-done.in_ref), custom_call_target="tpu_custom_call" | custom-call | bytes 4194304 | tf_op jit(solution)/shard_map/result/pallas_call | solution.py:353
  182.4 3.8 %all-to-all-done.4.refs_2_ = f32[32,8,128]{2,1,0:T(8,128)S(1)} async-done(((f32[32,8,128]{2,1,0:T(8,128)}), f32[32,8,128]{2,1,0:T(8,128)S(1)}, u32[]{:S(2)}, u32[]{:S(2)}) %all-to-all-start.4) | async-done | bytes 131104 | tf_op jit(solution)/shard_map/all_to_all | solution.py:44
  186.2 1.5 adam.1
  (15 shorter events, 0.1 us)
Async XLA Ops:
  7.2 85.6 %all-gather.3.cloned.1.call-start = ((), (), s32[]{:S(2)}) async-start(), calls=%async_computation.5 | async-start | bytes 4456448 | tf_op jit(solution)/shard_map/all_gather | solution.py:280
  7.2 0.9 copy-start
  8.3 33.7 %copy-start.2 = (bf16[128,1792]{1,0:T(8,128)(2,1)S(1)}, bf16[128,1792]{1,0:T(8,128)(2,1)}, u32[]{:S(2)}) copy-start(bf16[128,1792]{1,0:T(8,128)(2,1)} %gate_ref.1) | copy-start | bytes 1376260
  8.3 33.6 %copy-start.3 = (bf16[128,1792]{1,0:T(8,128)(2,1)S(1)}, bf16[128,1792]{1,0:T(8,128)(2,1)}, u32[]{:S(2)}) copy-start(bf16[128,1792]{1,0:T(8,128)(2,1)} %up_ref.1) | copy-start | bytes 1376260
  8.3 33.6 %copy-start.4 = (bf16[128,1792]{1,0:T(8,128)(2,1)S(1)}, bf16[128,1792]{1,0:T(8,128)(2,1)}, u32[]{:S(2)}) copy-start(bf16[128,1792]{1,0:T(8,128)(2,1)} %hidden_ref.1) | copy-start | bytes 1376260
  18.9 25.2 %copy-start.9 = (s32[1,64]{1,0:T(1,128)S(1)}, s32[1,64]{1,0:T(1,128)}, u32[]{:S(2)}) copy-start(s32[1,64]{1,0:T(1,128)} %refs_1_.1) | copy-start | bytes 772
  18.9 25.2 %copy-start.10 = (s32[1,112]{1,0:T(1,128)S(1)}, s32[1,112]{1,0:T(1,128)}, u32[]{:S(2)}) copy-start(s32[1,112]{1,0:T(1,128)} %rows_ref.7) | copy-start | bytes 1348
  18.9 25.2 %copy-start.11 = (s32[1,112]{1,0:T(1,128)S(1)}, s32[1,112]{1,0:T(1,128)}, u32[]{:S(2)}) copy-start(s32[1,112]{1,0:T(1,128)} %cols_ref.7) | copy-start | bytes 1348
  34.0 10.1 %collective-permute-start = (bf16[4,128,1024]{2,1,0:T(8,128)(2,1)S(1)}, bf16[4,128,1024]{2,1,0:T(8,128)(2,1)S(1)}, u32[]{:S(2)}, u32[]{:S(2)}) collective-permute-start(bf16[4,128,1024]{2,1,0:T(8,128)(2,1)S(1)} %all_to_all.26.own_ref), channel_id=1, source_target_pairs={{0,1},{1,0},{2,3},{3,2},{4,5},{5,4},{6,7},{7,6},{8,9},{9,8},{10,11... | collective-permute-start | bytes 3145736 | tf_op jit(solution)/shard_map/ppermute | solution.py:40
  43.0 11.7 %copy-start.5 = (bf16[14,128,128]{2,1,0:T(8,128)(2,1)}, bf16[14,128,128]{2,1,0:T(8,128)(2,1)S(1)}, u32[]{:S(2)}) copy-start(bf16[14,128,128]{2,1,0:T(8,128)(2,1)S(1)} %get-tuple-element.70.grad_ref) | copy-start | bytes 1376260
  46.2 17.0 %collective-permute-start.1 = (bf16[16,128,128]{2,1,0:T(8,128)(2,1)S(1)}, bf16[16,128,128]{2,1,0:T(8,128)(2,1)S(1)}, u32[]{:S(2)}, u32[]{:S(2)}) collective-permute-start(bf16[16,128,128]{2,1,0:T(8,128)(2,1)S(1)} %get-tuple-element.59), channel_id=1, source_target_pairs={{0,128},{128,256},{256,384},{384,0},{1,129},{129,257},{257,385},{3... | collective-permute-start | bytes 1572872 | tf_op jit(solution)/shard_map/ppermute | solution.py:40
  48.5 14.8 %collective-permute-start.2 = (bf16[16,128,128]{2,1,0:T(8,128)(2,1)S(1)}, bf16[16,128,128]{2,1,0:T(8,128)(2,1)S(1)}, u32[]{:S(2)}, u32[]{:S(2)}) collective-permute-start(bf16[16,128,128]{2,1,0:T(8,128)(2,1)S(1)} %get-tuple-element.61), channel_id=1, source_target_pairs={{0,384},{128,0},{256,128},{384,256},{1,385},{129,1},{257,129},{385... | collective-permute-start | bytes 1572872 | tf_op jit(solution)/shard_map/ppermute | solution.py:40
  57.8 16.7 %collective-permute-start.4 = (bf16[16,128,128]{2,1,0:T(8,128)(2,1)S(1)}, bf16[16,128,128]{2,1,0:T(8,128)(2,1)S(1)}, u32[]{:S(2)}, u32[]{:S(2)}) collective-permute-start(bf16[16,128,128]{2,1,0:T(8,128)(2,1)S(1)} %get-tuple-element.63), channel_id=1, source_target_pairs={{0,384},{128,0},{256,128},{384,256},{1,385},{129,1},{257,129},{385... | collective-permute-start | bytes 1572872 | tf_op jit(solution)/shard_map/ppermute | solution.py:40
  59.8 15.7 %collective-permute-start.5 = (bf16[16,128,128]{2,1,0:T(8,128)(2,1)S(1)}, bf16[16,128,128]{2,1,0:T(8,128)(2,1)S(1)}, u32[]{:S(2)}, u32[]{:S(2)}) collective-permute-start(bf16[16,128,128]{2,1,0:T(8,128)(2,1)S(1)} %get-tuple-element.64), channel_id=1, source_target_pairs={{0,128},{128,256},{256,384},{384,0},{1,129},{129,257},{257,385},{3... | collective-permute-start | bytes 1572872 | tf_op jit(solution)/shard_map/ppermute | solution.py:40
  63.5 23.2 %collective-permute-start.3 = (bf16[16,128,128]{2,1,0:T(8,128)(2,1)S(1)}, bf16[16,128,128]{2,1,0:T(8,128)(2,1)S(1)}, u32[]{:S(2)}, u32[]{:S(2)}) collective-permute-start(bf16[16,128,128]{2,1,0:T(8,128)(2,1)S(1)} %get-tuple-element.62), channel_id=1, source_target_pairs={{0,128},{128,256},{256,384},{384,0},{1,129},{129,257},{257,385},{3... | collective-permute-start | bytes 1572872 | tf_op jit(solution)/shard_map/ppermute | solution.py:40
  65.5 21.2 %collective-permute-start.6 = (bf16[16,128,128]{2,1,0:T(8,128)(2,1)S(1)}, bf16[16,128,128]{2,1,0:T(8,128)(2,1)S(1)}, u32[]{:S(2)}, u32[]{:S(2)}) collective-permute-start(bf16[16,128,128]{2,1,0:T(8,128)(2,1)S(1)} %get-tuple-element.65), channel_id=1, source_target_pairs={{0,384},{128,0},{256,128},{384,256},{1,385},{129,1},{257,129},{385... | collective-permute-start | bytes 1572872 | tf_op jit(solution)/shard_map/ppermute | solution.py:40
  88.3 18.0 %collective-permute-start.7 = (bf16[8,2,128,128]{3,2,1,0:T(8,128)(2,1)}, bf16[8,2,128,128]{3,2,1,0:T(8,128)(2,1)S(1)}, u32[]{:S(2)}, u32[]{:S(2)}) collective-permute-start(bf16[8,2,128,128]{3,2,1,0:T(8,128)(2,1)} %get-tuple-element.69), channel_id=1, source_target_pairs={{0,8},{8,0},{1,9},{9,1},{2,10},{10,2},{3,11},{11,3},{4,12},{12,4},... | collective-permute-start | bytes 1572872 | tf_op jit(solution)/shard_map/ppermute | solution.py:40
  92.8 1.0 copy-start.6
  107.2 33.7 %all-to-all-start.2 = ((bf16[8,2,128,128]{3,2,1,0:T(8,128)(2,1)}), bf16[8,2,128,128]{3,2,1,0:T(8,128)(2,1)S(1)}, u32[]{:S(2)}, u32[]{:S(2)}) async-start(bf16[8,2,128,128]{3,2,1,0:T(8,128)(2,1)} %pair_sum.1), calls=%async_computation.2 | async-start | bytes 1048576 | tf_op jit(solution)/shard_map/all_to_all | solution.py:44
  117.7 62.3 %all-gather.5.cloned.1.call-start = ((), (), s32[]{:S(2)}) async-start(), calls=%async_computation.6 | async-start | bytes 2359296 | tf_op jit(solution)/shard_map/all_gather | solution.py:352
  117.7 7.2 %collective-permute-start.8 = (bf16[64,8192]{1,0:T(8,128)(2,1)S(1)}, bf16[64,8192]{1,0:T(8,128)(2,1)S(1)}, u32[]{:S(2)}, u32[]{:S(2)}) collective-permute-start(bf16[64,8192]{1,0:T(8,128)(2,1)S(1)} %get-tuple-element.74._), channel_id=1, source_target_pairs={{0,1},{1,0},{2,3},{3,2},{4,5},{5,4},{6,7},{7,6},{8,9},{9,8},{10,11... | collective-permute-start | bytes 3145736 | tf_op jit(solution)/shard_map/ppermute | solution.py:40
  125.8 16.0 %collective-permute-start.9 = (bf16[16,8192]{1,0:T(8,128)(2,1)S(1)}, bf16[16,8192]{1,0:T(8,128)(2,1)S(1)}, u32[]{:S(2)}, u32[]{:S(2)}) collective-permute-start(bf16[16,8192]{1,0:T(8,128)(2,1)S(1)} %get-tuple-element.76), channel_id=1, source_target_pairs={{0,2},{2,4},{4,6},{6,0},{1,3},{3,5},{5,7},{7,1},{8,10},{10,12},{12... | collective-permute-start | bytes 786440 | tf_op jit(solution)/shard_map/ppermute | solution.py:40
  128.3 13.8 %collective-permute-start.10 = (bf16[16,8192]{1,0:T(8,128)(2,1)S(1)}, bf16[16,8192]{1,0:T(8,128)(2,1)S(1)}, u32[]{:S(2)}, u32[]{:S(2)}) collective-permute-start(bf16[16,8192]{1,0:T(8,128)(2,1)S(1)} %get-tuple-element.77), channel_id=1, source_target_pairs={{0,4},{2,6},{4,0},{6,2},{1,5},{3,7},{5,1},{7,3},{8,12},{10,14},{12... | collective-permute-start | bytes 786440 | tf_op jit(solution)/shard_map/ppermute | solution.py:40
  132.3 11.9 %collective-permute-start.11 = (bf16[16,8192]{1,0:T(8,128)(2,1)S(1)}, bf16[16,8192]{1,0:T(8,128)(2,1)S(1)}, u32[]{:S(2)}, u32[]{:S(2)}) collective-permute-start(bf16[16,8192]{1,0:T(8,128)(2,1)S(1)} %get-tuple-element.78), channel_id=1, source_target_pairs={{0,6},{2,0},{4,2},{6,4},{1,7},{3,1},{5,3},{7,5},{8,14},{10,8},{12,... | collective-permute-start | bytes 786440 | tf_op jit(solution)/shard_map/ppermute | solution.py:40
  168.9 17.3 %all-to-all-start.4 = ((f32[32,8,128]{2,1,0:T(8,128)}), f32[32,8,128]{2,1,0:T(8,128)S(1)}, u32[]{:S(2)}, u32[]{:S(2)}) async-start(f32[32,8,128]{2,1,0:T(8,128)} %relay.1), calls=%async_computation.4 | async-start | bytes 262144 | tf_op jit(solution)/shard_map/all_to_all | solution.py:44
  178.6 7.6 %copy-start.1 = (f32[1,2,128,128]{3,2,1,0:T(8,128)S(1)}, f32[1,2,128,128]{3,2,1,0:T(8,128)}, u32[]{:S(2)}) copy-start(f32[1,2,128,128]{3,2,1,0:T(8,128)} %refs_4_.1) | copy-start | bytes 393220
  178.6 7.6 %copy-start.7 = (f32[1,2,128,128]{3,2,1,0:T(8,128)S(1)}, f32[1,2,128,128]{3,2,1,0:T(8,128)}, u32[]{:S(2)}) copy-start(f32[1,2,128,128]{3,2,1,0:T(8,128)} %refs_5_.1) | copy-start | bytes 393220
  178.6 7.6 %copy-start.8 = (f32[1,2,128,128]{3,2,1,0:T(8,128)S(1)}, f32[1,2,128,128]{3,2,1,0:T(8,128)}, u32[]{:S(2)}) copy-start(f32[1,2,128,128]{3,2,1,0:T(8,128)} %refs_6_.1) | copy-start | bytes 393220
Sparse Core Ops, SparseCore 0:
  19.0 73.7 all-gather.2
  145.2 34.7 all-gather.4

commit v11 on v8

--- a/solution.py
+++ b/solution.py
@@ -35,9 +35,8 @@
     )
 
 
-def shift(value, axis, step):
-    size = lax.axis_size(axis)
-    return lax.ppermute(value, axis, [(i, (i + step) % size) for i in range(size)])
+def swap(value, axis, bits):
+    return lax.ppermute(value, axis, [(i, i ^ bits) for i in range(lax.axis_size(axis))])
 
 
 def exchange(value, axis):
@@ -111,43 +110,43 @@
 ):
     features, starts_ref, sems = refs[len(parts) :]
     load_features(own_ref, other_ref, features, sems, starts_ref, counts_ref)
-    for ref, (away, owners) in zip(refs, parts):
+    for ref, (bits, owners) in zip(refs, parts):
 
         def put(slot, term, ref=ref):
             ref[slot] = term
 
         slot_products(
-            (ids_ref[0] + away) & (NY - 1), owners, put,
+            ids_ref[0] ^ bits, owners, put,
             ids_ref, rows_ref, cols_ref, starts_ref, features, turned_ref,
         )
 
 
-def passing_kernel(up_ref, far_low_ref, down_ref, far_high_ref, up_out, down_out):
-    up_out[...] = (up_ref[...].astype(F32) + far_low_ref[...].astype(F32)).astype(BF16)
-    down_out[...] = (down_ref[...].astype(F32) + far_high_ref[...].astype(F32)).astype(BF16)
+def passing_kernel(one_ref, for_one_ref, other_ref, for_other_ref, one_out, other_out):
+    one_out[...] = (one_ref[...].astype(F32) + for_one_ref[...].astype(F32)).astype(BF16)
+    other_out[...] = (other_ref[...].astype(F32) + for_other_ref[...].astype(F32)).astype(BF16)
 
 
 def y_sum_kernel(
-    ids_ref, mine_ref, below_low_ref, above_low_ref, below_high_ref, above_high_ref,
+    ids_ref, mine_ref, one_low_ref, other_low_ref, one_high_ref, other_high_ref,
     keep_ref, give_ref,
 ):
     parity = ids_ref[1] & 1
     half = NM // 2
     for m in range(NM):
-        below, above = (below_low_ref, above_low_ref) if m < half else (below_high_ref, above_high_ref)
+        one, other = (one_low_ref, other_low_ref) if m < half else (one_high_ref, other_high_ref)
 
         def total(side):
             return (
                 mine_ref[m, side].astype(F32)
-                + below[m % half, side].astype(F32)
-                + above[m % half, side].astype(F32)
+                + one[m % half, side].astype(F32)
+                + other[m % half, side].astype(F32)
             ).astype(BF16)
 
         keep_ref[m] = total(parity)
         give_ref[m] = total(1 - parity)
 
 
-def pair_sum_kernel(keep_ref, taken_ref, out_ref):
+def pair_sum_kernel(keep_ref, taken_ref, _, out_ref):
     out_ref[...] = (keep_ref[...].astype(F32) + taken_ref[...].astype(F32)).astype(BF16)
 
 
@@ -195,8 +194,15 @@
 
 
 def contrib_kernel(
-    rows_ref, cols_ref, counts_ref, grad_ref, delta_ref, stay_ref, give_ref, places_ref
-):
+    rows_ref, cols_ref, counts_ref, grads_ref, deltas_ref, stay_ref, give_ref,
+    places_ref, grad_ref, delta_ref, sems,
+):
+    loads = [
+        pltpu.make_async_copy(deltas_ref, delta_ref, sems.at[0]),
+        pltpu.make_async_copy(grads_ref, grad_ref, sems.at[1]),
+    ]
+    for load in loads:
+        load.start()
     stay_ref[...] = jnp.zeros_like(stay_ref)
     give_ref[...] = jnp.zeros_like(give_ref)
     half = stay_ref.shape[0]
@@ -208,6 +214,8 @@
         return start + counts_ref[0, owner]
 
     lax.fori_loop(0, counts_ref.shape[1], owner_step, 0)
+    for load in loads:
+        load.wait()
     per_step = 28
 
     def step(index, carry):
@@ -232,8 +240,8 @@
 
 
 def core_sum_kernel(ids_ref, stay_ref, taken_ref, *out_refs):
-    for away, ref in enumerate(out_refs):
-        at = (ids_ref[2] + away) & (NX - 1)
+    for bits, ref in enumerate(out_refs):
+        at = ids_ref[2] ^ bits
         ref[...] = (stay_ref[at].astype(F32) + taken_ref[at].astype(F32)).astype(BF16)
 
 
@@ -271,7 +279,7 @@
     lists = (tile_rows, tile_cols, owner_counts)
 
     own = spread(features, "x")
-    other = shift(own, "core", 1)
+    other = swap(own, "core", 1)
 
     delta_half = kernel_call(
         turn_kernel, "turn", SHAPE(delta_value.shape[1:], BF16), [VMEM], VMEM
@@ -301,15 +309,15 @@
         return values, turned
 
     (far_low, far_high), turned = terms(turned, (2, LOW), (2, HIGH))
-    far_low, far_high = shift(far_low, "y", 1), shift(far_high, "y", -1)
-    (up_high, down_low), turned = terms(turned, (1, HIGH), (3, LOW))
-    below_high, above_low = shift(up_high, "y", 1), shift(down_low, "y", -1)
-    (up_low, down_high, mine), turned = terms(turned, (1, LOW), (3, HIGH), (0, (0, NZ)))
-    half = SHAPE(up_low.shape, BF16)
-    up_low, down_high = kernel_call(
+    far_low, far_high = swap(far_low, "y", 1), swap(far_high, "y", 3)
+    (one_low, other_high), turned = terms(turned, (1, LOW), (3, HIGH))
+    one_low, other_high = swap(one_low, "y", 1), swap(other_high, "y", 3)
+    (one_high, other_low, mine), turned = terms(turned, (1, HIGH), (3, LOW), (0, (0, NZ)))
+    half = SHAPE(one_high.shape, BF16)
+    one_high, other_low = kernel_call(
         passing_kernel, "passing", [half] * 2, [VMEM] * 4, [VMEM] * 2
-    )(up_low, far_low, down_high, far_high)
-    below_low, above_high = shift(up_low, "y", 1), shift(down_high, "y", -1)
+    )(one_high, far_high, other_low, far_low)
+    one_high, other_low = swap(one_high, "y", 1), swap(other_low, "y", 3)
 
     def parted(value):
         return value.reshape(-1, 2, SLOT_CAP, TILE, TILE)
@@ -317,17 +325,24 @@
     eight = SHAPE((NM, SLOT_CAP, TILE, TILE), BF16)
     keep, give = kernel_call(
         y_sum_kernel, "y_sum", [eight] * 2, [SMEM] + [VMEM] * 5, [VMEM] * 2
-    )(ids, *map(parted, (mine, below_low, above_low, below_high, above_high)))
+    )(ids, *map(parted, (mine, one_low, other_low, one_high, other_high)))
 
     keep, grads = lax.optimization_barrier((keep, grads))
-    partner = shift(give, "p", 1)
+    partner = swap(give, "p", 1)
     stay, give = kernel_call(
         contrib_kernel, "contribs", [SHAPE((tokens // 2, width), BF16)] * 2,
-        [SMEM] * 3 + [VMEM] * 2, [VMEM] * 2, [pltpu.SMEM((tile_total + 8,), jnp.int32)],
+        [SMEM] * 3 + [ANY] * 2, [VMEM] * 2,
+        [
+            pltpu.SMEM((tile_total + 8,), jnp.int32),
+            pltpu.VMEM(grads.shape, BF16),
+            pltpu.VMEM(delta_all.shape, BF16),
+            pltpu.SemaphoreType.DMA((2,)),
+        ],
         moved=1 << 12,
     )(*lists, grads, delta_all)
-    partner, give = lax.optimization_barrier((partner, give))
-    pairs = kernel_call(pair_sum_kernel, "pair_sum", eight, [VMEM] * 2, VMEM)(keep, partner)
+    pairs = kernel_call(pair_sum_kernel, "pair_sum", eight, [VMEM] * 2 + [ANY], VMEM)(
+        keep, partner, stay
+    )
     arrived = exchange(pairs, "m")
     own_grad, squares = kernel_call(
         own_grad_kernel, "own_grad",
@@ -338,12 +353,12 @@
 
     rows = tokens // (2 * NX)
     _, give = lax.optimization_barrier((pairs, give))
-    taken = shift(give, "core", 1)
+    taken = swap(give, "core", 1)
     share, *others = kernel_call(
         core_sum_kernel, "core_sum", [SHAPE((rows, width), BF16)] * NX,
         [SMEM] + [VMEM] * 2, [VMEM] * NX, moved=1 << 12,
     )(ids, stay.reshape(NX, rows, width), taken.reshape(NX, rows, width))
-    others = [shift(part, "x", away + 1) for away, part in enumerate(others)]
+    others = [swap(part, "x", bits + 1) for bits, part in enumerate(others)]
     squares, share, *others = lax.optimization_barrier((squares, share, *others))
     share = share.astype(F32)
     for part in others:

time: 193 us -> 194 us (level)
  waiting for transfers between devices: 45.9 us -> 51.6 us
  blocking collectives: 45.8 us -> 40.8 us
    all_to_all x3, blocking collectives: 45.8 us -> 40.8 us  [exchange(): return lax.all_to_all(value, axis, split_axis=0, concat_axis=0, tiled=True)]
    all_to_all x2, waiting for transfers between devices: 9.23 us -> 12.5 us  [exchange(): return lax.all_to_all(value, axis, split_axis=0, concat_axis=0, tiled=True)]
    all_to_all x2, starting transfers between devices: 16.5 us -> 18.6 us  [exchange(): return lax.all_to_all(value, axis, split_axis=0, concat_axis=0, tiled=True)]
    ppermute x12, waiting for transfers between devices: 27.9 us -> 29.9 us  [swap(): lax.ppermute(value, axis, [(i, i ^ bits) for i in range(lax.axis_size(axi...]
where the time goes in v11:
time: 194 us; the launch traced here: 193 us
  starting transfers between devices  61.5 us (32%)
  waiting for transfers between devices  51.6 us (27%)
  blocking collectives  40.8 us (21%)
  Pallas kernels  21.1 us (11%)
  between operations  14.4 us (7%)
  local copies, waits for them, and re-layouts  3.05 us (2%)
    ppermute x12, starting transfers between devices, swap(): lax.ppermute(value, axis, [(i, i ^ bits) for i in range(lax.axis_size(axi...  42.9 us
    all_to_all x3, blocking collectives, exchange(): return lax.all_to_all(value, axis, split_axis=0, concat_axis=0, tiled=True)  40.8 us
    ppermute x12, waiting for transfers between devices, swap(): lax.ppermute(value, axis, [(i, i ^ bits) for i in range(lax.axis_size(axi...  29.9 us
    all_to_all x2, starting transfers between devices, exchange(): return lax.all_to_all(value, axis, split_axis=0, concat_axis=0, tiled=True)  18.6 us
    all_to_all x2, waiting for transfers between devices, exchange(): return lax.all_to_all(value, axis, split_axis=0, concat_axis=0, tiled=True)  12.5 us
    pallas_call x3, Pallas kernels, terms(): kernel_call(functools.partial(tile_kernel, parts), 'tiles', [SHAPE(((last...  7.2 us
    all_gather x1, waiting for transfers between devices, body(): lax.all_gather(share.astype(BF16), ('x', 'core'), axis=0, tiled=True)  7.04 us
    pallas_call x1, Pallas kernels, body(): kernel_call(contrib_kernel, 'contribs', [SHAPE((tokens // 2, width), BF16...  4.45 us
  transfers between devices with their start and end apart: 16, of which 12 were waited for; matrix products, arithmetic and copies ran while one was open for 1% of the time, Pallas kernels for 10%

profile of v11, /device:TPU:1, one launch (start us, length us, event | category | flops | bytes accessed | tf_op | source)
XLA Modules:
  0.0 193.4 jit_solution(3480146083299659823)
XLA Ops:
  7.2 0.0 all-gather.3.cloned.1.call-start
  7.2 0.0 copy-start
  7.2 0.9 copy-done
  8.1 0.1 turn.1
  8.3 0.0 copy-start.2
  8.3 0.0 copy-start.3
  8.3 0.0 copy-start.4
  8.3 10.6 %all_to_all.25 = bf16[4,2,128,128]{3,2,1,0:T(8,128)(2,1)} all-to-all(bf16[4,2,128,128]{3,2,1,0:T(8,128)(2,1)S(1)} %broadcast_in_dim.5), channel_id=1, replica_groups=mesh['y'=4,'m'=8,'p'=2,'x'=4,'core'=2] {'y'}, dimensions={0} | all-to-all | bytes 524288 | tf_op jit(solution)/shard_map/all_to_all | solution.py:43
  18.9 0.0 all-gather.3.cloned.1.call-update
  18.9 0.0 copy-start.9
  18.9 0.0 copy-start.10
  18.9 0.0 copy-start.11
  18.9 1.1 broadcast_in_dim.4
  20.0 13.9 %all_to_all.26.own_ref = bf16[4,128,1024]{2,1,0:T(8,128)(2,1)S(1)} all-to-all(bf16[4,128,1024]{2,1,0:T(8,128)(2,1)S(1)} %broadcast_in_dim.4), channel_id=1, replica_groups=mesh['y'=4,'m'=8,'p'=2,'x'=4,'core'=2] {'x'}, dimensions={0} | all-to-all | bytes 2097152 | tf_op jit(solution)/shard_map/all_to_all | solution.py:43
  34.0 7.9 %collective-permute-start = (bf16[4,128,1024]{2,1,0:T(8,128)(2,1)S(1)}, bf16[4,128,1024]{2,1,0:T(8,128)(2,1)S(1)}, u32[]{:S(2)}, u32[]{:S(2)}) collective-permute-start(bf16[4,128,1024]{2,1,0:T(8,128)(2,1)S(1)} %all_to_all.26.own_ref), channel_id=1, source_target_pairs={{0,1},{1,0},{2,3},{3,2},{4,5},{5,4},{6,7},{7,6},{8,9},{9,8},{10,11... | collective-permute-start | bytes 3145736 | tf_op jit(solution)/shard_map/ppermute | solution.py:39
  41.8 0.1 pad_add_fusion.ids_ref.refs_0_
  41.9 1.1 gate.1
  43.1 1.0 collective-permute-done.other_ref
  44.1 2.1 %tiles.3 = (bf16[16,128,128]{2,1,0:T(8,128)(2,1)S(1)}, bf16[16,128,128]{2,1,0:T(8,128)(2,1)S(1)}) custom-call(s32[4]{0:T(128)S(1)} %pad_add_fusion.ids_ref.refs_0_, s32[1,112]{1,0:T(1,128)S(1)} %copy-done.10, s32[1,112]{1,0:T(1,128)S(1)} %copy-done.11, s32[1,64]{1,0:T(1,128)S(1)} %copy-done.9, bf16[4,128,1024]{2,1,0:T(8,128)(2,1)S(1)} %all_to_all.26.own_ref, ...), custom_call_target="tpu_custom_call" | custom-call | flops 117440512 | bytes 2097152 | tf_op jit(solution)/shard_map/tiles/pallas_call | solution.py:303
  46.2 2.8 %collective-permute-start.2 = (bf16[16,128,128]{2,1,0:T(8,128)(2,1)S(1)}, bf16[16,128,128]{2,1,0:T(8,128)(2,1)S(1)}, u32[]{:S(2)}, u32[]{:S(2)}) collective-permute-start(bf16[16,128,128]{2,1,0:T(8,128)(2,1)S(1)} %get-tuple-element.60), channel_id=1, source_target_pairs={{0,384},{128,256},{256,128},{384,0},{1,385},{129,257},{257,129},{3... | collective-permute-start | bytes 1572872 | tf_op jit(solution)/shard_map/ppermute | solution.py:39
  49.0 1.9 collective-permute-start.3
  50.9 2.1 %tiles.4 = (bf16[16,128,128]{2,1,0:T(8,128)(2,1)S(1)}, bf16[16,128,128]{2,1,0:T(8,128)(2,1)S(1)}) custom-call(s32[4]{0:T(128)S(1)} %pad_add_fusion.ids_ref.refs_0_, s32[1,112]{1,0:T(1,128)S(1)} %copy-done.10, s32[1,112]{1,0:T(1,128)S(1)} %copy-done.11, s32[1,64]{1,0:T(1,128)S(1)} %copy-done.9, bf16[4,128,1024]{2,1,0:T(8,128)(2,1)S(1)} %all_to_all.26.own_ref, ...), custom_call_target="tpu_custom_call" | custom-call | flops 117440512 | bytes 2097152 | tf_op jit(solution)/shard_map/tiles/pallas_call | solution.py:303
  53.0 3.1 %tiles.5 = (bf16[16,128,128]{2,1,0:T(8,128)(2,1)S(1)}, bf16[16,128,128]{2,1,0:T(8,128)(2,1)S(1)}, bf16[32,128,128]{2,1,0:T(8,128)(2,1)S(1)}) custom-call(s32[4]{0:T(128)S(1)} %pad_add_fusion.ids_ref.refs_0_, s32[1,112]{1,0:T(1,128)S(1)} %copy-done.10, s32[1,112]{1,0:T(1,128)S(1)} %copy-done.11, s32[1,64]{1,0:T(1,128)S(1)} %copy-done.9, ...), custom_call_target="tpu_custom_call" | custom-call | flops 117440512 | bytes 2097152 | tf_op jit(solution)/shard_map/tiles/pallas_call | solution.py:303
  56.0 3.4 %collective-permute-start.1 = (bf16[16,128,128]{2,1,0:T(8,128)(2,1)S(1)}, bf16[16,128,128]{2,1,0:T(8,128)(2,1)S(1)}, u32[]{:S(2)}, u32[]{:S(2)}) collective-permute-start(bf16[16,128,128]{2,1,0:T(8,128)(2,1)S(1)} %get-tuple-element.58), channel_id=1, source_target_pairs={{0,128},{128,0},{256,384},{384,256},{1,129},{129,1},{257,385},{385... | collective-permute-start | bytes 1572872 | tf_op jit(solution)/shard_map/ppermute | solution.py:39
  59.4 3.7 %collective-permute-start.6 = (bf16[16,128,128]{2,1,0:T(8,128)(2,1)S(1)}, bf16[16,128,128]{2,1,0:T(8,128)(2,1)S(1)}, u32[]{:S(2)}, u32[]{:S(2)}) collective-permute-start(bf16[16,128,128]{2,1,0:T(8,128)(2,1)S(1)} %get-tuple-element.65), channel_id=1, source_target_pairs={{0,384},{128,256},{256,128},{384,0},{1,385},{129,257},{257,129},{3... | collective-permute-start | bytes 1572872 | tf_op jit(solution)/shard_map/ppermute | solution.py:39
  63.1 0.6 collective-permute-done.3.for_other_ref
  63.8 0.2 passing.1
  64.0 0.0 copy-start.6
  64.0 3.9 %collective-permute-start.4 = (bf16[16,128,128]{2,1,0:T(8,128)(2,1)S(1)}, bf16[16,128,128]{2,1,0:T(8,128)(2,1)S(1)}, u32[]{:S(2)}, u32[]{:S(2)}) collective-permute-start(bf16[16,128,128]{2,1,0:T(8,128)(2,1)S(1)} %get-tuple-element.63), channel_id=1, source_target_pairs={{0,384},{128,256},{256,128},{384,0},{1,385},{129,257},{257,129},{3... | collective-permute-start | bytes 1572872 | tf_op jit(solution)/shard_map/ppermute | solution.py:39
  67.9 1.9 collective-permute-start.5
  69.8 5.2 %collective-permute-done.1 = bf16[16,128,128]{2,1,0:T(8,128)(2,1)S(1)} collective-permute-done((bf16[16,128,128]{2,1,0:T(8,128)(2,1)S(1)}, bf16[16,128,128]{2,1,0:T(8,128)(2,1)S(1)}, u32[]{:S(2)}, u32[]{:S(2)}) %collective-permute-start.1) | collective-permute-done | bytes 524320 | tf_op jit(solution)/shard_map/ppermute | solution.py:39
  75.0 11.0 %collective-permute-done.4 = bf16[16,128,128]{2,1,0:T(8,128)(2,1)S(1)} collective-permute-done((bf16[16,128,128]{2,1,0:T(8,128)(2,1)S(1)}, bf16[16,128,128]{2,1,0:T(8,128)(2,1)S(1)}, u32[]{:S(2)}, u32[]{:S(2)}) %collective-permute-start.4) | collective-permute-done | bytes 524320 | tf_op jit(solution)/shard_map/ppermute | solution.py:39
  86.0 0.2 collective-permute-done.5
  86.2 0.9 y_sum.1
  87.2 3.5 %collective-permute-start.7 = (bf16[8,2,128,128]{3,2,1,0:T(8,128)(2,1)S(1)}, bf16[8,2,128,128]{3,2,1,0:T(8,128)(2,1)S(1)}, u32[]{:S(2)}, u32[]{:S(2)}) collective-permute-start(bf16[8,2,128,128]{3,2,1,0:T(8,128)(2,1)S(1)} %get-tuple-element.69), channel_id=1, source_target_pairs={{0,8},{8,0},{1,9},{9,1},{2,10},{10,2},{3,11},{11,3},{4,12},{12,4},... | collective-permute-start | bytes 1572872 | tf_op jit(solution)/shard_map/ppermute | solution.py:39
  90.7 2.1 %all-gather.3.cloned.1.call-done.deltas_ref = bf16[128,128,128]{2,1,0:T(8,128)(2,1)} async-done(((bf16[8,128,128]{2,1,0:T(8,128)(2,1)}), bf16[128,128,128]{2,1,0:T(8,128)(2,1)}) %all-gather.3.cloned.1.call-update) | async-done | bytes 4194320 | tf_op jit(solution)/shard_map/all_gather | solution.py:288
  92.8 4.5 %contribs.1 = (bf16[64,8192]{1,0:T(8,128)(2,1)S(1)}, bf16[64,8192]{1,0:T(8,128)(2,1)S(1)}) custom-call(s32[1,112]{1,0:T(1,128)S(1)} %copy-done.10, s32[1,112]{1,0:T(1,128)S(1)} %copy-done.11, s32[1,64]{1,0:T(1,128)S(1)} %copy-done.9, bf16[14,128,128]{2,1,0:T(8,128)(2,1)S(1)} %copy-done.6, bf16[128,128,128]{2,1,0:T(8,128)(2,1)} %all-gather.3.cloned.1.call-done.deltas_ref), custom_call_target="tpu_custom_call" | custom-call | bytes 4096 | tf_op jit(solution)/shard_map/contribs/pallas_call | solution.py:332
  97.3 0.0 copy-start.12
  97.3 1.0 copy-done.12
  98.2 7.8 %collective-permute-done.7.taken_ref = bf16[8,2,128,128]{3,2,1,0:T(8,128)(2,1)S(1)} collective-permute-done((bf16[8,2,128,128]{3,2,1,0:T(8,128)(2,1)S(1)}, bf16[8,2,128,128]{3,2,1,0:T(8,128)(2,1)S(1)}, u32[]{:S(2)}, u32[]{:S(2)}) %collective-permute-start.7) | collective-permute-done | bytes 524320 | tf_op jit(solution)/shard_map/ppermute | solution.py:39
  106.0 0.9 pair_sum.1
  106.9 10.7 %all-to-all-start.2 = ((bf16[8,2,128,128]{3,2,1,0:T(8,128)(2,1)}), bf16[8,2,128,128]{3,2,1,0:T(8,128)(2,1)S(1)}, u32[]{:S(2)}, u32[]{:S(2)}) async-start(bf16[8,2,128,128]{3,2,1,0:T(8,128)(2,1)} %pair_sum.1), calls=%async_computation.2 | async-start | bytes 1048576 | tf_op jit(solution)/shard_map/all_to_all | solution.py:43
  117.6 0.0 all-gather.5.cloned.1.call-start
  117.7 4.3 %collective-permute-start.8 = (bf16[64,8192]{1,0:T(8,128)(2,1)S(1)}, bf16[64,8192]{1,0:T(8,128)(2,1)S(1)}, u32[]{:S(2)}, u32[]{:S(2)}) collective-permute-start(bf16[64,8192]{1,0:T(8,128)(2,1)S(1)} %copy-done.13), channel_id=1, source_target_pairs={{0,1},{1,0},{2,3},{3,2},{4,5},{5,4},{6,7},{7,6},{8,9},{9,8},{10,11... | collective-permute-start | bytes 3145736 | tf_op jit(solution)/shard_map/ppermute | solution.py:39
  122.0 2.3 %collective-permute-done.8 = bf16[64,8192]{1,0:T(8,128)(2,1)S(1)} collective-permute-done((bf16[64,8192]{1,0:T(8,128)(2,1)S(1)}, bf16[64,8192]{1,0:T(8,128)(2,1)S(1)}, u32[]{:S(2)}, u32[]{:S(2)}) %collective-permute-start.8) | collective-permute-done | bytes 1048608 | tf_op jit(solution)/shard_map/ppermute | solution.py:39
  124.3 0.8 core_sum.1
  125.1 2.3 %collective-permute-start.9 = (bf16[16,8192]{1,0:T(8,128)(2,1)S(1)}, bf16[16,8192]{1,0:T(8,128)(2,1)S(1)}, u32[]{:S(2)}, u32[]{:S(2)}) collective-permute-start(bf16[16,8192]{1,0:T(8,128)(2,1)S(1)} %get-tuple-element.76), channel_id=1, source_target_pairs={{0,2},{2,0},{4,6},{6,4},{1,3},{3,1},{5,7},{7,5},{8,10},{10,8},{12,... | collective-permute-start | bytes 786440 | tf_op jit(solution)/shard_map/ppermute | solution.py:39
  127.3 4.3 %collective-permute-start.10 = (bf16[16,8192]{1,0:T(8,128)(2,1)S(1)}, bf16[16,8192]{1,0:T(8,128)(2,1)S(1)}, u32[]{:S(2)}, u32[]{:S(2)}) collective-permute-start(bf16[16,8192]{1,0:T(8,128)(2,1)S(1)} %get-tuple-element.77), channel_id=1, source_target_pairs={{0,4},{2,6},{4,0},{6,2},{1,5},{3,7},{5,1},{7,3},{8,12},{10,14},{12... | collective-permute-start | bytes 786440 | tf_op jit(solution)/shard_map/ppermute | solution.py:39
  131.6 3.0 %collective-permute-start.11 = (bf16[16,8192]{1,0:T(8,128)(2,1)S(1)}, bf16[16,8192]{1,0:T(8,128)(2,1)S(1)}, u32[]{:S(2)}, u32[]{:S(2)}) collective-permute-start(bf16[16,8192]{1,0:T(8,128)(2,1)S(1)} %get-tuple-element.78), channel_id=1, source_target_pairs={{0,6},{2,4},{4,2},{6,0},{1,7},{3,5},{5,3},{7,1},{8,14},{10,12},{12... | collective-permute-start | bytes 786440 | tf_op jit(solution)/shard_map/ppermute | solution.py:39
  134.7 10.4 %all-to-all-done.2.arrived_ref = bf16[8,2,128,128]{3,2,1,0:T(8,128)(2,1)S(1)} async-done(((bf16[8,2,128,128]{3,2,1,0:T(8,128)(2,1)}), bf16[8,2,128,128]{3,2,1,0:T(8,128)(2,1)S(1)}, u32[]{:S(2)}, u32[]{:S(2)}) %all-to-all-start.2) | async-done | bytes 524320 | tf_op jit(solution)/shard_map/all_to_all | solution.py:43
  145.1 0.8 own_grad.1
  145.9 1.8 collective-permute-done.11
  147.7 0.8 add_convert_fusion
  148.5 0.0 all-gather.5.cloned.1.call-update
  148.6 16.3 %all_to_all.27.arrived_ref = f32[32,8,128]{2,1,0:T(8,128)S(1)} all-to-all(f32[32,8,128]{2,1,0:T(8,128)S(1)} %get-tuple-element.79), channel_id=1, replica_groups=mesh['y'=4,'m'=8,'p'=2,'x'=4,'core'=2] {'y','x','core'}, dimensions={0} | all-to-all | bytes 262144 | tf_op jit(solution)/shard_map/all_to_all | solution.py:43
  164.9 0.7 relay.1
  165.6 7.9 %all-to-all-start.4 = ((f32[16,8,128]{2,1,0:T(8,128)}), f32[16,8,128]{2,1,0:T(8,128)S(1)}, u32[]{:S(2)}, u32[]{:S(2)}) async-start(f32[16,8,128]{2,1,0:T(8,128)} %relay.1), calls=%async_computation.4 | async-start | bytes 131072 | tf_op jit(solution)/shard_map/all_to_all | solution.py:43
  173.5 0.0 copy-start.1
  173.5 0.0 copy-start.7
  173.5 0.0 copy-start.8
  173.5 7.0 %all-gather.5.cloned.1.call-done.in_ref = bf16[128,8192]{1,0:T(8,128)(2,1)} async-done(((bf16[16,8192]{1,0:T(8,128)(2,1)}), bf16[128,8192]{1,0:T(8,128)(2,1)}) %all-gather.5.cloned.1.call-update) | async-done | bytes 2097168 | tf_op jit(solution)/shard_map/all_gather | solution.py:366
  180.6 2.4 %result.1 = bf16[128,8192]{1,0:T(8,128)(2,1)} custom-call(bf16[128,8192]{1,0:T(8,128)(2,1)} %all-gather.5.cloned.1.call-done.in_ref), custom_call_target="tpu_custom_call" | custom-call | bytes 4194304 | tf_op jit(solution)/shard_map/result/pallas_call | solution.py:367
  183.0 2.1 %all-to-all-done.4.refs_2_ = f32[16,8,128]{2,1,0:T(8,128)S(1)} async-done(((f32[16,8,128]{2,1,0:T(8,128)}), f32[16,8,128]{2,1,0:T(8,128)S(1)}, u32[]{:S(2)}, u32[]{:S(2)}) %all-to-all-start.4) | async-done | bytes 65568 | tf_op jit(solution)/shard_map/all_to_all | solution.py:43
  185.1 1.5 adam.1
  (19 shorter events, 0.1 us)
Async XLA Ops:
  7.2 85.6 %all-gather.3.cloned.1.call-start = ((), (), s32[]{:S(2)}) async-start(), calls=%async_computation.5 | async-start | bytes 4456448 | tf_op jit(solution)/shard_map/all_gather | solution.py:288
  7.2 0.9 copy-start
  8.3 33.7 %copy-start.2 = (bf16[128,1792]{1,0:T(8,128)(2,1)S(1)}, bf16[128,1792]{1,0:T(8,128)(2,1)}, u32[]{:S(2)}) copy-start(bf16[128,1792]{1,0:T(8,128)(2,1)} %gate_ref.1) | copy-start | bytes 1376260
  8.3 33.6 %copy-start.3 = (bf16[128,1792]{1,0:T(8,128)(2,1)S(1)}, bf16[128,1792]{1,0:T(8,128)(2,1)}, u32[]{:S(2)}) copy-start(bf16[128,1792]{1,0:T(8,128)(2,1)} %up_ref.1) | copy-start | bytes 1376260
  8.3 33.6 %copy-start.4 = (bf16[128,1792]{1,0:T(8,128)(2,1)S(1)}, bf16[128,1792]{1,0:T(8,128)(2,1)}, u32[]{:S(2)}) copy-start(bf16[128,1792]{1,0:T(8,128)(2,1)} %hidden_ref.1) | copy-start | bytes 1376260
  18.9 25.2 %copy-start.9 = (s32[1,64]{1,0:T(1,128)S(1)}, s32[1,64]{1,0:T(1,128)}, u32[]{:S(2)}) copy-start(s32[1,64]{1,0:T(1,128)} %refs_1_.1) | copy-start | bytes 772
  18.9 25.2 %copy-start.10 = (s32[1,112]{1,0:T(1,128)S(1)}, s32[1,112]{1,0:T(1,128)}, u32[]{:S(2)}) copy-start(s32[1,112]{1,0:T(1,128)} %rows_ref.7) | copy-start | bytes 1348
  18.9 25.2 %copy-start.11 = (s32[1,112]{1,0:T(1,128)S(1)}, s32[1,112]{1,0:T(1,128)}, u32[]{:S(2)}) copy-start(s32[1,112]{1,0:T(1,128)} %cols_ref.7) | copy-start | bytes 1348
  34.0 10.1 %collective-permute-start = (bf16[4,128,1024]{2,1,0:T(8,128)(2,1)S(1)}, bf16[4,128,1024]{2,1,0:T(8,128)(2,1)S(1)}, u32[]{:S(2)}, u32[]{:S(2)}) collective-permute-start(bf16[4,128,1024]{2,1,0:T(8,128)(2,1)S(1)} %all_to_all.26.own_ref), channel_id=1, source_target_pairs={{0,1},{1,0},{2,3},{3,2},{4,5},{5,4},{6,7},{7,6},{8,9},{9,8},{10,11... | collective-permute-start | bytes 3145736 | tf_op jit(solution)/shard_map/ppermute | solution.py:39
  43.0 9.9 %copy-start.5 = (bf16[14,128,128]{2,1,0:T(8,128)(2,1)}, bf16[14,128,128]{2,1,0:T(8,128)(2,1)S(1)}, u32[]{:S(2)}) copy-start(bf16[14,128,128]{2,1,0:T(8,128)(2,1)S(1)} %get-tuple-element.70.grads_ref) | copy-start | bytes 1376260
  46.2 17.0 %collective-permute-start.2 = (bf16[16,128,128]{2,1,0:T(8,128)(2,1)S(1)}, bf16[16,128,128]{2,1,0:T(8,128)(2,1)S(1)}, u32[]{:S(2)}, u32[]{:S(2)}) collective-permute-start(bf16[16,128,128]{2,1,0:T(8,128)(2,1)S(1)} %get-tuple-element.60), channel_id=1, source_target_pairs={{0,384},{128,256},{256,128},{384,0},{1,385},{129,257},{257,129},{3... | collective-permute-start | bytes 1572872 | tf_op jit(solution)/shard_map/ppermute | solution.py:39
  49.0 14.8 %collective-permute-start.3 = (bf16[16,128,128]{2,1,0:T(8,128)(2,1)S(1)}, bf16[16,128,128]{2,1,0:T(8,128)(2,1)S(1)}, u32[]{:S(2)}, u32[]{:S(2)}) collective-permute-start(bf16[16,128,128]{2,1,0:T(8,128)(2,1)S(1)} %get-tuple-element.62), channel_id=1, source_target_pairs={{0,128},{128,0},{256,384},{384,256},{1,129},{129,1},{257,385},{385... | collective-permute-start | bytes 1572872 | tf_op jit(solution)/shard_map/ppermute | solution.py:39
  56.0 19.0 %collective-permute-start.1 = (bf16[16,128,128]{2,1,0:T(8,128)(2,1)S(1)}, bf16[16,128,128]{2,1,0:T(8,128)(2,1)S(1)}, u32[]{:S(2)}, u32[]{:S(2)}) collective-permute-start(bf16[16,128,128]{2,1,0:T(8,128)(2,1)S(1)} %get-tuple-element.58), channel_id=1, source_target_pairs={{0,128},{128,0},{256,384},{384,256},{1,129},{129,1},{257,385},{385... | collective-permute-start | bytes 1572872 | tf_op jit(solution)/shard_map/ppermute | solution.py:39
  59.4 15.6 %collective-permute-start.6 = (bf16[16,128,128]{2,1,0:T(8,128)(2,1)S(1)}, bf16[16,128,128]{2,1,0:T(8,128)(2,1)S(1)}, u32[]{:S(2)}, u32[]{:S(2)}) collective-permute-start(bf16[16,128,128]{2,1,0:T(8,128)(2,1)S(1)} %get-tuple-element.65), channel_id=1, source_target_pairs={{0,384},{128,256},{256,128},{384,0},{1,385},{129,257},{257,129},{3... | collective-permute-start | bytes 1572872 | tf_op jit(solution)/shard_map/ppermute | solution.py:39
  64.0 28.8 %copy-start.6 = (bf16[14,128,128]{2,1,0:T(8,128)(2,1)S(1)}, bf16[14,128,128]{2,1,0:T(8,128)(2,1)}, u32[]{:S(2)}) copy-start(bf16[14,128,128]{2,1,0:T(8,128)(2,1)} %copy-done.5) | copy-start | bytes 1376260
  64.0 22.0 %collective-permute-start.4 = (bf16[16,128,128]{2,1,0:T(8,128)(2,1)S(1)}, bf16[16,128,128]{2,1,0:T(8,128)(2,1)S(1)}, u32[]{:S(2)}, u32[]{:S(2)}) collective-permute-start(bf16[16,128,128]{2,1,0:T(8,128)(2,1)S(1)} %get-tuple-element.63), channel_id=1, source_target_pairs={{0,384},{128,256},{256,128},{384,0},{1,385},{129,257},{257,129},{3... | collective-permute-start | bytes 1572872 | tf_op jit(solution)/shard_map/ppermute | solution.py:39
  67.9 18.4 %collective-permute-start.5 = (bf16[16,128,128]{2,1,0:T(8,128)(2,1)S(1)}, bf16[16,128,128]{2,1,0:T(8,128)(2,1)S(1)}, u32[]{:S(2)}, u32[]{:S(2)}) collective-permute-start(bf16[16,128,128]{2,1,0:T(8,128)(2,1)S(1)} %get-tuple-element.64), channel_id=1, source_target_pairs={{0,128},{128,0},{256,384},{384,256},{1,129},{129,1},{257,385},{385... | collective-permute-start | bytes 1572872 | tf_op jit(solution)/shard_map/ppermute | solution.py:39
  87.2 18.8 %collective-permute-start.7 = (bf16[8,2,128,128]{3,2,1,0:T(8,128)(2,1)S(1)}, bf16[8,2,128,128]{3,2,1,0:T(8,128)(2,1)S(1)}, u32[]{:S(2)}, u32[]{:S(2)}) collective-permute-start(bf16[8,2,128,128]{3,2,1,0:T(8,128)(2,1)S(1)} %get-tuple-element.69), channel_id=1, source_target_pairs={{0,8},{8,0},{1,9},{9,1},{2,10},{10,2},{3,11},{11,3},{4,12},{12,4},... | collective-permute-start | bytes 1572872 | tf_op jit(solution)/shard_map/ppermute | solution.py:39
  97.3 1.0 copy-start.12
  106.0 11.6 %copy-start.13 = (bf16[64,8192]{1,0:T(8,128)(2,1)S(1)}, bf16[64,8192]{1,0:T(8,128)(2,1)}, u32[]{:S(2)}) copy-start(bf16[64,8192]{1,0:T(8,128)(2,1)} %copy-done.12) | copy-start | bytes 3145732
  106.9 38.2 %all-to-all-start.2 = ((bf16[8,2,128,128]{3,2,1,0:T(8,128)(2,1)}), bf16[8,2,128,128]{3,2,1,0:T(8,128)(2,1)S(1)}, u32[]{:S(2)}, u32[]{:S(2)}) async-start(bf16[8,2,128,128]{3,2,1,0:T(8,128)(2,1)} %pair_sum.1), calls=%async_computation.2 | async-start | bytes 1048576 | tf_op jit(solution)/shard_map/all_to_all | solution.py:43
  117.6 63.0 %all-gather.5.cloned.1.call-start = ((), (), s32[]{:S(2)}) async-start(), calls=%async_computation.6 | async-start | bytes 2359296 | tf_op jit(solution)/shard_map/all_gather | solution.py:366
  117.7 6.6 %collective-permute-start.8 = (bf16[64,8192]{1,0:T(8,128)(2,1)S(1)}, bf16[64,8192]{1,0:T(8,128)(2,1)S(1)}, u32[]{:S(2)}, u32[]{:S(2)}) collective-permute-start(bf16[64,8192]{1,0:T(8,128)(2,1)S(1)} %copy-done.13), channel_id=1, source_target_pairs={{0,1},{1,0},{2,3},{3,2},{4,5},{5,4},{6,7},{7,6},{8,9},{9,8},{10,11... | collective-permute-start | bytes 3145736 | tf_op jit(solution)/shard_map/ppermute | solution.py:39
  125.1 20.8 %collective-permute-start.9 = (bf16[16,8192]{1,0:T(8,128)(2,1)S(1)}, bf16[16,8192]{1,0:T(8,128)(2,1)S(1)}, u32[]{:S(2)}, u32[]{:S(2)}) collective-permute-start(bf16[16,8192]{1,0:T(8,128)(2,1)S(1)} %get-tuple-element.76), channel_id=1, source_target_pairs={{0,2},{2,0},{4,6},{6,4},{1,3},{3,1},{5,7},{7,5},{8,10},{10,8},{12,... | collective-permute-start | bytes 786440 | tf_op jit(solution)/shard_map/ppermute | solution.py:39
  127.3 18.5 %collective-permute-start.10 = (bf16[16,8192]{1,0:T(8,128)(2,1)S(1)}, bf16[16,8192]{1,0:T(8,128)(2,1)S(1)}, u32[]{:S(2)}, u32[]{:S(2)}) collective-permute-start(bf16[16,8192]{1,0:T(8,128)(2,1)S(1)} %get-tuple-element.77), channel_id=1, source_target_pairs={{0,4},{2,6},{4,0},{6,2},{1,5},{3,7},{5,1},{7,3},{8,12},{10,14},{12... | collective-permute-start | bytes 786440 | tf_op jit(solution)/shard_map/ppermute | solution.py:39
  131.6 16.1 %collective-permute-start.11 = (bf16[16,8192]{1,0:T(8,128)(2,1)S(1)}, bf16[16,8192]{1,0:T(8,128)(2,1)S(1)}, u32[]{:S(2)}, u32[]{:S(2)}) collective-permute-start(bf16[16,8192]{1,0:T(8,128)(2,1)S(1)} %get-tuple-element.78), channel_id=1, source_target_pairs={{0,6},{2,4},{4,2},{6,0},{1,7},{3,5},{5,3},{7,1},{8,14},{10,12},{12... | collective-permute-start | bytes 786440 | tf_op jit(solution)/shard_map/ppermute | solution.py:39
  165.6 19.5 %all-to-all-start.4 = ((f32[16,8,128]{2,1,0:T(8,128)}), f32[16,8,128]{2,1,0:T(8,128)S(1)}, u32[]{:S(2)}, u32[]{:S(2)}) async-start(f32[16,8,128]{2,1,0:T(8,128)} %relay.1), calls=%async_computation.4 | async-start | bytes 131072 | tf_op jit(solution)/shard_map/all_to_all | solution.py:43
  173.5 11.6 %copy-start.1 = (f32[1,2,128,128]{3,2,1,0:T(8,128)S(1)}, f32[1,2,128,128]{3,2,1,0:T(8,128)}, u32[]{:S(2)}) copy-start(f32[1,2,128,128]{3,2,1,0:T(8,128)} %refs_4_.1) | copy-start | bytes 393220
  173.5 11.6 %copy-start.7 = (f32[1,2,128,128]{3,2,1,0:T(8,128)S(1)}, f32[1,2,128,128]{3,2,1,0:T(8,128)}, u32[]{:S(2)}) copy-start(f32[1,2,128,128]{3,2,1,0:T(8,128)} %refs_5_.1) | copy-start | bytes 393220
  173.5 11.6 %copy-start.8 = (f32[1,2,128,128]{3,2,1,0:T(8,128)S(1)}, f32[1,2,128,128]{3,2,1,0:T(8,128)}, u32[]{:S(2)}) copy-start(f32[1,2,128,128]{3,2,1,0:T(8,128)} %refs_6_.1) | copy-start | bytes 393220
Sparse Core Ops, SparseCore 0:
  19.0 73.7 all-gather.2
  148.7 31.8 all-gather.4

commit v12 on v11

--- a/solution.py
+++ b/solution.py
@@ -99,7 +99,7 @@
                 lane = pl.multiple_of((row & 7) * TILE, TILE)
                 x = features[((row >> 3) & 1) ^ core, row >> 4, :, pl.ds(lane, TILE)]
                 term = jnp.dot(turned_ref[cols_ref[0, k]], x, preferred_element_type=F32)
-                put((index * per_step + part) * SLOT_CAP + rank, term.astype(BF16))
+                put((index * per_step + part) * SLOT_CAP + rank, term)
         return carry
 
     lax.fori_loop(0, (owners[1] - owners[0]) // per_step, step, 0)
@@ -108,22 +108,19 @@
 def tile_kernel(
     parts, ids_ref, rows_ref, cols_ref, counts_ref, own_ref, other_ref, turned_ref, *refs
 ):
-    features, starts_ref, sems = refs[len(parts) :]
+    features, starts_ref, sems = refs[-3:]
     load_features(own_ref, other_ref, features, sems, starts_ref, counts_ref)
-    for ref, (bits, owners) in zip(refs, parts):
-
-        def put(slot, term, ref=ref):
-            ref[slot] = term
+    for ref, (bits, owners, extra) in zip(refs[-3 - len(parts) :], parts):
+
+        def put(slot, term, ref=ref, extra=extra):
+            if extra is not None:
+                term = term + refs[extra][slot].astype(F32)
+            ref[slot] = term.astype(BF16)
 
         slot_products(
             ids_ref[0] ^ bits, owners, put,
             ids_ref, rows_ref, cols_ref, starts_ref, features, turned_ref,
         )
-
-
-def passing_kernel(one_ref, for_one_ref, other_ref, for_other_ref, one_out, other_out):
-    one_out[...] = (one_ref[...].astype(F32) + for_one_ref[...].astype(F32)).astype(BF16)
-    other_out[...] = (other_ref[...].astype(F32) + for_other_ref[...].astype(F32)).astype(BF16)
 
 
 def y_sum_kernel(
@@ -299,24 +296,22 @@
         pltpu.SemaphoreType.DMA((2,)),
     ]
 
-    def terms(turned, *parts):
-        *values, turned = lax.optimization_barrier((*kernel_call(
+    def terms(parts, *extras):
+        return kernel_call(
             functools.partial(tile_kernel, parts), "tiles",
-            [SHAPE(((last - first) * SLOT_CAP, TILE, TILE), BF16) for _, (first, last) in parts],
-            tile_ins, [VMEM] * len(parts), tile_scratch,
+            [SHAPE(((last - first) * SLOT_CAP, TILE, TILE), BF16) for _, (first, last), _ in parts],
+            tile_ins + [VMEM] * len(extras), [VMEM] * len(parts), tile_scratch,
             flops=2 * tile_total * TILE**3 // 4, moved=2 << 20,
-        )(ids, *lists, own, other, turned), turned))
-        return values, turned
-
-    (far_low, far_high), turned = terms(turned, (2, LOW), (2, HIGH))
+        )(ids, *lists, own, other, turned, *extras)
+
+    far_low, far_high, one_low, other_high = terms(
+        ((2, LOW, None), (2, HIGH, None), (1, LOW, None), (3, HIGH, None))
+    )
     far_low, far_high = swap(far_low, "y", 1), swap(far_high, "y", 3)
-    (one_low, other_high), turned = terms(turned, (1, LOW), (3, HIGH))
     one_low, other_high = swap(one_low, "y", 1), swap(other_high, "y", 3)
-    (one_high, other_low, mine), turned = terms(turned, (1, HIGH), (3, LOW), (0, (0, NZ)))
-    half = SHAPE(one_high.shape, BF16)
-    one_high, other_low = kernel_call(
-        passing_kernel, "passing", [half] * 2, [VMEM] * 4, [VMEM] * 2
-    )(one_high, far_high, other_low, far_low)
+    one_high, other_low, mine = terms(
+        ((1, HIGH, 0), (3, LOW, 1), (0, (0, NZ), None)), far_high, far_low
+    )
     one_high, other_low = swap(one_high, "y", 1), swap(other_low, "y", 3)
 
     def parted(value):
@@ -358,7 +353,7 @@
         core_sum_kernel, "core_sum", [SHAPE((rows, width), BF16)] * NX,
         [SMEM] + [VMEM] * 2, [VMEM] * NX, moved=1 << 12,
     )(ids, stay.reshape(NX, rows, width), taken.reshape(NX, rows, width))
-    others = [swap(part, "x", bits + 1) for bits, part in enumerate(others)]
+    others = [swap(others[bits - 1], "x", bits) for bits in (2, 1, 3)]
     squares, share, *others = lax.optimization_barrier((squares, share, *others))
     share = share.astype(F32)
     for part in others:

time: 194 us -> 190 us (0.979)
  blocking collectives: 40.8 us -> 45.5 us
  waiting for transfers between devices: 51.6 us -> 46.9 us
  starting transfers between devices: 61.5 us -> 58.9 us
    all_to_all x2, waiting for transfers between devices: 12.5 us -> 6.82 us  [exchange(): return lax.all_to_all(value, axis, split_axis=0, concat_axis=0, tiled=True)]
    all_to_all x3, blocking collectives: 40.8 us -> 45.5 us  [exchange(): return lax.all_to_all(value, axis, split_axis=0, concat_axis=0, tiled=True)]
    all_to_all x2, starting transfers between devices: 18.6 us -> 15.5 us  [exchange(): return lax.all_to_all(value, axis, split_axis=0, concat_axis=0, tiled=True)]
    pallas_call x3 -> x2, Pallas kernels: 7.2 us -> 6.08 us  [terms(): kernel_call(functools.partial(tile_kernel, parts), 'tiles', [SHAPE(((last...]
  transfers between devices with their start and end apart: 16 -> 16, of which waited for: 12 -> 14; matrix products, arithmetic and copies ran while one was open for 1% -> 1% of each run, Pallas kernels for 10% -> 9%
where the time goes in v12:
time: 190 us; the launch traced here: 189 us
  starting transfers between devices  58.9 us (31%)
  waiting for transfers between devices  46.9 us (25%)
  blocking collectives  45.5 us (24%)
  Pallas kernels  19.7 us (10%)
  between operations  14.4 us (8%)
  local copies, waits for them, and re-layouts  3.05 us (2%)
    all_to_all x3, blocking collectives, exchange(): return lax.all_to_all(value, axis, split_axis=0, concat_axis=0, tiled=True)  45.5 us
    ppermute x12, starting transfers between devices, swap(): lax.ppermute(value, axis, [(i, i ^ bits) for i in range(lax.axis_size(axi...  43.4 us
    ppermute x12, waiting for transfers between devices, swap(): lax.ppermute(value, axis, [(i, i ^ bits) for i in range(lax.axis_size(axi...  29.3 us
    all_to_all x2, starting transfers between devices, exchange(): return lax.all_to_all(value, axis, split_axis=0, concat_axis=0, tiled=True)  15.5 us
    all_gather x1, waiting for transfers between devices, body(): lax.all_gather(share.astype(BF16), ('x', 'core'), axis=0, tiled=True)  7.04 us
    all_to_all x2, waiting for transfers between devices, exchange(): return lax.all_to_all(value, axis, split_axis=0, concat_axis=0, tiled=True)  6.82 us
    pallas_call x2, Pallas kernels, terms(): kernel_call(functools.partial(tile_kernel, parts), 'tiles', [SHAPE(((last...  6.08 us
    pallas_call x1, Pallas kernels, body(): kernel_call(contrib_kernel, 'contribs', [SHAPE((tokens // 2, width), BF16...  4.46 us
  transfers between devices with their start and end apart: 16, of which 14 were waited for; matrix products, arithmetic and copies ran while one was open for 1% of the time, Pallas kernels for 9%

profile of v12, /device:TPU:1, one launch (start us, length us, event | category | flops | bytes accessed | tf_op | source)
XLA Modules:
  0.0 189.3 jit_solution(8998199510564625180)
XLA Ops:
  7.2 0.0 all-gather.3.cloned.1.call-start
  7.2 0.0 copy-start
  7.2 0.9 copy-done
  8.1 0.1 turn.1
  8.3 0.0 copy-start.2
  8.3 0.0 copy-start.3
  8.3 0.0 copy-start.4
  8.3 10.6 %all_to_all.25 = bf16[4,2,128,128]{3,2,1,0:T(8,128)(2,1)} all-to-all(bf16[4,2,128,128]{3,2,1,0:T(8,128)(2,1)S(1)} %broadcast_in_dim.5), channel_id=1, replica_groups=mesh['y'=4,'m'=8,'p'=2,'x'=4,'core'=2] {'y'}, dimensions={0} | all-to-all | bytes 524288 | tf_op jit(solution)/shard_map/all_to_all | solution.py:43
  18.9 0.0 all-gather.3.cloned.1.call-update
  18.9 0.0 copy-start.9
  18.9 0.0 copy-start.10
  18.9 0.0 copy-start.11
  18.9 1.1 broadcast_in_dim.4
  20.0 13.9 %all_to_all.26.own_ref = bf16[4,128,1024]{2,1,0:T(8,128)(2,1)S(1)} all-to-all(bf16[4,128,1024]{2,1,0:T(8,128)(2,1)S(1)} %broadcast_in_dim.4), channel_id=1, replica_groups=mesh['y'=4,'m'=8,'p'=2,'x'=4,'core'=2] {'x'}, dimensions={0} | all-to-all | bytes 2097152 | tf_op jit(solution)/shard_map/all_to_all | solution.py:43
  34.0 7.9 %collective-permute-start = (bf16[4,128,1024]{2,1,0:T(8,128)(2,1)S(1)}, bf16[4,128,1024]{2,1,0:T(8,128)(2,1)S(1)}, u32[]{:S(2)}, u32[]{:S(2)}) collective-permute-start(bf16[4,128,1024]{2,1,0:T(8,128)(2,1)S(1)} %all_to_all.26.own_ref), channel_id=1, source_target_pairs={{0,1},{1,0},{2,3},{3,2},{4,5},{5,4},{6,7},{7,6},{8,9},{9,8},{10,11... | collective-permute-start | bytes 3145736 | tf_op jit(solution)/shard_map/ppermute | solution.py:39
  41.8 0.1 pad_add_fusion.ids_ref.refs_0_
  41.9 1.1 gate.1
  43.1 1.0 collective-permute-done.other_ref
  44.1 3.0 %tiles.2 = (bf16[16,128,128]{2,1,0:T(8,128)(2,1)S(1)}, bf16[16,128,128]{2,1,0:T(8,128)(2,1)S(1)}, bf16[16,128,128]{2,1,0:T(8,128)(2,1)S(1)}, bf16[16,128,128]{2,1,0:T(8,128)(2,1)S(1)}) custom-call(s32[4]{0:T(128)S(1)} %pad_add_fusion.ids_ref.refs_0_, s32[1,112]{1,0:T(1,128)S(1)} %copy-done.10, s32[1,112]{1,0:T(1,128)S(1)} %copy-done.11, ...), custom_call_target="tpu_custom_call" | custom-call | flops 117440512 | bytes 2097152 | tf_op jit(solution)/shard_map/tiles/pallas_call | solution.py:300
  47.1 2.8 %collective-permute-start.1 = (bf16[16,128,128]{2,1,0:T(8,128)(2,1)S(1)}, bf16[16,128,128]{2,1,0:T(8,128)(2,1)S(1)}, u32[]{:S(2)}, u32[]{:S(2)}) collective-permute-start(bf16[16,128,128]{2,1,0:T(8,128)(2,1)S(1)} %get-tuple-element.37), channel_id=1, source_target_pairs={{0,384},{128,256},{256,128},{384,0},{1,385},{129,257},{257,129},{3... | collective-permute-start | bytes 1572872 | tf_op jit(solution)/shard_map/ppermute | solution.py:39
  49.9 1.9 %collective-permute-start.2 = (bf16[16,128,128]{2,1,0:T(8,128)(2,1)S(1)}, bf16[16,128,128]{2,1,0:T(8,128)(2,1)S(1)}, u32[]{:S(2)}, u32[]{:S(2)}) collective-permute-start(bf16[16,128,128]{2,1,0:T(8,128)(2,1)S(1)} %get-tuple-element.38), channel_id=1, source_target_pairs={{0,128},{128,0},{256,384},{384,256},{1,129},{129,1},{257,385},{385... | collective-permute-start | bytes 1572872 | tf_op jit(solution)/shard_map/ppermute | solution.py:39
  51.8 3.4 %collective-permute-start.3 = (bf16[16,128,128]{2,1,0:T(8,128)(2,1)S(1)}, bf16[16,128,128]{2,1,0:T(8,128)(2,1)S(1)}, u32[]{:S(2)}, u32[]{:S(2)}) collective-permute-start(bf16[16,128,128]{2,1,0:T(8,128)(2,1)S(1)} %get-tuple-element.40), channel_id=1, source_target_pairs={{0,128},{128,0},{256,384},{384,256},{1,129},{129,1},{257,385},{385... | collective-permute-start | bytes 1572872 | tf_op jit(solution)/shard_map/ppermute | solution.py:39
  55.2 3.7 %collective-permute-start.6 = (bf16[16,128,128]{2,1,0:T(8,128)(2,1)S(1)}, bf16[16,128,128]{2,1,0:T(8,128)(2,1)S(1)}, u32[]{:S(2)}, u32[]{:S(2)}) collective-permute-start(bf16[16,128,128]{2,1,0:T(8,128)(2,1)S(1)} %get-tuple-element.43), channel_id=1, source_target_pairs={{0,384},{128,256},{256,128},{384,0},{1,385},{129,257},{257,129},{3... | collective-permute-start | bytes 1572872 | tf_op jit(solution)/shard_map/ppermute | solution.py:39
  58.9 4.5 %collective-permute-done.1.refs_0_ = bf16[16,128,128]{2,1,0:T(8,128)(2,1)S(1)} collective-permute-done((bf16[16,128,128]{2,1,0:T(8,128)(2,1)S(1)}, bf16[16,128,128]{2,1,0:T(8,128)(2,1)S(1)}, u32[]{:S(2)}, u32[]{:S(2)}) %collective-permute-start.1) | collective-permute-done | bytes 524320 | tf_op jit(solution)/shard_map/ppermute | solution.py:39
  63.5 1.2 collective-permute-done.2.refs_1_
  64.6 3.0 %tiles.3 = (bf16[16,128,128]{2,1,0:T(8,128)(2,1)S(1)}, bf16[16,128,128]{2,1,0:T(8,128)(2,1)S(1)}, bf16[32,128,128]{2,1,0:T(8,128)(2,1)S(1)}) custom-call(s32[4]{0:T(128)S(1)} %pad_add_fusion.ids_ref.refs_0_, s32[1,112]{1,0:T(1,128)S(1)} %copy-done.10, s32[1,112]{1,0:T(1,128)S(1)} %copy-done.11, s32[1,64]{1,0:T(1,128)S(1)} %copy-done.9, ...), custom_call_target="tpu_custom_call" | custom-call | flops 117440512 | bytes 2097152 | tf_op jit(solution)/shard_map/tiles/pallas_call | solution.py:300
  67.7 0.0 copy-start.6
  67.7 3.9 %collective-permute-start.4 = (bf16[16,128,128]{2,1,0:T(8,128)(2,1)S(1)}, bf16[16,128,128]{2,1,0:T(8,128)(2,1)S(1)}, u32[]{:S(2)}, u32[]{:S(2)}) collective-permute-start(bf16[16,128,128]{2,1,0:T(8,128)(2,1)S(1)} %get-tuple-element.41), channel_id=1, source_target_pairs={{0,384},{128,256},{256,128},{384,0},{1,385},{129,257},{257,129},{3... | collective-permute-start | bytes 1572872 | tf_op jit(solution)/shard_map/ppermute | solution.py:39
  71.7 1.9 %collective-permute-start.5 = (bf16[16,128,128]{2,1,0:T(8,128)(2,1)S(1)}, bf16[16,128,128]{2,1,0:T(8,128)(2,1)S(1)}, u32[]{:S(2)}, u32[]{:S(2)}) collective-permute-start(bf16[16,128,128]{2,1,0:T(8,128)(2,1)S(1)} %get-tuple-element.42), channel_id=1, source_target_pairs={{0,128},{128,0},{256,384},{384,256},{1,129},{129,1},{257,385},{385... | collective-permute-start | bytes 1572872 | tf_op jit(solution)/shard_map/ppermute | solution.py:39
  73.6 2.4 %collective-permute-done.3 = bf16[16,128,128]{2,1,0:T(8,128)(2,1)S(1)} collective-permute-done((bf16[16,128,128]{2,1,0:T(8,128)(2,1)S(1)}, bf16[16,128,128]{2,1,0:T(8,128)(2,1)S(1)}, u32[]{:S(2)}, u32[]{:S(2)}) %collective-permute-start.3) | collective-permute-done | bytes 524320 | tf_op jit(solution)/shard_map/ppermute | solution.py:39
  76.0 9.3 %collective-permute-done.4 = bf16[16,128,128]{2,1,0:T(8,128)(2,1)S(1)} collective-permute-done((bf16[16,128,128]{2,1,0:T(8,128)(2,1)S(1)}, bf16[16,128,128]{2,1,0:T(8,128)(2,1)S(1)}, u32[]{:S(2)}, u32[]{:S(2)}) %collective-permute-start.4) | collective-permute-done | bytes 524320 | tf_op jit(solution)/shard_map/ppermute | solution.py:39
  85.3 0.4 collective-permute-done.5
  85.7 0.9 y_sum.1
  86.6 3.6 %collective-permute-start.7 = (bf16[8,2,128,128]{3,2,1,0:T(8,128)(2,1)S(1)}, bf16[8,2,128,128]{3,2,1,0:T(8,128)(2,1)S(1)}, u32[]{:S(2)}, u32[]{:S(2)}) collective-permute-start(bf16[8,2,128,128]{3,2,1,0:T(8,128)(2,1)S(1)} %get-tuple-element.47), channel_id=1, source_target_pairs={{0,8},{8,0},{1,9},{9,1},{2,10},{10,2},{3,11},{11,3},{4,12},{12,4},... | collective-permute-start | bytes 1572872 | tf_op jit(solution)/shard_map/ppermute | solution.py:39
  90.2 3.6 %all-gather.3.cloned.1.call-done.deltas_ref = bf16[128,128,128]{2,1,0:T(8,128)(2,1)} async-done(((bf16[8,128,128]{2,1,0:T(8,128)(2,1)}), bf16[128,128,128]{2,1,0:T(8,128)(2,1)}) %all-gather.3.cloned.1.call-update) | async-done | bytes 4194320 | tf_op jit(solution)/shard_map/all_gather | solution.py:285
  93.8 4.5 %contribs.1 = (bf16[64,8192]{1,0:T(8,128)(2,1)S(1)}, bf16[64,8192]{1,0:T(8,128)(2,1)S(1)}) custom-call(s32[1,112]{1,0:T(1,128)S(1)} %copy-done.10, s32[1,112]{1,0:T(1,128)S(1)} %copy-done.11, s32[1,64]{1,0:T(1,128)S(1)} %copy-done.9, bf16[14,128,128]{2,1,0:T(8,128)(2,1)S(1)} %copy-done.6, bf16[128,128,128]{2,1,0:T(8,128)(2,1)} %all-gather.3.cloned.1.call-done.deltas_ref), custom_call_target="tpu_custom_call" | custom-call | bytes 4096 | tf_op jit(solution)/shard_map/contribs/pallas_call | solution.py:327
  98.3 0.0 copy-start.12
  98.3 1.0 copy-done.12
  99.3 6.1 %collective-permute-done.7.taken_ref = bf16[8,2,128,128]{3,2,1,0:T(8,128)(2,1)S(1)} collective-permute-done((bf16[8,2,128,128]{3,2,1,0:T(8,128)(2,1)S(1)}, bf16[8,2,128,128]{3,2,1,0:T(8,128)(2,1)S(1)}, u32[]{:S(2)}, u32[]{:S(2)}) %collective-permute-start.7) | collective-permute-done | bytes 524320 | tf_op jit(solution)/shard_map/ppermute | solution.py:39
  105.3 0.9 pair_sum.1
  106.2 9.8 %all-to-all-start.2 = ((bf16[8,2,128,128]{3,2,1,0:T(8,128)(2,1)}), bf16[8,2,128,128]{3,2,1,0:T(8,128)(2,1)S(1)}, u32[]{:S(2)}, u32[]{:S(2)}) async-start(bf16[8,2,128,128]{3,2,1,0:T(8,128)(2,1)} %pair_sum.1), calls=%async_computation.2 | async-start | bytes 1048576 | tf_op jit(solution)/shard_map/all_to_all | solution.py:43
  116.1 0.0 all-gather.5.cloned.1.call-start
  116.1 5.4 %collective-permute-start.8 = (bf16[64,8192]{1,0:T(8,128)(2,1)S(1)}, bf16[64,8192]{1,0:T(8,128)(2,1)S(1)}, u32[]{:S(2)}, u32[]{:S(2)}) collective-permute-start(bf16[64,8192]{1,0:T(8,128)(2,1)S(1)} %copy-done.13), channel_id=1, source_target_pairs={{0,1},{1,0},{2,3},{3,2},{4,5},{5,4},{6,7},{7,6},{8,9},{9,8},{10,11... | collective-permute-start | bytes 3145736 | tf_op jit(solution)/shard_map/ppermute | solution.py:39
  121.5 2.3 %collective-permute-done.8 = bf16[64,8192]{1,0:T(8,128)(2,1)S(1)} collective-permute-done((bf16[64,8192]{1,0:T(8,128)(2,1)S(1)}, bf16[64,8192]{1,0:T(8,128)(2,1)S(1)}, u32[]{:S(2)}, u32[]{:S(2)}) %collective-permute-start.8) | collective-permute-done | bytes 1048608 | tf_op jit(solution)/shard_map/ppermute | solution.py:39
  123.8 0.8 core_sum.1
  124.6 3.4 %collective-permute-start.9 = (bf16[16,8192]{1,0:T(8,128)(2,1)S(1)}, bf16[16,8192]{1,0:T(8,128)(2,1)S(1)}, u32[]{:S(2)}, u32[]{:S(2)}) collective-permute-start(bf16[16,8192]{1,0:T(8,128)(2,1)S(1)} %get-tuple-element.54), channel_id=1, source_target_pairs={{0,4},{2,6},{4,0},{6,2},{1,5},{3,7},{5,1},{7,3},{8,12},{10,14},{12... | collective-permute-start | bytes 786440 | tf_op jit(solution)/shard_map/ppermute | solution.py:39
  128.0 2.7 %collective-permute-start.10 = (bf16[16,8192]{1,0:T(8,128)(2,1)S(1)}, bf16[16,8192]{1,0:T(8,128)(2,1)S(1)}, u32[]{:S(2)}, u32[]{:S(2)}) collective-permute-start(bf16[16,8192]{1,0:T(8,128)(2,1)S(1)} %get-tuple-element.55), channel_id=1, source_target_pairs={{0,2},{2,0},{4,6},{6,4},{1,3},{3,1},{5,7},{7,5},{8,10},{10,8},{12,... | collective-permute-start | bytes 786440 | tf_op jit(solution)/shard_map/ppermute | solution.py:39
  130.7 2.9 %collective-permute-start.11 = (bf16[16,8192]{1,0:T(8,128)(2,1)S(1)}, bf16[16,8192]{1,0:T(8,128)(2,1)S(1)}, u32[]{:S(2)}, u32[]{:S(2)}) collective-permute-start(bf16[16,8192]{1,0:T(8,128)(2,1)S(1)} %get-tuple-element.56), channel_id=1, source_target_pairs={{0,6},{2,4},{4,2},{6,0},{1,7},{3,5},{5,3},{7,1},{8,14},{10,12},{12... | collective-permute-start | bytes 786440 | tf_op jit(solution)/shard_map/ppermute | solution.py:39
  133.6 4.7 %all-to-all-done.2.arrived_ref = bf16[8,2,128,128]{3,2,1,0:T(8,128)(2,1)S(1)} async-done(((bf16[8,2,128,128]{3,2,1,0:T(8,128)(2,1)}), bf16[8,2,128,128]{3,2,1,0:T(8,128)(2,1)S(1)}, u32[]{:S(2)}, u32[]{:S(2)}) %all-to-all-start.2) | async-done | bytes 524320 | tf_op jit(solution)/shard_map/all_to_all | solution.py:43
  138.3 0.8 own_grad.1
  139.1 1.3 collective-permute-done.10
  140.4 0.9 collective-permute-done.11
  141.3 0.8 add_convert_fusion
  142.1 0.0 all-gather.5.cloned.1.call-update
  142.1 20.9 %all_to_all.27.arrived_ref = f32[32,8,128]{2,1,0:T(8,128)S(1)} all-to-all(f32[32,8,128]{2,1,0:T(8,128)S(1)} %get-tuple-element.57), channel_id=1, replica_groups=mesh['y'=4,'m'=8,'p'=2,'x'=4,'core'=2] {'y','x','core'}, dimensions={0} | all-to-all | bytes 262144 | tf_op jit(solution)/shard_map/all_to_all | solution.py:43
  163.1 0.7 relay.1
  163.8 5.6 %all-to-all-start.4 = ((f32[16,8,128]{2,1,0:T(8,128)}), f32[16,8,128]{2,1,0:T(8,128)S(1)}, u32[]{:S(2)}, u32[]{:S(2)}) async-start(f32[16,8,128]{2,1,0:T(8,128)} %relay.1), calls=%async_computation.4 | async-start | bytes 131072 | tf_op jit(solution)/shard_map/all_to_all | solution.py:43
  169.4 0.0 copy-start.1
  169.4 0.0 copy-start.7
  169.4 0.0 copy-start.8
  169.4 7.0 %all-gather.5.cloned.1.call-done.in_ref = bf16[128,8192]{1,0:T(8,128)(2,1)} async-done(((bf16[16,8192]{1,0:T(8,128)(2,1)}), bf16[128,8192]{1,0:T(8,128)(2,1)}) %all-gather.5.cloned.1.call-update) | async-done | bytes 2097168 | tf_op jit(solution)/shard_map/all_gather | solution.py:361
  176.5 2.4 %result.1 = bf16[128,8192]{1,0:T(8,128)(2,1)} custom-call(bf16[128,8192]{1,0:T(8,128)(2,1)} %all-gather.5.cloned.1.call-done.in_ref), custom_call_target="tpu_custom_call" | custom-call | bytes 4194304 | tf_op jit(solution)/shard_map/result/pallas_call | solution.py:362
  178.9 2.1 %all-to-all-done.4.refs_2_ = f32[16,8,128]{2,1,0:T(8,128)S(1)} async-done(((f32[16,8,128]{2,1,0:T(8,128)}), f32[16,8,128]{2,1,0:T(8,128)S(1)}, u32[]{:S(2)}, u32[]{:S(2)}) %all-to-all-start.4) | async-done | bytes 65568 | tf_op jit(solution)/shard_map/all_to_all | solution.py:43
  181.0 1.5 adam.1
  (17 shorter events, 0.1 us)
Async XLA Ops:
  7.2 86.7 %all-gather.3.cloned.1.call-start = ((), (), s32[]{:S(2)}) async-start(), calls=%async_computation.5 | async-start | bytes 4456448 | tf_op jit(solution)/shard_map/all_gather | solution.py:285
  7.2 0.9 copy-start
  8.3 33.7 %copy-start.2 = (bf16[128,1792]{1,0:T(8,128)(2,1)S(1)}, bf16[128,1792]{1,0:T(8,128)(2,1)}, u32[]{:S(2)}) copy-start(bf16[128,1792]{1,0:T(8,128)(2,1)} %gate_ref.1) | copy-start | bytes 1376260
  8.3 33.6 %copy-start.3 = (bf16[128,1792]{1,0:T(8,128)(2,1)S(1)}, bf16[128,1792]{1,0:T(8,128)(2,1)}, u32[]{:S(2)}) copy-start(bf16[128,1792]{1,0:T(8,128)(2,1)} %up_ref.1) | copy-start | bytes 1376260
  8.3 33.6 %copy-start.4 = (bf16[128,1792]{1,0:T(8,128)(2,1)S(1)}, bf16[128,1792]{1,0:T(8,128)(2,1)}, u32[]{:S(2)}) copy-start(bf16[128,1792]{1,0:T(8,128)(2,1)} %hidden_ref.1) | copy-start | bytes 1376260
  18.9 25.2 %copy-start.9 = (s32[1,64]{1,0:T(1,128)S(1)}, s32[1,64]{1,0:T(1,128)}, u32[]{:S(2)}) copy-start(s32[1,64]{1,0:T(1,128)} %refs_1_.1) | copy-start | bytes 772
  18.9 25.2 %copy-start.10 = (s32[1,112]{1,0:T(1,128)S(1)}, s32[1,112]{1,0:T(1,128)}, u32[]{:S(2)}) copy-start(s32[1,112]{1,0:T(1,128)} %rows_ref.5) | copy-start | bytes 1348
  18.9 25.2 %copy-start.11 = (s32[1,112]{1,0:T(1,128)S(1)}, s32[1,112]{1,0:T(1,128)}, u32[]{:S(2)}) copy-start(s32[1,112]{1,0:T(1,128)} %cols_ref.5) | copy-start | bytes 1348
  34.0 10.1 %collective-permute-start = (bf16[4,128,1024]{2,1,0:T(8,128)(2,1)S(1)}, bf16[4,128,1024]{2,1,0:T(8,128)(2,1)S(1)}, u32[]{:S(2)}, u32[]{:S(2)}) collective-permute-start(bf16[4,128,1024]{2,1,0:T(8,128)(2,1)S(1)} %all_to_all.26.own_ref), channel_id=1, source_target_pairs={{0,1},{1,0},{2,3},{3,2},{4,5},{5,4},{6,7},{7,6},{8,9},{9,8},{10,11... | collective-permute-start | bytes 3145736 | tf_op jit(solution)/shard_map/ppermute | solution.py:39
  43.0 24.7 %copy-start.5 = (bf16[14,128,128]{2,1,0:T(8,128)(2,1)}, bf16[14,128,128]{2,1,0:T(8,128)(2,1)S(1)}, u32[]{:S(2)}) copy-start(bf16[14,128,128]{2,1,0:T(8,128)(2,1)S(1)} %get-tuple-element.48.grads_ref) | copy-start | bytes 1376260
  47.1 16.3 %collective-permute-start.1 = (bf16[16,128,128]{2,1,0:T(8,128)(2,1)S(1)}, bf16[16,128,128]{2,1,0:T(8,128)(2,1)S(1)}, u32[]{:S(2)}, u32[]{:S(2)}) collective-permute-start(bf16[16,128,128]{2,1,0:T(8,128)(2,1)S(1)} %get-tuple-element.37), channel_id=1, source_target_pairs={{0,384},{128,256},{256,128},{384,0},{1,385},{129,257},{257,129},{3... | collective-permute-start | bytes 1572872 | tf_op jit(solution)/shard_map/ppermute | solution.py:39
  49.9 14.7 %collective-permute-start.2 = (bf16[16,128,128]{2,1,0:T(8,128)(2,1)S(1)}, bf16[16,128,128]{2,1,0:T(8,128)(2,1)S(1)}, u32[]{:S(2)}, u32[]{:S(2)}) collective-permute-start(bf16[16,128,128]{2,1,0:T(8,128)(2,1)S(1)} %get-tuple-element.38), channel_id=1, source_target_pairs={{0,128},{128,0},{256,384},{384,256},{1,129},{129,1},{257,385},{385... | collective-permute-start | bytes 1572872 | tf_op jit(solution)/shard_map/ppermute | solution.py:39
  51.8 24.1 %collective-permute-start.3 = (bf16[16,128,128]{2,1,0:T(8,128)(2,1)S(1)}, bf16[16,128,128]{2,1,0:T(8,128)(2,1)S(1)}, u32[]{:S(2)}, u32[]{:S(2)}) collective-permute-start(bf16[16,128,128]{2,1,0:T(8,128)(2,1)S(1)} %get-tuple-element.40), channel_id=1, source_target_pairs={{0,128},{128,0},{256,384},{384,256},{1,129},{129,1},{257,385},{385... | collective-permute-start | bytes 1572872 | tf_op jit(solution)/shard_map/ppermute | solution.py:39
  55.2 20.8 %collective-permute-start.6 = (bf16[16,128,128]{2,1,0:T(8,128)(2,1)S(1)}, bf16[16,128,128]{2,1,0:T(8,128)(2,1)S(1)}, u32[]{:S(2)}, u32[]{:S(2)}) collective-permute-start(bf16[16,128,128]{2,1,0:T(8,128)(2,1)S(1)} %get-tuple-element.43), channel_id=1, source_target_pairs={{0,384},{128,256},{256,128},{384,0},{1,385},{129,257},{257,129},{3... | collective-permute-start | bytes 1572872 | tf_op jit(solution)/shard_map/ppermute | solution.py:39
  67.7 26.1 %copy-start.6 = (bf16[14,128,128]{2,1,0:T(8,128)(2,1)S(1)}, bf16[14,128,128]{2,1,0:T(8,128)(2,1)}, u32[]{:S(2)}) copy-start(bf16[14,128,128]{2,1,0:T(8,128)(2,1)} %copy-done.5) | copy-start | bytes 1376260
  67.7 17.5 %collective-permute-start.4 = (bf16[16,128,128]{2,1,0:T(8,128)(2,1)S(1)}, bf16[16,128,128]{2,1,0:T(8,128)(2,1)S(1)}, u32[]{:S(2)}, u32[]{:S(2)}) collective-permute-start(bf16[16,128,128]{2,1,0:T(8,128)(2,1)S(1)} %get-tuple-element.41), channel_id=1, source_target_pairs={{0,384},{128,256},{256,128},{384,0},{1,385},{129,257},{257,129},{3... | collective-permute-start | bytes 1572872 | tf_op jit(solution)/shard_map/ppermute | solution.py:39
  71.7 14.0 %collective-permute-start.5 = (bf16[16,128,128]{2,1,0:T(8,128)(2,1)S(1)}, bf16[16,128,128]{2,1,0:T(8,128)(2,1)S(1)}, u32[]{:S(2)}, u32[]{:S(2)}) collective-permute-start(bf16[16,128,128]{2,1,0:T(8,128)(2,1)S(1)} %get-tuple-element.42), channel_id=1, source_target_pairs={{0,128},{128,0},{256,384},{384,256},{1,129},{129,1},{257,385},{385... | collective-permute-start | bytes 1572872 | tf_op jit(solution)/shard_map/ppermute | solution.py:39
  86.6 18.7 %collective-permute-start.7 = (bf16[8,2,128,128]{3,2,1,0:T(8,128)(2,1)S(1)}, bf16[8,2,128,128]{3,2,1,0:T(8,128)(2,1)S(1)}, u32[]{:S(2)}, u32[]{:S(2)}) collective-permute-start(bf16[8,2,128,128]{3,2,1,0:T(8,128)(2,1)S(1)} %get-tuple-element.47), channel_id=1, source_target_pairs={{0,8},{8,0},{1,9},{9,1},{2,10},{10,2},{3,11},{11,3},{4,12},{12,4},... | collective-permute-start | bytes 1572872 | tf_op jit(solution)/shard_map/ppermute | solution.py:39
  98.3 1.0 copy-start.12
  105.3 10.8 %copy-start.13 = (bf16[64,8192]{1,0:T(8,128)(2,1)S(1)}, bf16[64,8192]{1,0:T(8,128)(2,1)}, u32[]{:S(2)}) copy-start(bf16[64,8192]{1,0:T(8,128)(2,1)} %copy-done.12) | copy-start | bytes 3145732
  106.2 32.1 %all-to-all-start.2 = ((bf16[8,2,128,128]{3,2,1,0:T(8,128)(2,1)}), bf16[8,2,128,128]{3,2,1,0:T(8,128)(2,1)S(1)}, u32[]{:S(2)}, u32[]{:S(2)}) async-start(bf16[8,2,128,128]{3,2,1,0:T(8,128)(2,1)} %pair_sum.1), calls=%async_computation.2 | async-start | bytes 1048576 | tf_op jit(solution)/shard_map/all_to_all | solution.py:43
  116.1 60.4 %all-gather.5.cloned.1.call-start = ((), (), s32[]{:S(2)}) async-start(), calls=%async_computation.6 | async-start | bytes 2359296 | tf_op jit(solution)/shard_map/all_gather | solution.py:361
  116.1 7.6 %collective-permute-start.8 = (bf16[64,8192]{1,0:T(8,128)(2,1)S(1)}, bf16[64,8192]{1,0:T(8,128)(2,1)S(1)}, u32[]{:S(2)}, u32[]{:S(2)}) collective-permute-start(bf16[64,8192]{1,0:T(8,128)(2,1)S(1)} %copy-done.13), channel_id=1, source_target_pairs={{0,1},{1,0},{2,3},{3,2},{4,5},{5,4},{6,7},{7,6},{8,9},{9,8},{10,11... | collective-permute-start | bytes 3145736 | tf_op jit(solution)/shard_map/ppermute | solution.py:39
  124.6 14.5 %collective-permute-start.9 = (bf16[16,8192]{1,0:T(8,128)(2,1)S(1)}, bf16[16,8192]{1,0:T(8,128)(2,1)S(1)}, u32[]{:S(2)}, u32[]{:S(2)}) collective-permute-start(bf16[16,8192]{1,0:T(8,128)(2,1)S(1)} %get-tuple-element.54), channel_id=1, source_target_pairs={{0,4},{2,6},{4,0},{6,2},{1,5},{3,7},{5,1},{7,3},{8,12},{10,14},{12... | collective-permute-start | bytes 786440 | tf_op jit(solution)/shard_map/ppermute | solution.py:39
  128.0 12.4 %collective-permute-start.10 = (bf16[16,8192]{1,0:T(8,128)(2,1)S(1)}, bf16[16,8192]{1,0:T(8,128)(2,1)S(1)}, u32[]{:S(2)}, u32[]{:S(2)}) collective-permute-start(bf16[16,8192]{1,0:T(8,128)(2,1)S(1)} %get-tuple-element.55), channel_id=1, source_target_pairs={{0,2},{2,0},{4,6},{6,4},{1,3},{3,1},{5,7},{7,5},{8,10},{10,8},{12,... | collective-permute-start | bytes 786440 | tf_op jit(solution)/shard_map/ppermute | solution.py:39
  130.7 10.6 %collective-permute-start.11 = (bf16[16,8192]{1,0:T(8,128)(2,1)S(1)}, bf16[16,8192]{1,0:T(8,128)(2,1)S(1)}, u32[]{:S(2)}, u32[]{:S(2)}) collective-permute-start(bf16[16,8192]{1,0:T(8,128)(2,1)S(1)} %get-tuple-element.56), channel_id=1, source_target_pairs={{0,6},{2,4},{4,2},{6,0},{1,7},{3,5},{5,3},{7,1},{8,14},{10,12},{12... | collective-permute-start | bytes 786440 | tf_op jit(solution)/shard_map/ppermute | solution.py:39
  163.8 17.2 %all-to-all-start.4 = ((f32[16,8,128]{2,1,0:T(8,128)}), f32[16,8,128]{2,1,0:T(8,128)S(1)}, u32[]{:S(2)}, u32[]{:S(2)}) async-start(f32[16,8,128]{2,1,0:T(8,128)} %relay.1), calls=%async_computation.4 | async-start | bytes 131072 | tf_op jit(solution)/shard_map/all_to_all | solution.py:43
  169.4 11.6 %copy-start.1 = (f32[1,2,128,128]{3,2,1,0:T(8,128)S(1)}, f32[1,2,128,128]{3,2,1,0:T(8,128)}, u32[]{:S(2)}) copy-start(f32[1,2,128,128]{3,2,1,0:T(8,128)} %refs_4_.1) | copy-start | bytes 393220
  169.4 11.6 %copy-start.7 = (f32[1,2,128,128]{3,2,1,0:T(8,128)S(1)}, f32[1,2,128,128]{3,2,1,0:T(8,128)}, u32[]{:S(2)}) copy-start(f32[1,2,128,128]{3,2,1,0:T(8,128)} %refs_5_.1) | copy-start | bytes 393220
  169.4 11.6 %copy-start.8 = (f32[1,2,128,128]{3,2,1,0:T(8,128)S(1)}, f32[1,2,128,128]{3,2,1,0:T(8,128)}, u32[]{:S(2)}) copy-start(f32[1,2,128,128]{3,2,1,0:T(8,128)} %refs_6_.1) | copy-start | bytes 393220
Sparse Core Ops, SparseCore 0:
  19.0 74.7 all-gather.2
  142.3 34.1 all-gather.4

commit v13 on v12

--- a/solution.py
+++ b/solution.py
@@ -21,7 +21,7 @@
 
 
 def kernel_call(
-    kernel, name, outs, ins, out_specs, scratch=(), flops=0, moved=1 << 20, vmem=48
+    kernel, name, outs, ins, out_specs, scratch=(), flops=0, moved=1 << 20, vmem=16
 ):
     return pl.pallas_call(
         kernel,
@@ -185,13 +185,18 @@
         new_two_ref[0, rank] = jnp.where(live, second, two)
 
 
-def turn_kernel(delta_ref, out_ref):
+def turn_kernel(delta_ref, out_ref, held, sem):
+    load = pltpu.make_async_copy(delta_ref, held, sem)
+    load.start()
+    load.wait()
     for rank in range(SLOT_CAP):
-        out_ref[rank] = delta_ref[0, rank].T.astype(BF16)
+        turned = held[0, rank].T.astype(BF16)
+        for y in range(NY):
+            out_ref[y, rank] = turned
 
 
 def contrib_kernel(
-    rows_ref, cols_ref, counts_ref, grads_ref, deltas_ref, stay_ref, give_ref,
+    rows_ref, cols_ref, counts_ref, grads_ref, deltas_ref, _, stay_ref, give_ref, token_ref,
     places_ref, grad_ref, delta_ref, sems,
 ):
     loads = [
@@ -202,6 +207,7 @@
         load.start()
     stay_ref[...] = jnp.zeros_like(stay_ref)
     give_ref[...] = jnp.zeros_like(give_ref)
+    token_ref[...] = jnp.zeros_like(token_ref)
     half = stay_ref.shape[0]
 
     def owner_step(owner, start):
@@ -278,10 +284,11 @@
     own = spread(features, "x")
     other = swap(own, "core", 1)
 
-    delta_half = kernel_call(
-        turn_kernel, "turn", SHAPE(delta_value.shape[1:], BF16), [VMEM], VMEM
+    copies = kernel_call(
+        turn_kernel, "turn", SHAPE((NY,) + delta_value.shape[1:], BF16), [ANY], VMEM,
+        [pltpu.VMEM(delta_value.shape, F32), pltpu.SemaphoreType.DMA], vmem=63,
     )(delta_value)
-    delta_y = spread(delta_half, "y").reshape(NY * SLOT_CAP, TILE, TILE)
+    delta_y = exchange(copies, "y").reshape(NY * SLOT_CAP, TILE, TILE)
     delta_all = lax.all_gather(delta_y, Z, axis=0, tiled=True)
 
     grads, turned = kernel_call(
@@ -322,21 +329,21 @@
         y_sum_kernel, "y_sum", [eight] * 2, [SMEM] + [VMEM] * 5, [VMEM] * 2
     )(ids, *map(parted, (mine, one_low, other_low, one_high, other_high)))
 
-    keep, grads = lax.optimization_barrier((keep, grads))
     partner = swap(give, "p", 1)
-    stay, give = kernel_call(
-        contrib_kernel, "contribs", [SHAPE((tokens // 2, width), BF16)] * 2,
-        [SMEM] * 3 + [ANY] * 2, [VMEM] * 2,
+    stay, give, token = kernel_call(
+        contrib_kernel, "contribs",
+        [SHAPE((tokens // 2, width), BF16)] * 2 + [SHAPE((8, TILE), F32)],
+        [SMEM] * 3 + [ANY] * 3, [VMEM] * 3,
         [
             pltpu.SMEM((tile_total + 8,), jnp.int32),
             pltpu.VMEM(grads.shape, BF16),
             pltpu.VMEM(delta_all.shape, BF16),
             pltpu.SemaphoreType.DMA((2,)),
         ],
-        moved=1 << 12,
-    )(*lists, grads, delta_all)
-    pairs = kernel_call(pair_sum_kernel, "pair_sum", eight, [VMEM] * 2 + [ANY], VMEM)(
-        keep, partner, stay
+        moved=1 << 12, vmem=48,
+    )(*lists, grads, delta_all, keep)
+    pairs = kernel_call(pair_sum_kernel, "pair_sum", eight, [VMEM] * 3, VMEM)(
+        keep, partner, token
     )
     arrived = exchange(pairs, "m")
     own_grad, squares = kernel_call(

time: 190 us -> 191 us (level)
    all_to_all x2, waiting for transfers between devices: 6.82 us -> 9.57 us  [exchange(): return lax.all_to_all(value, axis, split_axis=0, concat_axis=0, tiled=True)]
  transfers between devices with their start and end apart: 16 -> 16, of which waited for: 14 -> 11; matrix products, arithmetic and copies ran while one was open for 1% -> 1% of each run, Pallas kernels for 9% -> 9%
where the time goes in v13:
time: 191 us
  starting transfers between devices  57.9 us (30%)
  waiting for transfers between devices  47.8 us (25%)
  blocking collectives  46.2 us (24%)
  Pallas kernels  21.4 us (11%)
  between operations  14.3 us (7%)
  local copies, waits for them, and re-layouts  2.16 us (1%)
    all_to_all x3, blocking collectives, exchange(): return lax.all_to_all(value, axis, split_axis=0, concat_axis=0, tiled=True)  46.2 us
    ppermute x12, starting transfers between devices, swap(): lax.ppermute(value, axis, [(i, i ^ bits) for i in range(lax.axis_size(axi...  43.2 us
    ppermute x12, waiting for transfers between devices, swap(): lax.ppermute(value, axis, [(i, i ^ bits) for i in range(lax.axis_size(axi...  27.9 us
    all_to_all x2, starting transfers between devices, exchange(): return lax.all_to_all(value, axis, split_axis=0, concat_axis=0, tiled=True)  14.6 us
    all_to_all x2, waiting for transfers between devices, exchange(): return lax.all_to_all(value, axis, split_axis=0, concat_axis=0, tiled=True)  9.57 us
    all_gather x1, waiting for transfers between devices, body(): lax.all_gather(share.astype(BF16), ('x', 'core'), axis=0, tiled=True)  7.04 us
    pallas_call x2, Pallas kernels, terms(): kernel_call(functools.partial(tile_kernel, parts), 'tiles', [SHAPE(((last...  6.1 us
    pallas_call x1, Pallas kernels, body(): kernel_call(contrib_kernel, 'contribs', [SHAPE((tokens // 2, width), BF16...  4.48 us
  transfers between devices with their start and end apart: 16, of which 11 were waited for; matrix products, arithmetic and copies ran while one was open for 1% of the time, Pallas kernels for 9%

profile of v13, /device:TPU:1, one launch (start us, length us, event | category | flops | bytes accessed | tf_op | source)
XLA Modules:
  0.0 190.6 jit_solution(11186495159776856113)
XLA Ops:
  7.2 0.0 all-gather.3.cloned.1.call-start
  7.2 1.7 turn.1
  8.9 0.0 copy-start.1
  9.0 0.0 copy-start.2
  9.0 10.8 %all_to_all.25 = bf16[4,2,128,128]{3,2,1,0:T(8,128)(2,1)} all-to-all(bf16[4,2,128,128]{3,2,1,0:T(8,128)(2,1)} %turn.1), channel_id=1, replica_groups=mesh['y'=4,'m'=8,'p'=2,'x'=4,'core'=2] {'y'}, dimensions={0} | all-to-all | bytes 524288 | tf_op jit(solution)/shard_map/all_to_all | solution.py:43
  19.8 0.0 all-gather.3.cloned.1.call-update
  19.8 0.0 copy-start.6
  19.8 0.0 copy-start.7
  19.8 0.0 copy-start.8
  19.8 1.1 broadcast_in_dim.2
  20.9 13.6 %all_to_all.26.own_ref = bf16[4,128,1024]{2,1,0:T(8,128)(2,1)S(1)} all-to-all(bf16[4,128,1024]{2,1,0:T(8,128)(2,1)S(1)} %broadcast_in_dim.2), channel_id=1, replica_groups=mesh['y'=4,'m'=8,'p'=2,'x'=4,'core'=2] {'x'}, dimensions={0} | all-to-all | bytes 2097152 | tf_op jit(solution)/shard_map/all_to_all | solution.py:43
  34.5 8.6 %collective-permute-start = (bf16[4,128,1024]{2,1,0:T(8,128)(2,1)S(1)}, bf16[4,128,1024]{2,1,0:T(8,128)(2,1)S(1)}, u32[]{:S(2)}, u32[]{:S(2)}) collective-permute-start(bf16[4,128,1024]{2,1,0:T(8,128)(2,1)S(1)} %all_to_all.26.own_ref), channel_id=1, source_target_pairs={{0,1},{1,0},{2,3},{3,2},{4,5},{5,4},{6,7},{7,6},{8,9},{9,8},{10,11... | collective-permute-start | bytes 3145736 | tf_op jit(solution)/shard_map/ppermute | solution.py:39
  43.1 0.1 pad_add_fusion.ids_ref.refs_0_
  43.2 0.0 copy-done.2
  43.2 1.0 copy-done.3
  44.2 1.1 gate.1
  45.4 0.0 collective-permute-done.other_ref
  45.4 3.0 %tiles.2 = (bf16[16,128,128]{2,1,0:T(8,128)(2,1)S(1)}, bf16[16,128,128]{2,1,0:T(8,128)(2,1)S(1)}, bf16[16,128,128]{2,1,0:T(8,128)(2,1)S(1)}, bf16[16,128,128]{2,1,0:T(8,128)(2,1)S(1)}) custom-call(s32[4]{0:T(128)S(1)} %pad_add_fusion.ids_ref.refs_0_, s32[1,112]{1,0:T(1,128)S(1)} %copy-done.7, s32[1,112]{1,0:T(1,128)S(1)} %copy-done.8, ...), custom_call_target="tpu_custom_call" | custom-call | flops 117440512 | bytes 2097152 | tf_op jit(solution)/shard_map/tiles/pallas_call | solution.py:307
  48.4 2.8 %collective-permute-start.1 = (bf16[16,128,128]{2,1,0:T(8,128)(2,1)S(1)}, bf16[16,128,128]{2,1,0:T(8,128)(2,1)S(1)}, u32[]{:S(2)}, u32[]{:S(2)}) collective-permute-start(bf16[16,128,128]{2,1,0:T(8,128)(2,1)S(1)} %get-tuple-element.36), channel_id=1, source_target_pairs={{0,384},{128,256},{256,128},{384,0},{1,385},{129,257},{257,129},{3... | collective-permute-start | bytes 1572872 | tf_op jit(solution)/shard_map/ppermute | solution.py:39
  51.2 1.9 %collective-permute-start.2 = (bf16[16,128,128]{2,1,0:T(8,128)(2,1)S(1)}, bf16[16,128,128]{2,1,0:T(8,128)(2,1)S(1)}, u32[]{:S(2)}, u32[]{:S(2)}) collective-permute-start(bf16[16,128,128]{2,1,0:T(8,128)(2,1)S(1)} %get-tuple-element.37), channel_id=1, source_target_pairs={{0,128},{128,0},{256,384},{384,256},{1,129},{129,1},{257,385},{385... | collective-permute-start | bytes 1572872 | tf_op jit(solution)/shard_map/ppermute | solution.py:39
  53.2 3.4 %collective-permute-start.3 = (bf16[16,128,128]{2,1,0:T(8,128)(2,1)S(1)}, bf16[16,128,128]{2,1,0:T(8,128)(2,1)S(1)}, u32[]{:S(2)}, u32[]{:S(2)}) collective-permute-start(bf16[16,128,128]{2,1,0:T(8,128)(2,1)S(1)} %get-tuple-element.39), channel_id=1, source_target_pairs={{0,128},{128,0},{256,384},{384,256},{1,129},{129,1},{257,385},{385... | collective-permute-start | bytes 1572872 | tf_op jit(solution)/shard_map/ppermute | solution.py:39
  56.5 3.7 %collective-permute-start.6 = (bf16[16,128,128]{2,1,0:T(8,128)(2,1)S(1)}, bf16[16,128,128]{2,1,0:T(8,128)(2,1)S(1)}, u32[]{:S(2)}, u32[]{:S(2)}) collective-permute-start(bf16[16,128,128]{2,1,0:T(8,128)(2,1)S(1)} %get-tuple-element.42), channel_id=1, source_target_pairs={{0,384},{128,256},{256,128},{384,0},{1,385},{129,257},{257,129},{3... | collective-permute-start | bytes 1572872 | tf_op jit(solution)/shard_map/ppermute | solution.py:39
  60.3 4.4 %collective-permute-done.1.refs_0_ = bf16[16,128,128]{2,1,0:T(8,128)(2,1)S(1)} collective-permute-done((bf16[16,128,128]{2,1,0:T(8,128)(2,1)S(1)}, bf16[16,128,128]{2,1,0:T(8,128)(2,1)S(1)}, u32[]{:S(2)}, u32[]{:S(2)}) %collective-permute-start.1) | collective-permute-done | bytes 524320 | tf_op jit(solution)/shard_map/ppermute | solution.py:39
  64.7 1.4 collective-permute-done.2.refs_1_
  66.0 3.1 %tiles.3 = (bf16[16,128,128]{2,1,0:T(8,128)(2,1)S(1)}, bf16[16,128,128]{2,1,0:T(8,128)(2,1)S(1)}, bf16[32,128,128]{2,1,0:T(8,128)(2,1)S(1)}) custom-call(s32[4]{0:T(128)S(1)} %pad_add_fusion.ids_ref.refs_0_, s32[1,112]{1,0:T(1,128)S(1)} %copy-done.7, s32[1,112]{1,0:T(1,128)S(1)} %copy-done.8, s32[1,64]{1,0:T(1,128)S(1)} %copy-done.6, ...), custom_call_target="tpu_custom_call" | custom-call | flops 117440512 | bytes 2097152 | tf_op jit(solution)/shard_map/tiles/pallas_call | solution.py:307
  69.1 3.6 %collective-permute-start.4 = (bf16[16,128,128]{2,1,0:T(8,128)(2,1)S(1)}, bf16[16,128,128]{2,1,0:T(8,128)(2,1)S(1)}, u32[]{:S(2)}, u32[]{:S(2)}) collective-permute-start(bf16[16,128,128]{2,1,0:T(8,128)(2,1)S(1)} %get-tuple-element.40), channel_id=1, source_target_pairs={{0,384},{128,256},{256,128},{384,0},{1,385},{129,257},{257,129},{3... | collective-permute-start | bytes 1572872 | tf_op jit(solution)/shard_map/ppermute | solution.py:39
  72.8 1.9 %collective-permute-start.5 = (bf16[16,128,128]{2,1,0:T(8,128)(2,1)S(1)}, bf16[16,128,128]{2,1,0:T(8,128)(2,1)S(1)}, u32[]{:S(2)}, u32[]{:S(2)}) collective-permute-start(bf16[16,128,128]{2,1,0:T(8,128)(2,1)S(1)} %get-tuple-element.41), channel_id=1, source_target_pairs={{0,128},{128,0},{256,384},{384,256},{1,129},{129,1},{257,385},{385... | collective-permute-start | bytes 1572872 | tf_op jit(solution)/shard_map/ppermute | solution.py:39
  74.7 2.6 %collective-permute-done.3 = bf16[16,128,128]{2,1,0:T(8,128)(2,1)S(1)} collective-permute-done((bf16[16,128,128]{2,1,0:T(8,128)(2,1)S(1)}, bf16[16,128,128]{2,1,0:T(8,128)(2,1)S(1)}, u32[]{:S(2)}, u32[]{:S(2)}) %collective-permute-start.3) | collective-permute-done | bytes 524320 | tf_op jit(solution)/shard_map/ppermute | solution.py:39
  77.3 0.0 collective-permute-done.6
  77.3 9.5 %collective-permute-done.4 = bf16[16,128,128]{2,1,0:T(8,128)(2,1)S(1)} collective-permute-done((bf16[16,128,128]{2,1,0:T(8,128)(2,1)S(1)}, bf16[16,128,128]{2,1,0:T(8,128)(2,1)S(1)}, u32[]{:S(2)}, u32[]{:S(2)}) %collective-permute-start.4) | collective-permute-done | bytes 524320 | tf_op jit(solution)/shard_map/ppermute | solution.py:39
  86.8 0.4 collective-permute-done.5
  87.2 0.9 y_sum.1
  88.1 3.1 %collective-permute-start.7 = (bf16[8,2,128,128]{3,2,1,0:T(8,128)(2,1)S(1)}, bf16[8,2,128,128]{3,2,1,0:T(8,128)(2,1)S(1)}, u32[]{:S(2)}, u32[]{:S(2)}) collective-permute-start(bf16[8,2,128,128]{3,2,1,0:T(8,128)(2,1)S(1)} %get-tuple-element.44), channel_id=1, source_target_pairs={{0,8},{8,0},{1,9},{9,1},{2,10},{10,2},{3,11},{11,3},{4,12},{12,4},... | collective-permute-start | bytes 1572872 | tf_op jit(solution)/shard_map/ppermute | solution.py:39
  91.2 3.2 %all-gather.3.cloned.1.call-done.deltas_ref = bf16[128,128,128]{2,1,0:T(8,128)(2,1)} async-done(((bf16[8,128,128]{2,1,0:T(8,128)(2,1)}), bf16[128,128,128]{2,1,0:T(8,128)(2,1)}) %all-gather.3.cloned.1.call-update) | async-done | bytes 4194320 | tf_op jit(solution)/shard_map/all_gather | solution.py:292
  94.4 4.5 %contribs.1 = (bf16[64,8192]{1,0:T(8,128)(2,1)S(1)}, bf16[64,8192]{1,0:T(8,128)(2,1)S(1)}, f32[8,128]{1,0:T(8,128)S(1)}) custom-call(s32[1,112]{1,0:T(1,128)S(1)} %copy-done.7, s32[1,112]{1,0:T(1,128)S(1)} %copy-done.8, s32[1,64]{1,0:T(1,128)S(1)} %copy-done.6, bf16[14,128,128]{2,1,0:T(8,128)(2,1)S(1)} %get-tuple-element.45.grads_ref, ...), custom_call_target="tpu_custom_call" | custom-call | bytes 4096 | tf_op jit(solution)/shard_map/contribs/pallas_call | solution.py:333
  98.9 0.0 copy-start.9
  98.9 7.1 %collective-permute-done.7.taken_ref = bf16[8,2,128,128]{3,2,1,0:T(8,128)(2,1)S(1)} collective-permute-done((bf16[8,2,128,128]{3,2,1,0:T(8,128)(2,1)S(1)}, bf16[8,2,128,128]{3,2,1,0:T(8,128)(2,1)S(1)}, u32[]{:S(2)}, u32[]{:S(2)}) %collective-permute-start.7) | collective-permute-done | bytes 524320 | tf_op jit(solution)/shard_map/ppermute | solution.py:39
  106.1 0.9 pair_sum.1
  107.0 10.3 %all-to-all-start.2 = ((bf16[8,2,128,128]{3,2,1,0:T(8,128)(2,1)}), bf16[8,2,128,128]{3,2,1,0:T(8,128)(2,1)S(1)}, u32[]{:S(2)}, u32[]{:S(2)}) async-start(bf16[8,2,128,128]{3,2,1,0:T(8,128)(2,1)} %pair_sum.1), calls=%async_computation.2 | async-start | bytes 1048576 | tf_op jit(solution)/shard_map/all_to_all | solution.py:43
  117.3 0.0 all-gather.5.cloned.1.call-start
  117.3 5.2 %collective-permute-start.8 = (bf16[64,8192]{1,0:T(8,128)(2,1)}, bf16[64,8192]{1,0:T(8,128)(2,1)S(1)}, u32[]{:S(2)}, u32[]{:S(2)}) collective-permute-start(bf16[64,8192]{1,0:T(8,128)(2,1)} %copy-done.9), channel_id=1, source_target_pairs={{0,1},{1,0},{2,3},{3,2},{4,5},{5,4},{6,7},{7,6},{8,9},{9,8},{10,11... | collective-permute-start | bytes 3145736 | tf_op jit(solution)/shard_map/ppermute | solution.py:39
  122.5 2.5 %collective-permute-done.8 = bf16[64,8192]{1,0:T(8,128)(2,1)S(1)} collective-permute-done((bf16[64,8192]{1,0:T(8,128)(2,1)}, bf16[64,8192]{1,0:T(8,128)(2,1)S(1)}, u32[]{:S(2)}, u32[]{:S(2)}) %collective-permute-start.8) | collective-permute-done | bytes 1048608 | tf_op jit(solution)/shard_map/ppermute | solution.py:39
  125.0 0.8 core_sum.1
  125.8 3.4 %collective-permute-start.9 = (bf16[16,8192]{1,0:T(8,128)(2,1)S(1)}, bf16[16,8192]{1,0:T(8,128)(2,1)S(1)}, u32[]{:S(2)}, u32[]{:S(2)}) collective-permute-start(bf16[16,8192]{1,0:T(8,128)(2,1)S(1)} %get-tuple-element.52), channel_id=1, source_target_pairs={{0,4},{2,6},{4,0},{6,2},{1,5},{3,7},{5,1},{7,3},{8,12},{10,14},{12... | collective-permute-start | bytes 786440 | tf_op jit(solution)/shard_map/ppermute | solution.py:39
  129.3 2.6 %collective-permute-start.10 = (bf16[16,8192]{1,0:T(8,128)(2,1)S(1)}, bf16[16,8192]{1,0:T(8,128)(2,1)S(1)}, u32[]{:S(2)}, u32[]{:S(2)}) collective-permute-start(bf16[16,8192]{1,0:T(8,128)(2,1)S(1)} %get-tuple-element.53), channel_id=1, source_target_pairs={{0,2},{2,0},{4,6},{6,4},{1,3},{3,1},{5,7},{7,5},{8,10},{10,8},{12,... | collective-permute-start | bytes 786440 | tf_op jit(solution)/shard_map/ppermute | solution.py:39
  131.9 3.0 %collective-permute-start.11 = (bf16[16,8192]{1,0:T(8,128)(2,1)S(1)}, bf16[16,8192]{1,0:T(8,128)(2,1)S(1)}, u32[]{:S(2)}, u32[]{:S(2)}) collective-permute-start(bf16[16,8192]{1,0:T(8,128)(2,1)S(1)} %get-tuple-element.54), channel_id=1, source_target_pairs={{0,6},{2,4},{4,2},{6,0},{1,7},{3,5},{5,3},{7,1},{8,14},{10,12},{12... | collective-permute-start | bytes 786440 | tf_op jit(solution)/shard_map/ppermute | solution.py:39
  134.8 7.5 %all-to-all-done.2.arrived_ref = bf16[8,2,128,128]{3,2,1,0:T(8,128)(2,1)S(1)} async-done(((bf16[8,2,128,128]{3,2,1,0:T(8,128)(2,1)}), bf16[8,2,128,128]{3,2,1,0:T(8,128)(2,1)S(1)}, u32[]{:S(2)}, u32[]{:S(2)}) %all-to-all-start.2) | async-done | bytes 524320 | tf_op jit(solution)/shard_map/all_to_all | solution.py:43
  142.3 0.8 own_grad.1
  143.1 0.0 collective-permute-done.9
  143.1 0.0 collective-permute-done.10
  143.1 0.0 collective-permute-done.11
  143.1 0.8 add_convert_fusion
  144.0 0.0 all-gather.5.cloned.1.call-update
  144.0 21.8 %all_to_all.27.arrived_ref = f32[32,8,128]{2,1,0:T(8,128)S(1)} all-to-all(f32[32,8,128]{2,1,0:T(8,128)S(1)} %get-tuple-element.55), channel_id=1, replica_groups=mesh['y'=4,'m'=8,'p'=2,'x'=4,'core'=2] {'y','x','core'}, dimensions={0} | all-to-all | bytes 262144 | tf_op jit(solution)/shard_map/all_to_all | solution.py:43
  165.8 0.7 relay.1
  166.4 4.2 %all-to-all-start.4 = ((f32[16,8,128]{2,1,0:T(8,128)}), f32[16,8,128]{2,1,0:T(8,128)S(1)}, u32[]{:S(2)}, u32[]{:S(2)}) async-start(f32[16,8,128]{2,1,0:T(8,128)} %relay.1), calls=%async_computation.4 | async-start | bytes 131072 | tf_op jit(solution)/shard_map/all_to_all | solution.py:43
  170.7 0.0 copy-start
  170.7 0.0 copy-start.4
  170.7 0.0 copy-start.5
  170.7 7.0 %all-gather.5.cloned.1.call-done.in_ref = bf16[128,8192]{1,0:T(8,128)(2,1)} async-done(((bf16[16,8192]{1,0:T(8,128)(2,1)}), bf16[128,8192]{1,0:T(8,128)(2,1)}) %all-gather.5.cloned.1.call-update) | async-done | bytes 2097168 | tf_op jit(solution)/shard_map/all_gather | solution.py:368
  177.8 2.4 %result.1 = bf16[128,8192]{1,0:T(8,128)(2,1)} custom-call(bf16[128,8192]{1,0:T(8,128)(2,1)} %all-gather.5.cloned.1.call-done.in_ref), custom_call_target="tpu_custom_call" | custom-call | bytes 4194304 | tf_op jit(solution)/shard_map/result/pallas_call | solution.py:369
  180.2 2.1 %all-to-all-done.4.refs_2_ = f32[16,8,128]{2,1,0:T(8,128)S(1)} async-done(((f32[16,8,128]{2,1,0:T(8,128)}), f32[16,8,128]{2,1,0:T(8,128)S(1)}, u32[]{:S(2)}, u32[]{:S(2)}) %all-to-all-start.4) | async-done | bytes 65568 | tf_op jit(solution)/shard_map/all_to_all | solution.py:43
  182.3 0.0 copy-done
  182.3 1.5 adam.1
  (8 shorter events, 0.0 us)
Async XLA Ops:
  7.2 87.3 %all-gather.3.cloned.1.call-start = ((), (), s32[]{:S(2)}) async-start(), calls=%async_computation.5 | async-start | bytes 4456448 | tf_op jit(solution)/shard_map/all_gather | solution.py:292
  8.9 34.3 %copy-start.1 = (bf16[128,1792]{1,0:T(8,128)(2,1)S(1)}, bf16[128,1792]{1,0:T(8,128)(2,1)}, u32[]{:S(2)}) copy-start(bf16[128,1792]{1,0:T(8,128)(2,1)} %gate_ref.1) | copy-start | bytes 1376260
  9.0 34.3 %copy-start.2 = (bf16[128,1792]{1,0:T(8,128)(2,1)S(1)}, bf16[128,1792]{1,0:T(8,128)(2,1)}, u32[]{:S(2)}) copy-start(bf16[128,1792]{1,0:T(8,128)(2,1)} %up_ref.1) | copy-start | bytes 1376260
  19.8 25.6 %copy-start.6 = (s32[1,64]{1,0:T(1,128)S(1)}, s32[1,64]{1,0:T(1,128)}, u32[]{:S(2)}) copy-start(s32[1,64]{1,0:T(1,128)} %refs_1_.1) | copy-start | bytes 772
  19.8 25.6 %copy-start.7 = (s32[1,112]{1,0:T(1,128)S(1)}, s32[1,112]{1,0:T(1,128)}, u32[]{:S(2)}) copy-start(s32[1,112]{1,0:T(1,128)} %rows_ref.5) | copy-start | bytes 1348
  19.8 25.6 %copy-start.8 = (s32[1,112]{1,0:T(1,128)S(1)}, s32[1,112]{1,0:T(1,128)}, u32[]{:S(2)}) copy-start(s32[1,112]{1,0:T(1,128)} %cols_ref.5) | copy-start | bytes 1348
  34.5 10.9 %collective-permute-start = (bf16[4,128,1024]{2,1,0:T(8,128)(2,1)S(1)}, bf16[4,128,1024]{2,1,0:T(8,128)(2,1)S(1)}, u32[]{:S(2)}, u32[]{:S(2)}) collective-permute-start(bf16[4,128,1024]{2,1,0:T(8,128)(2,1)S(1)} %all_to_all.26.own_ref), channel_id=1, source_target_pairs={{0,1},{1,0},{2,3},{3,2},{4,5},{5,4},{6,7},{7,6},{8,9},{9,8},{10,11... | collective-permute-start | bytes 3145736 | tf_op jit(solution)/shard_map/ppermute | solution.py:39
  43.2 1.0 copy-start.3
  48.4 16.2 %collective-permute-start.1 = (bf16[16,128,128]{2,1,0:T(8,128)(2,1)S(1)}, bf16[16,128,128]{2,1,0:T(8,128)(2,1)S(1)}, u32[]{:S(2)}, u32[]{:S(2)}) collective-permute-start(bf16[16,128,128]{2,1,0:T(8,128)(2,1)S(1)} %get-tuple-element.36), channel_id=1, source_target_pairs={{0,384},{128,256},{256,128},{384,0},{1,385},{129,257},{257,129},{3... | collective-permute-start | bytes 1572872 | tf_op jit(solution)/shard_map/ppermute | solution.py:39
  51.2 14.8 %collective-permute-start.2 = (bf16[16,128,128]{2,1,0:T(8,128)(2,1)S(1)}, bf16[16,128,128]{2,1,0:T(8,128)(2,1)S(1)}, u32[]{:S(2)}, u32[]{:S(2)}) collective-permute-start(bf16[16,128,128]{2,1,0:T(8,128)(2,1)S(1)} %get-tuple-element.37), channel_id=1, source_target_pairs={{0,128},{128,0},{256,384},{384,256},{1,129},{129,1},{257,385},{385... | collective-permute-start | bytes 1572872 | tf_op jit(solution)/shard_map/ppermute | solution.py:39
  53.2 24.1 %collective-permute-start.3 = (bf16[16,128,128]{2,1,0:T(8,128)(2,1)S(1)}, bf16[16,128,128]{2,1,0:T(8,128)(2,1)S(1)}, u32[]{:S(2)}, u32[]{:S(2)}) collective-permute-start(bf16[16,128,128]{2,1,0:T(8,128)(2,1)S(1)} %get-tuple-element.39), channel_id=1, source_target_pairs={{0,128},{128,0},{256,384},{384,256},{1,129},{129,1},{257,385},{385... | collective-permute-start | bytes 1572872 | tf_op jit(solution)/shard_map/ppermute | solution.py:39
  56.5 20.7 %collective-permute-start.6 = (bf16[16,128,128]{2,1,0:T(8,128)(2,1)S(1)}, bf16[16,128,128]{2,1,0:T(8,128)(2,1)S(1)}, u32[]{:S(2)}, u32[]{:S(2)}) collective-permute-start(bf16[16,128,128]{2,1,0:T(8,128)(2,1)S(1)} %get-tuple-element.42), channel_id=1, source_target_pairs={{0,384},{128,256},{256,128},{384,0},{1,385},{129,257},{257,129},{3... | collective-permute-start | bytes 1572872 | tf_op jit(solution)/shard_map/ppermute | solution.py:39
  69.1 17.7 %collective-permute-start.4 = (bf16[16,128,128]{2,1,0:T(8,128)(2,1)S(1)}, bf16[16,128,128]{2,1,0:T(8,128)(2,1)S(1)}, u32[]{:S(2)}, u32[]{:S(2)}) collective-permute-start(bf16[16,128,128]{2,1,0:T(8,128)(2,1)S(1)} %get-tuple-element.40), channel_id=1, source_target_pairs={{0,384},{128,256},{256,128},{384,0},{1,385},{129,257},{257,129},{3... | collective-permute-start | bytes 1572872 | tf_op jit(solution)/shard_map/ppermute | solution.py:39
  72.8 14.4 %collective-permute-start.5 = (bf16[16,128,128]{2,1,0:T(8,128)(2,1)S(1)}, bf16[16,128,128]{2,1,0:T(8,128)(2,1)S(1)}, u32[]{:S(2)}, u32[]{:S(2)}) collective-permute-start(bf16[16,128,128]{2,1,0:T(8,128)(2,1)S(1)} %get-tuple-element.41), channel_id=1, source_target_pairs={{0,128},{128,0},{256,384},{384,256},{1,129},{129,1},{257,385},{385... | collective-permute-start | bytes 1572872 | tf_op jit(solution)/shard_map/ppermute | solution.py:39
  88.1 18.0 %collective-permute-start.7 = (bf16[8,2,128,128]{3,2,1,0:T(8,128)(2,1)S(1)}, bf16[8,2,128,128]{3,2,1,0:T(8,128)(2,1)S(1)}, u32[]{:S(2)}, u32[]{:S(2)}) collective-permute-start(bf16[8,2,128,128]{3,2,1,0:T(8,128)(2,1)S(1)} %get-tuple-element.44), channel_id=1, source_target_pairs={{0,8},{8,0},{1,9},{9,1},{2,10},{10,2},{3,11},{11,3},{4,12},{12,4},... | collective-permute-start | bytes 1572872 | tf_op jit(solution)/shard_map/ppermute | solution.py:39
  98.9 7.1 %copy-start.9 = (bf16[64,8192]{1,0:T(8,128)(2,1)}, bf16[64,8192]{1,0:T(8,128)(2,1)S(1)}, u32[]{:S(2)}) copy-start(bf16[64,8192]{1,0:T(8,128)(2,1)S(1)} %get-tuple-element.50) | copy-start | bytes 3145732
  107.0 35.4 %all-to-all-start.2 = ((bf16[8,2,128,128]{3,2,1,0:T(8,128)(2,1)}), bf16[8,2,128,128]{3,2,1,0:T(8,128)(2,1)S(1)}, u32[]{:S(2)}, u32[]{:S(2)}) async-start(bf16[8,2,128,128]{3,2,1,0:T(8,128)(2,1)} %pair_sum.1), calls=%async_computation.2 | async-start | bytes 1048576 | tf_op jit(solution)/shard_map/all_to_all | solution.py:43
  117.3 60.5 %all-gather.5.cloned.1.call-start = ((), (), s32[]{:S(2)}) async-start(), calls=%async_computation.6 | async-start | bytes 2359296 | tf_op jit(solution)/shard_map/all_gather | solution.py:368
  117.3 7.7 %collective-permute-start.8 = (bf16[64,8192]{1,0:T(8,128)(2,1)}, bf16[64,8192]{1,0:T(8,128)(2,1)S(1)}, u32[]{:S(2)}, u32[]{:S(2)}) collective-permute-start(bf16[64,8192]{1,0:T(8,128)(2,1)} %copy-done.9), channel_id=1, source_target_pairs={{0,1},{1,0},{2,3},{3,2},{4,5},{5,4},{6,7},{7,6},{8,9},{9,8},{10,11... | collective-permute-start | bytes 3145736 | tf_op jit(solution)/shard_map/ppermute | solution.py:39
  125.8 17.3 %collective-permute-start.9 = (bf16[16,8192]{1,0:T(8,128)(2,1)S(1)}, bf16[16,8192]{1,0:T(8,128)(2,1)S(1)}, u32[]{:S(2)}, u32[]{:S(2)}) collective-permute-start(bf16[16,8192]{1,0:T(8,128)(2,1)S(1)} %get-tuple-element.52), channel_id=1, source_target_pairs={{0,4},{2,6},{4,0},{6,2},{1,5},{3,7},{5,1},{7,3},{8,12},{10,14},{12... | collective-permute-start | bytes 786440 | tf_op jit(solution)/shard_map/ppermute | solution.py:39
  129.3 13.9 %collective-permute-start.10 = (bf16[16,8192]{1,0:T(8,128)(2,1)S(1)}, bf16[16,8192]{1,0:T(8,128)(2,1)S(1)}, u32[]{:S(2)}, u32[]{:S(2)}) collective-permute-start(bf16[16,8192]{1,0:T(8,128)(2,1)S(1)} %get-tuple-element.53), channel_id=1, source_target_pairs={{0,2},{2,0},{4,6},{6,4},{1,3},{3,1},{5,7},{7,5},{8,10},{10,8},{12,... | collective-permute-start | bytes 786440 | tf_op jit(solution)/shard_map/ppermute | solution.py:39
  131.9 11.2 %collective-permute-start.11 = (bf16[16,8192]{1,0:T(8,128)(2,1)S(1)}, bf16[16,8192]{1,0:T(8,128)(2,1)S(1)}, u32[]{:S(2)}, u32[]{:S(2)}) collective-permute-start(bf16[16,8192]{1,0:T(8,128)(2,1)S(1)} %get-tuple-element.54), channel_id=1, source_target_pairs={{0,6},{2,4},{4,2},{6,0},{1,7},{3,5},{5,3},{7,1},{8,14},{10,12},{12... | collective-permute-start | bytes 786440 | tf_op jit(solution)/shard_map/ppermute | solution.py:39
  166.4 15.8 %all-to-all-start.4 = ((f32[16,8,128]{2,1,0:T(8,128)}), f32[16,8,128]{2,1,0:T(8,128)S(1)}, u32[]{:S(2)}, u32[]{:S(2)}) async-start(f32[16,8,128]{2,1,0:T(8,128)} %relay.1), calls=%async_computation.4 | async-start | bytes 131072 | tf_op jit(solution)/shard_map/all_to_all | solution.py:43
  170.7 11.6 %copy-start = (f32[1,2,128,128]{3,2,1,0:T(8,128)S(1)}, f32[1,2,128,128]{3,2,1,0:T(8,128)}, u32[]{:S(2)}) copy-start(f32[1,2,128,128]{3,2,1,0:T(8,128)} %refs_4_.1) | copy-start | bytes 393220
  170.7 11.6 %copy-start.4 = (f32[1,2,128,128]{3,2,1,0:T(8,128)S(1)}, f32[1,2,128,128]{3,2,1,0:T(8,128)}, u32[]{:S(2)}) copy-start(f32[1,2,128,128]{3,2,1,0:T(8,128)} %refs_5_.1) | copy-start | bytes 393220
  170.7 11.6 %copy-start.5 = (f32[1,2,128,128]{3,2,1,0:T(8,128)S(1)}, f32[1,2,128,128]{3,2,1,0:T(8,128)}, u32[]{:S(2)}) copy-start(f32[1,2,128,128]{3,2,1,0:T(8,128)} %refs_6_.1) | copy-start | bytes 393220
Sparse Core Ops, SparseCore 0:
  19.9 74.4 all-gather.2
  144.1 33.6 all-gather.4

commit v14 on v13

--- a/solution.py
+++ b/solution.py
@@ -185,14 +185,9 @@
         new_two_ref[0, rank] = jnp.where(live, second, two)
 
 
-def turn_kernel(delta_ref, out_ref, held, sem):
-    load = pltpu.make_async_copy(delta_ref, held, sem)
-    load.start()
-    load.wait()
+def turn_kernel(delta_ref, out_ref):
     for rank in range(SLOT_CAP):
-        turned = held[0, rank].T.astype(BF16)
-        for y in range(NY):
-            out_ref[y, rank] = turned
+        out_ref[rank] = delta_ref[0, rank].T.astype(BF16)
 
 
 def contrib_kernel(
@@ -284,11 +279,10 @@
     own = spread(features, "x")
     other = swap(own, "core", 1)
 
-    copies = kernel_call(
-        turn_kernel, "turn", SHAPE((NY,) + delta_value.shape[1:], BF16), [ANY], VMEM,
-        [pltpu.VMEM(delta_value.shape, F32), pltpu.SemaphoreType.DMA], vmem=63,
+    delta_half = kernel_call(
+        turn_kernel, "turn", SHAPE(delta_value.shape[1:], BF16), [VMEM], VMEM
     )(delta_value)
-    delta_y = exchange(copies, "y").reshape(NY * SLOT_CAP, TILE, TILE)
+    delta_y = spread(delta_half, "y").reshape(NY * SLOT_CAP, TILE, TILE)
     delta_all = lax.all_gather(delta_y, Z, axis=0, tiled=True)
 
     grads, turned = kernel_call(
@@ -351,7 +345,6 @@
         [SHAPE((SLOT_CAP, TILE, TILE), F32), SHAPE((NY * NX * 2, 8, TILE), F32)],
         [SMEM, SMEM, VMEM], [VMEM] * 2,
     )(ids, owner_counts, arrived)
-
 
     rows = tokens // (2 * NX)
     _, give = lax.optimization_barrier((pairs, give))

time: 191 us -> 191 us (level)
  waiting for transfers between devices: 47.8 us -> 45.6 us
    all_to_all x2, waiting for transfers between devices: 9.57 us -> 6.22 us  [exchange(): return lax.all_to_all(value, axis, split_axis=0, concat_axis=0, tiled=True)]
    ppermute x12, waiting for transfers between devices: 27.9 us -> 29.9 us  [swap(): lax.ppermute(value, axis, [(i, i ^ bits) for i in range(lax.axis_size(axi...]
  transfers between devices with their start and end apart: 16 -> 16, of which waited for: 11 -> 13; matrix products, arithmetic and copies ran while one was open for 1% -> 1% of each run, Pallas kernels for 9% -> 9%
where the time goes in v14:
time: 191 us; the launch traced here: 190 us
  starting transfers between devices  58.3 us (31%)
  blocking collectives  46.4 us (24%)
  waiting for transfers between devices  45.6 us (24%)
  Pallas kernels  20.4 us (11%)
  between operations  14.3 us (7%)
  local copies, waits for them, and re-layouts  4.05 us (2%)
    all_to_all x3, blocking collectives, exchange(): return lax.all_to_all(value, axis, split_axis=0, concat_axis=0, tiled=True)  46.4 us
    ppermute x12, starting transfers between devices, swap(): lax.ppermute(value, axis, [(i, i ^ bits) for i in range(lax.axis_size(axi...  43.4 us
    ppermute x12, waiting for transfers between devices, swap(): lax.ppermute(value, axis, [(i, i ^ bits) for i in range(lax.axis_size(axi...  29.9 us
    all_to_all x2, starting transfers between devices, exchange(): return lax.all_to_all(value, axis, split_axis=0, concat_axis=0, tiled=True)  14.8 us
    all_gather x1, waiting for transfers between devices, body(): lax.all_gather(share.astype(BF16), ('x', 'core'), axis=0, tiled=True)  7.04 us
    all_to_all x2, waiting for transfers between devices, exchange(): return lax.all_to_all(value, axis, split_axis=0, concat_axis=0, tiled=True)  6.22 us
    pallas_call x2, Pallas kernels, terms(): kernel_call(functools.partial(tile_kernel, parts), 'tiles', [SHAPE(((last...  6.09 us
    pallas_call x1, Pallas kernels, body(): kernel_call(contrib_kernel, 'contribs', [SHAPE((tokens // 2, width), BF16...  4.46 us
  transfers between devices with their start and end apart: 16, of which 13 were waited for; matrix products, arithmetic and copies ran while one was open for 1% of the time, Pallas kernels for 9%

profile of v14, /device:TPU:1, one launch (start us, length us, event | category | flops | bytes accessed | tf_op | source)
XLA Modules:
  0.0 190.1 jit_solution(12368029678021596152)
XLA Ops:
  7.2 0.0 all-gather.3.cloned.1.call-start
  7.2 0.0 copy-start
  7.2 0.9 copy-done
  8.1 0.1 turn.1
  8.3 0.0 copy-start.2
  8.3 0.0 copy-start.3
  8.3 10.6 %all_to_all.25 = bf16[4,2,128,128]{3,2,1,0:T(8,128)(2,1)} all-to-all(bf16[4,2,128,128]{3,2,1,0:T(8,128)(2,1)S(1)} %broadcast_in_dim.5), channel_id=1, replica_groups=mesh['y'=4,'m'=8,'p'=2,'x'=4,'core'=2] {'y'}, dimensions={0} | all-to-all | bytes 524288 | tf_op jit(solution)/shard_map/all_to_all | solution.py:43
  18.9 0.0 all-gather.3.cloned.1.call-update
  18.9 0.0 copy-start.7
  18.9 0.0 copy-start.8
  18.9 0.0 copy-start.9
  18.9 1.1 broadcast_in_dim.4
  20.0 13.9 %all_to_all.26.own_ref = bf16[4,128,1024]{2,1,0:T(8,128)(2,1)S(1)} all-to-all(bf16[4,128,1024]{2,1,0:T(8,128)(2,1)S(1)} %broadcast_in_dim.4), channel_id=1, replica_groups=mesh['y'=4,'m'=8,'p'=2,'x'=4,'core'=2] {'x'}, dimensions={0} | all-to-all | bytes 2097152 | tf_op jit(solution)/shard_map/all_to_all | solution.py:43
  34.0 7.9 %collective-permute-start = (bf16[4,128,1024]{2,1,0:T(8,128)(2,1)S(1)}, bf16[4,128,1024]{2,1,0:T(8,128)(2,1)S(1)}, u32[]{:S(2)}, u32[]{:S(2)}) collective-permute-start(bf16[4,128,1024]{2,1,0:T(8,128)(2,1)S(1)} %all_to_all.26.own_ref), channel_id=1, source_target_pairs={{0,1},{1,0},{2,3},{3,2},{4,5},{5,4},{6,7},{7,6},{8,9},{9,8},{10,11... | collective-permute-start | bytes 3145736 | tf_op jit(solution)/shard_map/ppermute | solution.py:39
  41.8 0.1 pad_add_fusion.ids_ref.refs_0_
  41.9 1.0 copy-done.4
  42.9 1.1 gate.1
  44.1 0.0 collective-permute-done.other_ref
  44.1 3.0 %tiles.2 = (bf16[16,128,128]{2,1,0:T(8,128)(2,1)S(1)}, bf16[16,128,128]{2,1,0:T(8,128)(2,1)S(1)}, bf16[16,128,128]{2,1,0:T(8,128)(2,1)S(1)}, bf16[16,128,128]{2,1,0:T(8,128)(2,1)S(1)}) custom-call(s32[4]{0:T(128)S(1)} %pad_add_fusion.ids_ref.refs_0_, s32[1,112]{1,0:T(1,128)S(1)} %copy-done.8, s32[1,112]{1,0:T(1,128)S(1)} %copy-done.9, ...), custom_call_target="tpu_custom_call" | custom-call | flops 117440512 | bytes 2097152 | tf_op jit(solution)/shard_map/tiles/pallas_call | solution.py:301
  47.1 2.8 %collective-permute-start.1 = (bf16[16,128,128]{2,1,0:T(8,128)(2,1)S(1)}, bf16[16,128,128]{2,1,0:T(8,128)(2,1)S(1)}, u32[]{:S(2)}, u32[]{:S(2)}) collective-permute-start(bf16[16,128,128]{2,1,0:T(8,128)(2,1)S(1)} %get-tuple-element.36), channel_id=1, source_target_pairs={{0,384},{128,256},{256,128},{384,0},{1,385},{129,257},{257,129},{3... | collective-permute-start | bytes 1572872 | tf_op jit(solution)/shard_map/ppermute | solution.py:39
  49.9 1.9 %collective-permute-start.2 = (bf16[16,128,128]{2,1,0:T(8,128)(2,1)S(1)}, bf16[16,128,128]{2,1,0:T(8,128)(2,1)S(1)}, u32[]{:S(2)}, u32[]{:S(2)}) collective-permute-start(bf16[16,128,128]{2,1,0:T(8,128)(2,1)S(1)} %get-tuple-element.37), channel_id=1, source_target_pairs={{0,128},{128,0},{256,384},{384,256},{1,129},{129,1},{257,385},{385... | collective-permute-start | bytes 1572872 | tf_op jit(solution)/shard_map/ppermute | solution.py:39
  51.8 3.4 %collective-permute-start.3 = (bf16[16,128,128]{2,1,0:T(8,128)(2,1)S(1)}, bf16[16,128,128]{2,1,0:T(8,128)(2,1)S(1)}, u32[]{:S(2)}, u32[]{:S(2)}) collective-permute-start(bf16[16,128,128]{2,1,0:T(8,128)(2,1)S(1)} %get-tuple-element.39), channel_id=1, source_target_pairs={{0,128},{128,0},{256,384},{384,256},{1,129},{129,1},{257,385},{385... | collective-permute-start | bytes 1572872 | tf_op jit(solution)/shard_map/ppermute | solution.py:39
  55.2 3.7 %collective-permute-start.6 = (bf16[16,128,128]{2,1,0:T(8,128)(2,1)S(1)}, bf16[16,128,128]{2,1,0:T(8,128)(2,1)S(1)}, u32[]{:S(2)}, u32[]{:S(2)}) collective-permute-start(bf16[16,128,128]{2,1,0:T(8,128)(2,1)S(1)} %get-tuple-element.42), channel_id=1, source_target_pairs={{0,384},{128,256},{256,128},{384,0},{1,385},{129,257},{257,129},{3... | collective-permute-start | bytes 1572872 | tf_op jit(solution)/shard_map/ppermute | solution.py:39
  58.9 4.5 %collective-permute-done.1.refs_0_ = bf16[16,128,128]{2,1,0:T(8,128)(2,1)S(1)} collective-permute-done((bf16[16,128,128]{2,1,0:T(8,128)(2,1)S(1)}, bf16[16,128,128]{2,1,0:T(8,128)(2,1)S(1)}, u32[]{:S(2)}, u32[]{:S(2)}) %collective-permute-start.1) | collective-permute-done | bytes 524320 | tf_op jit(solution)/shard_map/ppermute | solution.py:39
  63.5 1.1 collective-permute-done.2.refs_1_
  64.6 3.1 %tiles.3 = (bf16[16,128,128]{2,1,0:T(8,128)(2,1)S(1)}, bf16[16,128,128]{2,1,0:T(8,128)(2,1)S(1)}, bf16[32,128,128]{2,1,0:T(8,128)(2,1)S(1)}) custom-call(s32[4]{0:T(128)S(1)} %pad_add_fusion.ids_ref.refs_0_, s32[1,112]{1,0:T(1,128)S(1)} %copy-done.8, s32[1,112]{1,0:T(1,128)S(1)} %copy-done.9, s32[1,64]{1,0:T(1,128)S(1)} %copy-done.7, ...), custom_call_target="tpu_custom_call" | custom-call | flops 117440512 | bytes 2097152 | tf_op jit(solution)/shard_map/tiles/pallas_call | solution.py:301
  67.7 3.8 %collective-permute-start.4 = (bf16[16,128,128]{2,1,0:T(8,128)(2,1)S(1)}, bf16[16,128,128]{2,1,0:T(8,128)(2,1)S(1)}, u32[]{:S(2)}, u32[]{:S(2)}) collective-permute-start(bf16[16,128,128]{2,1,0:T(8,128)(2,1)S(1)} %get-tuple-element.40), channel_id=1, source_target_pairs={{0,384},{128,256},{256,128},{384,0},{1,385},{129,257},{257,129},{3... | collective-permute-start | bytes 1572872 | tf_op jit(solution)/shard_map/ppermute | solution.py:39
  71.5 1.9 %collective-permute-start.5 = (bf16[16,128,128]{2,1,0:T(8,128)(2,1)S(1)}, bf16[16,128,128]{2,1,0:T(8,128)(2,1)S(1)}, u32[]{:S(2)}, u32[]{:S(2)}) collective-permute-start(bf16[16,128,128]{2,1,0:T(8,128)(2,1)S(1)} %get-tuple-element.41), channel_id=1, source_target_pairs={{0,128},{128,0},{256,384},{384,256},{1,129},{129,1},{257,385},{385... | collective-permute-start | bytes 1572872 | tf_op jit(solution)/shard_map/ppermute | solution.py:39
  73.5 2.5 %collective-permute-done.3 = bf16[16,128,128]{2,1,0:T(8,128)(2,1)S(1)} collective-permute-done((bf16[16,128,128]{2,1,0:T(8,128)(2,1)S(1)}, bf16[16,128,128]{2,1,0:T(8,128)(2,1)S(1)}, u32[]{:S(2)}, u32[]{:S(2)}) %collective-permute-start.3) | collective-permute-done | bytes 524320 | tf_op jit(solution)/shard_map/ppermute | solution.py:39
  76.0 0.0 collective-permute-done.6
  76.0 9.4 %collective-permute-done.4 = bf16[16,128,128]{2,1,0:T(8,128)(2,1)S(1)} collective-permute-done((bf16[16,128,128]{2,1,0:T(8,128)(2,1)S(1)}, bf16[16,128,128]{2,1,0:T(8,128)(2,1)S(1)}, u32[]{:S(2)}, u32[]{:S(2)}) %collective-permute-start.4) | collective-permute-done | bytes 524320 | tf_op jit(solution)/shard_map/ppermute | solution.py:39
  85.4 0.4 collective-permute-done.5
  85.8 1.6 y_sum.1
  87.5 3.5 %collective-permute-start.7 = (bf16[8,2,128,128]{3,2,1,0:T(8,128)(2,1)}, bf16[8,2,128,128]{3,2,1,0:T(8,128)(2,1)S(1)}, u32[]{:S(2)}, u32[]{:S(2)}) collective-permute-start(bf16[8,2,128,128]{3,2,1,0:T(8,128)(2,1)} %get-tuple-element.44), channel_id=1, source_target_pairs={{0,8},{8,0},{1,9},{9,1},{2,10},{10,2},{3,11},{11,3},{4,12},{12,4},... | collective-permute-start | bytes 1572872 | tf_op jit(solution)/shard_map/ppermute | solution.py:39
  91.0 2.4 %all-gather.3.cloned.1.call-done.deltas_ref = bf16[128,128,128]{2,1,0:T(8,128)(2,1)} async-done(((bf16[8,128,128]{2,1,0:T(8,128)(2,1)}), bf16[128,128,128]{2,1,0:T(8,128)(2,1)}) %all-gather.3.cloned.1.call-update) | async-done | bytes 4194320 | tf_op jit(solution)/shard_map/all_gather | solution.py:286
  93.5 4.5 %contribs.1 = (bf16[64,8192]{1,0:T(8,128)(2,1)S(1)}, bf16[64,8192]{1,0:T(8,128)(2,1)S(1)}, f32[8,128]{1,0:T(8,128)S(1)}) custom-call(s32[1,112]{1,0:T(1,128)S(1)} %copy-done.8, s32[1,112]{1,0:T(1,128)S(1)} %copy-done.9, s32[1,64]{1,0:T(1,128)S(1)} %copy-done.7, bf16[14,128,128]{2,1,0:T(8,128)(2,1)S(1)} %get-tuple-element.45.grads_ref, ...), custom_call_target="tpu_custom_call" | custom-call | bytes 4096 | tf_op jit(solution)/shard_map/contribs/pallas_call | solution.py:327
  97.9 0.0 copy-start.10
  97.9 1.0 copy-done.10
  98.9 6.6 %collective-permute-done.7.taken_ref = bf16[8,2,128,128]{3,2,1,0:T(8,128)(2,1)S(1)} collective-permute-done((bf16[8,2,128,128]{3,2,1,0:T(8,128)(2,1)}, bf16[8,2,128,128]{3,2,1,0:T(8,128)(2,1)S(1)}, u32[]{:S(2)}, u32[]{:S(2)}) %collective-permute-start.7) | collective-permute-done | bytes 524320 | tf_op jit(solution)/shard_map/ppermute | solution.py:39
  105.5 0.9 pair_sum.1
  106.4 10.2 %all-to-all-start.2 = ((bf16[8,2,128,128]{3,2,1,0:T(8,128)(2,1)}), bf16[8,2,128,128]{3,2,1,0:T(8,128)(2,1)S(1)}, u32[]{:S(2)}, u32[]{:S(2)}) async-start(bf16[8,2,128,128]{3,2,1,0:T(8,128)(2,1)} %pair_sum.1), calls=%async_computation.2 | async-start | bytes 1048576 | tf_op jit(solution)/shard_map/all_to_all | solution.py:43
  116.6 0.0 all-gather.5.cloned.1.call-start
  116.7 5.5 %collective-permute-start.8 = (bf16[64,8192]{1,0:T(8,128)(2,1)}, bf16[64,8192]{1,0:T(8,128)(2,1)S(1)}, u32[]{:S(2)}, u32[]{:S(2)}) collective-permute-start(bf16[64,8192]{1,0:T(8,128)(2,1)} %copy-done.10), channel_id=1, source_target_pairs={{0,1},{1,0},{2,3},{3,2},{4,5},{5,4},{6,7},{7,6},{8,9},{9,8},{10,11... | collective-permute-start | bytes 3145736 | tf_op jit(solution)/shard_map/ppermute | solution.py:39
  122.2 2.5 %collective-permute-done.8 = bf16[64,8192]{1,0:T(8,128)(2,1)S(1)} collective-permute-done((bf16[64,8192]{1,0:T(8,128)(2,1)}, bf16[64,8192]{1,0:T(8,128)(2,1)S(1)}, u32[]{:S(2)}, u32[]{:S(2)}) %collective-permute-start.8) | collective-permute-done | bytes 1048608 | tf_op jit(solution)/shard_map/ppermute | solution.py:39
  124.7 0.8 core_sum.1
  125.5 3.3 %collective-permute-start.9 = (bf16[16,8192]{1,0:T(8,128)(2,1)S(1)}, bf16[16,8192]{1,0:T(8,128)(2,1)S(1)}, u32[]{:S(2)}, u32[]{:S(2)}) collective-permute-start(bf16[16,8192]{1,0:T(8,128)(2,1)S(1)} %get-tuple-element.52), channel_id=1, source_target_pairs={{0,4},{2,6},{4,0},{6,2},{1,5},{3,7},{5,1},{7,3},{8,12},{10,14},{12... | collective-permute-start | bytes 786440 | tf_op jit(solution)/shard_map/ppermute | solution.py:39
  128.8 2.4 %collective-permute-start.10 = (bf16[16,8192]{1,0:T(8,128)(2,1)S(1)}, bf16[16,8192]{1,0:T(8,128)(2,1)S(1)}, u32[]{:S(2)}, u32[]{:S(2)}) collective-permute-start(bf16[16,8192]{1,0:T(8,128)(2,1)S(1)} %get-tuple-element.53), channel_id=1, source_target_pairs={{0,2},{2,0},{4,6},{6,4},{1,3},{3,1},{5,7},{7,5},{8,10},{10,8},{12,... | collective-permute-start | bytes 786440 | tf_op jit(solution)/shard_map/ppermute | solution.py:39
  131.2 3.3 %collective-permute-start.11 = (bf16[16,8192]{1,0:T(8,128)(2,1)S(1)}, bf16[16,8192]{1,0:T(8,128)(2,1)S(1)}, u32[]{:S(2)}, u32[]{:S(2)}) collective-permute-start(bf16[16,8192]{1,0:T(8,128)(2,1)S(1)} %get-tuple-element.54), channel_id=1, source_target_pairs={{0,6},{2,4},{4,2},{6,0},{1,7},{3,5},{5,3},{7,1},{8,14},{10,12},{12... | collective-permute-start | bytes 786440 | tf_op jit(solution)/shard_map/ppermute | solution.py:39
  134.5 4.1 %all-to-all-done.2.arrived_ref = bf16[8,2,128,128]{3,2,1,0:T(8,128)(2,1)S(1)} async-done(((bf16[8,2,128,128]{3,2,1,0:T(8,128)(2,1)}), bf16[8,2,128,128]{3,2,1,0:T(8,128)(2,1)S(1)}, u32[]{:S(2)}, u32[]{:S(2)}) %all-to-all-start.2) | async-done | bytes 524320 | tf_op jit(solution)/shard_map/all_to_all | solution.py:43
  138.6 0.8 own_grad.1
  139.4 1.6 collective-permute-done.10
  141.0 1.2 collective-permute-done.11
  142.2 0.8 add_convert_fusion
  143.0 0.0 all-gather.5.cloned.1.call-update
  143.0 21.9 %all_to_all.27.arrived_ref = f32[32,8,128]{2,1,0:T(8,128)S(1)} all-to-all(f32[32,8,128]{2,1,0:T(8,128)S(1)} %get-tuple-element.55), channel_id=1, replica_groups=mesh['y'=4,'m'=8,'p'=2,'x'=4,'core'=2] {'y','x','core'}, dimensions={0} | all-to-all | bytes 262144 | tf_op jit(solution)/shard_map/all_to_all | solution.py:43
  165.0 0.7 relay.1
  165.6 4.5 %all-to-all-start.4 = ((f32[16,8,128]{2,1,0:T(8,128)}), f32[16,8,128]{2,1,0:T(8,128)S(1)}, u32[]{:S(2)}, u32[]{:S(2)}) async-start(f32[16,8,128]{2,1,0:T(8,128)} %relay.1), calls=%async_computation.4 | async-start | bytes 131072 | tf_op jit(solution)/shard_map/all_to_all | solution.py:43
  170.1 0.0 copy-start.1
  170.2 0.0 copy-start.5
  170.2 0.0 copy-start.6
  170.2 7.0 %all-gather.5.cloned.1.call-done.in_ref = bf16[128,8192]{1,0:T(8,128)(2,1)} async-done(((bf16[16,8192]{1,0:T(8,128)(2,1)}), bf16[128,8192]{1,0:T(8,128)(2,1)}) %all-gather.5.cloned.1.call-update) | async-done | bytes 2097168 | tf_op jit(solution)/shard_map/all_gather | solution.py:361
  177.2 2.4 %result.1 = bf16[128,8192]{1,0:T(8,128)(2,1)} custom-call(bf16[128,8192]{1,0:T(8,128)(2,1)} %all-gather.5.cloned.1.call-done.in_ref), custom_call_target="tpu_custom_call" | custom-call | bytes 4194304 | tf_op jit(solution)/shard_map/result/pallas_call | solution.py:362
  179.7 2.1 %all-to-all-done.4.refs_2_ = f32[16,8,128]{2,1,0:T(8,128)S(1)} async-done(((f32[16,8,128]{2,1,0:T(8,128)}), f32[16,8,128]{2,1,0:T(8,128)S(1)}, u32[]{:S(2)}, u32[]{:S(2)}) %all-to-all-start.4) | async-done | bytes 65568 | tf_op jit(solution)/shard_map/all_to_all | solution.py:43
  181.7 1.5 adam.1
  (11 shorter events, 0.1 us)
Async XLA Ops:
  7.2 86.3 %all-gather.3.cloned.1.call-start = ((), (), s32[]{:S(2)}) async-start(), calls=%async_computation.5 | async-start | bytes 4456448 | tf_op jit(solution)/shard_map/all_gather | solution.py:286
  7.2 0.9 copy-start
  8.3 33.6 %copy-start.2 = (bf16[128,1792]{1,0:T(8,128)(2,1)S(1)}, bf16[128,1792]{1,0:T(8,128)(2,1)}, u32[]{:S(2)}) copy-start(bf16[128,1792]{1,0:T(8,128)(2,1)} %gate_ref.1) | copy-start | bytes 1376260
  8.3 33.6 %copy-start.3 = (bf16[128,1792]{1,0:T(8,128)(2,1)S(1)}, bf16[128,1792]{1,0:T(8,128)(2,1)}, u32[]{:S(2)}) copy-start(bf16[128,1792]{1,0:T(8,128)(2,1)} %up_ref.1) | copy-start | bytes 1376260
  18.9 25.2 %copy-start.7 = (s32[1,64]{1,0:T(1,128)S(1)}, s32[1,64]{1,0:T(1,128)}, u32[]{:S(2)}) copy-start(s32[1,64]{1,0:T(1,128)} %refs_1_.1) | copy-start | bytes 772
  18.9 25.2 %copy-start.8 = (s32[1,112]{1,0:T(1,128)S(1)}, s32[1,112]{1,0:T(1,128)}, u32[]{:S(2)}) copy-start(s32[1,112]{1,0:T(1,128)} %rows_ref.5) | copy-start | bytes 1348
  18.9 25.2 %copy-start.9 = (s32[1,112]{1,0:T(1,128)S(1)}, s32[1,112]{1,0:T(1,128)}, u32[]{:S(2)}) copy-start(s32[1,112]{1,0:T(1,128)} %cols_ref.5) | copy-start | bytes 1348
  34.0 10.1 %collective-permute-start = (bf16[4,128,1024]{2,1,0:T(8,128)(2,1)S(1)}, bf16[4,128,1024]{2,1,0:T(8,128)(2,1)S(1)}, u32[]{:S(2)}, u32[]{:S(2)}) collective-permute-start(bf16[4,128,1024]{2,1,0:T(8,128)(2,1)S(1)} %all_to_all.26.own_ref), channel_id=1, source_target_pairs={{0,1},{1,0},{2,3},{3,2},{4,5},{5,4},{6,7},{7,6},{8,9},{9,8},{10,11... | collective-permute-start | bytes 3145736 | tf_op jit(solution)/shard_map/ppermute | solution.py:39
  41.9 1.0 copy-start.4
  47.1 16.3 %collective-permute-start.1 = (bf16[16,128,128]{2,1,0:T(8,128)(2,1)S(1)}, bf16[16,128,128]{2,1,0:T(8,128)(2,1)S(1)}, u32[]{:S(2)}, u32[]{:S(2)}) collective-permute-start(bf16[16,128,128]{2,1,0:T(8,128)(2,1)S(1)} %get-tuple-element.36), channel_id=1, source_target_pairs={{0,384},{128,256},{256,128},{384,0},{1,385},{129,257},{257,129},{3... | collective-permute-start | bytes 1572872 | tf_op jit(solution)/shard_map/ppermute | solution.py:39
  49.9 14.7 %collective-permute-start.2 = (bf16[16,128,128]{2,1,0:T(8,128)(2,1)S(1)}, bf16[16,128,128]{2,1,0:T(8,128)(2,1)S(1)}, u32[]{:S(2)}, u32[]{:S(2)}) collective-permute-start(bf16[16,128,128]{2,1,0:T(8,128)(2,1)S(1)} %get-tuple-element.37), channel_id=1, source_target_pairs={{0,128},{128,0},{256,384},{384,256},{1,129},{129,1},{257,385},{385... | collective-permute-start | bytes 1572872 | tf_op jit(solution)/shard_map/ppermute | solution.py:39
  51.8 24.1 %collective-permute-start.3 = (bf16[16,128,128]{2,1,0:T(8,128)(2,1)S(1)}, bf16[16,128,128]{2,1,0:T(8,128)(2,1)S(1)}, u32[]{:S(2)}, u32[]{:S(2)}) collective-permute-start(bf16[16,128,128]{2,1,0:T(8,128)(2,1)S(1)} %get-tuple-element.39), channel_id=1, source_target_pairs={{0,128},{128,0},{256,384},{384,256},{1,129},{129,1},{257,385},{385... | collective-permute-start | bytes 1572872 | tf_op jit(solution)/shard_map/ppermute | solution.py:39
  55.2 20.8 %collective-permute-start.6 = (bf16[16,128,128]{2,1,0:T(8,128)(2,1)S(1)}, bf16[16,128,128]{2,1,0:T(8,128)(2,1)S(1)}, u32[]{:S(2)}, u32[]{:S(2)}) collective-permute-start(bf16[16,128,128]{2,1,0:T(8,128)(2,1)S(1)} %get-tuple-element.42), channel_id=1, source_target_pairs={{0,384},{128,256},{256,128},{384,0},{1,385},{129,257},{257,129},{3... | collective-permute-start | bytes 1572872 | tf_op jit(solution)/shard_map/ppermute | solution.py:39
  67.7 17.7 %collective-permute-start.4 = (bf16[16,128,128]{2,1,0:T(8,128)(2,1)S(1)}, bf16[16,128,128]{2,1,0:T(8,128)(2,1)S(1)}, u32[]{:S(2)}, u32[]{:S(2)}) collective-permute-start(bf16[16,128,128]{2,1,0:T(8,128)(2,1)S(1)} %get-tuple-element.40), channel_id=1, source_target_pairs={{0,384},{128,256},{256,128},{384,0},{1,385},{129,257},{257,129},{3... | collective-permute-start | bytes 1572872 | tf_op jit(solution)/shard_map/ppermute | solution.py:39
  71.5 14.3 %collective-permute-start.5 = (bf16[16,128,128]{2,1,0:T(8,128)(2,1)S(1)}, bf16[16,128,128]{2,1,0:T(8,128)(2,1)S(1)}, u32[]{:S(2)}, u32[]{:S(2)}) collective-permute-start(bf16[16,128,128]{2,1,0:T(8,128)(2,1)S(1)} %get-tuple-element.41), channel_id=1, source_target_pairs={{0,128},{128,0},{256,384},{384,256},{1,129},{129,1},{257,385},{385... | collective-permute-start | bytes 1572872 | tf_op jit(solution)/shard_map/ppermute | solution.py:39
  87.5 18.0 %collective-permute-start.7 = (bf16[8,2,128,128]{3,2,1,0:T(8,128)(2,1)}, bf16[8,2,128,128]{3,2,1,0:T(8,128)(2,1)S(1)}, u32[]{:S(2)}, u32[]{:S(2)}) collective-permute-start(bf16[8,2,128,128]{3,2,1,0:T(8,128)(2,1)} %get-tuple-element.44), channel_id=1, source_target_pairs={{0,8},{8,0},{1,9},{9,1},{2,10},{10,2},{3,11},{11,3},{4,12},{12,4},... | collective-permute-start | bytes 1572872 | tf_op jit(solution)/shard_map/ppermute | solution.py:39
  97.9 1.0 copy-start.10
  106.4 32.2 %all-to-all-start.2 = ((bf16[8,2,128,128]{3,2,1,0:T(8,128)(2,1)}), bf16[8,2,128,128]{3,2,1,0:T(8,128)(2,1)S(1)}, u32[]{:S(2)}, u32[]{:S(2)}) async-start(bf16[8,2,128,128]{3,2,1,0:T(8,128)(2,1)} %pair_sum.1), calls=%async_computation.2 | async-start | bytes 1048576 | tf_op jit(solution)/shard_map/all_to_all | solution.py:43
  116.6 60.6 %all-gather.5.cloned.1.call-start = ((), (), s32[]{:S(2)}) async-start(), calls=%async_computation.6 | async-start | bytes 2359296 | tf_op jit(solution)/shard_map/all_gather | solution.py:361
  116.7 8.0 %collective-permute-start.8 = (bf16[64,8192]{1,0:T(8,128)(2,1)}, bf16[64,8192]{1,0:T(8,128)(2,1)S(1)}, u32[]{:S(2)}, u32[]{:S(2)}) collective-permute-start(bf16[64,8192]{1,0:T(8,128)(2,1)} %copy-done.10), channel_id=1, source_target_pairs={{0,1},{1,0},{2,3},{3,2},{4,5},{5,4},{6,7},{7,6},{8,9},{9,8},{10,11... | collective-permute-start | bytes 3145736 | tf_op jit(solution)/shard_map/ppermute | solution.py:39
  125.5 13.9 %collective-permute-start.9 = (bf16[16,8192]{1,0:T(8,128)(2,1)S(1)}, bf16[16,8192]{1,0:T(8,128)(2,1)S(1)}, u32[]{:S(2)}, u32[]{:S(2)}) collective-permute-start(bf16[16,8192]{1,0:T(8,128)(2,1)S(1)} %get-tuple-element.52), channel_id=1, source_target_pairs={{0,4},{2,6},{4,0},{6,2},{1,5},{3,7},{5,1},{7,3},{8,12},{10,14},{12... | collective-permute-start | bytes 786440 | tf_op jit(solution)/shard_map/ppermute | solution.py:39
  128.8 12.2 %collective-permute-start.10 = (bf16[16,8192]{1,0:T(8,128)(2,1)S(1)}, bf16[16,8192]{1,0:T(8,128)(2,1)S(1)}, u32[]{:S(2)}, u32[]{:S(2)}) collective-permute-start(bf16[16,8192]{1,0:T(8,128)(2,1)S(1)} %get-tuple-element.53), channel_id=1, source_target_pairs={{0,2},{2,0},{4,6},{6,4},{1,3},{3,1},{5,7},{7,5},{8,10},{10,8},{12,... | collective-permute-start | bytes 786440 | tf_op jit(solution)/shard_map/ppermute | solution.py:39
  131.2 11.0 %collective-permute-start.11 = (bf16[16,8192]{1,0:T(8,128)(2,1)S(1)}, bf16[16,8192]{1,0:T(8,128)(2,1)S(1)}, u32[]{:S(2)}, u32[]{:S(2)}) collective-permute-start(bf16[16,8192]{1,0:T(8,128)(2,1)S(1)} %get-tuple-element.54), channel_id=1, source_target_pairs={{0,6},{2,4},{4,2},{6,0},{1,7},{3,5},{5,3},{7,1},{8,14},{10,12},{12... | collective-permute-start | bytes 786440 | tf_op jit(solution)/shard_map/ppermute | solution.py:39
  165.6 16.1 %all-to-all-start.4 = ((f32[16,8,128]{2,1,0:T(8,128)}), f32[16,8,128]{2,1,0:T(8,128)S(1)}, u32[]{:S(2)}, u32[]{:S(2)}) async-start(f32[16,8,128]{2,1,0:T(8,128)} %relay.1), calls=%async_computation.4 | async-start | bytes 131072 | tf_op jit(solution)/shard_map/all_to_all | solution.py:43
  170.1 11.6 %copy-start.1 = (f32[1,2,128,128]{3,2,1,0:T(8,128)S(1)}, f32[1,2,128,128]{3,2,1,0:T(8,128)}, u32[]{:S(2)}) copy-start(f32[1,2,128,128]{3,2,1,0:T(8,128)} %refs_4_.1) | copy-start | bytes 393220
  170.2 11.6 %copy-start.5 = (f32[1,2,128,128]{3,2,1,0:T(8,128)S(1)}, f32[1,2,128,128]{3,2,1,0:T(8,128)}, u32[]{:S(2)}) copy-start(f32[1,2,128,128]{3,2,1,0:T(8,128)} %refs_5_.1) | copy-start | bytes 393220
  170.2 11.6 %copy-start.6 = (f32[1,2,128,128]{3,2,1,0:T(8,128)S(1)}, f32[1,2,128,128]{3,2,1,0:T(8,128)}, u32[]{:S(2)}) copy-start(f32[1,2,128,128]{3,2,1,0:T(8,128)} %refs_6_.1) | copy-start | bytes 393220
Sparse Core Ops, SparseCore 0:
  19.0 74.4 all-gather.2
  143.2 34.0 all-gather.4

commit v15 on v12

--- a/solution.py
+++ b/solution.py
@@ -87,7 +87,7 @@
 def slot_products(group, owners, put, ids_ref, rows_ref, cols_ref, starts_ref, features, turned_ref):
     core = ids_ref[3]
     last = rows_ref.shape[1] - 1
-    per_step = 4
+    per_step = 8
 
     def step(index, carry):
         for part in range(per_step):

time: 190 us -> 190 us (level)
  waiting for transfers between devices: 46.9 us -> 51.7 us
  starting transfers between devices: 58.9 us -> 56.6 us
    all_to_all x2, waiting for transfers between devices: 6.82 us -> 11.2 us  [exchange(): return lax.all_to_all(value, axis, split_axis=0, concat_axis=0, tiled=True)]
  transfers between devices with their start and end apart: 16 -> 16, of which waited for: 14 -> 12; matrix products, arithmetic and copies ran while one was open for 1% -> 1% of each run, Pallas kernels for 9% -> 8%
where the time goes in v15:
time: 190 us; the launch traced here: 189 us
  starting transfers between devices  56.6 us (30%)
  waiting for transfers between devices  51.7 us (27%)
  blocking collectives  44.8 us (24%)
  Pallas kernels  17.9 us (9%)
  between operations  14.4 us (8%)
  local copies, waits for them, and re-layouts  3.05 us (2%)
    all_to_all x3, blocking collectives, exchange(): return lax.all_to_all(value, axis, split_axis=0, concat_axis=0, tiled=True)  44.8 us
    ppermute x12, starting transfers between devices, swap(): lax.ppermute(value, axis, [(i, i ^ bits) for i in range(lax.axis_size(axi...  42.6 us
    ppermute x12, waiting for transfers between devices, swap(): lax.ppermute(value, axis, [(i, i ^ bits) for i in range(lax.axis_size(axi...  29.2 us
    all_to_all x2, starting transfers between devices, exchange(): return lax.all_to_all(value, axis, split_axis=0, concat_axis=0, tiled=True)  13.9 us
    all_to_all x2, waiting for transfers between devices, exchange(): return lax.all_to_all(value, axis, split_axis=0, concat_axis=0, tiled=True)  11.2 us
    all_gather x1, waiting for transfers between devices, body(): lax.all_gather(share.astype(BF16), ('x', 'core'), axis=0, tiled=True)  7.04 us
    pallas_call x1, Pallas kernels, body(): kernel_call(contrib_kernel, 'contribs', [SHAPE((tokens // 2, width), BF16...  4.47 us
    all_gather x1, waiting for transfers between devices, body(): delta_all = lax.all_gather(delta_y, Z, axis=0, tiled=True)  4.28 us
  transfers between devices with their start and end apart: 16, of which 12 were waited for; matrix products, arithmetic and copies ran while one was open for 1% of the time, Pallas kernels for 8%

profile of v15, /device:TPU:1, one launch (start us, length us, event | category | flops | bytes accessed | tf_op | source)
XLA Modules:
  0.0 189.4 jit_solution(10548623324956792687)
XLA Ops:
  7.2 0.0 all-gather.3.cloned.1.call-start
  7.2 0.0 copy-start
  7.2 0.9 copy-done
  8.1 0.1 turn.1
  8.3 0.0 copy-start.2
  8.3 0.0 copy-start.3
  8.3 0.0 copy-start.4
  8.3 10.6 %all_to_all.25 = bf16[4,2,128,128]{3,2,1,0:T(8,128)(2,1)} all-to-all(bf16[4,2,128,128]{3,2,1,0:T(8,128)(2,1)S(1)} %broadcast_in_dim.5), channel_id=1, replica_groups=mesh['y'=4,'m'=8,'p'=2,'x'=4,'core'=2] {'y'}, dimensions={0} | all-to-all | bytes 524288 | tf_op jit(solution)/shard_map/all_to_all | solution.py:43
  18.9 0.0 all-gather.3.cloned.1.call-update
  18.9 0.0 copy-start.9
  18.9 0.0 copy-start.10
  18.9 0.0 copy-start.11
  18.9 1.1 broadcast_in_dim.4
  20.0 13.9 %all_to_all.26.own_ref = bf16[4,128,1024]{2,1,0:T(8,128)(2,1)S(1)} all-to-all(bf16[4,128,1024]{2,1,0:T(8,128)(2,1)S(1)} %broadcast_in_dim.4), channel_id=1, replica_groups=mesh['y'=4,'m'=8,'p'=2,'x'=4,'core'=2] {'x'}, dimensions={0} | all-to-all | bytes 2097152 | tf_op jit(solution)/shard_map/all_to_all | solution.py:43
  34.0 7.9 %collective-permute-start = (bf16[4,128,1024]{2,1,0:T(8,128)(2,1)S(1)}, bf16[4,128,1024]{2,1,0:T(8,128)(2,1)S(1)}, u32[]{:S(2)}, u32[]{:S(2)}) collective-permute-start(bf16[4,128,1024]{2,1,0:T(8,128)(2,1)S(1)} %all_to_all.26.own_ref), channel_id=1, source_target_pairs={{0,1},{1,0},{2,3},{3,2},{4,5},{5,4},{6,7},{7,6},{8,9},{9,8},{10,11... | collective-permute-start | bytes 3145736 | tf_op jit(solution)/shard_map/ppermute | solution.py:39
  41.8 0.1 pad_add_fusion.ids_ref.refs_0_
  41.9 1.1 gate.1
  43.1 1.0 collective-permute-done.other_ref
  44.1 1.9 %tiles.2 = (bf16[16,128,128]{2,1,0:T(8,128)(2,1)S(1)}, bf16[16,128,128]{2,1,0:T(8,128)(2,1)S(1)}, bf16[16,128,128]{2,1,0:T(8,128)(2,1)S(1)}, bf16[16,128,128]{2,1,0:T(8,128)(2,1)S(1)}) custom-call(s32[4]{0:T(128)S(1)} %pad_add_fusion.ids_ref.refs_0_, s32[1,112]{1,0:T(1,128)S(1)} %copy-done.10, s32[1,112]{1,0:T(1,128)S(1)} %copy-done.11, ...), custom_call_target="tpu_custom_call" | custom-call | flops 117440512 | bytes 2097152 | tf_op jit(solution)/shard_map/tiles/pallas_call | solution.py:300
  46.0 2.8 %collective-permute-start.1 = (bf16[16,128,128]{2,1,0:T(8,128)(2,1)S(1)}, bf16[16,128,128]{2,1,0:T(8,128)(2,1)S(1)}, u32[]{:S(2)}, u32[]{:S(2)}) collective-permute-start(bf16[16,128,128]{2,1,0:T(8,128)(2,1)S(1)} %get-tuple-element.37), channel_id=1, source_target_pairs={{0,384},{128,256},{256,128},{384,0},{1,385},{129,257},{257,129},{3... | collective-permute-start | bytes 1572872 | tf_op jit(solution)/shard_map/ppermute | solution.py:39
  48.8 1.9 %collective-permute-start.2 = (bf16[16,128,128]{2,1,0:T(8,128)(2,1)S(1)}, bf16[16,128,128]{2,1,0:T(8,128)(2,1)S(1)}, u32[]{:S(2)}, u32[]{:S(2)}) collective-permute-start(bf16[16,128,128]{2,1,0:T(8,128)(2,1)S(1)} %get-tuple-element.38), channel_id=1, source_target_pairs={{0,128},{128,0},{256,384},{384,256},{1,129},{129,1},{257,385},{385... | collective-permute-start | bytes 1572872 | tf_op jit(solution)/shard_map/ppermute | solution.py:39
  50.7 3.4 %collective-permute-start.3 = (bf16[16,128,128]{2,1,0:T(8,128)(2,1)S(1)}, bf16[16,128,128]{2,1,0:T(8,128)(2,1)S(1)}, u32[]{:S(2)}, u32[]{:S(2)}) collective-permute-start(bf16[16,128,128]{2,1,0:T(8,128)(2,1)S(1)} %get-tuple-element.40), channel_id=1, source_target_pairs={{0,128},{128,0},{256,384},{384,256},{1,129},{129,1},{257,385},{385... | collective-permute-start | bytes 1572872 | tf_op jit(solution)/shard_map/ppermute | solution.py:39
  54.1 3.7 %collective-permute-start.6 = (bf16[16,128,128]{2,1,0:T(8,128)(2,1)S(1)}, bf16[16,128,128]{2,1,0:T(8,128)(2,1)S(1)}, u32[]{:S(2)}, u32[]{:S(2)}) collective-permute-start(bf16[16,128,128]{2,1,0:T(8,128)(2,1)S(1)} %get-tuple-element.43), channel_id=1, source_target_pairs={{0,384},{128,256},{256,128},{384,0},{1,385},{129,257},{257,129},{3... | collective-permute-start | bytes 1572872 | tf_op jit(solution)/shard_map/ppermute | solution.py:39
  57.8 4.5 %collective-permute-done.1.refs_0_ = bf16[16,128,128]{2,1,0:T(8,128)(2,1)S(1)} collective-permute-done((bf16[16,128,128]{2,1,0:T(8,128)(2,1)S(1)}, bf16[16,128,128]{2,1,0:T(8,128)(2,1)S(1)}, u32[]{:S(2)}, u32[]{:S(2)}) %collective-permute-start.1) | collective-permute-done | bytes 524320 | tf_op jit(solution)/shard_map/ppermute | solution.py:39
  62.4 1.3 collective-permute-done.2.refs_1_
  63.6 2.3 %tiles.3 = (bf16[16,128,128]{2,1,0:T(8,128)(2,1)S(1)}, bf16[16,128,128]{2,1,0:T(8,128)(2,1)S(1)}, bf16[32,128,128]{2,1,0:T(8,128)(2,1)S(1)}) custom-call(s32[4]{0:T(128)S(1)} %pad_add_fusion.ids_ref.refs_0_, s32[1,112]{1,0:T(1,128)S(1)} %copy-done.10, s32[1,112]{1,0:T(1,128)S(1)} %copy-done.11, s32[1,64]{1,0:T(1,128)S(1)} %copy-done.9, ...), custom_call_target="tpu_custom_call" | custom-call | flops 117440512 | bytes 2097152 | tf_op jit(solution)/shard_map/tiles/pallas_call | solution.py:300
  65.9 0.0 copy-start.6
  65.9 3.8 %collective-permute-start.4 = (bf16[16,128,128]{2,1,0:T(8,128)(2,1)S(1)}, bf16[16,128,128]{2,1,0:T(8,128)(2,1)S(1)}, u32[]{:S(2)}, u32[]{:S(2)}) collective-permute-start(bf16[16,128,128]{2,1,0:T(8,128)(2,1)S(1)} %get-tuple-element.41), channel_id=1, source_target_pairs={{0,384},{128,256},{256,128},{384,0},{1,385},{129,257},{257,129},{3... | collective-permute-start | bytes 1572872 | tf_op jit(solution)/shard_map/ppermute | solution.py:39
  69.8 1.9 %collective-permute-start.5 = (bf16[16,128,128]{2,1,0:T(8,128)(2,1)S(1)}, bf16[16,128,128]{2,1,0:T(8,128)(2,1)S(1)}, u32[]{:S(2)}, u32[]{:S(2)}) collective-permute-start(bf16[16,128,128]{2,1,0:T(8,128)(2,1)S(1)} %get-tuple-element.42), channel_id=1, source_target_pairs={{0,128},{128,0},{256,384},{384,256},{1,129},{129,1},{257,385},{385... | collective-permute-start | bytes 1572872 | tf_op jit(solution)/shard_map/ppermute | solution.py:39
  71.7 3.1 %collective-permute-done.3 = bf16[16,128,128]{2,1,0:T(8,128)(2,1)S(1)} collective-permute-done((bf16[16,128,128]{2,1,0:T(8,128)(2,1)S(1)}, bf16[16,128,128]{2,1,0:T(8,128)(2,1)S(1)}, u32[]{:S(2)}, u32[]{:S(2)}) %collective-permute-start.3) | collective-permute-done | bytes 524320 | tf_op jit(solution)/shard_map/ppermute | solution.py:39
  74.8 0.0 collective-permute-done.6
  74.8 10.0 %collective-permute-done.4 = bf16[16,128,128]{2,1,0:T(8,128)(2,1)S(1)} collective-permute-done((bf16[16,128,128]{2,1,0:T(8,128)(2,1)S(1)}, bf16[16,128,128]{2,1,0:T(8,128)(2,1)S(1)}, u32[]{:S(2)}, u32[]{:S(2)}) %collective-permute-start.4) | collective-permute-done | bytes 524320 | tf_op jit(solution)/shard_map/ppermute | solution.py:39
  84.8 0.5 collective-permute-done.5
  85.4 0.9 y_sum.1
  86.3 3.5 %collective-permute-start.7 = (bf16[8,2,128,128]{3,2,1,0:T(8,128)(2,1)S(1)}, bf16[8,2,128,128]{3,2,1,0:T(8,128)(2,1)S(1)}, u32[]{:S(2)}, u32[]{:S(2)}) collective-permute-start(bf16[8,2,128,128]{3,2,1,0:T(8,128)(2,1)S(1)} %get-tuple-element.47), channel_id=1, source_target_pairs={{0,8},{8,0},{1,9},{9,1},{2,10},{10,2},{3,11},{11,3},{4,12},{12,4},... | collective-permute-start | bytes 1572872 | tf_op jit(solution)/shard_map/ppermute | solution.py:39
  89.8 4.3 %all-gather.3.cloned.1.call-done.deltas_ref = bf16[128,128,128]{2,1,0:T(8,128)(2,1)} async-done(((bf16[8,128,128]{2,1,0:T(8,128)(2,1)}), bf16[128,128,128]{2,1,0:T(8,128)(2,1)}) %all-gather.3.cloned.1.call-update) | async-done | bytes 4194320 | tf_op jit(solution)/shard_map/all_gather | solution.py:285
  94.1 4.5 %contribs.1 = (bf16[64,8192]{1,0:T(8,128)(2,1)S(1)}, bf16[64,8192]{1,0:T(8,128)(2,1)S(1)}) custom-call(s32[1,112]{1,0:T(1,128)S(1)} %copy-done.10, s32[1,112]{1,0:T(1,128)S(1)} %copy-done.11, s32[1,64]{1,0:T(1,128)S(1)} %copy-done.9, bf16[14,128,128]{2,1,0:T(8,128)(2,1)S(1)} %copy-done.6, bf16[128,128,128]{2,1,0:T(8,128)(2,1)} %all-gather.3.cloned.1.call-done.deltas_ref), custom_call_target="tpu_custom_call" | custom-call | bytes 4096 | tf_op jit(solution)/shard_map/contribs/pallas_call | solution.py:327
  98.6 0.0 copy-start.12
  98.6 1.0 copy-done.12
  99.6 6.5 %collective-permute-done.7.taken_ref = bf16[8,2,128,128]{3,2,1,0:T(8,128)(2,1)S(1)} collective-permute-done((bf16[8,2,128,128]{3,2,1,0:T(8,128)(2,1)S(1)}, bf16[8,2,128,128]{3,2,1,0:T(8,128)(2,1)S(1)}, u32[]{:S(2)}, u32[]{:S(2)}) %collective-permute-start.7) | collective-permute-done | bytes 524320 | tf_op jit(solution)/shard_map/ppermute | solution.py:39
  106.0 0.9 pair_sum.1
  107.0 9.6 %all-to-all-start.2 = ((bf16[8,2,128,128]{3,2,1,0:T(8,128)(2,1)}), bf16[8,2,128,128]{3,2,1,0:T(8,128)(2,1)S(1)}, u32[]{:S(2)}, u32[]{:S(2)}) async-start(bf16[8,2,128,128]{3,2,1,0:T(8,128)(2,1)} %pair_sum.1), calls=%async_computation.2 | async-start | bytes 1048576 | tf_op jit(solution)/shard_map/all_to_all | solution.py:43
  116.6 0.0 all-gather.5.cloned.1.call-start
  116.6 4.6 %collective-permute-start.8 = (bf16[64,8192]{1,0:T(8,128)(2,1)S(1)}, bf16[64,8192]{1,0:T(8,128)(2,1)S(1)}, u32[]{:S(2)}, u32[]{:S(2)}) collective-permute-start(bf16[64,8192]{1,0:T(8,128)(2,1)S(1)} %copy-done.13), channel_id=1, source_target_pairs={{0,1},{1,0},{2,3},{3,2},{4,5},{5,4},{6,7},{7,6},{8,9},{9,8},{10,11... | collective-permute-start | bytes 3145736 | tf_op jit(solution)/shard_map/ppermute | solution.py:39
  121.2 2.3 %collective-permute-done.8 = bf16[64,8192]{1,0:T(8,128)(2,1)S(1)} collective-permute-done((bf16[64,8192]{1,0:T(8,128)(2,1)S(1)}, bf16[64,8192]{1,0:T(8,128)(2,1)S(1)}, u32[]{:S(2)}, u32[]{:S(2)}) %collective-permute-start.8) | collective-permute-done | bytes 1048608 | tf_op jit(solution)/shard_map/ppermute | solution.py:39
  123.5 0.8 core_sum.1
  124.3 3.5 %collective-permute-start.9 = (bf16[16,8192]{1,0:T(8,128)(2,1)S(1)}, bf16[16,8192]{1,0:T(8,128)(2,1)S(1)}, u32[]{:S(2)}, u32[]{:S(2)}) collective-permute-start(bf16[16,8192]{1,0:T(8,128)(2,1)S(1)} %get-tuple-element.54), channel_id=1, source_target_pairs={{0,4},{2,6},{4,0},{6,2},{1,5},{3,7},{5,1},{7,3},{8,12},{10,14},{12... | collective-permute-start | bytes 786440 | tf_op jit(solution)/shard_map/ppermute | solution.py:39
  127.8 2.7 %collective-permute-start.10 = (bf16[16,8192]{1,0:T(8,128)(2,1)S(1)}, bf16[16,8192]{1,0:T(8,128)(2,1)S(1)}, u32[]{:S(2)}, u32[]{:S(2)}) collective-permute-start(bf16[16,8192]{1,0:T(8,128)(2,1)S(1)} %get-tuple-element.55), channel_id=1, source_target_pairs={{0,2},{2,0},{4,6},{6,4},{1,3},{3,1},{5,7},{7,5},{8,10},{10,8},{12,... | collective-permute-start | bytes 786440 | tf_op jit(solution)/shard_map/ppermute | solution.py:39
  130.5 2.9 %collective-permute-start.11 = (bf16[16,8192]{1,0:T(8,128)(2,1)S(1)}, bf16[16,8192]{1,0:T(8,128)(2,1)S(1)}, u32[]{:S(2)}, u32[]{:S(2)}) collective-permute-start(bf16[16,8192]{1,0:T(8,128)(2,1)S(1)} %get-tuple-element.56), channel_id=1, source_target_pairs={{0,6},{2,4},{4,2},{6,0},{1,7},{3,5},{5,3},{7,1},{8,14},{10,12},{12... | collective-permute-start | bytes 786440 | tf_op jit(solution)/shard_map/ppermute | solution.py:39
  133.4 9.1 %all-to-all-done.2.arrived_ref = bf16[8,2,128,128]{3,2,1,0:T(8,128)(2,1)S(1)} async-done(((bf16[8,2,128,128]{3,2,1,0:T(8,128)(2,1)}), bf16[8,2,128,128]{3,2,1,0:T(8,128)(2,1)S(1)}, u32[]{:S(2)}, u32[]{:S(2)}) %all-to-all-start.2) | async-done | bytes 524320 | tf_op jit(solution)/shard_map/all_to_all | solution.py:43
  142.5 0.8 own_grad.1
  143.3 0.0 collective-permute-done.11
  143.3 0.8 add_convert_fusion
  144.2 0.0 all-gather.5.cloned.1.call-update
  144.2 20.3 %all_to_all.27.arrived_ref = f32[32,8,128]{2,1,0:T(8,128)S(1)} all-to-all(f32[32,8,128]{2,1,0:T(8,128)S(1)} %get-tuple-element.57), channel_id=1, replica_groups=mesh['y'=4,'m'=8,'p'=2,'x'=4,'core'=2] {'y','x','core'}, dimensions={0} | all-to-all | bytes 262144 | tf_op jit(solution)/shard_map/all_to_all | solution.py:43
  164.5 0.7 relay.1
  165.2 4.3 %all-to-all-start.4 = ((f32[16,8,128]{2,1,0:T(8,128)}), f32[16,8,128]{2,1,0:T(8,128)S(1)}, u32[]{:S(2)}, u32[]{:S(2)}) async-start(f32[16,8,128]{2,1,0:T(8,128)} %relay.1), calls=%async_computation.4 | async-start | bytes 131072 | tf_op jit(solution)/shard_map/all_to_all | solution.py:43
  169.4 0.0 copy-start.1
  169.5 0.0 copy-start.7
  169.5 0.0 copy-start.8
  169.5 7.0 %all-gather.5.cloned.1.call-done.in_ref = bf16[128,8192]{1,0:T(8,128)(2,1)} async-done(((bf16[16,8192]{1,0:T(8,128)(2,1)}), bf16[128,8192]{1,0:T(8,128)(2,1)}) %all-gather.5.cloned.1.call-update) | async-done | bytes 2097168 | tf_op jit(solution)/shard_map/all_gather | solution.py:361
  176.5 2.4 %result.1 = bf16[128,8192]{1,0:T(8,128)(2,1)} custom-call(bf16[128,8192]{1,0:T(8,128)(2,1)} %all-gather.5.cloned.1.call-done.in_ref), custom_call_target="tpu_custom_call" | custom-call | bytes 4194304 | tf_op jit(solution)/shard_map/result/pallas_call | solution.py:362
  179.0 2.1 %all-to-all-done.4.refs_2_ = f32[16,8,128]{2,1,0:T(8,128)S(1)} async-done(((f32[16,8,128]{2,1,0:T(8,128)}), f32[16,8,128]{2,1,0:T(8,128)S(1)}, u32[]{:S(2)}, u32[]{:S(2)}) %all-to-all-start.4) | async-done | bytes 65568 | tf_op jit(solution)/shard_map/all_to_all | solution.py:43
  181.0 1.5 adam.1
  (17 shorter events, 0.1 us)
Async XLA Ops:
  7.2 87.0 %all-gather.3.cloned.1.call-start = ((), (), s32[]{:S(2)}) async-start(), calls=%async_computation.5 | async-start | bytes 4456448 | tf_op jit(solution)/shard_map/all_gather | solution.py:285
  7.2 0.9 copy-start
  8.3 33.7 %copy-start.2 = (bf16[128,1792]{1,0:T(8,128)(2,1)S(1)}, bf16[128,1792]{1,0:T(8,128)(2,1)}, u32[]{:S(2)}) copy-start(bf16[128,1792]{1,0:T(8,128)(2,1)} %gate_ref.1) | copy-start | bytes 1376260
  8.3 33.6 %copy-start.3 = (bf16[128,1792]{1,0:T(8,128)(2,1)S(1)}, bf16[128,1792]{1,0:T(8,128)(2,1)}, u32[]{:S(2)}) copy-start(bf16[128,1792]{1,0:T(8,128)(2,1)} %up_ref.1) | copy-start | bytes 1376260
  8.3 33.6 %copy-start.4 = (bf16[128,1792]{1,0:T(8,128)(2,1)S(1)}, bf16[128,1792]{1,0:T(8,128)(2,1)}, u32[]{:S(2)}) copy-start(bf16[128,1792]{1,0:T(8,128)(2,1)} %hidden_ref.1) | copy-start | bytes 1376260
  18.9 25.2 %copy-start.9 = (s32[1,64]{1,0:T(1,128)S(1)}, s32[1,64]{1,0:T(1,128)}, u32[]{:S(2)}) copy-start(s32[1,64]{1,0:T(1,128)} %refs_1_.1) | copy-start | bytes 772
  18.9 25.2 %copy-start.10 = (s32[1,112]{1,0:T(1,128)S(1)}, s32[1,112]{1,0:T(1,128)}, u32[]{:S(2)}) copy-start(s32[1,112]{1,0:T(1,128)} %rows_ref.5) | copy-start | bytes 1348
  18.9 25.2 %copy-start.11 = (s32[1,112]{1,0:T(1,128)S(1)}, s32[1,112]{1,0:T(1,128)}, u32[]{:S(2)}) copy-start(s32[1,112]{1,0:T(1,128)} %cols_ref.5) | copy-start | bytes 1348
  34.0 10.1 %collective-permute-start = (bf16[4,128,1024]{2,1,0:T(8,128)(2,1)S(1)}, bf16[4,128,1024]{2,1,0:T(8,128)(2,1)S(1)}, u32[]{:S(2)}, u32[]{:S(2)}) collective-permute-start(bf16[4,128,1024]{2,1,0:T(8,128)(2,1)S(1)} %all_to_all.26.own_ref), channel_id=1, source_target_pairs={{0,1},{1,0},{2,3},{3,2},{4,5},{5,4},{6,7},{7,6},{8,9},{9,8},{10,11... | collective-permute-start | bytes 3145736 | tf_op jit(solution)/shard_map/ppermute | solution.py:39
  43.0 22.9 %copy-start.5 = (bf16[14,128,128]{2,1,0:T(8,128)(2,1)}, bf16[14,128,128]{2,1,0:T(8,128)(2,1)S(1)}, u32[]{:S(2)}) copy-start(bf16[14,128,128]{2,1,0:T(8,128)(2,1)S(1)} %get-tuple-element.48.grads_ref) | copy-start | bytes 1376260
  46.0 16.3 %collective-permute-start.1 = (bf16[16,128,128]{2,1,0:T(8,128)(2,1)S(1)}, bf16[16,128,128]{2,1,0:T(8,128)(2,1)S(1)}, u32[]{:S(2)}, u32[]{:S(2)}) collective-permute-start(bf16[16,128,128]{2,1,0:T(8,128)(2,1)S(1)} %get-tuple-element.37), channel_id=1, source_target_pairs={{0,384},{128,256},{256,128},{384,0},{1,385},{129,257},{257,129},{3... | collective-permute-start | bytes 1572872 | tf_op jit(solution)/shard_map/ppermute | solution.py:39
  48.8 14.8 %collective-permute-start.2 = (bf16[16,128,128]{2,1,0:T(8,128)(2,1)S(1)}, bf16[16,128,128]{2,1,0:T(8,128)(2,1)S(1)}, u32[]{:S(2)}, u32[]{:S(2)}) collective-permute-start(bf16[16,128,128]{2,1,0:T(8,128)(2,1)S(1)} %get-tuple-element.38), channel_id=1, source_target_pairs={{0,128},{128,0},{256,384},{384,256},{1,129},{129,1},{257,385},{385... | collective-permute-start | bytes 1572872 | tf_op jit(solution)/shard_map/ppermute | solution.py:39
  50.7 24.1 %collective-permute-start.3 = (bf16[16,128,128]{2,1,0:T(8,128)(2,1)S(1)}, bf16[16,128,128]{2,1,0:T(8,128)(2,1)S(1)}, u32[]{:S(2)}, u32[]{:S(2)}) collective-permute-start(bf16[16,128,128]{2,1,0:T(8,128)(2,1)S(1)} %get-tuple-element.40), channel_id=1, source_target_pairs={{0,128},{128,0},{256,384},{384,256},{1,129},{129,1},{257,385},{385... | collective-permute-start | bytes 1572872 | tf_op jit(solution)/shard_map/ppermute | solution.py:39
  54.1 20.7 %collective-permute-start.6 = (bf16[16,128,128]{2,1,0:T(8,128)(2,1)S(1)}, bf16[16,128,128]{2,1,0:T(8,128)(2,1)S(1)}, u32[]{:S(2)}, u32[]{:S(2)}) collective-permute-start(bf16[16,128,128]{2,1,0:T(8,128)(2,1)S(1)} %get-tuple-element.43), channel_id=1, source_target_pairs={{0,384},{128,256},{256,128},{384,0},{1,385},{129,257},{257,129},{3... | collective-permute-start | bytes 1572872 | tf_op jit(solution)/shard_map/ppermute | solution.py:39
  65.9 28.2 %copy-start.6 = (bf16[14,128,128]{2,1,0:T(8,128)(2,1)S(1)}, bf16[14,128,128]{2,1,0:T(8,128)(2,1)}, u32[]{:S(2)}) copy-start(bf16[14,128,128]{2,1,0:T(8,128)(2,1)} %copy-done.5) | copy-start | bytes 1376260
  65.9 18.9 %collective-permute-start.4 = (bf16[16,128,128]{2,1,0:T(8,128)(2,1)S(1)}, bf16[16,128,128]{2,1,0:T(8,128)(2,1)S(1)}, u32[]{:S(2)}, u32[]{:S(2)}) collective-permute-start(bf16[16,128,128]{2,1,0:T(8,128)(2,1)S(1)} %get-tuple-element.41), channel_id=1, source_target_pairs={{0,384},{128,256},{256,128},{384,0},{1,385},{129,257},{257,129},{3... | collective-permute-start | bytes 1572872 | tf_op jit(solution)/shard_map/ppermute | solution.py:39
  69.8 15.6 %collective-permute-start.5 = (bf16[16,128,128]{2,1,0:T(8,128)(2,1)S(1)}, bf16[16,128,128]{2,1,0:T(8,128)(2,1)S(1)}, u32[]{:S(2)}, u32[]{:S(2)}) collective-permute-start(bf16[16,128,128]{2,1,0:T(8,128)(2,1)S(1)} %get-tuple-element.42), channel_id=1, source_target_pairs={{0,128},{128,0},{256,384},{384,256},{1,129},{129,1},{257,385},{385... | collective-permute-start | bytes 1572872 | tf_op jit(solution)/shard_map/ppermute | solution.py:39
  86.3 19.7 %collective-permute-start.7 = (bf16[8,2,128,128]{3,2,1,0:T(8,128)(2,1)S(1)}, bf16[8,2,128,128]{3,2,1,0:T(8,128)(2,1)S(1)}, u32[]{:S(2)}, u32[]{:S(2)}) collective-permute-start(bf16[8,2,128,128]{3,2,1,0:T(8,128)(2,1)S(1)} %get-tuple-element.47), channel_id=1, source_target_pairs={{0,8},{8,0},{1,9},{9,1},{2,10},{10,2},{3,11},{11,3},{4,12},{12,4},... | collective-permute-start | bytes 1572872 | tf_op jit(solution)/shard_map/ppermute | solution.py:39
  98.6 1.0 copy-start.12
  106.0 10.6 %copy-start.13 = (bf16[64,8192]{1,0:T(8,128)(2,1)S(1)}, bf16[64,8192]{1,0:T(8,128)(2,1)}, u32[]{:S(2)}) copy-start(bf16[64,8192]{1,0:T(8,128)(2,1)} %copy-done.12) | copy-start | bytes 3145732
  107.0 35.6 %all-to-all-start.2 = ((bf16[8,2,128,128]{3,2,1,0:T(8,128)(2,1)}), bf16[8,2,128,128]{3,2,1,0:T(8,128)(2,1)S(1)}, u32[]{:S(2)}, u32[]{:S(2)}) async-start(bf16[8,2,128,128]{3,2,1,0:T(8,128)(2,1)} %pair_sum.1), calls=%async_computation.2 | async-start | bytes 1048576 | tf_op jit(solution)/shard_map/all_to_all | solution.py:43
  116.6 59.9 %all-gather.5.cloned.1.call-start = ((), (), s32[]{:S(2)}) async-start(), calls=%async_computation.6 | async-start | bytes 2359296 | tf_op jit(solution)/shard_map/all_gather | solution.py:361
  116.6 6.8 %collective-permute-start.8 = (bf16[64,8192]{1,0:T(8,128)(2,1)S(1)}, bf16[64,8192]{1,0:T(8,128)(2,1)S(1)}, u32[]{:S(2)}, u32[]{:S(2)}) collective-permute-start(bf16[64,8192]{1,0:T(8,128)(2,1)S(1)} %copy-done.13), channel_id=1, source_target_pairs={{0,1},{1,0},{2,3},{3,2},{4,5},{5,4},{6,7},{7,6},{8,9},{9,8},{10,11... | collective-permute-start | bytes 3145736 | tf_op jit(solution)/shard_map/ppermute | solution.py:39
  124.3 19.0 %collective-permute-start.9 = (bf16[16,8192]{1,0:T(8,128)(2,1)S(1)}, bf16[16,8192]{1,0:T(8,128)(2,1)S(1)}, u32[]{:S(2)}, u32[]{:S(2)}) collective-permute-start(bf16[16,8192]{1,0:T(8,128)(2,1)S(1)} %get-tuple-element.54), channel_id=1, source_target_pairs={{0,4},{2,6},{4,0},{6,2},{1,5},{3,7},{5,1},{7,3},{8,12},{10,14},{12... | collective-permute-start | bytes 786440 | tf_op jit(solution)/shard_map/ppermute | solution.py:39
  127.8 15.5 %collective-permute-start.10 = (bf16[16,8192]{1,0:T(8,128)(2,1)S(1)}, bf16[16,8192]{1,0:T(8,128)(2,1)S(1)}, u32[]{:S(2)}, u32[]{:S(2)}) collective-permute-start(bf16[16,8192]{1,0:T(8,128)(2,1)S(1)} %get-tuple-element.55), channel_id=1, source_target_pairs={{0,2},{2,0},{4,6},{6,4},{1,3},{3,1},{5,7},{7,5},{8,10},{10,8},{12,... | collective-permute-start | bytes 786440 | tf_op jit(solution)/shard_map/ppermute | solution.py:39
  130.5 12.8 %collective-permute-start.11 = (bf16[16,8192]{1,0:T(8,128)(2,1)S(1)}, bf16[16,8192]{1,0:T(8,128)(2,1)S(1)}, u32[]{:S(2)}, u32[]{:S(2)}) collective-permute-start(bf16[16,8192]{1,0:T(8,128)(2,1)S(1)} %get-tuple-element.56), channel_id=1, source_target_pairs={{0,6},{2,4},{4,2},{6,0},{1,7},{3,5},{5,3},{7,1},{8,14},{10,12},{12... | collective-permute-start | bytes 786440 | tf_op jit(solution)/shard_map/ppermute | solution.py:39
  165.2 15.9 %all-to-all-start.4 = ((f32[16,8,128]{2,1,0:T(8,128)}), f32[16,8,128]{2,1,0:T(8,128)S(1)}, u32[]{:S(2)}, u32[]{:S(2)}) async-start(f32[16,8,128]{2,1,0:T(8,128)} %relay.1), calls=%async_computation.4 | async-start | bytes 131072 | tf_op jit(solution)/shard_map/all_to_all | solution.py:43
  169.4 11.6 %copy-start.1 = (f32[1,2,128,128]{3,2,1,0:T(8,128)S(1)}, f32[1,2,128,128]{3,2,1,0:T(8,128)}, u32[]{:S(2)}) copy-start(f32[1,2,128,128]{3,2,1,0:T(8,128)} %refs_4_.1) | copy-start | bytes 393220
  169.5 11.6 %copy-start.7 = (f32[1,2,128,128]{3,2,1,0:T(8,128)S(1)}, f32[1,2,128,128]{3,2,1,0:T(8,128)}, u32[]{:S(2)}) copy-start(f32[1,2,128,128]{3,2,1,0:T(8,128)} %refs_5_.1) | copy-start | bytes 393220
  169.5 11.6 %copy-start.8 = (f32[1,2,128,128]{3,2,1,0:T(8,128)S(1)}, f32[1,2,128,128]{3,2,1,0:T(8,128)}, u32[]{:S(2)}) copy-start(f32[1,2,128,128]{3,2,1,0:T(8,128)} %refs_6_.1) | copy-start | bytes 393220
Sparse Core Ops, SparseCore 0:
  19.0 75.0 all-gather.2
  144.3 32.1 all-gather.4
